TPU v7x, 32 devices: a whole 2x2x4 slice. The times are simulated.
32 devices in a mesh: pipe: 2 (over x), seq: 4 (over z), dp: 4 (over y, core).
Axes of the slice: x: 2, y: 2, z: 4, core: 2. Of those that a mesh axis runs over, the one named last changes fastest.
Arguments:
- queries: bfloat16 [2, 4, 4, 384, 1536], P('pipe', 'dp', 'seq'), may hold values from -18 to 18
- keys: bfloat16 [2, 4, 4, 384, 1536], P('pipe', 'dp', 'seq'), may hold values from -18 to 18
- values: bfloat16 [2, 4, 4, 384, 1536], P('pipe', 'dp', 'seq'), may hold values from -6 to 6
- grad_out: bfloat16 [2, 4, 4, 384, 1536], P('pipe', 'dp', 'seq'), may hold values from -20 to 20
- norm_gains: float32 [2, 2, 128], P('pipe'), may hold values from 0.5 to 1.5
- kv_tiles: int32 [2, 4, 4, 3], P('pipe', 'dp', 'seq'), may hold values from -1 to 3, as said below
Outputs:
- qkv_grad: bfloat16 [2, 3, 4, 4, 384, 1536], P('pipe', None, 'dp', 'seq')
- gain_grads: float32 [2, 2, 128], P('pipe')
Inputs may be any that keep to these rules, and one draw needn't show every extreme that they name: `kv_tiles`: tile t covers frame tile t // 1 and spatial tile t % 1. The row of tile t names tile t itself and some of the other tiles of frame tiles t - 1, t // 1 and t + 1 inside the sample, each at most once, in some order; its other entries are -1.
All inputs are finite; a program needn't handle non-finite values.
Results may differ from a plain program's by a relative error of at most 0.007.
Values may be sent and summed in bfloat16 or wider, within the bound.
No kernel may reach another device: no remote copies, remote signals or barrier semaphores. Data moves between devices by JAX's collectives and lax.ppermute only.
A program may use at most 256 MiB of HBM per device.

v0:
```python
import math

import jax
import jax.numpy as jnp
from jax import lax
from jax.sharding import PartitionSpec as P

HEADS = 12
HEAD_DIM = 128


epsilon = 1e-06


def padded(shard, sides, width):
    for axis, dim in sides:
        size, length = (lax.axis_size(axis), shard.shape[dim])
        up = [(i, (i + 1) % size) for i in range(size - 1)]
        down = [(j, i) for i, j in up]
        last = lax.slice_in_dim(shard, length - width, length, axis=dim)
        initial = lax.slice_in_dim(shard, 0, width, axis=dim)
        before = lax.ppermute(last, axis, up)
        after = lax.ppermute(initial, axis, down)
        shard = jnp.concatenate([before, shard, after], axis=dim)
    return shard


def passed_along(value, axis, steps):
    count = lax.axis_size(axis)
    initial, last = (max(0, -steps), min(count, count - steps))
    return lax.ppermute(value, axis, [(source, source + steps) for source in range(initial, last)])


def passed_along_2(value, axis, steps):
    count = lax.axis_size(axis)
    pairs = [(source, (source + steps) % count) for source in range(count)]
    return lax.ppermute(value, axis, pairs)


def normalize(source, gain_row):
    floats = source.astype(jnp.float32).reshape(source.shape[:-1] + (HEADS, HEAD_DIM))
    scaled = lax.rsqrt(jnp.mean(floats * floats, axis=-1, keepdims=True) + epsilon)
    normed = (floats * scaled * gain_row).astype(jnp.bfloat16).reshape(source.shape)
    return (normed, floats, scaled)


def norm_back(grad_hat, floats, scaled, gain_row):
    projected = jnp.sum(gain_row * grad_hat * floats, axis=-1, keepdims=True)
    gradient = scaled * gain_row * grad_hat - scaled**3 * floats * projected / HEAD_DIM
    gain_part = jnp.sum((grad_hat * floats * scaled).reshape(-1, HEAD_DIM), axis=0)
    return (gradient.reshape(gradient.shape[:-2] + (HEADS * HEAD_DIM,)), gain_part)


def score_block(query_head, grad_head, key_head, value_head, key_mask):
    root_scale = HEAD_DIM ** (-0.5)
    scores = (
        jnp.einsum("nqhd,nkhd->nhqk", query_head, key_head, preferred_element_type=jnp.float32)
        * root_scale
    )
    exp_scores = jnp.exp(scores) * key_mask[:, None, None, :]
    grad_attn = jnp.einsum(
        "nqhd,nkhd->nhqk", grad_head, value_head, preferred_element_type=jnp.float32
    )
    totals = jnp.sum(exp_scores, axis=-1, keepdims=True)
    attention = exp_scores / totals
    deltas = jnp.sum(attention * grad_attn, axis=-1, keepdims=True)
    dscore = (attention * (grad_attn - deltas)).astype(jnp.bfloat16)
    return (dscore, attention.astype(jnp.bfloat16), totals, deltas)


def spread(slot_grad, targets, list_slots, target_span):
    row_count, key_rows, head_count, head_width = slot_grad.shape
    shaped = slot_grad.reshape(
        row_count * list_slots, key_rows // list_slots, head_count * head_width
    )
    flat_targets = targets.reshape(-1)
    placed = jnp.where(flat_targets >= 0, flat_targets, target_span)
    totals = jnp.zeros(
        (target_span + 1, key_rows // list_slots, head_count * head_width), jnp.float32
    )
    return totals.at[placed].add(shaped)[:target_span]


def tile_pass(
    query_hat, grad_in, key_gathered, value_gathered, key_mask, targets, list_slots, target_span
):
    row_count, tile_rows, lane_total = query_hat.shape
    key_rows = key_gathered.shape[1]
    root_scale = HEAD_DIM ** (-0.5)
    query_parts, key_parts, value_parts, total_parts, delta_parts = ([], [], [], [], [])
    for first_head in range(0, HEADS, 2):
        lane_span = slice(first_head * HEAD_DIM, (first_head + 2) * HEAD_DIM)
        query_head = query_hat[:, :, lane_span].reshape(row_count, tile_rows, 2, HEAD_DIM)
        grad_head = grad_in[:, :, lane_span].reshape(row_count, tile_rows, 2, HEAD_DIM)
        key_head = key_gathered[:, :, lane_span].reshape(row_count, key_rows, 2, HEAD_DIM)
        value_head = value_gathered[:, :, lane_span].reshape(row_count, key_rows, 2, HEAD_DIM)
        dscore, attn_low, totals, deltas = score_block(
            query_head, grad_head, key_head, value_head, key_mask
        )
        query_parts.append(
            jnp.einsum("nhqk,nkhd->nqhd", dscore, key_head, preferred_element_type=jnp.float32)
            * root_scale
        )
        key_slot = (
            jnp.einsum("nhqk,nqhd->nkhd", dscore, query_head, preferred_element_type=jnp.float32)
            * root_scale
        )
        value_slot = jnp.einsum(
            "nhqk,nqhd->nkhd", attn_low, grad_head, preferred_element_type=jnp.float32
        )
        key_parts.append(spread(key_slot, targets, list_slots, target_span))
        value_parts.append(spread(value_slot, targets, list_slots, target_span))
        total_parts.append(totals[..., 0])
        delta_parts.append(deltas[..., 0])
    query_grads = jnp.concatenate(query_parts, axis=2)
    return (
        query_grads,
        jnp.concatenate(key_parts, axis=-1),
        jnp.concatenate(value_parts, axis=-1),
        jnp.concatenate(total_parts, axis=1),
        jnp.concatenate(delta_parts, axis=1),
    )


def local(queries, keys, values, grad_out, norm_gains, kv_tiles):
    query_in = queries[0, 0]
    key_in = keys[0, 0]
    value_in = values[0, 0]
    grad_in = grad_out[0, 0]
    gain_rows = norm_gains[0]
    tile_lists = kv_tiles[0, 0]
    tiles_here, tile_rows, lane_total = query_in.shape
    list_slots = tile_lists.shape[1]
    position = lax.axis_index("seq")
    seq_count = lax.axis_size("seq")
    query_hat, query_floats, query_scale = normalize(query_in, gain_rows[0])
    key_hat, key_floats, key_scale = normalize(key_in, gain_rows[1])
    rim_pairs = padded(jnp.stack([key_hat, value_in]), (("seq", 1),), tiles_here)
    live_slots = tile_lists >= 0
    key_mask = jnp.repeat(live_slots.astype(jnp.float32), tile_rows, axis=1)
    local_ids = tile_lists - (position - 1) * tiles_here
    fetch_ids = jnp.clip(local_ids, 0, 3 * tiles_here - 1)
    key_gathered = rim_pairs[0][fetch_ids].reshape(tiles_here, list_slots * tile_rows, lane_total)
    value_gathered = rim_pairs[1][fetch_ids].reshape(tiles_here, list_slots * tile_rows, lane_total)
    targets = jnp.where(live_slots, local_ids, -1)
    target_span = 3 * tiles_here
    query_hat_grad, key_acc, value_acc, totals, deltas = tile_pass(
        query_hat, grad_in, key_gathered, value_gathered, key_mask, targets, list_slots, target_span
    )
    query_grad, query_gain = norm_back(query_hat_grad, query_floats, query_scale, gain_rows[0])
    query_low = query_grad.astype(jnp.bfloat16)
    from_right = passed_along(jnp.stack([key_acc[:tiles_here], value_acc[:tiles_here]]), "seq", -1)
    from_left = passed_along(
        jnp.stack([key_acc[2 * tiles_here :], value_acc[2 * tiles_here :]]), "seq", 1
    )
    key_hat_grad = key_acc[tiles_here : 2 * tiles_here] + from_right[0] + from_left[0]
    value_grad = value_acc[tiles_here : 2 * tiles_here] + from_right[1] + from_left[1]
    key_grad, key_gain = norm_back(
        key_hat_grad.reshape(tiles_here, tile_rows, HEADS, HEAD_DIM),
        key_floats,
        key_scale,
        gain_rows[1],
    )
    summed = lax.psum(jnp.stack([query_gain, key_gain]), ("seq", "dp"))
    gain_grads = summed / math.sqrt(
        lax.axis_size("dp") * seq_count * tiles_here * tile_rows * HEADS
    )
    key_low = key_grad.astype(jnp.bfloat16)
    value_low = value_grad.astype(jnp.bfloat16)
    passed = passed_along_2(jnp.stack([query_low, key_low, value_low]), "pipe", -1)
    return (passed[None, :, None], gain_grads[None])


def solution(mesh):
    placed = (
        P("pipe", "dp", "seq", None, None),
        P("pipe", "dp", "seq", None, None),
        P("pipe", "dp", "seq", None, None),
        P("pipe", "dp", "seq", None, None),
        P("pipe", None, None),
        P("pipe", "dp", "seq", None),
    )
    return jax.shard_map(
        local,
        mesh=mesh,
        in_specs=placed,
        out_specs=(P("pipe", None, "dp", "seq", None, None), P("pipe", None, None)),
        check_vma=False,
    )
```

profile of v0, /device:TPU:0, one launch (start us, length us, event | category | flops | bytes accessed | tf_op | source)
XLA Modules:
  0.0 616.2 jit_solution(8690754736987637561)
XLA Ops:
  10.4 6.5 %collective-permute-start = (bf16[2,1,384,1536]{3,2,1,0:T(8,128)(2,1)}, bf16[2,1,384,1536]{3,2,1,0:T(8,128)(2,1)}, u32[]{:S(2)}, u32[]{:S(2)}) collective-permute-start(bf16[2,1,384,1536]{3,2,1,0:T(8,128)(2,1)} %pad_maximum_fusion.4), channel_id=1, source_target_pairs={{0,4},{4,8},{8,12},{1,5},{5,9},{9,13},{2,6},{6,10},{10,14},{3,7},{... | collective-permute-start | bytes 7077896 | tf_op jit(solution)/shard_map/ppermute | solution.py:22
  41.5 24.8 %collective-permute-done = bf16[2,1,384,1536]{3,2,1,0:T(8,128)(2,1)} collective-permute-done((bf16[2,1,384,1536]{3,2,1,0:T(8,128)(2,1)}, bf16[2,1,384,1536]{3,2,1,0:T(8,128)(2,1)}, u32[]{:S(2)}, u32[]{:S(2)}) %collective-permute-start) | collective-permute-done | bytes 2359328 | tf_op jit(solution)/shard_map/ppermute | solution.py:22
  66.3 5.5 collective-permute-done.1
  79.1 4.7 gather_fusion.1
  88.4 4.7 gather_fusion
  102.3 5.2 multiply_reduce_fusion.5
  107.6 4.0 convolution_bitcast_fusion.11
  123.0 5.2 multiply_reduce_fusion.4
  128.2 4.0 convolution_bitcast_fusion.10
  143.7 5.2 multiply_reduce_fusion.3
  149.0 4.0 convolution_bitcast_fusion.9
  164.6 5.2 multiply_reduce_fusion.2
  169.9 4.0 convolution_bitcast_fusion.8
  185.4 5.2 multiply_reduce_fusion.1
  190.6 4.0 convolution_bitcast_fusion.7
  203.4 5.0 multiply_reduce_fusion
  208.5 4.0 convolution_bitcast_fusion.6
  297.8 5.0 slice_bitcast_fusion.9
  302.8 4.3 copy.292
  309.0 4.7 copy.289
  323.3 4.3 copy.295
  329.5 4.9 copy.298
  336.4 4.7 copy.301
  343.2 4.7 copy.304
  395.5 6.7 %collective-permute-start.3 = (f32[2,1,384,1536]{3,2,1,0:T(8,128)}, f32[2,1,384,1536]{3,2,1,0:T(8,128)}, u32[]{:S(2)}, u32[]{:S(2)}) collective-permute-start(f32[2,1,384,1536]{3,2,1,0:T(8,128)} %pad_maximum_fusion.2), channel_id=1, source_target_pairs={{0,4},{4,8},{8,12},{1,5},{5,9},{9,13},{2,6},{6,10},{10,14},{3,7},{... | collective-permute-start | bytes 14155784 | tf_op jit(solution)/shard_map/ppermute | solution.py:31
  421.8 75.9 %collective-permute-done.2 = f32[2,1,384,1536]{3,2,1,0:T(8,128)} collective-permute-done((f32[2,1,384,1536]{3,2,1,0:T(8,128)}, f32[2,1,384,1536]{3,2,1,0:T(8,128)}, u32[]{:S(2)}, u32[]{:S(2)}) %collective-permute-start.2) | collective-permute-done | bytes 4718624 | tf_op jit(solution)/shard_map/ppermute | solution.py:31
  501.3 7.3 %fusion.21 = (f32[1,384,1536]{2,1,0:T(8,128)S(1)}, bf16[1,1,384,1536]{3,2,1,0:T(8,128)(2,1)}) fusion(f32[2,1,384,1536]{3,2,1,0:T(8,128)} %collective-permute-done.3, f32[2,1,384,1536]{3,2,1,0:T(8,128)} %collective-permute-done.2, f32[3,384,1536]{2,1,0:T(8,128)} %slice_dynamic-update-slice_fusion.6, f32[3,384,1536]{2,1,0:T(8,128)} %slice_dynamic-update-slice_fusion), kind=kLoop, calls=%fused_computation.80 | loop fusion | flops 2949120 | bytes 17694720 | tf_op jit(solution)/shard_map/add | solution.py:156
  510.6 4.9 multiply_reduce_fusion.8
  525.0 4.5 fusion.65
  555.0 33.3 %psum.7 = f32[2,128]{1,0:T(2,128)S(1)} all-reduce(f32[2,128]{1,0:T(2,128)S(1)} %pad_maximum_fusion.5), channel_id=1, replica_groups=mesh['pipe'=2,'seq'=4,'dp'=4] {'seq','dp'}, use_global_device_ids=true, to_apply=%region_31.32 | all-reduce | flops 256 | bytes 2048 | tf_op jit(solution)/shard_map/psum | solution.py:164
  588.9 23.1 %collective-permute-done.4 = bf16[3,1,384,1536]{3,2,1,0:T(8,128)(2,1)} collective-permute-done((bf16[3,1,384,1536]{3,2,1,0:T(8,128)(2,1)}, bf16[3,1,384,1536]{3,2,1,0:T(8,128)(2,1)}, u32[]{:S(2)}, u32[]{:S(2)}) %collective-permute-start.4) | collective-permute-done | bytes 3538976 | tf_op jit(solution)/shard_map/ppermute | solution.py:37
  612.0 4.0 copy.394
  (305 shorter events, 321.2 us)
Async XLA Ops:
  7.0 17.0 %copy-start.70 = (f32[128]{0:T(128)}, f32[128]{0:T(128)S(1)}, u32[]{:S(2)}) copy-start(f32[128]{0:T(128)S(1)} %get-tuple-element.45) | copy-start | bytes 1540
  8.8 9.4 %copy-start.55 = (bf16[1,1,1,384,1536]{4,3,2,1,0:T(8,128)(2,1)S(1)}, bf16[1,1,1,384,1536]{4,3,2,1,0:T(8,128)(2,1)}, u32[]{:S(2)}) copy-start(bf16[1,1,1,384,1536]{4,3,2,1,0:T(8,128)(2,1)} %param.9) | copy-start | bytes 3538948
  10.4 9.2 %copy-start.7 = (bf16[1,1,1,384,1536]{4,3,2,1,0:T(8,128)(2,1)S(1)}, bf16[1,1,1,384,1536]{4,3,2,1,0:T(8,128)(2,1)}, u32[]{:S(2)}) copy-start(bf16[1,1,1,384,1536]{4,3,2,1,0:T(8,128)(2,1)} %param.6) | copy-start | bytes 3538948
  10.4 55.9 %collective-permute-start = (bf16[2,1,384,1536]{3,2,1,0:T(8,128)(2,1)}, bf16[2,1,384,1536]{3,2,1,0:T(8,128)(2,1)}, u32[]{:S(2)}, u32[]{:S(2)}) collective-permute-start(bf16[2,1,384,1536]{3,2,1,0:T(8,128)(2,1)} %pad_maximum_fusion.4), channel_id=1, source_target_pairs={{0,4},{4,8},{8,12},{1,5},{5,9},{9,13},{2,6},{6,10},{10,14},{3,7},{... | collective-permute-start | bytes 7077896 | tf_op jit(solution)/shard_map/ppermute | solution.py:22
  16.9 54.9 %collective-permute-start.1 = (bf16[2,1,384,1536]{3,2,1,0:T(8,128)(2,1)}, bf16[2,1,384,1536]{3,2,1,0:T(8,128)(2,1)}, u32[]{:S(2)}, u32[]{:S(2)}) collective-permute-start(bf16[2,1,384,1536]{3,2,1,0:T(8,128)(2,1)} %pad_maximum_fusion.4), channel_id=1, source_target_pairs={{4,0},{8,4},{12,8},{5,1},{9,5},{13,9},{6,2},{10,6},{14,10},{7,3},{... | collective-permute-start | bytes 7077896 | tf_op jit(solution)/shard_map/ppermute | solution.py:23
  21.8 380.4 %copy-start = (f32[384,12,128]{0,2,1:T(8,128)}, f32[384,12,128]{0,2,1:T(8,128)S(1)}, u32[]{:S(2)}) copy-start(f32[384,12,128]{0,2,1:T(8,128)S(1)} %mul.607) | copy-start | bytes 7077892
  27.1 44.7 %copy-start.24 = (bf16[1,1,384,1536]{3,2,1,0:T(8,128)(2,1)S(1)}, bf16[1,1,384,1536]{3,2,1,0:T(8,128)(2,1)}, u32[]{:S(2)}) copy-start(bf16[1,1,384,1536]{3,2,1,0:T(8,128)(2,1)} %copy-done.23) | copy-start | bytes 3538948
  37.7 34.1 %copy-start.33 = (bf16[1,1,1,384,1536]{4,3,2,1,0:T(8,128)(2,1)S(1)}, bf16[1,1,1,384,1536]{4,3,2,1,0:T(8,128)(2,1)}, u32[]{:S(2)}) copy-start(bf16[1,1,1,384,1536]{4,3,2,1,0:T(8,128)(2,1)} %param.8) | copy-start | bytes 3538948
  107.6 4.0 copy-start.18
  128.2 4.0 copy-start.19
  149.0 4.0 copy-start.20
  169.9 4.0 copy-start.21
  190.6 4.0 copy-start.22
  199.6 8.9 %copy-start.52 = (bf16[1,1152,256]{1,2,0:T(8,128)(2,1)}, bf16[1,1152,256]{1,2,0:T(8,128)(2,1)S(1)}, u32[]{:S(2)}) copy-start(bf16[1,1152,256]{1,2,0:T(8,128)(2,1)S(1)} %copy.364) | copy-start | bytes 1769476
  203.4 5.0 copy-start.54
  208.4 4.0 copy-start.17
  259.2 4.5 copy-start.36
  266.9 3.9 copy-start.42
  297.8 5.0 copy-start.34
  362.0 3.9 copy-start.44
  376.1 3.9 copy-start.37
  389.2 3.9 copy-start.29
  391.7 105.9 %collective-permute-start.2 = (f32[2,1,384,1536]{3,2,1,0:T(8,128)}, f32[2,1,384,1536]{3,2,1,0:T(8,128)}, u32[]{:S(2)}, u32[]{:S(2)}) collective-permute-start(f32[2,1,384,1536]{3,2,1,0:T(8,128)} %pad_maximum_fusion.1), channel_id=1, source_target_pairs={{4,0},{8,4},{12,8},{5,1},{9,5},{13,9},{6,2},{10,6},{14,10},{7,3},{... | collective-permute-start | bytes 14155784 | tf_op jit(solution)/shard_map/ppermute | solution.py:31
  395.5 105.8 %collective-permute-start.3 = (f32[2,1,384,1536]{3,2,1,0:T(8,128)}, f32[2,1,384,1536]{3,2,1,0:T(8,128)}, u32[]{:S(2)}, u32[]{:S(2)}) collective-permute-start(f32[2,1,384,1536]{3,2,1,0:T(8,128)} %pad_maximum_fusion.2), channel_id=1, source_target_pairs={{0,4},{4,8},{8,12},{1,5},{5,9},{9,13},{2,6},{6,10},{10,14},{3,7},{... | collective-permute-start | bytes 14155784 | tf_op jit(solution)/shard_map/ppermute | solution.py:31
  411.2 4.3 copy-start.48
  524.9 4.6 copy-start.8
  524.9 4.6 copy-start.25
  524.9 4.8 copy-start.26
  524.9 5.5 copy-start.27
  524.9 6.2 %copy-start.28 = (f32[1,1,384,1536]{3,2,1,0:T(8,128)S(1)}, f32[1,1,384,1536]{3,2,1,0:T(8,128)}, u32[]{:S(2)}) copy-start(f32[1,1,384,1536]{3,2,1,0:T(8,128)} %copy.279) | copy-start | bytes 7077892
  525.0 6.2 %copy-start.67 = (f32[1536]{0:T(1024)S(1)}, f32[1536]{0:T(1024)}, u32[]{:S(2)}) copy-start(f32[1536]{0:T(1024)} %copy-done.66) | copy-start | bytes 18436
  534.4 77.6 %collective-permute-start.4 = (bf16[3,1,384,1536]{3,2,1,0:T(8,128)(2,1)}, bf16[3,1,384,1536]{3,2,1,0:T(8,128)(2,1)}, u32[]{:S(2)}, u32[]{:S(2)}) collective-permute-start(bf16[3,1,384,1536]{3,2,1,0:T(8,128)(2,1)} %pad_maximum_fusion.3), channel_id=1, source_target_pairs={{0,16},{16,0},{1,17},{17,1},{2,18},{18,2},{3,19},{19,3},{4,20},{20... | collective-permute-start | bytes 10616840 | tf_op jit(solution)/shard_map/ppermute | solution.py:37
  (47 other events, 113.9 us)
where the time goes:
time: 623 us; the launch traced here: 616 us
  local copies, waits for them, and re-layouts  235 us (38%)
  waiting for transfers between devices  133 us (21%)
  other arithmetic  105 us (17%)
  matrix products  91.6 us (15%)
  blocking collectives  33.3 us (5%)
  starting transfers between devices  17.2 us (3%)
    ppermute x2, waiting for transfers between devices, passed_along(): lax.ppermute(value, axis, [(source, source + steps) for source in range(i...  79.6 us
    unnamed x172, local copies, waits for them, and re-layouts  58.3 us
    scatter-add x12, other arithmetic, spread(): return totals.at[placed].add(shaped)[:target_span]  39.6 us
    psum x1, blocking collectives, local(): summed = lax.psum(jnp.stack([query_gain, key_gain]), ('seq', 'dp'))  33.3 us
    div x6, matrix products, score_block(): attention = exp_scores / totals  31.2 us
    reshape x12, local copies, waits for them, and re-layouts, spread(): slot_grad.reshape(row_count * list_slots, key_rows // list_slots, head_co...  30 us
    transpose x6, local copies, waits for them, and re-layouts, tile_pass(): jnp.einsum('nhqk,nqhd->nkhd', attn_low, grad_head, preferred_element_type...  27.7 us
    ppermute x1, waiting for transfers between devices, padded(): before = lax.ppermute(last, axis, up)  24.8 us
  transfers between devices with their start and end apart: 5, of which 5 were waited for; matrix products, arithmetic and copies ran while one was open for 10% of the time, Pallas kernels for 0%

commit v1 on v0

v1 whole, which is shorter than its diff:
```python
import functools
import math

import jax
import jax.numpy as jnp
from jax import lax
from jax.experimental import pallas as pl
from jax.experimental.pallas import tpu as pltpu
from jax.sharding import PartitionSpec as P

HEADS = 12
HEAD_DIM = 128
EPSILON = 1e-06
ROOT_SCALE = HEAD_DIM ** (-0.5)
EXP2_SCALE = ROOT_SCALE * math.log2(math.e)
GROUPS = ((0, 4, False), (4, 4, False), (8, 4, True))
VMEM_LIMIT = 48 * 1024 * 1024


def dot_nt(left, right):
    return lax.dot_general(
        left, right, (((1,), (1,)), ((), ())), preferred_element_type=jnp.float32
    )


def dot_nn(left, right):
    return lax.dot_general(
        left, right, (((1,), (0,)), ((), ())), preferred_element_type=jnp.float32
    )


def dot_tn(left, right):
    return lax.dot_general(
        left, right, (((0,), (0,)), ((), ())), preferred_element_type=jnp.float32
    )


def normalize(source, gain):
    floats = source.astype(jnp.float32)
    scaled = lax.rsqrt(jnp.mean(floats * floats, axis=-1, keepdims=True) + EPSILON)
    normed = floats * scaled
    return floats, scaled, normed, (normed * gain).astype(jnp.bfloat16)


def norm_back(grad_hat, floats, scaled, gain):
    scaled_grad = gain * grad_hat
    projected = jnp.sum(scaled_grad * floats, axis=-1, keepdims=True)
    return scaled * scaled_grad - (scaled**3 * projected * (1.0 / HEAD_DIM)) * floats


def main_kernel(
    info, query, grad, key, value, pair_prev, pair_next,
    query_out, own_out, prev_out, next_out, gain_out,
):
    query_gain = info[0:1, :HEAD_DIM]
    key_gain = info[1:2, :HEAD_DIM]
    query_floats, query_scale, query_normed, query_hat = normalize(query[...], query_gain)
    grad_in = grad[...]
    sides = (
        (key[...], value[...], None),
        (pair_prev[0], pair_prev[1], info[2:3, :]),
        (pair_next[0], pair_next[1], info[3:4, :]),
    )
    parts = []
    totals = None
    for key_in, value_in, live in sides:
        _, _, key_normed, key_hat = normalize(key_in, key_gain)
        weights = jnp.exp2(dot_nt(key_hat, query_hat) * EXP2_SCALE)
        grad_probs = dot_nt(value_in, grad_in)
        weight_sum = jnp.sum(weights, axis=0, keepdims=True)
        cross_sum = jnp.sum(weights * grad_probs, axis=0, keepdims=True)
        if live is not None:
            weight_sum = weight_sum * live
            cross_sum = cross_sum * live
        totals = weight_sum if totals is None else totals + weight_sum
        crosses = cross_sum if live is None else crosses + cross_sum
        parts.append((key_normed, key_hat, weights, grad_probs, live))
    inverse = 1.0 / totals
    deltas = crosses * inverse
    query_grad_t = None
    key_gain_sum = None
    for (key_normed, key_hat, weights, grad_probs, live), out in zip(
        parts, (own_out, prev_out, next_out)
    ):
        probs = weights * (inverse if live is None else inverse * live)
        dscores = (probs * (grad_probs - deltas)).astype(jnp.bfloat16)
        key_part = dot_nn(dscores, query_hat) * ROOT_SCALE
        value_part = dot_nn(probs.astype(jnp.bfloat16), grad_in)
        out[0] = key_part.astype(out.dtype)
        out[1] = value_part.astype(out.dtype)
        gain_part = jnp.sum(key_part * key_normed, axis=0, keepdims=True)
        key_gain_sum = gain_part if key_gain_sum is None else key_gain_sum + gain_part
        query_part = dot_tn(key_hat, dscores)
        query_grad_t = query_part if query_grad_t is None else query_grad_t + query_part
    query_grad = query_grad_t.T * ROOT_SCALE
    query_out[...] = norm_back(query_grad, query_floats, query_scale, query_gain).astype(
        query_out.dtype
    )
    query_gain_sum = jnp.sum(query_grad * query_normed, axis=0, keepdims=True)

    @pl.when(pl.program_id(0) == 0)
    def _():
        gain_out[...] = jnp.zeros_like(gain_out)

    gain_out[0:1, :] += query_gain_sum
    gain_out[1:2, :] += key_gain_sum


def finish_kernel(info, key, own, from_prev, from_next, out):
    key_gain = info[1:2, :HEAD_DIM]
    key_floats, key_scale, _, _ = normalize(key[...], key_gain)
    key_grad = own[0] + from_prev[0].astype(jnp.float32) + from_next[0].astype(jnp.float32)
    out[0] = norm_back(key_grad, key_floats, key_scale, key_gain).astype(out.dtype)
    value_grad = own[1] + from_prev[1].astype(jnp.float32) + from_next[1].astype(jnp.float32)
    out[1] = value_grad.astype(out.dtype)


def head_block(rows, first):
    return pl.BlockSpec((rows, HEAD_DIM), lambda head: (0, first + head))


def pair_block(rows):
    return pl.BlockSpec((2, rows, HEAD_DIM), lambda head: (0, 0, head))


def whole_block(shape):
    return pl.BlockSpec(shape, lambda head: (0,) * len(shape))


def main_call(info, query, grad, key, value, pair_prev, pair_next, first, count):
    rows = query.shape[0]
    lanes = count * HEAD_DIM
    return pl.pallas_call(
        main_kernel,
        grid=(count,),
        in_specs=[whole_block(info.shape)]
        + [head_block(rows, first)] * 4
        + [pair_block(rows)] * 2,
        out_specs=[head_block(rows, 0)] + [pair_block(rows)] * 3 + [whole_block((8, HEAD_DIM))],
        out_shape=[
            jax.ShapeDtypeStruct((rows, lanes), jnp.bfloat16),
            jax.ShapeDtypeStruct((2, rows, lanes), jnp.float32),
            jax.ShapeDtypeStruct((2, rows, lanes), jnp.bfloat16),
            jax.ShapeDtypeStruct((2, rows, lanes), jnp.bfloat16),
            jax.ShapeDtypeStruct((8, HEAD_DIM), jnp.float32),
        ],
        compiler_params=pltpu.CompilerParams(vmem_limit_bytes=VMEM_LIMIT),
        cost_estimate=pl.CostEstimate(
            flops=count * 30 * rows * rows * HEAD_DIM,
            bytes_accessed=count * 14 * rows * HEAD_DIM * 2,
            transcendentals=count * 3 * rows * rows,
        ),
    )(info, query, grad, key, value, pair_prev, pair_next)


def finish_call(info, key, own, from_prev, from_next, first, count):
    rows = key.shape[0]
    lanes = count * HEAD_DIM
    return pl.pallas_call(
        finish_kernel,
        grid=(count,),
        in_specs=[whole_block(info.shape), head_block(rows, first)] + [pair_block(rows)] * 3,
        out_specs=pair_block(rows),
        out_shape=jax.ShapeDtypeStruct((2, rows, lanes), jnp.bfloat16),
        compiler_params=pltpu.CompilerParams(vmem_limit_bytes=VMEM_LIMIT),
        cost_estimate=pl.CostEstimate(
            flops=count * 20 * rows * HEAD_DIM,
            bytes_accessed=count * 12 * rows * HEAD_DIM * 2,
            transcendentals=0,
        ),
    )(info, key, own, from_prev, from_next)


def shifted(value, axis, step):
    count = lax.axis_size(axis)
    pairs = [(i, i + step) for i in range(count) if 0 <= i + step < count]
    return lax.ppermute(value, axis, pairs)


def swapped(value):
    count = lax.axis_size("pipe")
    return lax.ppermute(value, "pipe", [(i, (i - 1) % count) for i in range(count)])


def local(queries, keys, values, grad_out, norm_gains, kv_tiles):
    query, key, value, grad = (a[0, 0, 0] for a in (queries, keys, values, grad_out))
    rows = query.shape[0]
    tile = lax.axis_index("seq")
    listed = kv_tiles[0, 0, 0]
    has_prev = (jnp.any(listed == tile - 1) & (tile > 0)).astype(jnp.float32)
    has_next = jnp.any(listed == tile + 1).astype(jnp.float32)
    info = jnp.concatenate(
        [
            jnp.pad(norm_gains[0], ((0, 0), (0, rows - HEAD_DIM))),
            jnp.full((1, rows), has_prev),
            jnp.full((1, rows), has_next),
            jnp.zeros((4, rows), jnp.float32),
        ],
        axis=0,
    )

    def lanes(array, first, count):
        return array[:, first * HEAD_DIM : (first + count) * HEAD_DIM]

    sources = []
    for first, count, away in GROUPS:
        if away:
            moved = swapped(
                jnp.stack([lanes(a, first, count) for a in (query, grad, key, value)])
            )
            sources.append((swapped(info), tuple(moved[i] for i in range(4)), 0, moved[2:]))
        else:
            pair = jnp.stack([lanes(key, first, count), lanes(value, first, count)])
            sources.append((info, (query, grad, key, value), first, pair))
    gathered = [
        (shifted(pair, "seq", 1), shifted(pair, "seq", -1)) for _, _, _, pair in sources
    ]
    gain_sums = [jnp.zeros((2, HEAD_DIM), jnp.float32)] * 2
    query_parts, pair_parts = [], []
    for (first, count, away), (group_info, arrays, offset, _), (prev, following) in zip(
        GROUPS, sources, gathered
    ):
        query_low, own, to_prev, to_next, gain = main_call(
            group_info, *arrays, prev, following, offset, count
        )
        gain_sums[away] = gain_sums[away] + gain[:2]
        from_next = shifted(to_prev, "seq", -1)
        from_prev = shifted(to_next, "seq", 1)
        pair_low = finish_call(group_info, arrays[2], own, from_prev, from_next, offset, count)
        query_parts.append(query_low if away else swapped(query_low))
        pair_parts.append(pair_low if away else swapped(pair_low))
    mine = lax.axis_index("pipe")
    segments = lax.axis_size("pipe")
    here = jnp.arange(segments)[:, None, None] == mine
    contribution = jnp.where(here, gain_sums[0][None], gain_sums[1][None])
    summed = lax.psum(contribution, ("pipe", "seq", "dp"))
    tokens = lax.axis_size("dp") * lax.axis_size("seq") * rows * HEADS
    gain_grads = lax.dynamic_index_in_dim(summed, mine, 0, keepdims=True) / math.sqrt(tokens)
    out = jnp.concatenate(
        [jnp.concatenate(query_parts, axis=-1)[None], jnp.concatenate(pair_parts, axis=-1)], axis=0
    )
    return (out[None, :, None, None], gain_grads)


def solution(mesh):
    placed = (
        P("pipe", "dp", "seq", None, None),
        P("pipe", "dp", "seq", None, None),
        P("pipe", "dp", "seq", None, None),
        P("pipe", "dp", "seq", None, None),
        P("pipe", None, None),
        P("pipe", "dp", "seq", None),
    )
    return jax.shard_map(
        local,
        mesh=mesh,
        in_specs=placed,
        out_specs=(P("pipe", None, "dp", "seq", None, None), P("pipe", None, None)),
        check_vma=False,
    )
```

time: 623 us -> 171 us (0.27); the launches traced: 616 us -> 171 us
  local copies, waits for them, and re-layouts: 235 us -> 7.13 us
  waiting for transfers between devices: 133 us -> 21.7 us
  other arithmetic: 105 us -> 10.3 us
  matrix products: 91.6 us -> 0 us
  Pallas kernels: 0 us -> 37.5 us
  starting transfers between devices: 17.2 us -> 43.1 us
  blocking collectives: 33.3 us -> 48.8 us
    ppermute x5 -> x18, waiting for transfers between devices: 133 us -> 21.7 us  [the longest x12 21.7 us: shifted(): return lax.ppermute(value, axis, pairs)]
    dot_general x24 -> x0, matrix products: 60.3 us -> none  [the longest x6 23.8 us: tile_pass(): jnp.einsum('nhqk,nqhd->nkhd', attn_low, grad_head, preferred_element_type...]
    unnamed x172 -> x26, local copies, waits for them, and re-layouts: 58.3 us -> 1.37 us
    mul x24 -> x0, local copies, waits for them, and re-layouts: 41 us -> none  [the longest x8 16.4 us: norm_back(): scaled ** 3 * floats * projected / HEAD_DIM]
    scatter-add x12 -> x0, other arithmetic: 39.6 us -> none  [spread(): return totals.at[placed].add(shaped)[:target_span]]
    pallas_call x0 -> x6, Pallas kernels: none -> 37.5 us  [the longest x3 31 us: main_call(): pl.pallas_call(main_kernel, grid=(count,), in_specs=[whole_block(info.sha...]
    reshape x13 -> x0, local copies, waits for them, and re-layouts: 31.5 us -> none  [the longest x12 30 us: spread(): slot_grad.reshape(row_count * list_slots, key_rows // list_slots, head_co...]
    div x6 -> x0, matrix products: 31.2 us -> none  [score_block(): attention = exp_scores / totals]
  transfers between devices with their start and end apart: 5 -> 18, of which waited for: 5 -> 6; matrix products, arithmetic and copies ran while one was open for 10% -> 6% of each run, Pallas kernels for 0% -> 22%
where the time goes in v1:
time: 171 us
  blocking collectives  48.8 us (29%)
  starting transfers between devices  43.1 us (25%)
  Pallas kernels  37.5 us (22%)
  waiting for transfers between devices  21.7 us (13%)
  other arithmetic  10.3 us (6%)
  local copies, waits for them, and re-layouts  7.13 us (4%)
  between operations  2.15 us (1%)
    psum x1, blocking collectives, local(): summed = lax.psum(contribution, ('pipe', 'seq', 'dp'))  48.8 us
    ppermute x12, starting transfers between devices, shifted(): return lax.ppermute(value, axis, pairs)  35 us
    pallas_call x3, Pallas kernels, main_call(): pl.pallas_call(main_kernel, grid=(count,), in_specs=[whole_block(info.sha...  31 us
    ppermute x12, waiting for transfers between devices, shifted(): return lax.ppermute(value, axis, pairs)  21.7 us
    ppermute x6, starting transfers between devices, swapped(): lax.ppermute(value, 'pipe', [(i, (i - 1) % count) for i in range(count)])  8.02 us
    pallas_call x3, Pallas kernels, finish_call(): pl.pallas_call(finish_kernel, grid=(count,), in_specs=[whole_block(info.s...  6.53 us
  transfers between devices with their start and end apart: 18, of which 6 were waited for; matrix products, arithmetic and copies ran while one was open for 6% of the time, Pallas kernels for 22%

profile of v1, /device:TPU:0, one launch (start us, length us, event | category | flops | bytes accessed | tf_op | source)
XLA Modules:
  0.0 170.6 jit_solution(9548069376952786735)
XLA Ops:
  0.6 1.9 %slice_bitcast_fusion.10 = (bf16[1,384,512]{2,1,0:T(8,128)(2,1)S(1)}, bf16[1,384,512]{2,1,0:T(8,128)(2,1)S(1)}, bf16[1,384,512]{2,1,0:T(8,128)(2,1)S(1)}, bf16[1...) fusion(bf16[384,1536]{1,0:T(8,128)(2,1)} %bitcast.48, ...), kind=kLoop, calls=%fused_computation.15 | loop fusion | bytes 4718592 | tf_op jit(solution)/shard_map/stack | solution.py:213
  3.6 5.0 %collective-permute-start.3 = (bf16[2,384,512]{2,1,0:T(8,128)(2,1)}, bf16[2,384,512]{2,1,0:T(8,128)(2,1)S(1)}, u32[]{:S(2)}, u32[]{:S(2)}) collective-permute-start(bf16[2,384,512]{2,1,0:T(8,128)(2,1)} %pad_maximum_fusion.2), channel_id=1, source_target_pairs={{0,4},{4,8},{8,12},{1,5},{5,9},{9,13},{2,6},{6,10},{10,14},{3,7},{... | collective-permute-start | bytes 2359304 | tf_op jit(solution)/shard_map/ppermute | solution.py:177
  8.5 1.3 collective-permute-start.4
  9.9 1.3 pad_maximum_fusion
  11.3 1.5 collective-permute-start.7
  13.7 5.5 %collective-permute-start = (bf16[2,384,512]{2,1,0:T(8,128)(2,1)}, bf16[2,384,512]{2,1,0:T(8,128)(2,1)}, u32[]{:S(2)}, u32[]{:S(2)}) collective-permute-start(bf16[2,384,512]{2,1,0:T(8,128)(2,1)} %pad_maximum_fusion.1), channel_id=1, source_target_pairs={{0,4},{4,8},{8,12},{1,5},{5,9},{9,13},{2,6},{6,10},{10,14},{3,7},{... | collective-permute-start | bytes 2359304 | tf_op jit(solution)/shard_map/ppermute | solution.py:177
  22.6 4.1 %collective-permute-done.3.pair_prev = bf16[2,384,512]{2,1,0:T(8,128)(2,1)S(1)} collective-permute-done((bf16[2,384,512]{2,1,0:T(8,128)(2,1)}, bf16[2,384,512]{2,1,0:T(8,128)(2,1)S(1)}, u32[]{:S(2)}, u32[]{:S(2)}) %collective-permute-start.3) | collective-permute-done | bytes 786464 | tf_op jit(solution)/shard_map/ppermute | solution.py:177
  26.7 4.5 %collective-permute-done.4.pair_next = bf16[2,384,512]{2,1,0:T(8,128)(2,1)} collective-permute-done((bf16[2,384,512]{2,1,0:T(8,128)(2,1)}, bf16[2,384,512]{2,1,0:T(8,128)(2,1)}, u32[]{:S(2)}, u32[]{:S(2)}) %collective-permute-start.4) | collective-permute-done | bytes 786464 | tf_op jit(solution)/shard_map/ppermute | solution.py:177
  31.2 10.3 %shard_map.78 = (bf16[384,512]{1,0:T(8,128)(2,1)}, f32[2,384,512]{2,1,0:T(8,128)}, bf16[2,384,512]{2,1,0:T(8,128)(2,1)}, bf16[2,384,512]{2,1,0:T(8,128)(2,1)S(1)}, f32[8,128]{1,0:T(8,128)S(1)}) custom-call(f32[8,384]{1,0:T(8,128)S(1)} %fusion.1.info, bf16[384,1536]{1,0:T(8,128)(2,1)S(1)} %bitcast.46, bf16[384,1536]{1,0:T(8,128)(2,1)S(1)} %bitcast.43, ...), custom_call_target="tpu_custom_call" | custom-call | flops 2264924160 | bytes 5505024 | tf_op jit(solution)/shard_map/pallas_call | solution.py:133
  41.6 3.5 %collective-permute-start.13 = (bf16[2,384,512]{2,1,0:T(8,128)(2,1)S(1)}, bf16[2,384,512]{2,1,0:T(8,128)(2,1)S(1)}, u32[]{:S(2)}, u32[]{:S(2)}) collective-permute-start(bf16[2,384,512]{2,1,0:T(8,128)(2,1)S(1)} %get-tuple-element.24), channel_id=1, source_target_pairs={{0,4},{4,8},{8,12},{1,5},{5,9},{9,13},{2,6},{6,10},{10,14},{3,7},{... | collective-permute-start | bytes 2359304 | tf_op jit(solution)/shard_map/ppermute | solution.py:177
  45.0 1.3 collective-permute-start.14
  46.6 10.3 %shard_map.77 = (bf16[384,512]{1,0:T(8,128)(2,1)}, f32[2,384,512]{2,1,0:T(8,128)}, bf16[2,384,512]{2,1,0:T(8,128)(2,1)}, bf16[2,384,512]{2,1,0:T(8,128)(2,1)}, f32[8,128]{1,0:T(8,128)S(1)}) custom-call(f32[8,384]{1,0:T(8,128)S(1)} %fusion.1.info, bf16[384,1536]{1,0:T(8,128)(2,1)S(1)} %bitcast.47, bf16[384,1536]{1,0:T(8,128)(2,1)S(1)} %bitcast.44, ...), custom_call_target="tpu_custom_call" | custom-call | flops 2264924160 | bytes 5505024 | tf_op jit(solution)/shard_map/pallas_call | solution.py:133
  57.5 4.4 %collective-permute-start.10 = (bf16[2,384,512]{2,1,0:T(8,128)(2,1)}, bf16[2,384,512]{2,1,0:T(8,128)(2,1)S(1)}, u32[]{:S(2)}, u32[]{:S(2)}) collective-permute-start(bf16[2,384,512]{2,1,0:T(8,128)(2,1)} %get-tuple-element.21), channel_id=1, source_target_pairs={{0,4},{4,8},{8,12},{1,5},{5,9},{9,13},{2,6},{6,10},{10,14},{3,7},{... | collective-permute-start | bytes 2359304 | tf_op jit(solution)/shard_map/ppermute | solution.py:177
  61.9 1.3 collective-permute-start.11
  63.2 2.1 %slice.76 = bf16[2,384,512]{2,1,0:T(8,128)(2,1)} slice(bf16[4,384,512]{2,1,0:T(8,128)(2,1)} %collective-permute-done.7), slice={[2:4], [0:384], [0:512]} | slice | bytes 1572864 | tf_op jit(solution)/shard_map/slice | solution.py:211
  65.3 5.5 %collective-permute-start.8 = (bf16[2,384,512]{2,1,0:T(8,128)(2,1)}, bf16[2,384,512]{2,1,0:T(8,128)(2,1)}, u32[]{:S(2)}, u32[]{:S(2)}) collective-permute-start(bf16[2,384,512]{2,1,0:T(8,128)(2,1)} %slice.76), channel_id=1, source_target_pairs={{0,4},{4,8},{8,12},{1,5},{5,9},{9,13},{2,6},{6,10},{10,14},{3,7},{... | collective-permute-start | bytes 2359304 | tf_op jit(solution)/shard_map/ppermute | solution.py:177
  72.1 1.5 collective-permute-start.6
  73.6 6.6 %collective-permute-done.10.from_prev = bf16[2,384,512]{2,1,0:T(8,128)(2,1)S(1)} collective-permute-done((bf16[2,384,512]{2,1,0:T(8,128)(2,1)}, bf16[2,384,512]{2,1,0:T(8,128)(2,1)S(1)}, u32[]{:S(2)}, u32[]{:S(2)}) %collective-permute-start.10) | collective-permute-done | bytes 786464 | tf_op jit(solution)/shard_map/ppermute | solution.py:177
  80.2 1.5 collective-permute-start.5
  81.6 1.5 slice_bitcast_fusion
  83.1 2.5 %shard_map.81 = bf16[2,384,512]{2,1,0:T(8,128)(2,1)} custom-call(f32[8,384]{1,0:T(8,128)S(1)} %fusion.1.info, bf16[384,1536]{1,0:T(8,128)(2,1)S(1)} %bitcast.40, f32[2,384,512]{2,1,0:T(8,128)S(1)} %copy-done.2, bf16[2,384,512]{2,1,0:T(8,128)(2,1)S(1)} %collective-permute-done.13.from_prev, bf16[2,384,512]{2,1,0:T(8,128)(2,1)S(1)} %collective-permute-done.14.from_next), custom_call_target="tpu_custom_call" | custom-call | flops 3932160 | bytes 4718592 | tf_op jit(solution)/shard_map/pallas_call | solution.py:159
  86.5 2.4 %shard_map.80 = bf16[2,384,512]{2,1,0:T(8,128)(2,1)} custom-call(f32[8,384]{1,0:T(8,128)S(1)} %fusion.1.info, bf16[384,1536]{1,0:T(8,128)(2,1)S(1)} %bitcast.41, f32[2,384,512]{2,1,0:T(8,128)S(1)} %copy-done.3, bf16[2,384,512]{2,1,0:T(8,128)(2,1)S(1)} %collective-permute-done.10.from_prev, bf16[2,384,512]{2,1,0:T(8,128)(2,1)S(1)} %collective-permute-done.11.from_next), custom_call_target="tpu_custom_call" | custom-call | flops 3932160 | bytes 4718592 | tf_op jit(solution)/shard_map/pallas_call | solution.py:159
  90.1 3.6 %collective-permute-done.8.pair_prev = bf16[2,384,512]{2,1,0:T(8,128)(2,1)} collective-permute-done((bf16[2,384,512]{2,1,0:T(8,128)(2,1)}, bf16[2,384,512]{2,1,0:T(8,128)(2,1)}, u32[]{:S(2)}, u32[]{:S(2)}) %collective-permute-start.8) | collective-permute-done | bytes 786464 | tf_op jit(solution)/shard_map/ppermute | solution.py:177
  93.7 1.5 collective-permute-start.12
  95.2 2.7 %collective-permute-done.9.pair_next = bf16[2,384,512]{2,1,0:T(8,128)(2,1)} collective-permute-done((bf16[2,384,512]{2,1,0:T(8,128)(2,1)}, bf16[2,384,512]{2,1,0:T(8,128)(2,1)}, u32[]{:S(2)}, u32[]{:S(2)}) %collective-permute-start.9) | collective-permute-done | bytes 786464 | tf_op jit(solution)/shard_map/ppermute | solution.py:177
  97.9 10.3 %shard_map.79 = (bf16[384,512]{1,0:T(8,128)(2,1)S(1)}, f32[2,384,512]{2,1,0:T(8,128)}, bf16[2,384,512]{2,1,0:T(8,128)(2,1)}, bf16[2,384,512]{2,1,0:T(8,128)(2,1)}, f32[8,128]{1,0:T(8,128)S(1)}) custom-call(f32[8,384]{1,0:T(8,128)S(1)} %collective-permute-done.6.info, bf16[384,512]{1,0:T(8,128)(2,1)S(1)} %get-tuple-element.39.query, ...), custom_call_target="tpu_custom_call" | custom-call | flops 2264924160 | bytes 5505024 | tf_op jit(solution)/shard_map/pallas_call | solution.py:133
  108.9 3.6 %collective-permute-start.16 = (bf16[2,384,512]{2,1,0:T(8,128)(2,1)}, bf16[2,384,512]{2,1,0:T(8,128)(2,1)S(1)}, u32[]{:S(2)}, u32[]{:S(2)}) collective-permute-start(bf16[2,384,512]{2,1,0:T(8,128)(2,1)} %get-tuple-element.27), channel_id=1, source_target_pairs={{0,4},{4,8},{8,12},{1,5},{5,9},{9,13},{2,6},{6,10},{10,14},{3,7},{... | collective-permute-start | bytes 2359304 | tf_op jit(solution)/shard_map/ppermute | solution.py:177
  112.6 1.3 collective-permute-start.17
  114.6 48.8 %psum.7 = f32[2,2,128]{2,1,0:T(2,128)} all-reduce(f32[2,2,128]{2,1,0:T(2,128)S(1)} %broadcast_select_fusion), channel_id=1, replica_groups=mesh['pipe'=2,'seq'=4,'dp'=4] {'pipe','seq','dp'}, use_global_device_ids=true, to_apply=%region_2.3 | all-reduce | flops 512 | bytes 4096 | tf_op jit(solution)/shard_map/psum | solution.py:236
  164.6 1.3 maximum_bitcast_fusion.1
  166.0 1.6 shard_map.82
  167.6 3.1 %maximum_bitcast_fusion = bf16[1,3,1,1,384,1536]{5,4,3,2,1,0:T(8,128)(2,1)} fusion(bf16[2,384,512]{2,1,0:T(8,128)(2,1)S(1)} %shard_map.82, bf16[2,384,512]{2,1,0:T(8,128)(2,1)} %collective-permute-done.15, bf16[2,384,512]{2,1,0:T(8,128)(2,1)} %collective-permute-done.12, bf16[1,384,1536]{2,1,0:T(8,128)(2,1)S(1)} %maximum_bitcast_fusion.1), kind=kLoop, calls=%fused_computation | loop fusion | flops 14155776 | bytes 7077888
  (57 shorter events, 11.2 us)
Async XLA Ops:
  0.6 9.2 %copy-start.6 = (bf16[1,1,1,384,1536]{4,3,2,1,0:T(8,128)(2,1)S(1)}, bf16[1,1,1,384,1536]{4,3,2,1,0:T(8,128)(2,1)}, u32[]{:S(2)}) copy-start(bf16[1,1,1,384,1536]{4,3,2,1,0:T(8,128)(2,1)} %param.6) | copy-start | bytes 3538948
  2.6 7.3 %copy-start.5 = (bf16[1,1,1,384,1536]{4,3,2,1,0:T(8,128)(2,1)S(1)}, bf16[1,1,1,384,1536]{4,3,2,1,0:T(8,128)(2,1)}, u32[]{:S(2)}) copy-start(bf16[1,1,1,384,1536]{4,3,2,1,0:T(8,128)(2,1)} %param.9) | copy-start | bytes 3538948
  3.6 23.2 %collective-permute-start.3 = (bf16[2,384,512]{2,1,0:T(8,128)(2,1)}, bf16[2,384,512]{2,1,0:T(8,128)(2,1)S(1)}, u32[]{:S(2)}, u32[]{:S(2)}) collective-permute-start(bf16[2,384,512]{2,1,0:T(8,128)(2,1)} %pad_maximum_fusion.2), channel_id=1, source_target_pairs={{0,4},{4,8},{8,12},{1,5},{5,9},{9,13},{2,6},{6,10},{10,14},{3,7},{... | collective-permute-start | bytes 2359304 | tf_op jit(solution)/shard_map/ppermute | solution.py:177
  8.5 22.7 %collective-permute-start.4 = (bf16[2,384,512]{2,1,0:T(8,128)(2,1)}, bf16[2,384,512]{2,1,0:T(8,128)(2,1)}, u32[]{:S(2)}, u32[]{:S(2)}) collective-permute-start(bf16[2,384,512]{2,1,0:T(8,128)(2,1)} %pad_maximum_fusion.2), channel_id=1, source_target_pairs={{4,0},{8,4},{12,8},{5,1},{9,5},{13,9},{6,2},{10,6},{14,10},{7,3},{... | collective-permute-start | bytes 2359304 | tf_op jit(solution)/shard_map/ppermute | solution.py:177
  11.3 9.2 %copy-start.12 = (s32[1,1,1,3]{3,2,1,0:T(1,128)S(1)}, s32[1,1,1,3]{3,2,1,0:T(1,128)}, u32[]{:S(2)}) copy-start(s32[1,1,1,3]{3,2,1,0:T(1,128)} %param.11) | copy-start | bytes 40
  11.3 11.3 %copy-start.11 = (f32[1,2,128]{2,1,0:T(2,128)S(1)}, f32[1,2,128]{2,1,0:T(2,128)}, u32[]{:S(2)}) copy-start(f32[1,2,128]{2,1,0:T(2,128)} %param.10) | copy-start | bytes 3076
  11.3 51.9 %collective-permute-start.7 = (bf16[4,384,512]{2,1,0:T(8,128)(2,1)}, bf16[4,384,512]{2,1,0:T(8,128)(2,1)}, u32[]{:S(2)}, u32[]{:S(2)}) collective-permute-start(bf16[4,384,512]{2,1,0:T(8,128)(2,1)} %pad_maximum_fusion), channel_id=1, source_target_pairs={{0,16},{16,0},{1,17},{17,1},{2,18},{18,2},{3,19},{19,3},{4,20},{20... | collective-permute-start | bytes 4718600 | tf_op jit(solution)/shard_map/ppermute | solution.py:182
  13.7 32.6 %collective-permute-start = (bf16[2,384,512]{2,1,0:T(8,128)(2,1)}, bf16[2,384,512]{2,1,0:T(8,128)(2,1)}, u32[]{:S(2)}, u32[]{:S(2)}) collective-permute-start(bf16[2,384,512]{2,1,0:T(8,128)(2,1)} %pad_maximum_fusion.1), channel_id=1, source_target_pairs={{0,4},{4,8},{8,12},{1,5},{5,9},{9,13},{2,6},{6,10},{10,14},{3,7},{... | collective-permute-start | bytes 2359304 | tf_op jit(solution)/shard_map/ppermute | solution.py:177
  19.2 27.4 %collective-permute-start.1 = (bf16[2,384,512]{2,1,0:T(8,128)(2,1)}, bf16[2,384,512]{2,1,0:T(8,128)(2,1)}, u32[]{:S(2)}, u32[]{:S(2)}) collective-permute-start(bf16[2,384,512]{2,1,0:T(8,128)(2,1)} %pad_maximum_fusion.1), channel_id=1, source_target_pairs={{4,0},{8,4},{12,8},{5,1},{9,5},{13,9},{6,2},{10,6},{14,10},{7,3},{... | collective-permute-start | bytes 2359304 | tf_op jit(solution)/shard_map/ppermute | solution.py:177
  22.6 24.0 %copy-start.7 = (bf16[1,1,1,384,1536]{4,3,2,1,0:T(8,128)(2,1)S(1)}, bf16[1,1,1,384,1536]{4,3,2,1,0:T(8,128)(2,1)}, u32[]{:S(2)}) copy-start(bf16[1,1,1,384,1536]{4,3,2,1,0:T(8,128)(2,1)} %param.6) | copy-start | bytes 3538948
  41.6 29.2 %collective-permute-start.13 = (bf16[2,384,512]{2,1,0:T(8,128)(2,1)S(1)}, bf16[2,384,512]{2,1,0:T(8,128)(2,1)S(1)}, u32[]{:S(2)}, u32[]{:S(2)}) collective-permute-start(bf16[2,384,512]{2,1,0:T(8,128)(2,1)S(1)} %get-tuple-element.24), channel_id=1, source_target_pairs={{0,4},{4,8},{8,12},{1,5},{5,9},{9,13},{2,6},{6,10},{10,14},{3,7},{... | collective-permute-start | bytes 2359304 | tf_op jit(solution)/shard_map/ppermute | solution.py:177
  45.0 27.0 %collective-permute-start.14 = (bf16[2,384,512]{2,1,0:T(8,128)(2,1)}, bf16[2,384,512]{2,1,0:T(8,128)(2,1)S(1)}, u32[]{:S(2)}, u32[]{:S(2)}) collective-permute-start(bf16[2,384,512]{2,1,0:T(8,128)(2,1)} %get-tuple-element.25), channel_id=1, source_target_pairs={{4,0},{8,4},{12,8},{5,1},{9,5},{13,9},{6,2},{10,6},{14,10},{7,3},{... | collective-permute-start | bytes 2359304 | tf_op jit(solution)/shard_map/ppermute | solution.py:177
  57.0 0.6 copy-start.10
  57.5 22.6 %collective-permute-start.10 = (bf16[2,384,512]{2,1,0:T(8,128)(2,1)}, bf16[2,384,512]{2,1,0:T(8,128)(2,1)S(1)}, u32[]{:S(2)}, u32[]{:S(2)}) collective-permute-start(bf16[2,384,512]{2,1,0:T(8,128)(2,1)} %get-tuple-element.21), channel_id=1, source_target_pairs={{0,4},{4,8},{8,12},{1,5},{5,9},{9,13},{2,6},{6,10},{10,14},{3,7},{... | collective-permute-start | bytes 2359304 | tf_op jit(solution)/shard_map/ppermute | solution.py:177
  61.9 23.7 %collective-permute-start.11 = (bf16[2,384,512]{2,1,0:T(8,128)(2,1)}, bf16[2,384,512]{2,1,0:T(8,128)(2,1)S(1)}, u32[]{:S(2)}, u32[]{:S(2)}) collective-permute-start(bf16[2,384,512]{2,1,0:T(8,128)(2,1)} %get-tuple-element.22), channel_id=1, source_target_pairs={{4,0},{8,4},{12,8},{5,1},{9,5},{13,9},{6,2},{10,6},{14,10},{7,3},{... | collective-permute-start | bytes 2359304 | tf_op jit(solution)/shard_map/ppermute | solution.py:177
  65.3 28.5 %collective-permute-start.8 = (bf16[2,384,512]{2,1,0:T(8,128)(2,1)}, bf16[2,384,512]{2,1,0:T(8,128)(2,1)}, u32[]{:S(2)}, u32[]{:S(2)}) collective-permute-start(bf16[2,384,512]{2,1,0:T(8,128)(2,1)} %slice.76), channel_id=1, source_target_pairs={{0,4},{4,8},{8,12},{1,5},{5,9},{9,13},{2,6},{6,10},{10,14},{3,7},{... | collective-permute-start | bytes 2359304 | tf_op jit(solution)/shard_map/ppermute | solution.py:177
  70.7 27.2 %collective-permute-start.9 = (bf16[2,384,512]{2,1,0:T(8,128)(2,1)}, bf16[2,384,512]{2,1,0:T(8,128)(2,1)}, u32[]{:S(2)}, u32[]{:S(2)}) collective-permute-start(bf16[2,384,512]{2,1,0:T(8,128)(2,1)} %slice.76), channel_id=1, source_target_pairs={{4,0},{8,4},{12,8},{5,1},{9,5},{13,9},{6,2},{10,6},{14,10},{7,3},{... | collective-permute-start | bytes 2359304 | tf_op jit(solution)/shard_map/ppermute | solution.py:177
  72.1 16.9 %collective-permute-start.6 = (f32[8,384]{1,0:T(8,128)S(1)}, f32[8,384]{1,0:T(8,128)S(1)}, u32[]{:S(2)}, u32[]{:S(2)}) collective-permute-start(f32[8,384]{1,0:T(8,128)S(1)} %fusion.1.info), channel_id=1, source_target_pairs={{0,16},{16,0},{1,17},{17,1},{2,18},{18,2},{3,19},{19,3},{4,20},{20... | collective-permute-start | bytes 36872 | tf_op jit(solution)/shard_map/ppermute | solution.py:182
  80.2 3.0 %copy-start = (bf16[1,1,1,384,1536]{4,3,2,1,0:T(8,128)(2,1)S(1)}, bf16[1,1,1,384,1536]{4,3,2,1,0:T(8,128)(2,1)}, u32[]{:S(2)}) copy-start(bf16[1,1,1,384,1536]{4,3,2,1,0:T(8,128)(2,1)} %param.7) | copy-start | bytes 3538948
  80.2 3.0 %copy-start.2 = (f32[2,384,512]{2,1,0:T(8,128)S(1)}, f32[2,384,512]{2,1,0:T(8,128)}, u32[]{:S(2)}) copy-start(f32[2,384,512]{2,1,0:T(8,128)} %get-tuple-element.23.own) | copy-start | bytes 4718596
  80.2 32.4 %collective-permute-start.5 = (bf16[384,512]{1,0:T(8,128)(2,1)}, bf16[384,512]{1,0:T(8,128)(2,1)}, u32[]{:S(2)}, u32[]{:S(2)}) collective-permute-start(bf16[384,512]{1,0:T(8,128)(2,1)} %get-tuple-element.18), channel_id=1, source_target_pairs={{0,16},{16,0},{1,17},{17,1},{2,18},{18,2},{3,19},{19,3},{4,20},{20... | collective-permute-start | bytes 1179656 | tf_op jit(solution)/shard_map/ppermute | solution.py:182
  83.1 3.3 %copy-start.3 = (f32[2,384,512]{2,1,0:T(8,128)S(1)}, f32[2,384,512]{2,1,0:T(8,128)}, u32[]{:S(2)}) copy-start(f32[2,384,512]{2,1,0:T(8,128)} %get-tuple-element.20.own) | copy-start | bytes 4718596
  85.6 79.0 %collective-permute-start.2 = (bf16[384,512]{1,0:T(8,128)(2,1)}, bf16[384,512]{1,0:T(8,128)(2,1)}, u32[]{:S(2)}, u32[]{:S(2)}) collective-permute-start(bf16[384,512]{1,0:T(8,128)(2,1)} %get-tuple-element.17), channel_id=1, source_target_pairs={{0,16},{16,0},{1,17},{17,1},{2,18},{18,2},{3,19},{19,3},{4,20},{20... | collective-permute-start | bytes 1179656 | tf_op jit(solution)/shard_map/ppermute | solution.py:182
  88.9 19.3 %copy-start.8 = (f32[8,384]{1,0:T(8,128)}, f32[8,384]{1,0:T(8,128)S(1)}, u32[]{:S(2)}) copy-start(f32[8,384]{1,0:T(8,128)S(1)} %collective-permute-done.6.info) | copy-start | bytes 36868
  88.9 78.6 %collective-permute-start.15 = (bf16[2,384,512]{2,1,0:T(8,128)(2,1)}, bf16[2,384,512]{2,1,0:T(8,128)(2,1)}, u32[]{:S(2)}, u32[]{:S(2)}) collective-permute-start(bf16[2,384,512]{2,1,0:T(8,128)(2,1)} %shard_map.81), channel_id=1, source_target_pairs={{0,16},{16,0},{1,17},{17,1},{2,18},{18,2},{3,19},{19,3},{4,20},{20... | collective-permute-start | bytes 2359304 | tf_op jit(solution)/shard_map/ppermute | solution.py:182
  93.7 73.8 %collective-permute-start.12 = (bf16[2,384,512]{2,1,0:T(8,128)(2,1)}, bf16[2,384,512]{2,1,0:T(8,128)(2,1)}, u32[]{:S(2)}, u32[]{:S(2)}) collective-permute-start(bf16[2,384,512]{2,1,0:T(8,128)(2,1)} %shard_map.80), channel_id=1, source_target_pairs={{0,16},{16,0},{1,17},{17,1},{2,18},{18,2},{3,19},{19,3},{4,20},{20... | collective-permute-start | bytes 2359304 | tf_op jit(solution)/shard_map/ppermute | solution.py:182
  108.2 0.7 copy-start.4
  108.9 57.0 %copy-start.1 = (f32[2,384,512]{2,1,0:T(8,128)S(1)}, f32[2,384,512]{2,1,0:T(8,128)}, u32[]{:S(2)}) copy-start(f32[2,384,512]{2,1,0:T(8,128)} %get-tuple-element.26.own) | copy-start | bytes 4718596
  108.9 57.0 %copy-start.9 = (f32[8,384]{1,0:T(8,128)S(1)}, f32[8,384]{1,0:T(8,128)}, u32[]{:S(2)}) copy-start(f32[8,384]{1,0:T(8,128)} %copy-done.8) | copy-start | bytes 36868
  108.9 57.0 %collective-permute-start.16 = (bf16[2,384,512]{2,1,0:T(8,128)(2,1)}, bf16[2,384,512]{2,1,0:T(8,128)(2,1)S(1)}, u32[]{:S(2)}, u32[]{:S(2)}) collective-permute-start(bf16[2,384,512]{2,1,0:T(8,128)(2,1)} %get-tuple-element.27), channel_id=1, source_target_pairs={{0,4},{4,8},{8,12},{1,5},{5,9},{9,13},{2,6},{6,10},{10,14},{3,7},{... | collective-permute-start | bytes 2359304 | tf_op jit(solution)/shard_map/ppermute | solution.py:177
  112.6 53.4 %collective-permute-start.17 = (bf16[2,384,512]{2,1,0:T(8,128)(2,1)}, bf16[2,384,512]{2,1,0:T(8,128)(2,1)S(1)}, u32[]{:S(2)}, u32[]{:S(2)}) collective-permute-start(bf16[2,384,512]{2,1,0:T(8,128)(2,1)} %get-tuple-element.28), channel_id=1, source_target_pairs={{4,0},{8,4},{12,8},{5,1},{9,5},{13,9},{6,2},{10,6},{14,10},{7,3},{... | collective-permute-start | bytes 2359304 | tf_op jit(solution)/shard_map/ppermute | solution.py:177

commit v2 on v1

v2 whole, which is shorter than its diff:
```python
import functools
import math

import jax
import jax.numpy as jnp
from jax import lax
from jax.experimental import pallas as pl
from jax.experimental.pallas import tpu as pltpu
from jax.sharding import PartitionSpec as P

HEADS = 12
HEAD_DIM = 128
EPSILON = 1e-06
ROOT_SCALE = HEAD_DIM ** (-0.5)
EXP2_SCALE = ROOT_SCALE * math.log2(math.e)
GROUPS = ((0, 4, False), (4, 4, False), (8, 4, True))
VMEM_LIMIT = 48 * 1024 * 1024
COST = pl.CostEstimate(flops=1, bytes_accessed=1, transcendentals=0)


def dot_nt(left, right):
    return lax.dot_general(
        left, right, (((1,), (1,)), ((), ())), preferred_element_type=jnp.float32
    )


def dot_nn(left, right):
    return lax.dot_general(
        left, right, (((1,), (0,)), ((), ())), preferred_element_type=jnp.float32
    )


def dot_tn(left, right):
    return lax.dot_general(
        left, right, (((0,), (0,)), ((), ())), preferred_element_type=jnp.float32
    )


def normalize(source, gain):
    floats = source.astype(jnp.float32)
    scaled = lax.rsqrt(jnp.mean(floats * floats, axis=-1, keepdims=True) + EPSILON)
    normed = floats * scaled
    return floats, scaled, normed, (normed * gain).astype(jnp.bfloat16)


def norm_back(grad_hat, floats, scaled, gain):
    scaled_grad = gain * grad_hat
    projected = jnp.sum(scaled_grad * floats, axis=-1, keepdims=True)
    return scaled * scaled_grad - (scaled**3 * projected * (1.0 / HEAD_DIM)) * floats


def pack_kernel(first_in, second_in, out):
    out[0] = first_in[...]
    out[1] = second_in[...]


def main_kernel(
    info, query, grad, key, value, pair_even, pair_odd,
    query_out, own_out, even_out, odd_out, gain_out,
):
    query_gain = info[0:1, :HEAD_DIM]
    key_gain = info[1:2, :HEAD_DIM]
    query_floats, query_scale, query_normed, query_hat = normalize(query[...], query_gain)
    grad_in = grad[...]
    sides = (
        (key[...], value[...], None),
        (pair_even[0], pair_even[1], info[2:3, :]),
        (pair_odd[0], pair_odd[1], info[3:4, :]),
    )
    parts = []
    totals = None
    for key_in, value_in, live in sides:
        _, _, key_normed, key_hat = normalize(key_in, key_gain)
        weights = jnp.exp2(dot_nt(key_hat, query_hat) * EXP2_SCALE)
        grad_probs = dot_nt(value_in, grad_in)
        weight_sum = jnp.sum(weights, axis=0, keepdims=True)
        cross_sum = jnp.sum(weights * grad_probs, axis=0, keepdims=True)
        if live is not None:
            weight_sum = weight_sum * live
            cross_sum = cross_sum * live
        totals = weight_sum if totals is None else totals + weight_sum
        crosses = cross_sum if live is None else crosses + cross_sum
        parts.append((key_normed, key_hat, weights, grad_probs, live))
    inverse = 1.0 / totals
    deltas = crosses * inverse
    query_grad_t = None
    key_gain_sum = None
    for (key_normed, key_hat, weights, grad_probs, live), out in zip(
        parts, (own_out, even_out, odd_out)
    ):
        probs = weights * (inverse if live is None else inverse * live)
        dscores = (probs * (grad_probs - deltas)).astype(jnp.bfloat16)
        key_part = dot_nn(dscores, query_hat) * ROOT_SCALE
        value_part = dot_nn(probs.astype(jnp.bfloat16), grad_in)
        out[0] = key_part.astype(out.dtype)
        out[1] = value_part.astype(out.dtype)
        gain_part = jnp.sum(key_part * key_normed, axis=0, keepdims=True)
        key_gain_sum = gain_part if key_gain_sum is None else key_gain_sum + gain_part
        query_part = dot_tn(key_hat, dscores)
        query_grad_t = query_part if query_grad_t is None else query_grad_t + query_part
    query_grad = query_grad_t.T * ROOT_SCALE
    query_out[...] = norm_back(query_grad, query_floats, query_scale, query_gain).astype(
        query_out.dtype
    )
    query_gain_sum = jnp.sum(query_grad * query_normed, axis=0, keepdims=True)

    @pl.when(pl.program_id(0) == 0)
    def _():
        gain_out[...] = jnp.zeros_like(gain_out)

    gain_out[0:1, :] += query_gain_sum
    gain_out[1:2, :] += key_gain_sum


def finished(info, key, own, from_even, from_odd):
    key_gain = info[1:2, :HEAD_DIM]
    key_floats, key_scale, _, _ = normalize(key[...], key_gain)
    key_grad = own[0] + from_even[0].astype(jnp.float32) + from_odd[0].astype(jnp.float32)
    value_grad = own[1] + from_even[1].astype(jnp.float32) + from_odd[1].astype(jnp.float32)
    return norm_back(key_grad, key_floats, key_scale, key_gain), value_grad


def finish_kernel(info, key, own, from_even, from_odd, out):
    key_grad, value_grad = finished(info, key, own, from_even, from_odd)
    out[0] = key_grad.astype(out.dtype)
    out[1] = value_grad.astype(out.dtype)


def last_kernel(info, key, own, from_even, from_odd, *rest, places, first, count):
    pieces, (out, held, sems) = rest[: len(places)], rest[len(places) :]
    head = pl.program_id(0)
    copies = [
        pltpu.make_async_copy(
            piece, out.at[planes, :, start : start + piece.shape[-1]], sems.at[slot]
        )
        for slot, (piece, (planes, start)) in enumerate(zip(pieces, places))
    ]

    def head_copy(index):
        start = pl.multiple_of((first + index) * HEAD_DIM, HEAD_DIM)
        return pltpu.make_async_copy(
            held.at[index],
            out.at[pl.ds(1, 2), :, pl.ds(start, HEAD_DIM)],
            sems.at[len(places) + index],
        )

    @pl.when(head == 0)
    def _():
        for copy in copies:
            copy.start()

    key_grad, value_grad = finished(info, key, own, from_even, from_odd)
    held[head, 0] = key_grad.astype(held.dtype)
    held[head, 1] = value_grad.astype(held.dtype)
    head_copy(head).start()

    @pl.when(head == count - 1)
    def _():
        for copy in copies:
            copy.wait()
        for index in range(count):
            head_copy(index).wait()


def head_block(rows, first, slot=None):
    if slot is None:
        return pl.BlockSpec((rows, HEAD_DIM), lambda head: (0, first + head))
    return pl.BlockSpec((None, rows, HEAD_DIM), lambda head: (slot, 0, first + head))


def pair_block(rows):
    return pl.BlockSpec((2, rows, HEAD_DIM), lambda head: (0, 0, head))


def whole_block(shape):
    return pl.BlockSpec(shape, lambda head: (0,) * len(shape))


def pack_call(first_in, second_in, first, count):
    rows = first_in.shape[0]
    return pl.pallas_call(
        pack_kernel,
        grid=(count,),
        in_specs=[head_block(rows, first)] * 2,
        out_specs=pair_block(rows),
        out_shape=jax.ShapeDtypeStruct((2, rows, count * HEAD_DIM), jnp.bfloat16),
        cost_estimate=COST,
    )(first_in, second_in)


def main_call(info, operands, pair_even, pair_odd, count):
    rows = pair_even.shape[1]
    lanes = count * HEAD_DIM
    return pl.pallas_call(
        main_kernel,
        grid=(count,),
        in_specs=[whole_block(info.shape)]
        + [head_block(rows, first, slot) for _, first, slot in operands]
        + [pair_block(rows)] * 2,
        out_specs=[head_block(rows, 0)] + [pair_block(rows)] * 3 + [whole_block((8, HEAD_DIM))],
        out_shape=[
            jax.ShapeDtypeStruct((rows, lanes), jnp.bfloat16),
            jax.ShapeDtypeStruct((2, rows, lanes), jnp.float32),
            jax.ShapeDtypeStruct((2, rows, lanes), jnp.bfloat16),
            jax.ShapeDtypeStruct((2, rows, lanes), jnp.bfloat16),
            jax.ShapeDtypeStruct((8, HEAD_DIM), jnp.float32),
        ],
        compiler_params=pltpu.CompilerParams(vmem_limit_bytes=VMEM_LIMIT),
        cost_estimate=COST,
    )(info, *[array for array, _, _ in operands], pair_even, pair_odd)


def finish_call(info, key, own, from_even, from_odd, count):
    array, first, slot = key
    rows = own.shape[1]
    return pl.pallas_call(
        finish_kernel,
        grid=(count,),
        in_specs=[whole_block(info.shape), head_block(rows, first, slot)] + [pair_block(rows)] * 3,
        out_specs=pair_block(rows),
        out_shape=jax.ShapeDtypeStruct((2, rows, count * HEAD_DIM), jnp.bfloat16),
        compiler_params=pltpu.CompilerParams(vmem_limit_bytes=VMEM_LIMIT),
        cost_estimate=COST,
    )(info, array, own, from_even, from_odd)


def last_call(info, key, own, from_even, from_odd, pieces, places, first, count):
    array, offset, slot = key
    rows = own.shape[1]
    anywhere = pl.BlockSpec(memory_space=pl.ANY)
    return pl.pallas_call(
        functools.partial(last_kernel, places=places, first=first, count=count),
        grid=(count,),
        in_specs=[whole_block(info.shape), head_block(rows, offset, slot)]
        + [pair_block(rows)] * 3
        + [anywhere] * len(pieces),
        out_specs=anywhere,
        out_shape=jax.ShapeDtypeStruct((3, rows, HEADS * HEAD_DIM), jnp.bfloat16),
        scratch_shapes=[
            pltpu.VMEM((count, 2, rows, HEAD_DIM), jnp.bfloat16),
            pltpu.SemaphoreType.DMA((len(pieces) + count,)),
        ],
        compiler_params=pltpu.CompilerParams(vmem_limit_bytes=VMEM_LIMIT),
        cost_estimate=COST,
    )(info, array, own, from_even, from_odd, *pieces)


def partner(tile, parity, count):
    other = tile + 1 if tile % 2 == parity else tile - 1
    return other if 0 <= other < count else tile


def exchanged(value, parity):
    count, width = lax.axis_size("seq"), lax.axis_size("dp")
    pairs = []
    for tile in range(count):
        other = partner(tile, parity, count)
        for sample in range(width):
            moved = sample ^ 1 if other == tile and width % 2 == 0 else sample
            pairs.append((tile * width + sample, other * width + moved))
    return lax.ppermute(value, ("seq", "dp"), pairs)


def total_over(value, axis):
    count = lax.axis_size(axis)
    step = 1
    while step < count:
        value = value + lax.ppermute(value, axis, [(i, i ^ step) for i in range(count)])
        step *= 2
    return value


def turned(value, step):
    count = lax.axis_size("pipe")
    return lax.ppermute(value, "pipe", [(i, (i + step) % count) for i in range(count)])


def listing(listed, tile, seq_count, parity):
    step = jnp.where(tile % 2 == parity, 1, -1)
    other = tile + step
    inside = (other >= 0) & (other < seq_count)
    return (inside & jnp.any(listed == other)).astype(jnp.float32)


def local(queries, keys, values, grad_out, norm_gains, kv_tiles):
    query, key, value, grad = (a[0, 0, 0] for a in (queries, keys, values, grad_out))
    rows = query.shape[0]
    tile = lax.axis_index("seq")
    seq_count = lax.axis_size("seq")
    listed = kv_tiles[0, 0, 0]
    info = jnp.concatenate(
        [
            jnp.pad(norm_gains[0], ((0, 0), (0, rows - HEAD_DIM))),
            jnp.full((1, rows), listing(listed, tile, seq_count, 0)),
            jnp.full((1, rows), listing(listed, tile, seq_count, 1)),
            jnp.zeros((4, rows), jnp.float32),
        ],
        axis=0,
    )
    sources = []
    for first, count, away in GROUPS:
        pair = pack_call(key, value, first, count)
        if away:
            pair = turned(pair, -1)
            asked = turned(pack_call(query, grad, first, count), -1)
            operands = ((asked, 0, 0), (asked, 0, 1), (pair, 0, 0), (pair, 0, 1))
            sources.append((turned(info, -1), operands, pair))
        else:
            operands = tuple((a, first, None) for a in (query, grad, key, value))
            sources.append((info, operands, pair))
    gathered = [(exchanged(pair, 0), exchanged(pair, 1)) for _, _, pair in sources]
    gain_sums = [jnp.zeros((2, HEAD_DIM), jnp.float32)] * 2
    pieces, places = [], []
    out = None
    for (first, count, away), (group_info, operands, _), (even, odd) in zip(
        GROUPS, sources, gathered
    ):
        query_low, own, to_even, to_odd, gain = main_call(
            group_info, operands, even, odd, count
        )
        gain_sums[away] = gain_sums[away] + gain[:2]
        from_even = exchanged(to_even, 0)
        from_odd = exchanged(to_odd, 1)
        last = (first, count, away) == GROUPS[-1]
        pieces.append(query_low if away else turned(query_low, -1))
        places.append((0, first * HEAD_DIM))
        if last:
            out = last_call(
                group_info, operands[2], own, from_even, from_odd, pieces, tuple(places), first, count
            )
        else:
            pair_low = finish_call(group_info, operands[2], own, from_even, from_odd, count)
            pieces.append(pair_low if away else turned(pair_low, -1))
            places.append((slice(1, 3), first * HEAD_DIM))
    summed = gain_sums[0] + turned(gain_sums[1], 1)
    for axis in ("seq", "dp"):
        summed = total_over(summed, axis)
    tokens = lax.axis_size("dp") * seq_count * rows * HEADS
    return (out[None, :, None, None], (summed / math.sqrt(tokens))[None])


def solution(mesh):
    placed = (
        P("pipe", "dp", "seq", None, None),
        P("pipe", "dp", "seq", None, None),
        P("pipe", "dp", "seq", None, None),
        P("pipe", "dp", "seq", None, None),
        P("pipe", None, None),
        P("pipe", "dp", "seq", None),
    )
    return jax.shard_map(
        local,
        mesh=mesh,
        in_specs=placed,
        out_specs=(P("pipe", None, "dp", "seq", None, None), P("pipe", None, None)),
        check_vma=False,
    )
```

time: 171 us -> 157 us (0.918)
  waiting for transfers between devices: 21.7 us -> 71.1 us
  blocking collectives: 48.8 us -> 0 us
  starting transfers between devices: 43.1 us -> 28.8 us
  Pallas kernels: 37.5 us -> 51 us
  other arithmetic: 10.3 us -> 1.3 us
  local copies, waits for them, and re-layouts: 7.13 us -> 1.77 us
    ppermute x18 -> x24, waiting for transfers between devices: 21.7 us -> 71.1 us  [the longest x8 46.2 us: turned(): lax.ppermute(value, 'pipe', [(i, (i + step) % count) for i in range(count)])]
    psum x1 -> x0, blocking collectives: 48.8 us -> none  [local(): summed = lax.psum(contribution, ('pipe', 'seq', 'dp'))]
    pallas_call x0 -> x5, Pallas kernels: none -> 17.5 us  [the longest x4 13.5 us: pack_call(): pl.pallas_call(pack_kernel, grid=(count,), in_specs=[head_block(rows, fir...]
    ppermute x18 -> x24, starting transfers between devices: 43.1 us -> 28.8 us  [the longest x12 13.8 us: exchanged(): return lax.ppermute(value, ('seq', 'dp'), pairs)]
    pallas_call x3 -> x2, Pallas kernels: 6.53 us -> 3.09 us  [finish_call(): pl.pallas_call(finish_kernel, grid=(count,), in_specs=[whole_block(info.s...]
    another operation x3 -> x0, other arithmetic: 3.27 us -> none  [the longest x2 1.93 us: local(): pair = jnp.stack([lanes(key, first, count), lanes(value, first, count)])]
    unnamed x1 -> x0, other arithmetic: 3.06 us -> none
    slice x1 -> x0, local copies, waits for them, and re-layouts: 2.06 us -> none  [local(): moved[2:]]
  transfers between devices with their start and end apart: 18 -> 24, of which waited for: 6 -> 10; matrix products, arithmetic and copies ran while one was open for 6% -> 1% of each run, Pallas kernels for 22% -> 28%
where the time goes in v2:
time: 157 us; the launch traced here: 156 us
  waiting for transfers between devices  71.1 us (45%)
  Pallas kernels  51 us (32%)
  starting transfers between devices  28.8 us (18%)
  between operations  2.04 us (1%)
  local copies, waits for them, and re-layouts  1.77 us (1%)
    ppermute x8, waiting for transfers between devices, turned(): lax.ppermute(value, 'pipe', [(i, (i + step) % count) for i in range(count)])  46.2 us
    pallas_call x3, Pallas kernels, main_call(): pl.pallas_call(main_kernel, grid=(count,), in_specs=[whole_block(info.sha...  30.4 us
    ppermute x4, waiting for transfers between devices, total_over(): lax.ppermute(value, axis, [(i, i ^ step) for i in range(count)])  19.8 us
    ppermute x12, starting transfers between devices, exchanged(): return lax.ppermute(value, ('seq', 'dp'), pairs)  13.8 us
    pallas_call x4, Pallas kernels, pack_call(): pl.pallas_call(pack_kernel, grid=(count,), in_specs=[head_block(rows, fir...  13.5 us
    ppermute x8, starting transfers between devices, turned(): lax.ppermute(value, 'pipe', [(i, (i + step) % count) for i in range(count)])  7.73 us
    ppermute x4, starting transfers between devices, total_over(): lax.ppermute(value, axis, [(i, i ^ step) for i in range(count)])  7.23 us
    ppermute x12, waiting for transfers between devices, exchanged(): return lax.ppermute(value, ('seq', 'dp'), pairs)  5.11 us
  transfers between devices with their start and end apart: 24, of which 10 were waited for; matrix products, arithmetic and copies ran while one was open for 1% of the time, Pallas kernels for 28%

profile of v2, /device:TPU:0, one launch (start us, length us, event | category | flops | bytes accessed | tf_op | source)
XLA Modules:
  0.0 156.0 jit_solution(11413698338177717291)
XLA Ops:
  0.6 3.3 %shard_map.77 = bf16[2,384,512]{2,1,0:T(8,128)(2,1)} custom-call(bf16[384,1536]{1,0:T(8,128)(2,1)} %bitcast.12, bf16[384,1536]{1,0:T(8,128)(2,1)} %bitcast.25), custom_call_target="tpu_custom_call" | custom-call | flops 1 | bytes 1 | tf_op jit(solution)/shard_map/pallas_call | solution.py:181
  3.9 2.9 %collective-permute-start.1 = (bf16[2,384,512]{2,1,0:T(8,128)(2,1)}, bf16[2,384,512]{2,1,0:T(8,128)(2,1)S(1)}, u32[]{:S(2)}, u32[]{:S(2)}) collective-permute-start(bf16[2,384,512]{2,1,0:T(8,128)(2,1)} %shard_map.77), channel_id=1, source_target_pairs={{0,16},{16,0},{1,17},{17,1},{2,18},{18,2},{3,19},{19,3},{4,20},{20... | collective-permute-start | bytes 2359304 | tf_op jit(solution)/shard_map/ppermute | solution.py:275
  6.9 3.3 %shard_map.80 = bf16[2,384,512]{2,1,0:T(8,128)(2,1)} custom-call(bf16[384,1536]{1,0:T(8,128)(2,1)} %bitcast.13, bf16[384,1536]{1,0:T(8,128)(2,1)} %bitcast.26), custom_call_target="tpu_custom_call" | custom-call | flops 1 | bytes 1 | tf_op jit(solution)/shard_map/pallas_call | solution.py:181
  10.2 1.6 %collective-permute-start.7 = (bf16[2,384,512]{2,1,0:T(8,128)(2,1)}, bf16[2,384,512]{2,1,0:T(8,128)(2,1)}, u32[]{:S(2)}, u32[]{:S(2)}) collective-permute-start(bf16[2,384,512]{2,1,0:T(8,128)(2,1)} %shard_map.80), channel_id=1, source_target_pairs={{0,4},{1,5},{2,6},{3,7},{4,0},{5,1},{6,2},{7,3},{8,12},{9,13},{10,... | collective-permute-start | bytes 2359304 | tf_op jit(solution)/shard_map/ppermute | solution.py:261
  14.6 3.3 %shard_map.83 = bf16[2,384,512]{2,1,0:T(8,128)(2,1)} custom-call(bf16[384,1536]{1,0:T(8,128)(2,1)} %bitcast.14, bf16[384,1536]{1,0:T(8,128)(2,1)} %bitcast.27), custom_call_target="tpu_custom_call" | custom-call | flops 1 | bytes 1 | tf_op jit(solution)/shard_map/pallas_call | solution.py:181
  17.9 3.1 %collective-permute-start.13 = (bf16[2,384,512]{2,1,0:T(8,128)(2,1)}, bf16[2,384,512]{2,1,0:T(8,128)(2,1)}, u32[]{:S(2)}, u32[]{:S(2)}) collective-permute-start(bf16[2,384,512]{2,1,0:T(8,128)(2,1)} %shard_map.83), channel_id=1, source_target_pairs={{0,4},{1,5},{2,6},{3,7},{4,0},{5,1},{6,2},{7,3},{8,12},{9,13},{10,... | collective-permute-start | bytes 2359304 | tf_op jit(solution)/shard_map/ppermute | solution.py:261
  21.1 3.8 %collective-permute-done.info = f32[8,384]{1,0:T(8,128)S(1)} collective-permute-done((f32[8,384]{1,0:T(8,128)S(1)}, f32[8,384]{1,0:T(8,128)S(1)}, u32[]{:S(2)}, u32[]{:S(2)}) %collective-permute-start) | collective-permute-done | bytes 12320 | tf_op jit(solution)/shard_map/ppermute | solution.py:275
  24.9 3.5 %shard_map.78 = bf16[2,384,512]{2,1,0:T(8,128)(2,1)} custom-call(bf16[384,1536]{1,0:T(8,128)(2,1)} %bitcast.19, bf16[384,1536]{1,0:T(8,128)(2,1)} %bitcast.22), custom_call_target="tpu_custom_call" | custom-call | flops 1 | bytes 1 | tf_op jit(solution)/shard_map/pallas_call | solution.py:181
  28.4 1.7 %collective-permute-start.2 = (bf16[2,384,512]{2,1,0:T(8,128)(2,1)}, bf16[2,384,512]{2,1,0:T(8,128)(2,1)S(1)}, u32[]{:S(2)}, u32[]{:S(2)}) collective-permute-start(bf16[2,384,512]{2,1,0:T(8,128)(2,1)} %shard_map.78), channel_id=1, source_target_pairs={{0,16},{16,0},{1,17},{17,1},{2,18},{18,2},{3,19},{19,3},{4,20},{20... | collective-permute-start | bytes 2359304 | tf_op jit(solution)/shard_map/ppermute | solution.py:275
  30.2 0.8 collective-permute-done.7.pair_even
  31.0 2.3 %collective-permute-start.3 = (bf16[2,384,512]{2,1,0:T(8,128)(2,1)S(1)}, bf16[2,384,512]{2,1,0:T(8,128)(2,1)S(1)}, u32[]{:S(2)}, u32[]{:S(2)}) collective-permute-start(bf16[2,384,512]{2,1,0:T(8,128)(2,1)S(1)} %collective-permute-done.1.key.value), channel_id=1, source_target_pairs={{0,4},{1,5},{2,6},{3,7},{4,0},{5,1},{6,2},{7,3},{8,12},{9,13},{10,... | collective-permute-start | bytes 2359304 | tf_op jit(solution)/shard_map/ppermute | solution.py:261
  33.3 10.3 %shard_map.81 = (bf16[384,512]{1,0:T(8,128)(2,1)S(1)}, f32[2,384,512]{2,1,0:T(8,128)}, bf16[2,384,512]{2,1,0:T(8,128)(2,1)}, bf16[2,384,512]{2,1,0:T(8,128)(2,1)S(1)}, f32[8,128]{1,0:T(8,128)S(1)}) custom-call(f32[8,384]{1,0:T(8,128)S(1)} %fusion.1.info, bf16[384,1536]{1,0:T(8,128)(2,1)S(1)} %bitcast.20, bf16[384,1536]{1,0:T(8,128)(2,1)S(1)} %bitcast.23, ...), custom_call_target="tpu_custom_call" | custom-call | flops 1 | bytes 1 | tf_op jit(solution)/shard_map/pallas_call | solution.py:194
  44.4 3.4 %collective-permute-done.13.pair_even = bf16[2,384,512]{2,1,0:T(8,128)(2,1)} collective-permute-done((bf16[2,384,512]{2,1,0:T(8,128)(2,1)}, bf16[2,384,512]{2,1,0:T(8,128)(2,1)}, u32[]{:S(2)}, u32[]{:S(2)}) %collective-permute-start.13) | collective-permute-done | bytes 786464 | tf_op jit(solution)/shard_map/ppermute | solution.py:261
  47.9 1.6 %collective-permute-start.10 = (bf16[2,384,512]{2,1,0:T(8,128)(2,1)}, bf16[2,384,512]{2,1,0:T(8,128)(2,1)S(1)}, u32[]{:S(2)}, u32[]{:S(2)}) collective-permute-start(bf16[2,384,512]{2,1,0:T(8,128)(2,1)} %get-tuple-element.22), channel_id=1, source_target_pairs={{0,4},{1,5},{2,6},{3,7},{4,0},{5,1},{6,2},{7,3},{8,12},{9,13},{10,... | collective-permute-start | bytes 2359304 | tf_op jit(solution)/shard_map/ppermute | solution.py:261
  49.4 10.4 %shard_map.84 = (bf16[384,512]{1,0:T(8,128)(2,1)S(1)}, f32[2,384,512]{2,1,0:T(8,128)}, bf16[2,384,512]{2,1,0:T(8,128)(2,1)}, bf16[2,384,512]{2,1,0:T(8,128)(2,1)}, f32[8,128]{1,0:T(8,128)S(1)}) custom-call(f32[8,384]{1,0:T(8,128)S(1)} %fusion.1.info, bf16[384,1536]{1,0:T(8,128)(2,1)S(1)} %bitcast.21, bf16[384,1536]{1,0:T(8,128)(2,1)S(1)} %bitcast.24, ...), custom_call_target="tpu_custom_call" | custom-call | flops 1 | bytes 1 | tf_op jit(solution)/shard_map/pallas_call | solution.py:194
  60.6 3.2 %collective-permute-start.16 = (bf16[2,384,512]{2,1,0:T(8,128)(2,1)}, bf16[2,384,512]{2,1,0:T(8,128)(2,1)S(1)}, u32[]{:S(2)}, u32[]{:S(2)}) collective-permute-start(bf16[2,384,512]{2,1,0:T(8,128)(2,1)} %get-tuple-element.26), channel_id=1, source_target_pairs={{0,4},{1,5},{2,6},{3,7},{4,0},{5,1},{6,2},{7,3},{8,12},{9,13},{10,... | collective-permute-start | bytes 2359304 | tf_op jit(solution)/shard_map/ppermute | solution.py:261
  63.8 0.8 collective-permute-done.3.pair_even
  64.6 9.7 %shard_map.79 = (bf16[384,512]{1,0:T(8,128)(2,1)S(1)}, f32[2,384,512]{2,1,0:T(8,128)}, bf16[2,384,512]{2,1,0:T(8,128)(2,1)S(1)}, bf16[2,384,512]{2,1,0:T(8,128)(2,1)S(1)}, f32[8,128]{1,0:T(8,128)S(1)}) custom-call(f32[8,384]{1,0:T(8,128)S(1)} %collective-permute-done.info, bf16[2,384,512]{2,1,0:T(8,128)(2,1)S(1)} %collective-permute-done.2.query.grad, ...), custom_call_target="tpu_custom_call" | custom-call | flops 1 | bytes 1 | tf_op jit(solution)/shard_map/pallas_call | solution.py:194
  74.4 3.5 %collective-permute-done.19 = f32[2,128]{1,0:T(2,128)S(1)} collective-permute-done((f32[2,128]{1,0:T(2,128)S(1)}, f32[2,128]{1,0:T(2,128)S(1)}, u32[]{:S(2)}, u32[]{:S(2)}) %collective-permute-start.19) | collective-permute-done | bytes 1056 | tf_op jit(solution)/shard_map/ppermute | solution.py:275
  77.9 3.1 %collective-permute-start.20 = (f32[2,128]{1,0:T(2,128)S(1)}, f32[2,128]{1,0:T(2,128)S(1)}, u32[]{:S(2)}, u32[]{:S(2)}) collective-permute-start(f32[2,128]{1,0:T(2,128)S(1)} %add_add_fusion), channel_id=1, source_target_pairs={{0,4},{4,0},{8,12},{12,8},{1,5},{5,1},{9,13},{13,9},{2,6},{6,2},{1... | collective-permute-start | bytes 3080 | tf_op jit(solution)/shard_map/ppermute | solution.py:268
  81.0 15.9 %collective-permute-done.20 = f32[2,128]{1,0:T(2,128)S(1)} collective-permute-done((f32[2,128]{1,0:T(2,128)S(1)}, f32[2,128]{1,0:T(2,128)S(1)}, u32[]{:S(2)}, u32[]{:S(2)}) %collective-permute-start.20) | collective-permute-done | bytes 1056 | tf_op jit(solution)/shard_map/ppermute | solution.py:268
  96.9 2.6 %collective-permute-start.21 = (f32[2,128]{1,0:T(2,128)S(1)}, f32[2,128]{1,0:T(2,128)S(1)}, u32[]{:S(2)}, u32[]{:S(2)}) collective-permute-start(f32[2,128]{1,0:T(2,128)S(1)} %add.36), channel_id=1, source_target_pairs={{0,8},{4,12},{8,0},{12,4},{1,9},{5,13},{9,1},{13,5},{2,10},{6,14},... | collective-permute-start | bytes 3080 | tf_op jit(solution)/shard_map/ppermute | solution.py:268
  99.5 1.9 %collective-permute-done.21 = f32[2,128]{1,0:T(2,128)S(1)} collective-permute-done((f32[2,128]{1,0:T(2,128)S(1)}, f32[2,128]{1,0:T(2,128)S(1)}, u32[]{:S(2)}, u32[]{:S(2)}) %collective-permute-start.21) | collective-permute-done | bytes 1056 | tf_op jit(solution)/shard_map/ppermute | solution.py:268
  101.8 1.8 %collective-permute-start.5 = (bf16[2,384,512]{2,1,0:T(8,128)(2,1)S(1)}, bf16[2,384,512]{2,1,0:T(8,128)(2,1)S(1)}, u32[]{:S(2)}, u32[]{:S(2)}) collective-permute-start(bf16[2,384,512]{2,1,0:T(8,128)(2,1)S(1)} %get-tuple-element.18), channel_id=1, source_target_pairs={{0,4},{1,5},{2,6},{3,7},{4,0},{5,1},{6,2},{7,3},{8,12},{9,13},{10,... | collective-permute-start | bytes 2359304 | tf_op jit(solution)/shard_map/ppermute | solution.py:261
  103.6 1.6 %shard_map.82 = bf16[2,384,512]{2,1,0:T(8,128)(2,1)S(1)} custom-call(f32[8,384]{1,0:T(8,128)S(1)} %fusion.1.info, bf16[384,1536]{1,0:T(8,128)(2,1)S(1)} %bitcast.17, f32[2,384,512]{2,1,0:T(8,128)S(1)} %copy-done.3, bf16[2,384,512]{2,1,0:T(8,128)(2,1)S(1)} %collective-permute-done.10.from_even, bf16[2,384,512]{2,1,0:T(8,128)(2,1)S(1)} %collective-permute-done.11.from_odd), custom_call_target="tpu_custom_call" | custom-call | flops 1 | bytes 1 | tf_op jit(solution)/shard_map/pallas_call | solution.py:216
  105.4 1.5 collective-permute-start.12
  106.9 1.5 shard_map.85
  109.0 2.3 %collective-permute-done.9.rest_0_ = bf16[384,512]{1,0:T(8,128)(2,1)S(1)} collective-permute-done((bf16[384,512]{1,0:T(8,128)(2,1)S(1)}, bf16[384,512]{1,0:T(8,128)(2,1)S(1)}, u32[]{:S(2)}, u32[]{:S(2)}) %collective-permute-start.9) | collective-permute-done | bytes 393248 | tf_op jit(solution)/shard_map/ppermute | solution.py:275
  111.3 1.5 collective-permute-start.23
  112.8 2.0 %collective-permute-done.23 = f32[2,128]{1,0:T(2,128)S(1)} collective-permute-done((f32[2,128]{1,0:T(2,128)S(1)}, f32[2,128]{1,0:T(2,128)S(1)}, u32[]{:S(2)}, u32[]{:S(2)}) %collective-permute-start.23) | collective-permute-done | bytes 1056 | tf_op jit(solution)/shard_map/ppermute | solution.py:268
  115.5 36.5 %collective-permute-done.15.rest_2_ = bf16[384,512]{1,0:T(8,128)(2,1)S(1)} collective-permute-done((bf16[384,512]{1,0:T(8,128)(2,1)S(1)}, bf16[384,512]{1,0:T(8,128)(2,1)S(1)}, u32[]{:S(2)}, u32[]{:S(2)}) %collective-permute-start.15) | collective-permute-done | bytes 393248 | tf_op jit(solution)/shard_map/ppermute | solution.py:275
  152.0 4.0 %shard_map.86 = bf16[3,384,1536]{2,1,0:T(8,128)(2,1)} custom-call(f32[8,384]{1,0:T(8,128)S(1)} %collective-permute-done.info, bf16[2,384,512]{2,1,0:T(8,128)(2,1)S(1)} %collective-permute-done.1.key.value, f32[2,384,512]{2,1,0:T(8,128)} %get-tuple-element.17.own, bf16[2,384,512]{2,1,0:T(8,128)(2,1)S(1)} %collective-permute-done.5.from_even, ...), custom_call_target="tpu_custom_call" | custom-call | flops 1 | bytes 1 | tf_op jit(solution)/shard_map/pallas_call | solution.py:231
  (60 shorter events, 4.9 us)
Async XLA Ops:
  3.9 7.9 %copy-start.10 = (s32[1,1,1,3]{3,2,1,0:T(1,128)S(1)}, s32[1,1,1,3]{3,2,1,0:T(1,128)}, u32[]{:S(2)}) copy-start(s32[1,1,1,3]{3,2,1,0:T(1,128)} %param.11) | copy-start | bytes 40
  3.9 10.0 %copy-start.9 = (f32[1,2,128]{2,1,0:T(2,128)S(1)}, f32[1,2,128]{2,1,0:T(2,128)}, u32[]{:S(2)}) copy-start(f32[1,2,128]{2,1,0:T(2,128)} %param.10) | copy-start | bytes 3076
  3.9 24.5 %collective-permute-start.1 = (bf16[2,384,512]{2,1,0:T(8,128)(2,1)}, bf16[2,384,512]{2,1,0:T(8,128)(2,1)S(1)}, u32[]{:S(2)}, u32[]{:S(2)}) collective-permute-start(bf16[2,384,512]{2,1,0:T(8,128)(2,1)} %shard_map.77), channel_id=1, source_target_pairs={{0,16},{16,0},{1,17},{17,1},{2,18},{18,2},{3,19},{19,3},{4,20},{20... | collective-permute-start | bytes 2359304 | tf_op jit(solution)/shard_map/ppermute | solution.py:275
  10.2 20.8 %collective-permute-start.7 = (bf16[2,384,512]{2,1,0:T(8,128)(2,1)}, bf16[2,384,512]{2,1,0:T(8,128)(2,1)}, u32[]{:S(2)}, u32[]{:S(2)}) collective-permute-start(bf16[2,384,512]{2,1,0:T(8,128)(2,1)} %shard_map.80), channel_id=1, source_target_pairs={{0,4},{1,5},{2,6},{3,7},{4,0},{5,1},{6,2},{7,3},{8,12},{9,13},{10,... | collective-permute-start | bytes 2359304 | tf_op jit(solution)/shard_map/ppermute | solution.py:261
  11.8 21.5 %collective-permute-start.8 = (bf16[2,384,512]{2,1,0:T(8,128)(2,1)}, bf16[2,384,512]{2,1,0:T(8,128)(2,1)}, u32[]{:S(2)}, u32[]{:S(2)}) collective-permute-start(bf16[2,384,512]{2,1,0:T(8,128)(2,1)} %shard_map.80), channel_id=1, source_target_pairs={{0,1},{1,0},{2,3},{3,2},{4,8},{5,9},{6,10},{7,11},{8,4},{9,5},{10,... | collective-permute-start | bytes 2359304 | tf_op jit(solution)/shard_map/ppermute | solution.py:261
  14.0 10.9 %collective-permute-start = (f32[8,384]{1,0:T(8,128)S(1)}, f32[8,384]{1,0:T(8,128)S(1)}, u32[]{:S(2)}, u32[]{:S(2)}) collective-permute-start(f32[8,384]{1,0:T(8,128)S(1)} %fusion.1.info), channel_id=1, source_target_pairs={{0,16},{16,0},{1,17},{17,1},{2,18},{18,2},{3,19},{19,3},{4,20},{20... | collective-permute-start | bytes 36872 | tf_op jit(solution)/shard_map/ppermute | solution.py:275
  17.9 29.9 %collective-permute-start.13 = (bf16[2,384,512]{2,1,0:T(8,128)(2,1)}, bf16[2,384,512]{2,1,0:T(8,128)(2,1)}, u32[]{:S(2)}, u32[]{:S(2)}) collective-permute-start(bf16[2,384,512]{2,1,0:T(8,128)(2,1)} %shard_map.83), channel_id=1, source_target_pairs={{0,4},{1,5},{2,6},{3,7},{4,0},{5,1},{6,2},{7,3},{8,12},{9,13},{10,... | collective-permute-start | bytes 2359304 | tf_op jit(solution)/shard_map/ppermute | solution.py:261
  24.9 24.5 %collective-permute-start.14 = (bf16[2,384,512]{2,1,0:T(8,128)(2,1)}, bf16[2,384,512]{2,1,0:T(8,128)(2,1)}, u32[]{:S(2)}, u32[]{:S(2)}) collective-permute-start(bf16[2,384,512]{2,1,0:T(8,128)(2,1)} %shard_map.83), channel_id=1, source_target_pairs={{0,1},{1,0},{2,3},{3,2},{4,8},{5,9},{6,10},{7,11},{8,4},{9,5},{10,... | collective-permute-start | bytes 2359304 | tf_op jit(solution)/shard_map/ppermute | solution.py:261
  24.9 8.4 %copy-start.1 = (bf16[1,1,1,384,1536]{4,3,2,1,0:T(8,128)(2,1)S(1)}, bf16[1,1,1,384,1536]{4,3,2,1,0:T(8,128)(2,1)}, u32[]{:S(2)}) copy-start(bf16[1,1,1,384,1536]{4,3,2,1,0:T(8,128)(2,1)} %param.6) | copy-start | bytes 3538948
  24.9 8.4 %copy-start.2 = (bf16[1,1,1,384,1536]{4,3,2,1,0:T(8,128)(2,1)S(1)}, bf16[1,1,1,384,1536]{4,3,2,1,0:T(8,128)(2,1)}, u32[]{:S(2)}) copy-start(bf16[1,1,1,384,1536]{4,3,2,1,0:T(8,128)(2,1)} %param.9) | copy-start | bytes 3538948
  28.4 32.2 %collective-permute-start.2 = (bf16[2,384,512]{2,1,0:T(8,128)(2,1)}, bf16[2,384,512]{2,1,0:T(8,128)(2,1)S(1)}, u32[]{:S(2)}, u32[]{:S(2)}) collective-permute-start(bf16[2,384,512]{2,1,0:T(8,128)(2,1)} %shard_map.78), channel_id=1, source_target_pairs={{0,16},{16,0},{1,17},{17,1},{2,18},{18,2},{3,19},{19,3},{4,20},{20... | collective-permute-start | bytes 2359304 | tf_op jit(solution)/shard_map/ppermute | solution.py:275
  31.0 33.6 %collective-permute-start.3 = (bf16[2,384,512]{2,1,0:T(8,128)(2,1)S(1)}, bf16[2,384,512]{2,1,0:T(8,128)(2,1)S(1)}, u32[]{:S(2)}, u32[]{:S(2)}) collective-permute-start(bf16[2,384,512]{2,1,0:T(8,128)(2,1)S(1)} %collective-permute-done.1.key.value), channel_id=1, source_target_pairs={{0,4},{1,5},{2,6},{3,7},{4,0},{5,1},{6,2},{7,3},{8,12},{9,13},{10,... | collective-permute-start | bytes 2359304 | tf_op jit(solution)/shard_map/ppermute | solution.py:261
  33.3 31.3 %collective-permute-start.4 = (bf16[2,384,512]{2,1,0:T(8,128)(2,1)S(1)}, bf16[2,384,512]{2,1,0:T(8,128)(2,1)S(1)}, u32[]{:S(2)}, u32[]{:S(2)}) collective-permute-start(bf16[2,384,512]{2,1,0:T(8,128)(2,1)S(1)} %collective-permute-done.1.key.value), channel_id=1, source_target_pairs={{0,1},{1,0},{2,3},{3,2},{4,8},{5,9},{6,10},{7,11},{8,4},{9,5},{10,... | collective-permute-start | bytes 2359304 | tf_op jit(solution)/shard_map/ppermute | solution.py:261
  47.9 53.9 %collective-permute-start.10 = (bf16[2,384,512]{2,1,0:T(8,128)(2,1)}, bf16[2,384,512]{2,1,0:T(8,128)(2,1)S(1)}, u32[]{:S(2)}, u32[]{:S(2)}) collective-permute-start(bf16[2,384,512]{2,1,0:T(8,128)(2,1)} %get-tuple-element.22), channel_id=1, source_target_pairs={{0,4},{1,5},{2,6},{3,7},{4,0},{5,1},{6,2},{7,3},{8,12},{9,13},{10,... | collective-permute-start | bytes 2359304 | tf_op jit(solution)/shard_map/ppermute | solution.py:261
  49.4 52.3 %collective-permute-start.11 = (bf16[2,384,512]{2,1,0:T(8,128)(2,1)S(1)}, bf16[2,384,512]{2,1,0:T(8,128)(2,1)S(1)}, u32[]{:S(2)}, u32[]{:S(2)}) collective-permute-start(bf16[2,384,512]{2,1,0:T(8,128)(2,1)S(1)} %get-tuple-element.23), channel_id=1, source_target_pairs={{0,1},{1,0},{2,3},{3,2},{4,8},{5,9},{6,10},{7,11},{8,4},{9,5},{10,... | collective-permute-start | bytes 2359304 | tf_op jit(solution)/shard_map/ppermute | solution.py:261
  60.6 44.6 %collective-permute-start.16 = (bf16[2,384,512]{2,1,0:T(8,128)(2,1)}, bf16[2,384,512]{2,1,0:T(8,128)(2,1)S(1)}, u32[]{:S(2)}, u32[]{:S(2)}) collective-permute-start(bf16[2,384,512]{2,1,0:T(8,128)(2,1)} %get-tuple-element.26), channel_id=1, source_target_pairs={{0,4},{1,5},{2,6},{3,7},{4,0},{5,1},{6,2},{7,3},{8,12},{9,13},{10,... | collective-permute-start | bytes 2359304 | tf_op jit(solution)/shard_map/ppermute | solution.py:261
  64.6 36.8 %copy-start.6 = (bf16[384,512]{1,0:T(8,128)(2,1)S(1)}, bf16[384,512]{1,0:T(8,128)(2,1)}, u32[]{:S(2)}) copy-start(bf16[384,512]{1,0:T(8,128)(2,1)} %copy-done.5) | copy-start | bytes 1179652
  64.6 39.0 %copy-start = (bf16[1,1,1,384,1536]{4,3,2,1,0:T(8,128)(2,1)S(1)}, bf16[1,1,1,384,1536]{4,3,2,1,0:T(8,128)(2,1)}, u32[]{:S(2)}) copy-start(bf16[1,1,1,384,1536]{4,3,2,1,0:T(8,128)(2,1)} %param.7) | copy-start | bytes 3538948
  64.6 39.0 %copy-start.3 = (f32[2,384,512]{2,1,0:T(8,128)S(1)}, f32[2,384,512]{2,1,0:T(8,128)}, u32[]{:S(2)}) copy-start(f32[2,384,512]{2,1,0:T(8,128)} %get-tuple-element.21.own) | copy-start | bytes 4718596
  64.6 40.8 %collective-permute-start.17 = (bf16[2,384,512]{2,1,0:T(8,128)(2,1)}, bf16[2,384,512]{2,1,0:T(8,128)(2,1)S(1)}, u32[]{:S(2)}, u32[]{:S(2)}) collective-permute-start(bf16[2,384,512]{2,1,0:T(8,128)(2,1)} %get-tuple-element.27), channel_id=1, source_target_pairs={{0,1},{1,0},{2,3},{3,2},{4,8},{5,9},{6,10},{7,11},{8,4},{9,5},{10,... | collective-permute-start | bytes 2359304 | tf_op jit(solution)/shard_map/ppermute | solution.py:261
  74.3 3.6 %collective-permute-start.19 = (f32[2,128]{1,0:T(2,128)S(1)}, f32[2,128]{1,0:T(2,128)S(1)}, u32[]{:S(2)}, u32[]{:S(2)}) collective-permute-start(f32[2,128]{1,0:T(2,128)S(1)} %slice.11), channel_id=1, source_target_pairs={{0,16},{16,0},{1,17},{17,1},{2,18},{18,2},{3,19},{19,3},{4,20},{20... | collective-permute-start | bytes 3080 | tf_op jit(solution)/shard_map/ppermute | solution.py:275
  77.9 19.0 %collective-permute-start.20 = (f32[2,128]{1,0:T(2,128)S(1)}, f32[2,128]{1,0:T(2,128)S(1)}, u32[]{:S(2)}, u32[]{:S(2)}) collective-permute-start(f32[2,128]{1,0:T(2,128)S(1)} %add_add_fusion), channel_id=1, source_target_pairs={{0,4},{4,0},{8,12},{12,8},{1,5},{5,1},{9,13},{13,9},{2,6},{6,2},{1... | collective-permute-start | bytes 3080 | tf_op jit(solution)/shard_map/ppermute | solution.py:268
  96.9 4.5 %collective-permute-start.21 = (f32[2,128]{1,0:T(2,128)S(1)}, f32[2,128]{1,0:T(2,128)S(1)}, u32[]{:S(2)}, u32[]{:S(2)}) collective-permute-start(f32[2,128]{1,0:T(2,128)S(1)} %add.36), channel_id=1, source_target_pairs={{0,8},{4,12},{8,0},{12,4},{1,9},{5,13},{9,1},{13,5},{2,10},{6,14},... | collective-permute-start | bytes 3080 | tf_op jit(solution)/shard_map/ppermute | solution.py:268
  101.4 9.9 %collective-permute-start.9 = (bf16[384,512]{1,0:T(8,128)(2,1)S(1)}, bf16[384,512]{1,0:T(8,128)(2,1)S(1)}, u32[]{:S(2)}, u32[]{:S(2)}) collective-permute-start(bf16[384,512]{1,0:T(8,128)(2,1)S(1)} %copy-done.6), channel_id=1, source_target_pairs={{0,16},{16,0},{1,17},{17,1},{2,18},{18,2},{3,19},{19,3},{4,20},{20... | collective-permute-start | bytes 1179656 | tf_op jit(solution)/shard_map/ppermute | solution.py:275
  101.8 6.7 %collective-permute-start.22 = (f32[2,128]{1,0:T(2,128)S(1)}, f32[2,128]{1,0:T(2,128)S(1)}, u32[]{:S(2)}, u32[]{:S(2)}) collective-permute-start(f32[2,128]{1,0:T(2,128)S(1)} %add.37), channel_id=1, source_target_pairs={{0,1},{1,0},{2,3},{3,2},{4,5},{5,4},{6,7},{7,6},{8,9},{9,8},{10,11... | collective-permute-start | bytes 3080 | tf_op jit(solution)/shard_map/ppermute | solution.py:268
  101.8 50.2 %collective-permute-start.5 = (bf16[2,384,512]{2,1,0:T(8,128)(2,1)S(1)}, bf16[2,384,512]{2,1,0:T(8,128)(2,1)S(1)}, u32[]{:S(2)}, u32[]{:S(2)}) collective-permute-start(bf16[2,384,512]{2,1,0:T(8,128)(2,1)S(1)} %get-tuple-element.18), channel_id=1, source_target_pairs={{0,4},{1,5},{2,6},{3,7},{4,0},{5,1},{6,2},{7,3},{8,12},{9,13},{10,... | collective-permute-start | bytes 2359304 | tf_op jit(solution)/shard_map/ppermute | solution.py:261
  105.2 46.8 %collective-permute-start.6 = (bf16[2,384,512]{2,1,0:T(8,128)(2,1)S(1)}, bf16[2,384,512]{2,1,0:T(8,128)(2,1)S(1)}, u32[]{:S(2)}, u32[]{:S(2)}) collective-permute-start(bf16[2,384,512]{2,1,0:T(8,128)(2,1)S(1)} %get-tuple-element.19), channel_id=1, source_target_pairs={{0,1},{1,0},{2,3},{3,2},{4,8},{5,9},{6,10},{7,11},{8,4},{9,5},{10,... | collective-permute-start | bytes 2359304 | tf_op jit(solution)/shard_map/ppermute | solution.py:261
  105.4 46.6 %collective-permute-start.12 = (bf16[2,384,512]{2,1,0:T(8,128)(2,1)S(1)}, bf16[2,384,512]{2,1,0:T(8,128)(2,1)S(1)}, u32[]{:S(2)}, u32[]{:S(2)}) collective-permute-start(bf16[2,384,512]{2,1,0:T(8,128)(2,1)S(1)} %shard_map.82), channel_id=1, source_target_pairs={{0,16},{16,0},{1,17},{17,1},{2,18},{18,2},{3,19},{19,3},{4,20},{20... | collective-permute-start | bytes 2359304 | tf_op jit(solution)/shard_map/ppermute | solution.py:275
  106.9 8.0 %copy-start.8 = (bf16[384,512]{1,0:T(8,128)(2,1)S(1)}, bf16[384,512]{1,0:T(8,128)(2,1)}, u32[]{:S(2)}) copy-start(bf16[384,512]{1,0:T(8,128)(2,1)} %copy-done.7) | copy-start | bytes 1179652
  108.4 43.6 %collective-permute-start.18 = (bf16[2,384,512]{2,1,0:T(8,128)(2,1)S(1)}, bf16[2,384,512]{2,1,0:T(8,128)(2,1)S(1)}, u32[]{:S(2)}, u32[]{:S(2)}) collective-permute-start(bf16[2,384,512]{2,1,0:T(8,128)(2,1)S(1)} %shard_map.85), channel_id=1, source_target_pairs={{0,16},{16,0},{1,17},{17,1},{2,18},{18,2},{3,19},{19,3},{4,20},{20... | collective-permute-start | bytes 2359304 | tf_op jit(solution)/shard_map/ppermute | solution.py:275
  111.3 3.6 %collective-permute-start.23 = (f32[2,128]{1,0:T(2,128)S(1)}, f32[2,128]{1,0:T(2,128)S(1)}, u32[]{:S(2)}, u32[]{:S(2)}) collective-permute-start(f32[2,128]{1,0:T(2,128)S(1)} %add.38), channel_id=1, source_target_pairs={{0,2},{1,3},{2,0},{3,1},{4,6},{5,7},{6,4},{7,5},{8,10},{9,11},{10,... | collective-permute-start | bytes 3080 | tf_op jit(solution)/shard_map/ppermute | solution.py:268
  114.9 37.1 %collective-permute-start.15 = (bf16[384,512]{1,0:T(8,128)(2,1)S(1)}, bf16[384,512]{1,0:T(8,128)(2,1)S(1)}, u32[]{:S(2)}, u32[]{:S(2)}) collective-permute-start(bf16[384,512]{1,0:T(8,128)(2,1)S(1)} %copy-done.8), channel_id=1, source_target_pairs={{0,16},{16,0},{1,17},{17,1},{2,18},{18,2},{3,19},{19,3},{4,20},{20... | collective-permute-start | bytes 1179656 | tf_op jit(solution)/shard_map/ppermute | solution.py:275
  (3 other events, 4.8 us)

commit v3 on v2

--- a/solution.py
+++ b/solution.py
@@ -14,8 +14,11 @@
 ROOT_SCALE = HEAD_DIM ** (-0.5)
 EXP2_SCALE = ROOT_SCALE * math.log2(math.e)
 GROUPS = ((0, 4, False), (4, 4, False), (8, 4, True))
-VMEM_LIMIT = 48 * 1024 * 1024
+MAIN_VMEM = 20 * 1024 * 1024
+SMALL_VMEM = 12 * 1024 * 1024
+PACK_VMEM = 4 * 1024 * 1024
 COST = pl.CostEstimate(flops=1, bytes_accessed=1, transcendentals=0)
+MAIN_COST = pl.CostEstimate(flops=6 * 10**9, bytes_accessed=1, transcendentals=0)
 
 
 def dot_nt(left, right):
@@ -49,23 +52,69 @@
     return scaled * scaled_grad - (scaled**3 * projected * (1.0 / HEAD_DIM)) * floats
 
 
-def pack_kernel(first_in, second_in, out):
-    out[0] = first_in[...]
-    out[1] = second_in[...]
+def pack_kernel(first_in, second_in, out, sems, *, start, width):
+    rows = first_in.shape[0]
+    copies = [
+        pltpu.make_async_copy(
+            source.at[:, start : start + width], out.at[slot, :rows], sems.at[slot]
+        )
+        for slot, source in enumerate((first_in, second_in))
+    ]
+    for copy in copies:
+        copy.start()
+    for copy in copies:
+        copy.wait()
+
+
+def info_kernel(listed, gains, info):
+    tile = lax.axis_index("seq")
+    last = lax.axis_size("seq") - 1
+    info[...] = jnp.zeros_like(info)
+    info[0:2, :] = gains[...]
+    for parity in range(2):
+        other = jnp.where(lax.rem(tile, 2) == parity, tile + 1, tile - 1)
+        found = listed[0] == other
+        for slot in range(1, listed.shape[0]):
+            found = found | (listed[slot] == other)
+        found = found & (other >= 0) & (other <= last)
+        live = jnp.where(found, 1.0, 0.0)
+        info[2 + parity : 3 + parity, :] = jnp.full((1, HEAD_DIM), live, jnp.float32)
+
+
+def ask_kernel(info, query, grad, out, sems, *, start, width):
+    rows = query.shape[0]
+    value = info[...]
+    planes = []
+    for _ in range(3):
+        low = value.astype(jnp.bfloat16)
+        planes.append(low)
+        value = value - low.astype(jnp.float32)
+    planes.append(jnp.zeros_like(planes[0]))
+    out[0, rows : rows + 16, :HEAD_DIM] = jnp.concatenate(planes[:2], axis=0)
+    out[1, rows : rows + 16, :HEAD_DIM] = jnp.concatenate(planes[2:], axis=0)
+    pack_kernel(query, grad, out, sems, start=start, width=width)
+
+
+def told_info(told):
+    floats = told[...].astype(jnp.float32)
+    return floats[0, 0:8] + floats[0, 8:16] + floats[1, 0:8]
 
 
 def main_kernel(
-    info, query, grad, key, value, pair_even, pair_odd,
-    query_out, own_out, even_out, odd_out, gain_out,
+    info, query, grad, key, value, pair_even, pair_odd, *rest
 ):
-    query_gain = info[0:1, :HEAD_DIM]
-    key_gain = info[1:2, :HEAD_DIM]
+    query_out, own_out, even_out, odd_out, gain_out = rest[-5:]
+    told = told_info(info) if len(info.shape) == 3 else info[...]
+    query_gain = told[0:1]
+    key_gain = told[1:2]
+    rows = query.shape[0]
+    lives = [jnp.concatenate([told[row : row + 1]] * (rows // HEAD_DIM), axis=1) for row in (2, 3)]
     query_floats, query_scale, query_normed, query_hat = normalize(query[...], query_gain)
     grad_in = grad[...]
     sides = (
         (key[...], value[...], None),
-        (pair_even[0], pair_even[1], info[2:3, :]),
-        (pair_odd[0], pair_odd[1], info[3:4, :]),
+        (pair_even[0], pair_even[1], lives[0]),
+        (pair_odd[0], pair_odd[1], lives[1]),
     )
     parts = []
     totals = None
@@ -113,7 +162,8 @@
 
 
 def finished(info, key, own, from_even, from_odd):
-    key_gain = info[1:2, :HEAD_DIM]
+    told = told_info(info) if len(info.shape) == 3 else info[...]
+    key_gain = told[1:2]
     key_floats, key_scale, _, _ = normalize(key[...], key_gain)
     key_grad = own[0] + from_even[0].astype(jnp.float32) + from_odd[0].astype(jnp.float32)
     value_grad = own[1] + from_even[1].astype(jnp.float32) + from_odd[1].astype(jnp.float32)
@@ -127,13 +177,19 @@
 
 
 def last_kernel(info, key, own, from_even, from_odd, *rest, places, first, count):
-    pieces, (out, held, sems) = rest[: len(places)], rest[len(places) :]
+    amount = len(places)
+    pieces, (out, held) = rest[:amount], rest[amount : amount + 2]
+    staged, (load_sems, store_sems) = rest[amount + 2 : -2], rest[-2:]
     head = pl.program_id(0)
-    copies = [
+    loads = [
+        pltpu.make_async_copy(piece, stage, load_sems.at[slot])
+        for slot, (piece, stage) in enumerate(zip(pieces, staged))
+    ]
+    stores = [
         pltpu.make_async_copy(
-            piece, out.at[planes, :, start : start + piece.shape[-1]], sems.at[slot]
+            stage, out.at[planes, :, start : start + stage.shape[-1]], store_sems.at[slot]
         )
-        for slot, (piece, (planes, start)) in enumerate(zip(pieces, places))
+        for slot, (stage, (planes, start)) in enumerate(zip(staged, places))
     ]
 
     def head_copy(index):
@@ -141,13 +197,19 @@
         return pltpu.make_async_copy(
             held.at[index],
             out.at[pl.ds(1, 2), :, pl.ds(start, HEAD_DIM)],
-            sems.at[len(places) + index],
+            store_sems.at[amount + index],
         )
 
     @pl.when(head == 0)
     def _():
-        for copy in copies:
-            copy.start()
+        for load in loads:
+            load.start()
+
+    @pl.when(head == min(1, count - 1))
+    def _():
+        for load, store in zip(loads, stores):
+            load.wait()
+            store.start()
 
     key_grad, value_grad = finished(info, key, own, from_even, from_odd)
     held[head, 0] = key_grad.astype(held.dtype)
@@ -156,8 +218,8 @@
 
     @pl.when(head == count - 1)
     def _():
-        for copy in copies:
-            copy.wait()
+        for store in stores:
+            store.wait()
         for index in range(count):
             head_copy(index).wait()
 
@@ -168,46 +230,93 @@
     return pl.BlockSpec((None, rows, HEAD_DIM), lambda head: (slot, 0, first + head))
 
 
-def pair_block(rows):
-    return pl.BlockSpec((2, rows, HEAD_DIM), lambda head: (0, 0, head))
+def pair_block(rows, first=0):
+    return pl.BlockSpec((2, rows, HEAD_DIM), lambda head: (0, 0, first + head))
 
 
 def whole_block(shape):
     return pl.BlockSpec(shape, lambda head: (0,) * len(shape))
 
 
+def pack_params():
+    return dict(
+        scratch_shapes=[pltpu.SemaphoreType.DMA((2,))],
+        compiler_params=pltpu.CompilerParams(vmem_limit_bytes=PACK_VMEM),
+        cost_estimate=COST,
+    )
+
+
 def pack_call(first_in, second_in, first, count):
     rows = first_in.shape[0]
-    return pl.pallas_call(
-        pack_kernel,
-        grid=(count,),
-        in_specs=[head_block(rows, first)] * 2,
-        out_specs=pair_block(rows),
-        out_shape=jax.ShapeDtypeStruct((2, rows, count * HEAD_DIM), jnp.bfloat16),
+    width = count * HEAD_DIM
+    return pl.pallas_call(
+        functools.partial(pack_kernel, start=first * HEAD_DIM, width=width),
+        grid=(1,),
+        in_specs=[pl.BlockSpec(memory_space=pl.ANY)] * 2,
+        out_specs=whole_block((2, rows, width)),
+        out_shape=jax.ShapeDtypeStruct((2, rows, width), jnp.bfloat16),
+        **pack_params(),
+    )(first_in, second_in)
+
+
+def ask_call(info, query, grad, first, count):
+    rows = query.shape[0]
+    width = count * HEAD_DIM
+    return pl.pallas_call(
+        functools.partial(ask_kernel, start=first * HEAD_DIM, width=width),
+        grid=(1,),
+        in_specs=[whole_block(info.shape)] + [pl.BlockSpec(memory_space=pl.ANY)] * 2,
+        out_specs=whole_block((2, rows + 16, width)),
+        out_shape=jax.ShapeDtypeStruct((2, rows + 16, width), jnp.bfloat16),
+        **pack_params(),
+    )(info, query, grad)
+
+
+def info_call(listed, gains):
+    return pl.pallas_call(
+        info_kernel,
+        in_specs=[pl.BlockSpec(memory_space=pltpu.SMEM), pl.BlockSpec(memory_space=pltpu.VMEM)],
+        out_specs=pl.BlockSpec(memory_space=pltpu.VMEM),
+        out_shape=jax.ShapeDtypeStruct((8, HEAD_DIM), jnp.float32),
+        compiler_params=pltpu.CompilerParams(vmem_limit_bytes=PACK_VMEM),
         cost_estimate=COST,
-    )(first_in, second_in)
-
-
-def main_call(info, operands, pair_even, pair_odd, count):
+    )(listed, gains)
+
+
+def info_block(info):
+    if info.ndim == 2:
+        return whole_block(info.shape)
+    below = info.shape[1] // 16 - 1
+    return pl.BlockSpec((2, 16, HEAD_DIM), lambda head: (0, below, 0))
+
+
+def main_call(
+    info, operands, pair_even, pair_odd, pair_first, count, query_grads, query_heads, query_first
+):
     rows = pair_even.shape[1]
     lanes = count * HEAD_DIM
+    earlier = [] if query_grads is None else [query_grads]
     return pl.pallas_call(
         main_kernel,
         grid=(count,),
-        in_specs=[whole_block(info.shape)]
+        in_specs=[info_block(info)]
         + [head_block(rows, first, slot) for _, first, slot in operands]
-        + [pair_block(rows)] * 2,
-        out_specs=[head_block(rows, 0)] + [pair_block(rows)] * 3 + [whole_block((8, HEAD_DIM))],
+        + [pair_block(rows, pair_first)] * 2
+        + [pl.BlockSpec(memory_space=pl.ANY)] * len(earlier),
+        out_specs=[head_block(rows, query_first)]
+        + [pair_block(rows)] * 3
+        + [whole_block((8, HEAD_DIM))],
         out_shape=[
-            jax.ShapeDtypeStruct((rows, lanes), jnp.bfloat16),
+            jax.ShapeDtypeStruct((rows, query_heads * HEAD_DIM), jnp.bfloat16),
             jax.ShapeDtypeStruct((2, rows, lanes), jnp.float32),
             jax.ShapeDtypeStruct((2, rows, lanes), jnp.bfloat16),
             jax.ShapeDtypeStruct((2, rows, lanes), jnp.bfloat16),
             jax.ShapeDtypeStruct((8, HEAD_DIM), jnp.float32),
         ],
-        compiler_params=pltpu.CompilerParams(vmem_limit_bytes=VMEM_LIMIT),
-        cost_estimate=COST,
-    )(info, *[array for array, _, _ in operands], pair_even, pair_odd)
+        input_output_aliases={7: 0} if earlier else {},
+        compiler_params=pltpu.CompilerParams(vmem_limit_bytes=MAIN_VMEM),
+        cost_estimate=MAIN_COST,
+    )(info, *[array for array, _, _ in operands], pair_even, pair_odd, *earlier)
 
 
 def finish_call(info, key, own, from_even, from_odd, count):
@@ -216,10 +325,10 @@
     return pl.pallas_call(
         finish_kernel,
         grid=(count,),
-        in_specs=[whole_block(info.shape), head_block(rows, first, slot)] + [pair_block(rows)] * 3,
+        in_specs=[info_block(info), head_block(rows, first, slot)] + [pair_block(rows)] * 3,
         out_specs=pair_block(rows),
         out_shape=jax.ShapeDtypeStruct((2, rows, count * HEAD_DIM), jnp.bfloat16),
-        compiler_params=pltpu.CompilerParams(vmem_limit_bytes=VMEM_LIMIT),
+        compiler_params=pltpu.CompilerParams(vmem_limit_bytes=SMALL_VMEM),
         cost_estimate=COST,
     )(info, array, own, from_even, from_odd)
 
@@ -231,16 +340,18 @@
     return pl.pallas_call(
         functools.partial(last_kernel, places=places, first=first, count=count),
         grid=(count,),
-        in_specs=[whole_block(info.shape), head_block(rows, offset, slot)]
+        in_specs=[info_block(info), head_block(rows, offset, slot)]
         + [pair_block(rows)] * 3
         + [anywhere] * len(pieces),
         out_specs=anywhere,
         out_shape=jax.ShapeDtypeStruct((3, rows, HEADS * HEAD_DIM), jnp.bfloat16),
         scratch_shapes=[
             pltpu.VMEM((count, 2, rows, HEAD_DIM), jnp.bfloat16),
+            *[pltpu.VMEM(piece.shape, piece.dtype) for piece in pieces],
+            pltpu.SemaphoreType.DMA((len(pieces),)),
             pltpu.SemaphoreType.DMA((len(pieces) + count,)),
         ],
-        compiler_params=pltpu.CompilerParams(vmem_limit_bytes=VMEM_LIMIT),
+        compiler_params=pltpu.CompilerParams(vmem_limit_bytes=SMALL_VMEM),
         cost_estimate=COST,
     )(info, array, own, from_even, from_odd, *pieces)
 
@@ -261,6 +372,15 @@
     return lax.ppermute(value, ("seq", "dp"), pairs)
 
 
+def after(value, *others):
+    return lax.optimization_barrier((value, *others))[0]
+
+
+def turned(value, step):
+    count = lax.axis_size("pipe")
+    return lax.ppermute(value, "pipe", [(i, (i + step) % count) for i in range(count)])
+
+
 def total_over(value, axis):
     count = lax.axis_size(axis)
     step = 1
@@ -270,71 +390,54 @@
     return value
 
 
-def turned(value, step):
-    count = lax.axis_size("pipe")
-    return lax.ppermute(value, "pipe", [(i, (i + step) % count) for i in range(count)])
-
-
-def listing(listed, tile, seq_count, parity):
-    step = jnp.where(tile % 2 == parity, 1, -1)
-    other = tile + step
-    inside = (other >= 0) & (other < seq_count)
-    return (inside & jnp.any(listed == other)).astype(jnp.float32)
-
-
 def local(queries, keys, values, grad_out, norm_gains, kv_tiles):
     query, key, value, grad = (a[0, 0, 0] for a in (queries, keys, values, grad_out))
     rows = query.shape[0]
-    tile = lax.axis_index("seq")
     seq_count = lax.axis_size("seq")
-    listed = kv_tiles[0, 0, 0]
-    info = jnp.concatenate(
-        [
-            jnp.pad(norm_gains[0], ((0, 0), (0, rows - HEAD_DIM))),
-            jnp.full((1, rows), listing(listed, tile, seq_count, 0)),
-            jnp.full((1, rows), listing(listed, tile, seq_count, 1)),
-            jnp.zeros((4, rows), jnp.float32),
-        ],
-        axis=0,
-    )
-    sources = []
+    home_heads = sum(count for _, count, away in GROUPS if not away)
+    home_pair = pack_call(key, value, 0, home_heads)
+    away_pair = pack_call(after(key, home_pair), value, home_heads, HEADS - home_heads)
+    home_gathered = (exchanged(home_pair, 0), exchanged(home_pair, 1))
+    info = info_call(kv_tiles[0, 0, 0], after(norm_gains[0], away_pair))
+    away_pair = turned(away_pair, -1)
+    asked = ask_call(info, after(query, away_pair), grad, home_heads, HEADS - home_heads)
+    asked = turned(asked, -1)
+    away_gathered = (exchanged(away_pair, 0), exchanged(away_pair, 1))
+    sources, parts, sums = [], [], []
+    query_grads = None
     for first, count, away in GROUPS:
-        pair = pack_call(key, value, first, count)
         if away:
-            pair = turned(pair, -1)
-            asked = turned(pack_call(query, grad, first, count), -1)
-            operands = ((asked, 0, 0), (asked, 0, 1), (pair, 0, 0), (pair, 0, 1))
-            sources.append((turned(info, -1), operands, pair))
+            asked = after(asked, query_grads)
+            operands = [(asked, 0, 0), (asked, 0, 1), (away_pair, 0, 0), (away_pair, 0, 1)]
+            sources.append((asked, operands))
+            query_low, own, to_even, to_odd, gain = main_call(
+                *sources[-1], *away_gathered, 0, count, None, count, 0
+            )
+            sums.append(turned(gain[:2], 1))
         else:
-            operands = tuple((a, first, None) for a in (query, grad, key, value))
-            sources.append((info, operands, pair))
-    gathered = [(exchanged(pair, 0), exchanged(pair, 1)) for _, _, pair in sources]
-    gain_sums = [jnp.zeros((2, HEAD_DIM), jnp.float32)] * 2
-    pieces, places = [], []
-    out = None
-    for (first, count, away), (group_info, operands, _), (even, odd) in zip(
-        GROUPS, sources, gathered
+            sources.append((info, [(a, first, None) for a in (query, grad, key, value)]))
+            query_grads, own, to_even, to_odd, gain = main_call(
+                *sources[-1], *home_gathered, first, count, query_grads, home_heads, first
+            )
+            sums.append(gain[:2])
+        parts.append((own, exchanged(to_even, 0), exchanged(to_odd, 1)))
+    query_grads = turned(query_grads, -1)
+    pieces = [query_grads, query_low]
+    places = [(0, 0), (0, home_heads * HEAD_DIM)]
+    for index, ((first, count, away), (group_info, operands), part) in enumerate(
+        zip(GROUPS, sources, parts)
     ):
-        query_low, own, to_even, to_odd, gain = main_call(
-            group_info, operands, even, odd, count
-        )
-        gain_sums[away] = gain_sums[away] + gain[:2]
-        from_even = exchanged(to_even, 0)
-        from_odd = exchanged(to_odd, 1)
-        last = (first, count, away) == GROUPS[-1]
-        pieces.append(query_low if away else turned(query_low, -1))
-        places.append((0, first * HEAD_DIM))
-        if last:
+        own, from_even, from_odd = part
+        if away:
             out = last_call(
                 group_info, operands[2], own, from_even, from_odd, pieces, tuple(places), first, count
             )
         else:
+            own = after(own, query_grads, *(sums[-1:] if index == 0 else ()))
             pair_low = finish_call(group_info, operands[2], own, from_even, from_odd, count)
-            pieces.append(pair_low if away else turned(pair_low, -1))
+            pieces.append(turned(pair_low, -1))
             places.append((slice(1, 3), first * HEAD_DIM))
-    summed = gain_sums[0] + turned(gain_sums[1], 1)
-    for axis in ("seq", "dp"):
-        summed = total_over(summed, axis)
+    summed = total_over(total_over(sum(sums), "dp"), "seq")
     tokens = lax.axis_size("dp") * seq_count * rows * HEADS
     return (out[None, :, None, None], (summed / math.sqrt(tokens))[None])
 

time: 157 us -> 127 us (0.81)
  Pallas kernels: 51 us -> 34.8 us
  waiting for transfers between devices: 71.1 us -> 62.6 us
  starting transfers between devices: 28.8 us -> 25.7 us
    ppermute x12 -> x10, waiting for transfers between devices: 5.11 us -> 28.2 us  [exchanged(): return lax.ppermute(value, ('seq', 'dp'), pairs)]
    ppermute x8 -> x6, waiting for transfers between devices: 46.2 us -> 24.7 us  [turned(): lax.ppermute(value, 'pipe', [(i, (i + step) % count) for i in range(count)])]
    pallas_call x9, Pallas kernels: 47 us -> 31.9 us  [the longest x3 28 us: main_call(): pl.pallas_call(main_kernel, grid=(count,), in_specs=[info_block(info)] +...]
    ppermute x4, waiting for transfers between devices: 19.8 us -> 9.75 us  [total_over(): lax.ppermute(value, axis, [(i, i ^ step) for i in range(count)])]
    ppermute x12 -> x10, starting transfers between devices: 13.8 us -> 11.8 us  [exchanged(): return lax.ppermute(value, ('seq', 'dp'), pairs)]
    ppermute x8 -> x6, starting transfers between devices: 7.73 us -> 7.63 us  [turned(): lax.ppermute(value, 'pipe', [(i, (i + step) % count) for i in range(count)])]
  transfers between devices with their start and end apart: 24 -> 20, of which waited for: 10 -> 10; matrix products, arithmetic and copies ran while one was open for 1% -> 0% of each run, Pallas kernels for 28% -> 25%
where the time goes in v3:
time: 127 us
  waiting for transfers between devices  62.6 us (49%)
  Pallas kernels  34.8 us (27%)
  starting transfers between devices  25.7 us (20%)
  local copies, waits for them, and re-layouts  2.57 us (2%)
    ppermute x10, waiting for transfers between devices, exchanged(): return lax.ppermute(value, ('seq', 'dp'), pairs)  28.2 us
    pallas_call x3, Pallas kernels, main_call(): pl.pallas_call(main_kernel, grid=(count,), in_specs=[info_block(info)] +...  28 us
    ppermute x6, waiting for transfers between devices, turned(): lax.ppermute(value, 'pipe', [(i, (i + step) % count) for i in range(count)])  24.7 us
    ppermute x10, starting transfers between devices, exchanged(): return lax.ppermute(value, ('seq', 'dp'), pairs)  11.8 us
    ppermute x4, waiting for transfers between devices, total_over(): lax.ppermute(value, axis, [(i, i ^ step) for i in range(count)])  9.75 us
    ppermute x6, starting transfers between devices, turned(): lax.ppermute(value, 'pipe', [(i, (i + step) % count) for i in range(count)])  7.63 us
    ppermute x4, starting transfers between devices, total_over(): lax.ppermute(value, axis, [(i, i ^ step) for i in range(count)])  6.24 us
    pallas_call x2, Pallas kernels, finish_call(): pl.pallas_call(finish_kernel, grid=(count,), in_specs=[info_block(info),...  3.09 us
  transfers between devices with their start and end apart: 20, of which 10 were waited for; matrix products, arithmetic and copies ran while one was open for 0% of the time, Pallas kernels for 25%

profile of v3, /device:TPU:0, one launch (start us, length us, event | category | flops | bytes accessed | tf_op | source)
XLA Modules:
  0.0 127.0 jit_solution(12990137788944443348)
XLA Ops:
  0.6 1.3 copy-done
  1.9 1.3 copy-done.2
  3.4 3.1 %collective-permute-start.2 = (bf16[2,384,1024]{2,1,0:T(8,128)(2,1)S(1)}, bf16[2,384,1024]{2,1,0:T(8,128)(2,1)S(1)}, u32[]{:S(2)}, u32[]{:S(2)}) collective-permute-start(bf16[2,384,1024]{2,1,0:T(8,128)(2,1)S(1)} %shard_map.77), channel_id=1, source_target_pairs={{0,4},{1,5},{2,6},{3,7},{4,0},{5,1},{6,2},{7,3},{8,12},{9,13},{10,... | collective-permute-start | bytes 4718600 | tf_op jit(solution)/shard_map/ppermute | solution.py:372
  6.5 1.6 %collective-permute-start = (bf16[2,384,512]{2,1,0:T(8,128)(2,1)S(1)}, bf16[2,384,512]{2,1,0:T(8,128)(2,1)S(1)}, u32[]{:S(2)}, u32[]{:S(2)}) collective-permute-start(bf16[2,384,512]{2,1,0:T(8,128)(2,1)S(1)} %shard_map.78), channel_id=1, source_target_pairs={{0,16},{16,0},{1,17},{17,1},{2,18},{18,2},{3,19},{19,3},{4,20},{20... | collective-permute-start | bytes 2359304 | tf_op jit(solution)/shard_map/ppermute | solution.py:381
  8.7 17.9 %collective-permute-done.key.value = bf16[2,384,512]{2,1,0:T(8,128)(2,1)S(1)} collective-permute-done((bf16[2,384,512]{2,1,0:T(8,128)(2,1)S(1)}, bf16[2,384,512]{2,1,0:T(8,128)(2,1)S(1)}, u32[]{:S(2)}, u32[]{:S(2)}) %collective-permute-start) | collective-permute-done | bytes 786464 | tf_op jit(solution)/shard_map/ppermute | solution.py:381
  26.7 1.6 %collective-permute-start.1 = (bf16[2,400,512]{2,1,0:T(8,128)(2,1)S(1)}, bf16[2,400,512]{2,1,0:T(8,128)(2,1)S(1)}, u32[]{:S(2)}, u32[]{:S(2)}) collective-permute-start(bf16[2,400,512]{2,1,0:T(8,128)(2,1)S(1)} %shard_map.80), channel_id=1, source_target_pairs={{0,16},{16,0},{1,17},{17,1},{2,18},{18,2},{3,19},{19,3},{4,20},{20... | collective-permute-start | bytes 2457608 | tf_op jit(solution)/shard_map/ppermute | solution.py:381
  28.2 1.9 %collective-permute-start.4 = (bf16[2,384,512]{2,1,0:T(8,128)(2,1)S(1)}, bf16[2,384,512]{2,1,0:T(8,128)(2,1)S(1)}, u32[]{:S(2)}, u32[]{:S(2)}) collective-permute-start(bf16[2,384,512]{2,1,0:T(8,128)(2,1)S(1)} %collective-permute-done.key.value), channel_id=1, source_target_pairs={{0,4},{1,5},{2,6},{3,7},{4,0},{5,1},{6,2},{7,3},{8,12},{9,13},{10,... | collective-permute-start | bytes 2359304 | tf_op jit(solution)/shard_map/ppermute | solution.py:372
  30.2 11.5 %collective-permute-done.2.pair_even = bf16[2,384,1024]{2,1,0:T(8,128)(2,1)S(1)} collective-permute-done((bf16[2,384,1024]{2,1,0:T(8,128)(2,1)S(1)}, bf16[2,384,1024]{2,1,0:T(8,128)(2,1)S(1)}, u32[]{:S(2)}, u32[]{:S(2)}) %collective-permute-start.2) | collective-permute-done | bytes 1572896 | tf_op jit(solution)/shard_map/ppermute | solution.py:372
  41.7 9.4 %shard_map.81 = (bf16[384,1024]{1,0:T(8,128)(2,1)S(1)}, f32[2,384,512]{2,1,0:T(8,128)S(1)}, bf16[2,384,512]{2,1,0:T(8,128)(2,1)S(1)}, bf16[2,384,512]{2,1,0:T(8,128)(2,1)S(1)}, f32[8,128]{1,0:T(8,128)S(1)}) custom-call(f32[8,128]{1,0:T(8,128)S(1)} %shard_map.79.info, bf16[384,1536]{1,0:T(8,128)(2,1)S(1)} %bitcast.22, bf16[384,1536]{1,0:T(8,128)(2,1)S(1)} %bitcast.25, ...), custom_call_target="tpu_custom_call" | custom-call | flops 6000000000 | bytes 1 | tf_op jit(solution)/shard_map/pallas_call | solution.py:299
  51.1 9.4 %shard_map.82 = (bf16[384,1024]{1,0:T(8,128)(2,1)S(1)}, f32[2,384,512]{2,1,0:T(8,128)S(1)}, bf16[2,384,512]{2,1,0:T(8,128)(2,1)S(1)}, bf16[2,384,512]{2,1,0:T(8,128)(2,1)S(1)}, f32[8,128]{1,0:T(8,128)S(1)}) custom-call(f32[8,128]{1,0:T(8,128)S(1)} %shard_map.79.info, bf16[384,1536]{1,0:T(8,128)(2,1)S(1)} %bitcast.23, ...), custom_call_target="tpu_custom_call", output_to_operand_aliasing={{0}: (7, {})} | custom-call | flops 6000000000 | bytes 1 | tf_op jit(solution)/shard_map/pallas_call | solution.py:299
  60.5 2.0 %collective-permute-start.8 = (bf16[384,1024]{1,0:T(8,128)(2,1)S(1)}, bf16[384,1024]{1,0:T(8,128)(2,1)S(1)}, u32[]{:S(2)}, u32[]{:S(2)}) collective-permute-start(bf16[384,1024]{1,0:T(8,128)(2,1)S(1)} %get-tuple-element.27), channel_id=1, source_target_pairs={{0,16},{16,0},{1,17},{17,1},{2,18},{18,2},{3,19},{19,3},{4,20},{20... | collective-permute-start | bytes 2359304 | tf_op jit(solution)/shard_map/ppermute | solution.py:381
  62.5 2.7 %collective-permute-start.13 = (bf16[2,384,512]{2,1,0:T(8,128)(2,1)S(1)}, bf16[2,384,512]{2,1,0:T(8,128)(2,1)S(1)}, u32[]{:S(2)}, u32[]{:S(2)}) collective-permute-start(bf16[2,384,512]{2,1,0:T(8,128)(2,1)S(1)} %get-tuple-element.40), channel_id=1, source_target_pairs={{0,4},{1,5},{2,6},{3,7},{4,0},{5,1},{6,2},{7,3},{8,12},{9,13},{10,... | collective-permute-start | bytes 2359304 | tf_op jit(solution)/shard_map/ppermute | solution.py:372
  65.2 2.0 %collective-permute-start.10 = (bf16[2,384,512]{2,1,0:T(8,128)(2,1)S(1)}, bf16[2,384,512]{2,1,0:T(8,128)(2,1)S(1)}, u32[]{:S(2)}, u32[]{:S(2)}) collective-permute-start(bf16[2,384,512]{2,1,0:T(8,128)(2,1)S(1)} %get-tuple-element.36), channel_id=1, source_target_pairs={{0,4},{1,5},{2,6},{3,7},{4,0},{5,1},{6,2},{7,3},{8,12},{9,13},{10,... | collective-permute-start | bytes 2359304 | tf_op jit(solution)/shard_map/ppermute | solution.py:372
  67.3 9.2 %shard_map.83 = (bf16[384,512]{1,0:T(8,128)(2,1)S(1)}, f32[2,384,512]{2,1,0:T(8,128)S(1)}, bf16[2,384,512]{2,1,0:T(8,128)(2,1)S(1)}, bf16[2,384,512]{2,1,0:T(8,128)(2,1)S(1)}, f32[8,128]{1,0:T(8,128)S(1)}) custom-call(bf16[2,400,512]{2,1,0:T(8,128)(2,1)S(1)} %collective-permute-done.1.info.query.grad, ...), custom_call_target="tpu_custom_call" | custom-call | flops 6000000000 | bytes 1 | tf_op jit(solution)/shard_map/pallas_call | solution.py:299
  76.5 1.9 %collective-permute-done.8.rest_0_ = bf16[384,1024]{1,0:T(8,128)(2,1)S(1)} collective-permute-done((bf16[384,1024]{1,0:T(8,128)(2,1)S(1)}, bf16[384,1024]{1,0:T(8,128)(2,1)S(1)}, u32[]{:S(2)}, u32[]{:S(2)}) %collective-permute-start.8) | collective-permute-done | bytes 786464 | tf_op jit(solution)/shard_map/ppermute | solution.py:381
  78.4 1.4 %collective-permute-start.9 = (f32[2,128]{1,0:T(2,128)S(1)}, f32[2,128]{1,0:T(2,128)S(1)}, u32[]{:S(2)}, u32[]{:S(2)}) collective-permute-start(f32[2,128]{1,0:T(2,128)S(1)} %slice.9), channel_id=1, source_target_pairs={{0,16},{16,0},{1,17},{17,1},{2,18},{18,2},{3,19},{19,3},{4,20},{20... | collective-permute-start | bytes 3080 | tf_op jit(solution)/shard_map/ppermute | solution.py:381
  79.8 3.9 %collective-permute-done.13.from_even = bf16[2,384,512]{2,1,0:T(8,128)(2,1)S(1)} collective-permute-done((bf16[2,384,512]{2,1,0:T(8,128)(2,1)S(1)}, bf16[2,384,512]{2,1,0:T(8,128)(2,1)S(1)}, u32[]{:S(2)}, u32[]{:S(2)}) %collective-permute-start.13) | collective-permute-done | bytes 786464 | tf_op jit(solution)/shard_map/ppermute | solution.py:372
  83.7 2.0 %collective-permute-start.6 = (bf16[2,384,512]{2,1,0:T(8,128)(2,1)S(1)}, bf16[2,384,512]{2,1,0:T(8,128)(2,1)S(1)}, u32[]{:S(2)}, u32[]{:S(2)}) collective-permute-start(bf16[2,384,512]{2,1,0:T(8,128)(2,1)S(1)} %get-tuple-element.30), channel_id=1, source_target_pairs={{0,4},{1,5},{2,6},{3,7},{4,0},{5,1},{6,2},{7,3},{8,12},{9,13},{10,... | collective-permute-start | bytes 2359304 | tf_op jit(solution)/shard_map/ppermute | solution.py:372
  85.7 1.5 %shard_map.85 = bf16[2,384,512]{2,1,0:T(8,128)(2,1)S(1)} custom-call(f32[8,128]{1,0:T(8,128)S(1)} %shard_map.79.info, bf16[384,1536]{1,0:T(8,128)(2,1)S(1)} %bitcast.15, f32[2,384,512]{2,1,0:T(8,128)S(1)} %get-tuple-element.39.own, bf16[2,384,512]{2,1,0:T(8,128)(2,1)S(1)} %collective-permute-done.13.from_even, ...), custom_call_target="tpu_custom_call" | custom-call | flops 1 | bytes 1 | tf_op jit(solution)/shard_map/pallas_call | solution.py:325
  87.2 0.6 collective-permute-start.15
  87.8 12.7 %collective-permute-done.10.from_even = bf16[2,384,512]{2,1,0:T(8,128)(2,1)S(1)} collective-permute-done((bf16[2,384,512]{2,1,0:T(8,128)(2,1)S(1)}, bf16[2,384,512]{2,1,0:T(8,128)(2,1)S(1)}, u32[]{:S(2)}, u32[]{:S(2)}) %collective-permute-start.10) | collective-permute-done | bytes 786464 | tf_op jit(solution)/shard_map/ppermute | solution.py:372
  100.5 1.6 %shard_map.84 = bf16[2,384,512]{2,1,0:T(8,128)(2,1)S(1)} custom-call(f32[8,128]{1,0:T(8,128)S(1)} %shard_map.79.info, bf16[384,1536]{1,0:T(8,128)(2,1)S(1)} %bitcast.16, f32[2,384,512]{2,1,0:T(8,128)S(1)} %get-tuple-element.35.own, bf16[2,384,512]{2,1,0:T(8,128)(2,1)S(1)} %collective-permute-done.10.from_even, ...), custom_call_target="tpu_custom_call" | custom-call | flops 1 | bytes 1 | tf_op jit(solution)/shard_map/pallas_call | solution.py:325
  102.1 0.6 collective-permute-start.12
  102.7 1.1 collective-permute-done.16
  103.8 1.5 %collective-permute-start.17 = (f32[2,128]{1,0:T(2,128)S(1)}, f32[2,128]{1,0:T(2,128)S(1)}, u32[]{:S(2)}, u32[]{:S(2)}) collective-permute-start(f32[2,128]{1,0:T(2,128)S(1)} %add.20), channel_id=1, source_target_pairs={{0,2},{1,3},{2,0},{3,1},{4,6},{5,7},{6,4},{7,5},{8,10},{9,11},{10,... | collective-permute-start | bytes 3080 | tf_op jit(solution)/shard_map/ppermute | solution.py:388
  105.4 2.0 %collective-permute-done.17 = f32[2,128]{1,0:T(2,128)S(1)} collective-permute-done((f32[2,128]{1,0:T(2,128)S(1)}, f32[2,128]{1,0:T(2,128)S(1)}, u32[]{:S(2)}, u32[]{:S(2)}) %collective-permute-start.17) | collective-permute-done | bytes 1056 | tf_op jit(solution)/shard_map/ppermute | solution.py:388
  107.4 2.1 %collective-permute-start.18 = (f32[2,128]{1,0:T(2,128)S(1)}, f32[2,128]{1,0:T(2,128)S(1)}, u32[]{:S(2)}, u32[]{:S(2)}) collective-permute-start(f32[2,128]{1,0:T(2,128)S(1)} %add.21), channel_id=1, source_target_pairs={{0,4},{4,0},{8,12},{12,8},{1,5},{5,1},{9,13},{13,9},{2,6},{6,2},{1... | collective-permute-start | bytes 3080 | tf_op jit(solution)/shard_map/ppermute | solution.py:388
  109.5 4.7 %collective-permute-done.18 = f32[2,128]{1,0:T(2,128)S(1)} collective-permute-done((f32[2,128]{1,0:T(2,128)S(1)}, f32[2,128]{1,0:T(2,128)S(1)}, u32[]{:S(2)}, u32[]{:S(2)}) %collective-permute-start.18) | collective-permute-done | bytes 1056 | tf_op jit(solution)/shard_map/ppermute | solution.py:388
  114.2 2.6 %collective-permute-start.19 = (f32[2,128]{1,0:T(2,128)S(1)}, f32[2,128]{1,0:T(2,128)S(1)}, u32[]{:S(2)}, u32[]{:S(2)}) collective-permute-start(f32[2,128]{1,0:T(2,128)S(1)} %add.22), channel_id=1, source_target_pairs={{0,8},{4,12},{8,0},{12,4},{1,9},{5,13},{9,1},{13,5},{2,10},{6,14},... | collective-permute-start | bytes 3080 | tf_op jit(solution)/shard_map/ppermute | solution.py:388
  116.9 1.9 %collective-permute-done.19 = f32[2,128]{1,0:T(2,128)S(1)} collective-permute-done((f32[2,128]{1,0:T(2,128)S(1)}, f32[2,128]{1,0:T(2,128)S(1)}, u32[]{:S(2)}, u32[]{:S(2)}) %collective-permute-start.19) | collective-permute-done | bytes 1056 | tf_op jit(solution)/shard_map/ppermute | solution.py:388
  119.3 4.8 %collective-permute-done.12.rest_2_ = bf16[2,384,512]{2,1,0:T(8,128)(2,1)S(1)} collective-permute-done((bf16[2,384,512]{2,1,0:T(8,128)(2,1)S(1)}, bf16[2,384,512]{2,1,0:T(8,128)(2,1)S(1)}, u32[]{:S(2)}, u32[]{:S(2)}) %collective-permute-start.12) | collective-permute-done | bytes 786464 | tf_op jit(solution)/shard_map/ppermute | solution.py:381
  124.1 2.8 %shard_map.86 = bf16[3,384,1536]{2,1,0:T(8,128)(2,1)} custom-call(bf16[2,400,512]{2,1,0:T(8,128)(2,1)S(1)} %collective-permute-done.1.info.query.grad, bf16[2,384,512]{2,1,0:T(8,128)(2,1)S(1)} %collective-permute-done.key.value, f32[2,384,512]{2,1,0:T(8,128)S(1)} %get-tuple-element.29.own, bf16[2,384,512]{2,1,0:T(8,128)(2,1)S(1)} %collective-permute-done.6.from_even, ...), custom_call_target="tpu_custom_call" | custom-call | flops 1 | bytes 1 | tf_op jit(solution)/shard_map/pallas_call | solution.py:340
  (40 shorter events, 1.5 us)
Async XLA Ops:
  0.6 1.3 %copy-start = (bf16[1,1,1,384,1536]{4,3,2,1,0:T(8,128)(2,1)S(1)}, bf16[1,1,1,384,1536]{4,3,2,1,0:T(8,128)(2,1)}, u32[]{:S(2)}) copy-start(bf16[1,1,1,384,1536]{4,3,2,1,0:T(8,128)(2,1)} %param.7) | copy-start | bytes 3538948
  1.9 1.3 %copy-start.2 = (bf16[1,1,1,384,1536]{4,3,2,1,0:T(8,128)(2,1)S(1)}, bf16[1,1,1,384,1536]{4,3,2,1,0:T(8,128)(2,1)}, u32[]{:S(2)}) copy-start(bf16[1,1,1,384,1536]{4,3,2,1,0:T(8,128)(2,1)} %param.8) | copy-start | bytes 3538948
  3.3 4.8 %copy-start.6 = (f32[1,2,128]{2,1,0:T(2,128)S(1)}, f32[1,2,128]{2,1,0:T(2,128)}, u32[]{:S(2)}) copy-start(f32[1,2,128]{2,1,0:T(2,128)} %param.10) | copy-start | bytes 3076
  3.3 4.8 %copy-start.7 = (s32[1,1,1,3]{3,2,1,0:T(1,128)S(1)}, s32[1,1,1,3]{3,2,1,0:T(1,128)}, u32[]{:S(2)}) copy-start(s32[1,1,1,3]{3,2,1,0:T(1,128)} %param.11) | copy-start | bytes 40
  3.3 23.2 %copy-start.4 = (bf16[1,1,1,384,1536]{4,3,2,1,0:T(8,128)(2,1)S(1)}, bf16[1,1,1,384,1536]{4,3,2,1,0:T(8,128)(2,1)}, u32[]{:S(2)}) copy-start(bf16[1,1,1,384,1536]{4,3,2,1,0:T(8,128)(2,1)} %param.6) | copy-start | bytes 3538948
  3.4 23.2 %copy-start.5 = (bf16[1,1,1,384,1536]{4,3,2,1,0:T(8,128)(2,1)S(1)}, bf16[1,1,1,384,1536]{4,3,2,1,0:T(8,128)(2,1)}, u32[]{:S(2)}) copy-start(bf16[1,1,1,384,1536]{4,3,2,1,0:T(8,128)(2,1)} %param.9) | copy-start | bytes 3538948
  3.4 38.3 %collective-permute-start.2 = (bf16[2,384,1024]{2,1,0:T(8,128)(2,1)S(1)}, bf16[2,384,1024]{2,1,0:T(8,128)(2,1)S(1)}, u32[]{:S(2)}, u32[]{:S(2)}) collective-permute-start(bf16[2,384,1024]{2,1,0:T(8,128)(2,1)S(1)} %shard_map.77), channel_id=1, source_target_pairs={{0,4},{1,5},{2,6},{3,7},{4,0},{5,1},{6,2},{7,3},{8,12},{9,13},{10,... | collective-permute-start | bytes 4718600 | tf_op jit(solution)/shard_map/ppermute | solution.py:372
  6.5 35.2 %collective-permute-start.3 = (bf16[2,384,1024]{2,1,0:T(8,128)(2,1)S(1)}, bf16[2,384,1024]{2,1,0:T(8,128)(2,1)S(1)}, u32[]{:S(2)}, u32[]{:S(2)}) collective-permute-start(bf16[2,384,1024]{2,1,0:T(8,128)(2,1)S(1)} %shard_map.77), channel_id=1, source_target_pairs={{0,1},{1,0},{2,3},{3,2},{4,8},{5,9},{6,10},{7,11},{8,4},{9,5},{10,... | collective-permute-start | bytes 4718600 | tf_op jit(solution)/shard_map/ppermute | solution.py:372
  6.5 20.0 %collective-permute-start = (bf16[2,384,512]{2,1,0:T(8,128)(2,1)S(1)}, bf16[2,384,512]{2,1,0:T(8,128)(2,1)S(1)}, u32[]{:S(2)}, u32[]{:S(2)}) collective-permute-start(bf16[2,384,512]{2,1,0:T(8,128)(2,1)S(1)} %shard_map.78), channel_id=1, source_target_pairs={{0,16},{16,0},{1,17},{17,1},{2,18},{18,2},{3,19},{19,3},{4,20},{20... | collective-permute-start | bytes 2359304 | tf_op jit(solution)/shard_map/ppermute | solution.py:381
  26.6 15.1 %copy-start.1 = (bf16[1,1,1,384,1536]{4,3,2,1,0:T(8,128)(2,1)S(1)}, bf16[1,1,1,384,1536]{4,3,2,1,0:T(8,128)(2,1)}, u32[]{:S(2)}) copy-start(bf16[1,1,1,384,1536]{4,3,2,1,0:T(8,128)(2,1)} %param.7) | copy-start | bytes 3538948
  26.6 15.1 %copy-start.3 = (bf16[1,1,1,384,1536]{4,3,2,1,0:T(8,128)(2,1)S(1)}, bf16[1,1,1,384,1536]{4,3,2,1,0:T(8,128)(2,1)}, u32[]{:S(2)}) copy-start(bf16[1,1,1,384,1536]{4,3,2,1,0:T(8,128)(2,1)} %param.8) | copy-start | bytes 3538948
  26.7 40.6 %collective-permute-start.1 = (bf16[2,400,512]{2,1,0:T(8,128)(2,1)S(1)}, bf16[2,400,512]{2,1,0:T(8,128)(2,1)S(1)}, u32[]{:S(2)}, u32[]{:S(2)}) collective-permute-start(bf16[2,400,512]{2,1,0:T(8,128)(2,1)S(1)} %shard_map.80), channel_id=1, source_target_pairs={{0,16},{16,0},{1,17},{17,1},{2,18},{18,2},{3,19},{19,3},{4,20},{20... | collective-permute-start | bytes 2457608 | tf_op jit(solution)/shard_map/ppermute | solution.py:381
  28.2 37.0 %collective-permute-start.4 = (bf16[2,384,512]{2,1,0:T(8,128)(2,1)S(1)}, bf16[2,384,512]{2,1,0:T(8,128)(2,1)S(1)}, u32[]{:S(2)}, u32[]{:S(2)}) collective-permute-start(bf16[2,384,512]{2,1,0:T(8,128)(2,1)S(1)} %collective-permute-done.key.value), channel_id=1, source_target_pairs={{0,4},{1,5},{2,6},{3,7},{4,0},{5,1},{6,2},{7,3},{8,12},{9,13},{10,... | collective-permute-start | bytes 2359304 | tf_op jit(solution)/shard_map/ppermute | solution.py:372
  30.1 35.1 %collective-permute-start.5 = (bf16[2,384,512]{2,1,0:T(8,128)(2,1)S(1)}, bf16[2,384,512]{2,1,0:T(8,128)(2,1)S(1)}, u32[]{:S(2)}, u32[]{:S(2)}) collective-permute-start(bf16[2,384,512]{2,1,0:T(8,128)(2,1)S(1)} %collective-permute-done.key.value), channel_id=1, source_target_pairs={{0,1},{1,0},{2,3},{3,2},{4,8},{5,9},{6,10},{7,11},{8,4},{9,5},{10,... | collective-permute-start | bytes 2359304 | tf_op jit(solution)/shard_map/ppermute | solution.py:372
  60.5 17.9 %collective-permute-start.8 = (bf16[384,1024]{1,0:T(8,128)(2,1)S(1)}, bf16[384,1024]{1,0:T(8,128)(2,1)S(1)}, u32[]{:S(2)}, u32[]{:S(2)}) collective-permute-start(bf16[384,1024]{1,0:T(8,128)(2,1)S(1)} %get-tuple-element.27), channel_id=1, source_target_pairs={{0,16},{16,0},{1,17},{17,1},{2,18},{18,2},{3,19},{19,3},{4,20},{20... | collective-permute-start | bytes 2359304 | tf_op jit(solution)/shard_map/ppermute | solution.py:381
  62.5 21.2 %collective-permute-start.13 = (bf16[2,384,512]{2,1,0:T(8,128)(2,1)S(1)}, bf16[2,384,512]{2,1,0:T(8,128)(2,1)S(1)}, u32[]{:S(2)}, u32[]{:S(2)}) collective-permute-start(bf16[2,384,512]{2,1,0:T(8,128)(2,1)S(1)} %get-tuple-element.40), channel_id=1, source_target_pairs={{0,4},{1,5},{2,6},{3,7},{4,0},{5,1},{6,2},{7,3},{8,12},{9,13},{10,... | collective-permute-start | bytes 2359304 | tf_op jit(solution)/shard_map/ppermute | solution.py:372
  65.2 20.5 %collective-permute-start.14 = (bf16[2,384,512]{2,1,0:T(8,128)(2,1)S(1)}, bf16[2,384,512]{2,1,0:T(8,128)(2,1)S(1)}, u32[]{:S(2)}, u32[]{:S(2)}) collective-permute-start(bf16[2,384,512]{2,1,0:T(8,128)(2,1)S(1)} %get-tuple-element.41), channel_id=1, source_target_pairs={{0,1},{1,0},{2,3},{3,2},{4,8},{5,9},{6,10},{7,11},{8,4},{9,5},{10,... | collective-permute-start | bytes 2359304 | tf_op jit(solution)/shard_map/ppermute | solution.py:372
  65.2 35.3 %collective-permute-start.10 = (bf16[2,384,512]{2,1,0:T(8,128)(2,1)S(1)}, bf16[2,384,512]{2,1,0:T(8,128)(2,1)S(1)}, u32[]{:S(2)}, u32[]{:S(2)}) collective-permute-start(bf16[2,384,512]{2,1,0:T(8,128)(2,1)S(1)} %get-tuple-element.36), channel_id=1, source_target_pairs={{0,4},{1,5},{2,6},{3,7},{4,0},{5,1},{6,2},{7,3},{8,12},{9,13},{10,... | collective-permute-start | bytes 2359304 | tf_op jit(solution)/shard_map/ppermute | solution.py:372
  67.3 33.3 %collective-permute-start.11 = (bf16[2,384,512]{2,1,0:T(8,128)(2,1)S(1)}, bf16[2,384,512]{2,1,0:T(8,128)(2,1)S(1)}, u32[]{:S(2)}, u32[]{:S(2)}) collective-permute-start(bf16[2,384,512]{2,1,0:T(8,128)(2,1)S(1)} %get-tuple-element.37), channel_id=1, source_target_pairs={{0,1},{1,0},{2,3},{3,2},{4,8},{5,9},{6,10},{7,11},{8,4},{9,5},{10,... | collective-permute-start | bytes 2359304 | tf_op jit(solution)/shard_map/ppermute | solution.py:372
  78.4 8.8 %collective-permute-start.9 = (f32[2,128]{1,0:T(2,128)S(1)}, f32[2,128]{1,0:T(2,128)S(1)}, u32[]{:S(2)}, u32[]{:S(2)}) collective-permute-start(f32[2,128]{1,0:T(2,128)S(1)} %slice.9), channel_id=1, source_target_pairs={{0,16},{16,0},{1,17},{17,1},{2,18},{18,2},{3,19},{19,3},{4,20},{20... | collective-permute-start | bytes 3080 | tf_op jit(solution)/shard_map/ppermute | solution.py:381
  83.7 35.6 %collective-permute-start.6 = (bf16[2,384,512]{2,1,0:T(8,128)(2,1)S(1)}, bf16[2,384,512]{2,1,0:T(8,128)(2,1)S(1)}, u32[]{:S(2)}, u32[]{:S(2)}) collective-permute-start(bf16[2,384,512]{2,1,0:T(8,128)(2,1)S(1)} %get-tuple-element.30), channel_id=1, source_target_pairs={{0,4},{1,5},{2,6},{3,7},{4,0},{5,1},{6,2},{7,3},{8,12},{9,13},{10,... | collective-permute-start | bytes 2359304 | tf_op jit(solution)/shard_map/ppermute | solution.py:372
  85.7 33.6 %collective-permute-start.7 = (bf16[2,384,512]{2,1,0:T(8,128)(2,1)S(1)}, bf16[2,384,512]{2,1,0:T(8,128)(2,1)S(1)}, u32[]{:S(2)}, u32[]{:S(2)}) collective-permute-start(bf16[2,384,512]{2,1,0:T(8,128)(2,1)S(1)} %get-tuple-element.31), channel_id=1, source_target_pairs={{0,1},{1,0},{2,3},{3,2},{4,8},{5,9},{6,10},{7,11},{8,4},{9,5},{10,... | collective-permute-start | bytes 2359304 | tf_op jit(solution)/shard_map/ppermute | solution.py:372
  87.2 32.0 %collective-permute-start.15 = (bf16[2,384,512]{2,1,0:T(8,128)(2,1)S(1)}, bf16[2,384,512]{2,1,0:T(8,128)(2,1)S(1)}, u32[]{:S(2)}, u32[]{:S(2)}) collective-permute-start(bf16[2,384,512]{2,1,0:T(8,128)(2,1)S(1)} %shard_map.85), channel_id=1, source_target_pairs={{0,16},{16,0},{1,17},{17,1},{2,18},{18,2},{3,19},{19,3},{4,20},{20... | collective-permute-start | bytes 2359304 | tf_op jit(solution)/shard_map/ppermute | solution.py:381
  102.1 22.0 %collective-permute-start.12 = (bf16[2,384,512]{2,1,0:T(8,128)(2,1)S(1)}, bf16[2,384,512]{2,1,0:T(8,128)(2,1)S(1)}, u32[]{:S(2)}, u32[]{:S(2)}) collective-permute-start(bf16[2,384,512]{2,1,0:T(8,128)(2,1)S(1)} %shard_map.84), channel_id=1, source_target_pairs={{0,16},{16,0},{1,17},{17,1},{2,18},{18,2},{3,19},{19,3},{4,20},{20... | collective-permute-start | bytes 2359304 | tf_op jit(solution)/shard_map/ppermute | solution.py:381
  102.7 1.1 collective-permute-start.16
  103.8 3.6 %collective-permute-start.17 = (f32[2,128]{1,0:T(2,128)S(1)}, f32[2,128]{1,0:T(2,128)S(1)}, u32[]{:S(2)}, u32[]{:S(2)}) collective-permute-start(f32[2,128]{1,0:T(2,128)S(1)} %add.20), channel_id=1, source_target_pairs={{0,2},{1,3},{2,0},{3,1},{4,6},{5,7},{6,4},{7,5},{8,10},{9,11},{10,... | collective-permute-start | bytes 3080 | tf_op jit(solution)/shard_map/ppermute | solution.py:388
  107.4 6.8 %collective-permute-start.18 = (f32[2,128]{1,0:T(2,128)S(1)}, f32[2,128]{1,0:T(2,128)S(1)}, u32[]{:S(2)}, u32[]{:S(2)}) collective-permute-start(f32[2,128]{1,0:T(2,128)S(1)} %add.21), channel_id=1, source_target_pairs={{0,4},{4,0},{8,12},{12,8},{1,5},{5,1},{9,13},{13,9},{2,6},{6,2},{1... | collective-permute-start | bytes 3080 | tf_op jit(solution)/shard_map/ppermute | solution.py:388
  114.2 4.5 %collective-permute-start.19 = (f32[2,128]{1,0:T(2,128)S(1)}, f32[2,128]{1,0:T(2,128)S(1)}, u32[]{:S(2)}, u32[]{:S(2)}) collective-permute-start(f32[2,128]{1,0:T(2,128)S(1)} %add.22), channel_id=1, source_target_pairs={{0,8},{4,12},{8,0},{12,4},{1,9},{5,13},{9,1},{13,5},{2,10},{6,14},... | collective-permute-start | bytes 3080 | tf_op jit(solution)/shard_map/ppermute | solution.py:388

commit v4 on v3

--- a/solution.py
+++ b/solution.py
@@ -13,7 +13,7 @@
 EPSILON = 1e-06
 ROOT_SCALE = HEAD_DIM ** (-0.5)
 EXP2_SCALE = ROOT_SCALE * math.log2(math.e)
-GROUPS = ((0, 4, False), (4, 4, False), (8, 4, True))
+GROUPS = ((0, 4, False), (4, 3, False), (7, 5, True))
 MAIN_VMEM = 20 * 1024 * 1024
 SMALL_VMEM = 12 * 1024 * 1024
 PACK_VMEM = 4 * 1024 * 1024
@@ -415,7 +415,8 @@
             )
             sums.append(turned(gain[:2], 1))
         else:
-            sources.append((info, [(a, first, None) for a in (query, grad, key, value)]))
+            group_info = after(info, asked) if first else info
+            sources.append((group_info, [(a, first, None) for a in (query, grad, key, value)]))
             query_grads, own, to_even, to_odd, gain = main_call(
                 *sources[-1], *home_gathered, first, count, query_grads, home_heads, first
             )

time: 127 us -> 119 us (0.937)
  waiting for transfers between devices: 62.6 us -> 53.1 us
  starting transfers between devices: 25.7 us -> 28.1 us
    ppermute x10, waiting for transfers between devices: 28.2 us -> 18.8 us  [exchanged(): return lax.ppermute(value, ('seq', 'dp'), pairs)]
    ppermute x6, waiting for transfers between devices: 24.7 us -> 19.4 us  [turned(): lax.ppermute(value, 'pipe', [(i, (i + step) % count) for i in range(count)])]
    ppermute x4, waiting for transfers between devices: 9.75 us -> 14.9 us  [total_over(): lax.ppermute(value, axis, [(i, i ^ step) for i in range(count)])]
    ppermute x4, starting transfers between devices: 6.24 us -> 7.55 us  [total_over(): lax.ppermute(value, axis, [(i, i ^ step) for i in range(count)])]
  transfers between devices with their start and end apart: 20 -> 20, of which waited for: 10 -> 11; matrix products, arithmetic and copies ran while one was open for 0% -> 0% of each run, Pallas kernels for 25% -> 26%
where the time goes in v4:
time: 119 us
  waiting for transfers between devices  53.1 us (45%)
  Pallas kernels  34.2 us (29%)
  starting transfers between devices  28.1 us (24%)
  local copies, waits for them, and re-layouts  2.57 us (2%)
    pallas_call x3, Pallas kernels, main_call(): pl.pallas_call(main_kernel, grid=(count,), in_specs=[info_block(info)] +...  27.3 us
    ppermute x6, waiting for transfers between devices, turned(): lax.ppermute(value, 'pipe', [(i, (i + step) % count) for i in range(count)])  19.4 us
    ppermute x10, waiting for transfers between devices, exchanged(): return lax.ppermute(value, ('seq', 'dp'), pairs)  18.8 us
    ppermute x4, waiting for transfers between devices, total_over(): lax.ppermute(value, axis, [(i, i ^ step) for i in range(count)])  14.9 us
    ppermute x10, starting transfers between devices, exchanged(): return lax.ppermute(value, ('seq', 'dp'), pairs)  12.5 us
    ppermute x6, starting transfers between devices, turned(): lax.ppermute(value, 'pipe', [(i, (i + step) % count) for i in range(count)])  8.06 us
    ppermute x4, starting transfers between devices, total_over(): lax.ppermute(value, axis, [(i, i ^ step) for i in range(count)])  7.55 us
    pallas_call x1, Pallas kernels, last_call(): pl.pallas_call(functools.partial(last_kernel, places=places, first=first,...  3.31 us
  transfers between devices with their start and end apart: 20, of which 11 were waited for; matrix products, arithmetic and copies ran while one was open for 0% of the time, Pallas kernels for 26%

profile of v4, /device:TPU:0, one launch (start us, length us, event | category | flops | bytes accessed | tf_op | source)
XLA Modules:
  0.0 119.3 jit_solution(17207340468914000109)
XLA Ops:
  0.6 1.3 %copy-done = bf16[1,1,1,384,1536]{4,3,2,1,0:T(8,128)(2,1)S(1)} copy-done((bf16[1,1,1,384,1536]{4,3,2,1,0:T(8,128)(2,1)S(1)}, bf16[1,1,1,384,1536]{4,3,2,1,0:T(8,128)(2,1)}, u32[]{:S(2)}) %copy-start) | copy-done | bytes 1179672
  1.9 1.3 %copy-done.2 = bf16[1,1,1,384,1536]{4,3,2,1,0:T(8,128)(2,1)S(1)} copy-done((bf16[1,1,1,384,1536]{4,3,2,1,0:T(8,128)(2,1)S(1)}, bf16[1,1,1,384,1536]{4,3,2,1,0:T(8,128)(2,1)}, u32[]{:S(2)}) %copy-start.2) | copy-done | bytes 1179672
  3.5 3.0 %collective-permute-start = (bf16[2,384,640]{2,1,0:T(8,128)(2,1)S(1)}, bf16[2,384,640]{2,1,0:T(8,128)(2,1)S(1)}, u32[]{:S(2)}, u32[]{:S(2)}) collective-permute-start(bf16[2,384,640]{2,1,0:T(8,128)(2,1)S(1)} %shard_map.78), channel_id=1, source_target_pairs={{0,16},{16,0},{1,17},{17,1},{2,18},{18,2},{3,19},{19,3},{4,20},{20... | collective-permute-start | bytes 2949128 | tf_op jit(solution)/shard_map/ppermute | solution.py:381
  6.5 3.1 %collective-permute-start.2 = (bf16[2,384,896]{2,1,0:T(8,128)(2,1)S(1)}, bf16[2,384,896]{2,1,0:T(8,128)(2,1)S(1)}, u32[]{:S(2)}, u32[]{:S(2)}) collective-permute-start(bf16[2,384,896]{2,1,0:T(8,128)(2,1)S(1)} %shard_map.77), channel_id=1, source_target_pairs={{0,4},{1,5},{2,6},{3,7},{4,0},{5,1},{6,2},{7,3},{8,12},{9,13},{10,... | collective-permute-start | bytes 4128776 | tf_op jit(solution)/shard_map/ppermute | solution.py:372
  10.2 18.0 %collective-permute-done.key.value = bf16[2,384,640]{2,1,0:T(8,128)(2,1)S(1)} collective-permute-done((bf16[2,384,640]{2,1,0:T(8,128)(2,1)S(1)}, bf16[2,384,640]{2,1,0:T(8,128)(2,1)S(1)}, u32[]{:S(2)}, u32[]{:S(2)}) %collective-permute-start) | collective-permute-done | bytes 983072 | tf_op jit(solution)/shard_map/ppermute | solution.py:381
  28.4 1.8 %collective-permute-start.1 = (bf16[2,400,640]{2,1,0:T(8,128)(2,1)S(1)}, bf16[2,400,640]{2,1,0:T(8,128)(2,1)S(1)}, u32[]{:S(2)}, u32[]{:S(2)}) collective-permute-start(bf16[2,400,640]{2,1,0:T(8,128)(2,1)S(1)} %shard_map.80), channel_id=1, source_target_pairs={{0,16},{16,0},{1,17},{17,1},{2,18},{18,2},{3,19},{19,3},{4,20},{20... | collective-permute-start | bytes 3072008 | tf_op jit(solution)/shard_map/ppermute | solution.py:381
  30.2 3.1 %collective-permute-start.4 = (bf16[2,384,640]{2,1,0:T(8,128)(2,1)S(1)}, bf16[2,384,640]{2,1,0:T(8,128)(2,1)S(1)}, u32[]{:S(2)}, u32[]{:S(2)}) collective-permute-start(bf16[2,384,640]{2,1,0:T(8,128)(2,1)S(1)} %collective-permute-done.key.value), channel_id=1, source_target_pairs={{0,4},{1,5},{2,6},{3,7},{4,0},{5,1},{6,2},{7,3},{8,12},{9,13},{10,... | collective-permute-start | bytes 2949128 | tf_op jit(solution)/shard_map/ppermute | solution.py:372
  33.3 7.4 %collective-permute-done.2.pair_even = bf16[2,384,896]{2,1,0:T(8,128)(2,1)S(1)} collective-permute-done((bf16[2,384,896]{2,1,0:T(8,128)(2,1)S(1)}, bf16[2,384,896]{2,1,0:T(8,128)(2,1)S(1)}, u32[]{:S(2)}, u32[]{:S(2)}) %collective-permute-start.2) | collective-permute-done | bytes 1376288 | tf_op jit(solution)/shard_map/ppermute | solution.py:372
  40.7 9.1 %shard_map.81 = (bf16[384,896]{1,0:T(8,128)(2,1)S(1)}, f32[2,384,512]{2,1,0:T(8,128)S(1)}, bf16[2,384,512]{2,1,0:T(8,128)(2,1)S(1)}, bf16[2,384,512]{2,1,0:T(8,128)(2,1)S(1)}, f32[8,128]{1,0:T(8,128)S(1)}) custom-call(f32[8,128]{1,0:T(8,128)S(1)} %shard_map.79.info, bf16[384,1536]{1,0:T(8,128)(2,1)S(1)} %bitcast.22, bf16[384,1536]{1,0:T(8,128)(2,1)S(1)} %bitcast.25, ...), custom_call_target="tpu_custom_call" | custom-call | flops 6000000000 | bytes 1 | tf_op jit(solution)/shard_map/pallas_call | solution.py:299
  49.9 2.1 %collective-permute-start.10 = (bf16[2,384,512]{2,1,0:T(8,128)(2,1)S(1)}, bf16[2,384,512]{2,1,0:T(8,128)(2,1)S(1)}, u32[]{:S(2)}, u32[]{:S(2)}) collective-permute-start(bf16[2,384,512]{2,1,0:T(8,128)(2,1)S(1)} %get-tuple-element.38), channel_id=1, source_target_pairs={{0,4},{1,5},{2,6},{3,7},{4,0},{5,1},{6,2},{7,3},{8,12},{9,13},{10,... | collective-permute-start | bytes 2359304 | tf_op jit(solution)/shard_map/ppermute | solution.py:372
  52.3 6.8 %shard_map.82 = (bf16[384,896]{1,0:T(8,128)(2,1)S(1)}, f32[2,384,384]{2,1,0:T(8,128)S(1)}, bf16[2,384,384]{2,1,0:T(8,128)(2,1)S(1)}, bf16[2,384,384]{2,1,0:T(8,128)(2,1)S(1)}, f32[8,128]{1,0:T(8,128)S(1)}) custom-call(f32[8,128]{1,0:T(8,128)S(1)} %shard_map.79.info, bf16[384,1536]{1,0:T(8,128)(2,1)S(1)} %bitcast.23, ...), custom_call_target="tpu_custom_call", output_to_operand_aliasing={{0}: (7, {})} | custom-call | flops 6000000000 | bytes 1 | tf_op jit(solution)/shard_map/pallas_call | solution.py:299
  59.1 1.5 %collective-permute-start.8 = (bf16[384,896]{1,0:T(8,128)(2,1)S(1)}, bf16[384,896]{1,0:T(8,128)(2,1)S(1)}, u32[]{:S(2)}, u32[]{:S(2)}) collective-permute-start(bf16[384,896]{1,0:T(8,128)(2,1)S(1)} %get-tuple-element.29), channel_id=1, source_target_pairs={{0,16},{16,0},{1,17},{17,1},{2,18},{18,2},{3,19},{19,3},{4,20},{20... | collective-permute-start | bytes 2064392 | tf_op jit(solution)/shard_map/ppermute | solution.py:381
  60.6 1.2 %collective-permute-done.4.pair_even = bf16[2,384,640]{2,1,0:T(8,128)(2,1)S(1)} collective-permute-done((bf16[2,384,640]{2,1,0:T(8,128)(2,1)S(1)}, bf16[2,384,640]{2,1,0:T(8,128)(2,1)S(1)}, u32[]{:S(2)}, u32[]{:S(2)}) %collective-permute-start.4) | collective-permute-done | bytes 983072 | tf_op jit(solution)/shard_map/ppermute | solution.py:372
  61.8 11.3 %shard_map.83 = (bf16[384,640]{1,0:T(8,128)(2,1)S(1)}, f32[2,384,640]{2,1,0:T(8,128)S(1)}, bf16[2,384,640]{2,1,0:T(8,128)(2,1)S(1)}, bf16[2,384,640]{2,1,0:T(8,128)(2,1)S(1)}, f32[8,128]{1,0:T(8,128)S(1)}) custom-call(bf16[2,400,640]{2,1,0:T(8,128)(2,1)S(1)} %collective-permute-done.1.info.query.grad, ...), custom_call_target="tpu_custom_call" | custom-call | flops 6000000000 | bytes 1 | tf_op jit(solution)/shard_map/pallas_call | solution.py:299
  73.1 0.6 collective-permute-start.9
  73.7 2.0 %collective-permute-start.13 = (bf16[2,384,384]{2,1,0:T(8,128)(2,1)S(1)}, bf16[2,384,384]{2,1,0:T(8,128)(2,1)S(1)}, u32[]{:S(2)}, u32[]{:S(2)}) collective-permute-start(bf16[2,384,384]{2,1,0:T(8,128)(2,1)S(1)} %get-tuple-element.42), channel_id=1, source_target_pairs={{0,4},{1,5},{2,6},{3,7},{4,0},{5,1},{6,2},{7,3},{8,12},{9,13},{10,... | collective-permute-start | bytes 1769480 | tf_op jit(solution)/shard_map/ppermute | solution.py:372
  75.8 1.1 collective-permute-done.9
  76.8 1.8 %collective-permute-done.10.from_even = bf16[2,384,512]{2,1,0:T(8,128)(2,1)S(1)} collective-permute-done((bf16[2,384,512]{2,1,0:T(8,128)(2,1)S(1)}, bf16[2,384,512]{2,1,0:T(8,128)(2,1)S(1)}, u32[]{:S(2)}, u32[]{:S(2)}) %collective-permute-start.10) | collective-permute-done | bytes 786464 | tf_op jit(solution)/shard_map/ppermute | solution.py:372
  78.6 2.0 %collective-permute-start.6 = (bf16[2,384,640]{2,1,0:T(8,128)(2,1)S(1)}, bf16[2,384,640]{2,1,0:T(8,128)(2,1)S(1)}, u32[]{:S(2)}, u32[]{:S(2)}) collective-permute-start(bf16[2,384,640]{2,1,0:T(8,128)(2,1)S(1)} %get-tuple-element.32), channel_id=1, source_target_pairs={{0,4},{1,5},{2,6},{3,7},{4,0},{5,1},{6,2},{7,3},{8,12},{9,13},{10,... | collective-permute-start | bytes 2949128 | tf_op jit(solution)/shard_map/ppermute | solution.py:372
  80.7 1.6 %shard_map.84 = bf16[2,384,512]{2,1,0:T(8,128)(2,1)S(1)} custom-call(f32[8,128]{1,0:T(8,128)S(1)} %shard_map.79.info, bf16[384,1536]{1,0:T(8,128)(2,1)S(1)} %bitcast.15, f32[2,384,512]{2,1,0:T(8,128)S(1)} %get-tuple-element.37.own, bf16[2,384,512]{2,1,0:T(8,128)(2,1)S(1)} %collective-permute-done.10.from_even, ...), custom_call_target="tpu_custom_call" | custom-call | flops 1 | bytes 1 | tf_op jit(solution)/shard_map/pallas_call | solution.py:325
  82.3 0.6 collective-permute-start.12
  82.9 8.4 %collective-permute-done.13.from_even = bf16[2,384,384]{2,1,0:T(8,128)(2,1)S(1)} collective-permute-done((bf16[2,384,384]{2,1,0:T(8,128)(2,1)S(1)}, bf16[2,384,384]{2,1,0:T(8,128)(2,1)S(1)}, u32[]{:S(2)}, u32[]{:S(2)}) %collective-permute-start.13) | collective-permute-done | bytes 589856 | tf_op jit(solution)/shard_map/ppermute | solution.py:372
  91.3 1.1 shard_map.85
  92.4 0.6 collective-permute-start.15
  93.0 1.1 collective-permute-done.16
  94.1 1.5 %collective-permute-start.17 = (f32[2,128]{1,0:T(2,128)S(1)}, f32[2,128]{1,0:T(2,128)S(1)}, u32[]{:S(2)}, u32[]{:S(2)}) collective-permute-start(f32[2,128]{1,0:T(2,128)S(1)} %add.20), channel_id=1, source_target_pairs={{0,2},{1,3},{2,0},{3,1},{4,6},{5,7},{6,4},{7,5},{8,10},{9,11},{10,... | collective-permute-start | bytes 3080 | tf_op jit(solution)/shard_map/ppermute | solution.py:388
  95.6 2.0 %collective-permute-done.17 = f32[2,128]{1,0:T(2,128)S(1)} collective-permute-done((f32[2,128]{1,0:T(2,128)S(1)}, f32[2,128]{1,0:T(2,128)S(1)}, u32[]{:S(2)}, u32[]{:S(2)}) %collective-permute-start.17) | collective-permute-done | bytes 1056 | tf_op jit(solution)/shard_map/ppermute | solution.py:388
  97.7 3.8 %collective-permute-start.18 = (f32[2,128]{1,0:T(2,128)S(1)}, f32[2,128]{1,0:T(2,128)S(1)}, u32[]{:S(2)}, u32[]{:S(2)}) collective-permute-start(f32[2,128]{1,0:T(2,128)S(1)} %add.21), channel_id=1, source_target_pairs={{0,4},{4,0},{8,12},{12,8},{1,5},{5,1},{9,13},{13,9},{2,6},{6,2},{1... | collective-permute-start | bytes 3080 | tf_op jit(solution)/shard_map/ppermute | solution.py:388
  101.5 9.5 %collective-permute-done.18 = f32[2,128]{1,0:T(2,128)S(1)} collective-permute-done((f32[2,128]{1,0:T(2,128)S(1)}, f32[2,128]{1,0:T(2,128)S(1)}, u32[]{:S(2)}, u32[]{:S(2)}) %collective-permute-start.18) | collective-permute-done | bytes 1056 | tf_op jit(solution)/shard_map/ppermute | solution.py:388
  110.9 2.2 %collective-permute-start.19 = (f32[2,128]{1,0:T(2,128)S(1)}, f32[2,128]{1,0:T(2,128)S(1)}, u32[]{:S(2)}, u32[]{:S(2)}) collective-permute-start(f32[2,128]{1,0:T(2,128)S(1)} %add.22), channel_id=1, source_target_pairs={{0,8},{4,12},{8,0},{12,4},{1,9},{5,13},{9,1},{13,5},{2,10},{6,14},... | collective-permute-start | bytes 3080 | tf_op jit(solution)/shard_map/ppermute | solution.py:388
  113.2 2.2 %collective-permute-done.19 = f32[2,128]{1,0:T(2,128)S(1)} collective-permute-done((f32[2,128]{1,0:T(2,128)S(1)}, f32[2,128]{1,0:T(2,128)S(1)}, u32[]{:S(2)}, u32[]{:S(2)}) %collective-permute-start.19) | collective-permute-done | bytes 1056 | tf_op jit(solution)/shard_map/ppermute | solution.py:388
  116.0 3.3 %shard_map.86 = bf16[3,384,1536]{2,1,0:T(8,128)(2,1)} custom-call(bf16[2,400,640]{2,1,0:T(8,128)(2,1)S(1)} %collective-permute-done.1.info.query.grad, bf16[2,384,640]{2,1,0:T(8,128)(2,1)S(1)} %collective-permute-done.key.value, f32[2,384,640]{2,1,0:T(8,128)S(1)} %get-tuple-element.31.own, bf16[2,384,640]{2,1,0:T(8,128)(2,1)S(1)} %collective-permute-done.6.from_even, ...), custom_call_target="tpu_custom_call" | custom-call | flops 1 | bytes 1 | tf_op jit(solution)/shard_map/pallas_call | solution.py:340
  (40 shorter events, 1.9 us)
Async XLA Ops:
  0.6 1.3 %copy-start = (bf16[1,1,1,384,1536]{4,3,2,1,0:T(8,128)(2,1)S(1)}, bf16[1,1,1,384,1536]{4,3,2,1,0:T(8,128)(2,1)}, u32[]{:S(2)}) copy-start(bf16[1,1,1,384,1536]{4,3,2,1,0:T(8,128)(2,1)} %param.7) | copy-start | bytes 3538948
  1.9 1.3 %copy-start.2 = (bf16[1,1,1,384,1536]{4,3,2,1,0:T(8,128)(2,1)S(1)}, bf16[1,1,1,384,1536]{4,3,2,1,0:T(8,128)(2,1)}, u32[]{:S(2)}) copy-start(bf16[1,1,1,384,1536]{4,3,2,1,0:T(8,128)(2,1)} %param.8) | copy-start | bytes 3538948
  3.3 6.3 %copy-start.6 = (f32[1,2,128]{2,1,0:T(2,128)S(1)}, f32[1,2,128]{2,1,0:T(2,128)}, u32[]{:S(2)}) copy-start(f32[1,2,128]{2,1,0:T(2,128)} %param.10) | copy-start | bytes 3076
  3.3 6.3 %copy-start.7 = (s32[1,1,1,3]{3,2,1,0:T(1,128)S(1)}, s32[1,1,1,3]{3,2,1,0:T(1,128)}, u32[]{:S(2)}) copy-start(s32[1,1,1,3]{3,2,1,0:T(1,128)} %param.11) | copy-start | bytes 40
  3.3 24.9 %copy-start.4 = (bf16[1,1,1,384,1536]{4,3,2,1,0:T(8,128)(2,1)S(1)}, bf16[1,1,1,384,1536]{4,3,2,1,0:T(8,128)(2,1)}, u32[]{:S(2)}) copy-start(bf16[1,1,1,384,1536]{4,3,2,1,0:T(8,128)(2,1)} %param.6) | copy-start | bytes 3538948
  3.4 24.9 %copy-start.5 = (bf16[1,1,1,384,1536]{4,3,2,1,0:T(8,128)(2,1)S(1)}, bf16[1,1,1,384,1536]{4,3,2,1,0:T(8,128)(2,1)}, u32[]{:S(2)}) copy-start(bf16[1,1,1,384,1536]{4,3,2,1,0:T(8,128)(2,1)} %param.9) | copy-start | bytes 3538948
  3.5 24.8 %collective-permute-start = (bf16[2,384,640]{2,1,0:T(8,128)(2,1)S(1)}, bf16[2,384,640]{2,1,0:T(8,128)(2,1)S(1)}, u32[]{:S(2)}, u32[]{:S(2)}) collective-permute-start(bf16[2,384,640]{2,1,0:T(8,128)(2,1)S(1)} %shard_map.78), channel_id=1, source_target_pairs={{0,16},{16,0},{1,17},{17,1},{2,18},{18,2},{3,19},{19,3},{4,20},{20... | collective-permute-start | bytes 2949128 | tf_op jit(solution)/shard_map/ppermute | solution.py:381
  6.5 26.9 %collective-permute-start.3 = (bf16[2,384,896]{2,1,0:T(8,128)(2,1)S(1)}, bf16[2,384,896]{2,1,0:T(8,128)(2,1)S(1)}, u32[]{:S(2)}, u32[]{:S(2)}) collective-permute-start(bf16[2,384,896]{2,1,0:T(8,128)(2,1)S(1)} %shard_map.77), channel_id=1, source_target_pairs={{0,1},{1,0},{2,3},{3,2},{4,8},{5,9},{6,10},{7,11},{8,4},{9,5},{10,... | collective-permute-start | bytes 4128776 | tf_op jit(solution)/shard_map/ppermute | solution.py:372
  6.5 34.2 %collective-permute-start.2 = (bf16[2,384,896]{2,1,0:T(8,128)(2,1)S(1)}, bf16[2,384,896]{2,1,0:T(8,128)(2,1)S(1)}, u32[]{:S(2)}, u32[]{:S(2)}) collective-permute-start(bf16[2,384,896]{2,1,0:T(8,128)(2,1)S(1)} %shard_map.77), channel_id=1, source_target_pairs={{0,4},{1,5},{2,6},{3,7},{4,0},{5,1},{6,2},{7,3},{8,12},{9,13},{10,... | collective-permute-start | bytes 4128776 | tf_op jit(solution)/shard_map/ppermute | solution.py:372
  28.2 12.5 %copy-start.1 = (bf16[1,1,1,384,1536]{4,3,2,1,0:T(8,128)(2,1)S(1)}, bf16[1,1,1,384,1536]{4,3,2,1,0:T(8,128)(2,1)}, u32[]{:S(2)}) copy-start(bf16[1,1,1,384,1536]{4,3,2,1,0:T(8,128)(2,1)} %param.7) | copy-start | bytes 3538948
  28.2 12.5 %copy-start.3 = (bf16[1,1,1,384,1536]{4,3,2,1,0:T(8,128)(2,1)S(1)}, bf16[1,1,1,384,1536]{4,3,2,1,0:T(8,128)(2,1)}, u32[]{:S(2)}) copy-start(bf16[1,1,1,384,1536]{4,3,2,1,0:T(8,128)(2,1)} %param.8) | copy-start | bytes 3538948
  28.4 23.9 %collective-permute-start.1 = (bf16[2,400,640]{2,1,0:T(8,128)(2,1)S(1)}, bf16[2,400,640]{2,1,0:T(8,128)(2,1)S(1)}, u32[]{:S(2)}, u32[]{:S(2)}) collective-permute-start(bf16[2,400,640]{2,1,0:T(8,128)(2,1)S(1)} %shard_map.80), channel_id=1, source_target_pairs={{0,16},{16,0},{1,17},{17,1},{2,18},{18,2},{3,19},{19,3},{4,20},{20... | collective-permute-start | bytes 3072008 | tf_op jit(solution)/shard_map/ppermute | solution.py:381
  30.2 30.4 %collective-permute-start.5 = (bf16[2,384,640]{2,1,0:T(8,128)(2,1)S(1)}, bf16[2,384,640]{2,1,0:T(8,128)(2,1)S(1)}, u32[]{:S(2)}, u32[]{:S(2)}) collective-permute-start(bf16[2,384,640]{2,1,0:T(8,128)(2,1)S(1)} %collective-permute-done.key.value), channel_id=1, source_target_pairs={{0,1},{1,0},{2,3},{3,2},{4,8},{5,9},{6,10},{7,11},{8,4},{9,5},{10,... | collective-permute-start | bytes 2949128 | tf_op jit(solution)/shard_map/ppermute | solution.py:372
  30.2 31.6 %collective-permute-start.4 = (bf16[2,384,640]{2,1,0:T(8,128)(2,1)S(1)}, bf16[2,384,640]{2,1,0:T(8,128)(2,1)S(1)}, u32[]{:S(2)}, u32[]{:S(2)}) collective-permute-start(bf16[2,384,640]{2,1,0:T(8,128)(2,1)S(1)} %collective-permute-done.key.value), channel_id=1, source_target_pairs={{0,4},{1,5},{2,6},{3,7},{4,0},{5,1},{6,2},{7,3},{8,12},{9,13},{10,... | collective-permute-start | bytes 2949128 | tf_op jit(solution)/shard_map/ppermute | solution.py:372
  49.9 28.8 %collective-permute-start.10 = (bf16[2,384,512]{2,1,0:T(8,128)(2,1)S(1)}, bf16[2,384,512]{2,1,0:T(8,128)(2,1)S(1)}, u32[]{:S(2)}, u32[]{:S(2)}) collective-permute-start(bf16[2,384,512]{2,1,0:T(8,128)(2,1)S(1)} %get-tuple-element.38), channel_id=1, source_target_pairs={{0,4},{1,5},{2,6},{3,7},{4,0},{5,1},{6,2},{7,3},{8,12},{9,13},{10,... | collective-permute-start | bytes 2359304 | tf_op jit(solution)/shard_map/ppermute | solution.py:372
  52.0 28.7 %collective-permute-start.11 = (bf16[2,384,512]{2,1,0:T(8,128)(2,1)S(1)}, bf16[2,384,512]{2,1,0:T(8,128)(2,1)S(1)}, u32[]{:S(2)}, u32[]{:S(2)}) collective-permute-start(bf16[2,384,512]{2,1,0:T(8,128)(2,1)S(1)} %get-tuple-element.39), channel_id=1, source_target_pairs={{0,1},{1,0},{2,3},{3,2},{4,8},{5,9},{6,10},{7,11},{8,4},{9,5},{10,... | collective-permute-start | bytes 2359304 | tf_op jit(solution)/shard_map/ppermute | solution.py:372
  59.1 21.6 %collective-permute-start.8 = (bf16[384,896]{1,0:T(8,128)(2,1)S(1)}, bf16[384,896]{1,0:T(8,128)(2,1)S(1)}, u32[]{:S(2)}, u32[]{:S(2)}) collective-permute-start(bf16[384,896]{1,0:T(8,128)(2,1)S(1)} %get-tuple-element.29), channel_id=1, source_target_pairs={{0,16},{16,0},{1,17},{17,1},{2,18},{18,2},{3,19},{19,3},{4,20},{20... | collective-permute-start | bytes 2064392 | tf_op jit(solution)/shard_map/ppermute | solution.py:381
  73.1 3.7 %collective-permute-start.9 = (f32[2,128]{1,0:T(2,128)S(1)}, f32[2,128]{1,0:T(2,128)S(1)}, u32[]{:S(2)}, u32[]{:S(2)}) collective-permute-start(f32[2,128]{1,0:T(2,128)S(1)} %slice.9), channel_id=1, source_target_pairs={{0,16},{16,0},{1,17},{17,1},{2,18},{18,2},{3,19},{19,3},{4,20},{20... | collective-permute-start | bytes 3080 | tf_op jit(solution)/shard_map/ppermute | solution.py:381
  73.7 17.6 %collective-permute-start.13 = (bf16[2,384,384]{2,1,0:T(8,128)(2,1)S(1)}, bf16[2,384,384]{2,1,0:T(8,128)(2,1)S(1)}, u32[]{:S(2)}, u32[]{:S(2)}) collective-permute-start(bf16[2,384,384]{2,1,0:T(8,128)(2,1)S(1)} %get-tuple-element.42), channel_id=1, source_target_pairs={{0,4},{1,5},{2,6},{3,7},{4,0},{5,1},{6,2},{7,3},{8,12},{9,13},{10,... | collective-permute-start | bytes 1769480 | tf_op jit(solution)/shard_map/ppermute | solution.py:372
  76.8 14.5 %collective-permute-start.14 = (bf16[2,384,384]{2,1,0:T(8,128)(2,1)S(1)}, bf16[2,384,384]{2,1,0:T(8,128)(2,1)S(1)}, u32[]{:S(2)}, u32[]{:S(2)}) collective-permute-start(bf16[2,384,384]{2,1,0:T(8,128)(2,1)S(1)} %get-tuple-element.43), channel_id=1, source_target_pairs={{0,1},{1,0},{2,3},{3,2},{4,8},{5,9},{6,10},{7,11},{8,4},{9,5},{10,... | collective-permute-start | bytes 1769480 | tf_op jit(solution)/shard_map/ppermute | solution.py:372
  78.6 37.3 %collective-permute-start.6 = (bf16[2,384,640]{2,1,0:T(8,128)(2,1)S(1)}, bf16[2,384,640]{2,1,0:T(8,128)(2,1)S(1)}, u32[]{:S(2)}, u32[]{:S(2)}) collective-permute-start(bf16[2,384,640]{2,1,0:T(8,128)(2,1)S(1)} %get-tuple-element.32), channel_id=1, source_target_pairs={{0,4},{1,5},{2,6},{3,7},{4,0},{5,1},{6,2},{7,3},{8,12},{9,13},{10,... | collective-permute-start | bytes 2949128 | tf_op jit(solution)/shard_map/ppermute | solution.py:372
  80.7 35.3 %collective-permute-start.7 = (bf16[2,384,640]{2,1,0:T(8,128)(2,1)S(1)}, bf16[2,384,640]{2,1,0:T(8,128)(2,1)S(1)}, u32[]{:S(2)}, u32[]{:S(2)}) collective-permute-start(bf16[2,384,640]{2,1,0:T(8,128)(2,1)S(1)} %get-tuple-element.33), channel_id=1, source_target_pairs={{0,1},{1,0},{2,3},{3,2},{4,8},{5,9},{6,10},{7,11},{8,4},{9,5},{10,... | collective-permute-start | bytes 2949128 | tf_op jit(solution)/shard_map/ppermute | solution.py:372
  82.3 33.7 %collective-permute-start.12 = (bf16[2,384,512]{2,1,0:T(8,128)(2,1)S(1)}, bf16[2,384,512]{2,1,0:T(8,128)(2,1)S(1)}, u32[]{:S(2)}, u32[]{:S(2)}) collective-permute-start(bf16[2,384,512]{2,1,0:T(8,128)(2,1)S(1)} %shard_map.84), channel_id=1, source_target_pairs={{0,16},{16,0},{1,17},{17,1},{2,18},{18,2},{3,19},{19,3},{4,20},{20... | collective-permute-start | bytes 2359304 | tf_op jit(solution)/shard_map/ppermute | solution.py:381
  92.4 23.6 %collective-permute-start.15 = (bf16[2,384,384]{2,1,0:T(8,128)(2,1)S(1)}, bf16[2,384,384]{2,1,0:T(8,128)(2,1)S(1)}, u32[]{:S(2)}, u32[]{:S(2)}) collective-permute-start(bf16[2,384,384]{2,1,0:T(8,128)(2,1)S(1)} %shard_map.85), channel_id=1, source_target_pairs={{0,16},{16,0},{1,17},{17,1},{2,18},{18,2},{3,19},{19,3},{4,20},{20... | collective-permute-start | bytes 1769480 | tf_op jit(solution)/shard_map/ppermute | solution.py:381
  93.0 1.1 collective-permute-start.16
  94.1 3.6 %collective-permute-start.17 = (f32[2,128]{1,0:T(2,128)S(1)}, f32[2,128]{1,0:T(2,128)S(1)}, u32[]{:S(2)}, u32[]{:S(2)}) collective-permute-start(f32[2,128]{1,0:T(2,128)S(1)} %add.20), channel_id=1, source_target_pairs={{0,2},{1,3},{2,0},{3,1},{4,6},{5,7},{6,4},{7,5},{8,10},{9,11},{10,... | collective-permute-start | bytes 3080 | tf_op jit(solution)/shard_map/ppermute | solution.py:388
  97.7 13.3 %collective-permute-start.18 = (f32[2,128]{1,0:T(2,128)S(1)}, f32[2,128]{1,0:T(2,128)S(1)}, u32[]{:S(2)}, u32[]{:S(2)}) collective-permute-start(f32[2,128]{1,0:T(2,128)S(1)} %add.21), channel_id=1, source_target_pairs={{0,4},{4,0},{8,12},{12,8},{1,5},{5,1},{9,13},{13,9},{2,6},{6,2},{1... | collective-permute-start | bytes 3080 | tf_op jit(solution)/shard_map/ppermute | solution.py:388
  110.9 4.5 %collective-permute-start.19 = (f32[2,128]{1,0:T(2,128)S(1)}, f32[2,128]{1,0:T(2,128)S(1)}, u32[]{:S(2)}, u32[]{:S(2)}) collective-permute-start(f32[2,128]{1,0:T(2,128)S(1)} %add.22), channel_id=1, source_target_pairs={{0,8},{4,12},{8,0},{12,4},{1,9},{5,13},{9,1},{13,5},{2,10},{6,14},... | collective-permute-start | bytes 3080 | tf_op jit(solution)/shard_map/ppermute | solution.py:388

commit v5 on v4

--- a/solution.py
+++ b/solution.py
@@ -18,6 +18,7 @@
 SMALL_VMEM = 12 * 1024 * 1024
 PACK_VMEM = 4 * 1024 * 1024
 COST = pl.CostEstimate(flops=1, bytes_accessed=1, transcendentals=0)
+LONG_COST = pl.CostEstimate(flops=2 * 10**10, bytes_accessed=1, transcendentals=0)
 MAIN_COST = pl.CostEstimate(flops=6 * 10**9, bytes_accessed=1, transcendentals=0)
 
 
@@ -279,7 +280,7 @@
         out_specs=pl.BlockSpec(memory_space=pltpu.VMEM),
         out_shape=jax.ShapeDtypeStruct((8, HEAD_DIM), jnp.float32),
         compiler_params=pltpu.CompilerParams(vmem_limit_bytes=PACK_VMEM),
-        cost_estimate=COST,
+        cost_estimate=LONG_COST,
     )(listed, gains)
 
 
@@ -329,7 +330,7 @@
         out_specs=pair_block(rows),
         out_shape=jax.ShapeDtypeStruct((2, rows, count * HEAD_DIM), jnp.bfloat16),
         compiler_params=pltpu.CompilerParams(vmem_limit_bytes=SMALL_VMEM),
-        cost_estimate=COST,
+        cost_estimate=LONG_COST,
     )(info, array, own, from_even, from_odd)
 
 
@@ -381,12 +382,13 @@
     return lax.ppermute(value, "pipe", [(i, (i + step) % count) for i in range(count)])
 
 
-def total_over(value, axis):
+def total_over(value, axis, *late):
     count = lax.axis_size(axis)
     step = 1
     while step < count:
-        value = value + lax.ppermute(value, axis, [(i, i ^ step) for i in range(count)])
+        other = lax.ppermute(value, axis, [(i, i ^ step) for i in range(count)])
         step *= 2
+        value = value + (other if step < count else after(other, *late))
     return value
 
 
@@ -438,7 +440,7 @@
             pair_low = finish_call(group_info, operands[2], own, from_even, from_odd, count)
             pieces.append(turned(pair_low, -1))
             places.append((slice(1, 3), first * HEAD_DIM))
-    summed = total_over(total_over(sum(sums), "dp"), "seq")
+    summed = total_over(total_over(sum(sums), "dp"), "seq", out)
     tokens = lax.axis_size("dp") * seq_count * rows * HEADS
     return (out[None, :, None, None], (summed / math.sqrt(tokens))[None])
 

time: 119 us -> 119 us (level)
    ppermute x6, waiting for transfers between devices: 19.4 us -> 30.8 us  [turned(): lax.ppermute(value, 'pipe', [(i, (i + step) % count) for i in range(count)])]
    ppermute x10, waiting for transfers between devices: 18.8 us -> 10.9 us  [exchanged(): return lax.ppermute(value, ('seq', 'dp'), pairs)]
    ppermute x4, waiting for transfers between devices: 14.9 us -> 10.7 us  [total_over(): other = lax.ppermute(value, axis, [(i, i ^ step) for i in range(count)])]
  transfers between devices with their start and end apart: 20 -> 20, of which waited for: 11 -> 9; matrix products, arithmetic and copies ran while one was open for 0% -> 0% of each run, Pallas kernels for 26% -> 29%
where the time goes in v5:
time: 119 us
  waiting for transfers between devices  52.4 us (44%)
  Pallas kernels  34.2 us (29%)
  starting transfers between devices  28.7 us (24%)
  local copies, waits for them, and re-layouts  2.57 us (2%)
    ppermute x6, waiting for transfers between devices, turned(): lax.ppermute(value, 'pipe', [(i, (i + step) % count) for i in range(count)])  30.8 us
    pallas_call x3, Pallas kernels, main_call(): pl.pallas_call(main_kernel, grid=(count,), in_specs=[info_block(info)] +...  27.3 us
    ppermute x10, starting transfers between devices, exchanged(): return lax.ppermute(value, ('seq', 'dp'), pairs)  13.4 us
    ppermute x10, waiting for transfers between devices, exchanged(): return lax.ppermute(value, ('seq', 'dp'), pairs)  10.9 us
    ppermute x4, waiting for transfers between devices, total_over(): other = lax.ppermute(value, axis, [(i, i ^ step) for i in range(count)])  10.7 us
    ppermute x6, starting transfers between devices, turned(): lax.ppermute(value, 'pipe', [(i, (i + step) % count) for i in range(count)])  7.7 us
    ppermute x4, starting transfers between devices, total_over(): other = lax.ppermute(value, axis, [(i, i ^ step) for i in range(count)])  7.57 us
    pallas_call x1, Pallas kernels, last_call(): pl.pallas_call(functools.partial(last_kernel, places=places, first=first,...  3.29 us
  transfers between devices with their start and end apart: 20, of which 9 were waited for; matrix products, arithmetic and copies ran while one was open for 0% of the time, Pallas kernels for 29%

profile of v5, /device:TPU:0, one launch (start us, length us, event | category | flops | bytes accessed | tf_op | source)
XLA Modules:
  0.0 119.3 jit_solution(17540589621709565783)
XLA Ops:
  0.6 1.3 %copy-done = bf16[1,1,1,384,1536]{4,3,2,1,0:T(8,128)(2,1)S(1)} copy-done((bf16[1,1,1,384,1536]{4,3,2,1,0:T(8,128)(2,1)S(1)}, bf16[1,1,1,384,1536]{4,3,2,1,0:T(8,128)(2,1)}, u32[]{:S(2)}) %copy-start) | copy-done | bytes 1179672
  1.9 1.3 %copy-done.2 = bf16[1,1,1,384,1536]{4,3,2,1,0:T(8,128)(2,1)S(1)} copy-done((bf16[1,1,1,384,1536]{4,3,2,1,0:T(8,128)(2,1)S(1)}, bf16[1,1,1,384,1536]{4,3,2,1,0:T(8,128)(2,1)}, u32[]{:S(2)}) %copy-start.2) | copy-done | bytes 1179672
  3.9 4.1 %collective-permute-start.2 = (bf16[2,384,896]{2,1,0:T(8,128)(2,1)S(1)}, bf16[2,384,896]{2,1,0:T(8,128)(2,1)S(1)}, u32[]{:S(2)}, u32[]{:S(2)}) collective-permute-start(bf16[2,384,896]{2,1,0:T(8,128)(2,1)S(1)} %shard_map.77), channel_id=1, source_target_pairs={{0,4},{1,5},{2,6},{3,7},{4,0},{5,1},{6,2},{7,3},{8,12},{9,13},{10,... | collective-permute-start | bytes 4128776 | tf_op jit(solution)/shard_map/ppermute | solution.py:373
  8.1 1.6 %collective-permute-start = (bf16[2,384,640]{2,1,0:T(8,128)(2,1)S(1)}, bf16[2,384,640]{2,1,0:T(8,128)(2,1)S(1)}, u32[]{:S(2)}, u32[]{:S(2)}) collective-permute-start(bf16[2,384,640]{2,1,0:T(8,128)(2,1)S(1)} %shard_map.78), channel_id=1, source_target_pairs={{0,16},{16,0},{1,17},{17,1},{2,18},{18,2},{3,19},{19,3},{4,20},{20... | collective-permute-start | bytes 2949128 | tf_op jit(solution)/shard_map/ppermute | solution.py:382
  10.3 20.9 %collective-permute-done.key.value = bf16[2,384,640]{2,1,0:T(8,128)(2,1)S(1)} collective-permute-done((bf16[2,384,640]{2,1,0:T(8,128)(2,1)S(1)}, bf16[2,384,640]{2,1,0:T(8,128)(2,1)S(1)}, u32[]{:S(2)}, u32[]{:S(2)}) %collective-permute-start) | collective-permute-done | bytes 983072 | tf_op jit(solution)/shard_map/ppermute | solution.py:382
  31.3 1.6 %collective-permute-start.1 = (bf16[2,400,640]{2,1,0:T(8,128)(2,1)S(1)}, bf16[2,400,640]{2,1,0:T(8,128)(2,1)S(1)}, u32[]{:S(2)}, u32[]{:S(2)}) collective-permute-start(bf16[2,400,640]{2,1,0:T(8,128)(2,1)S(1)} %shard_map.80), channel_id=1, source_target_pairs={{0,16},{16,0},{1,17},{17,1},{2,18},{18,2},{3,19},{19,3},{4,20},{20... | collective-permute-start | bytes 3072008 | tf_op jit(solution)/shard_map/ppermute | solution.py:382
  32.8 2.5 %collective-permute-start.4 = (bf16[2,384,640]{2,1,0:T(8,128)(2,1)S(1)}, bf16[2,384,640]{2,1,0:T(8,128)(2,1)S(1)}, u32[]{:S(2)}, u32[]{:S(2)}) collective-permute-start(bf16[2,384,640]{2,1,0:T(8,128)(2,1)S(1)} %collective-permute-done.key.value), channel_id=1, source_target_pairs={{0,4},{1,5},{2,6},{3,7},{4,0},{5,1},{6,2},{7,3},{8,12},{9,13},{10,... | collective-permute-start | bytes 2949128 | tf_op jit(solution)/shard_map/ppermute | solution.py:373
  35.4 3.7 %collective-permute-done.2.pair_even = bf16[2,384,896]{2,1,0:T(8,128)(2,1)S(1)} collective-permute-done((bf16[2,384,896]{2,1,0:T(8,128)(2,1)S(1)}, bf16[2,384,896]{2,1,0:T(8,128)(2,1)S(1)}, u32[]{:S(2)}, u32[]{:S(2)}) %collective-permute-start.2) | collective-permute-done | bytes 1376288 | tf_op jit(solution)/shard_map/ppermute | solution.py:373
  39.1 9.2 %shard_map.81 = (bf16[384,896]{1,0:T(8,128)(2,1)S(1)}, f32[2,384,512]{2,1,0:T(8,128)S(1)}, bf16[2,384,512]{2,1,0:T(8,128)(2,1)S(1)}, bf16[2,384,512]{2,1,0:T(8,128)(2,1)S(1)}, f32[8,128]{1,0:T(8,128)S(1)}) custom-call(f32[8,128]{1,0:T(8,128)S(1)} %shard_map.79.info, bf16[384,1536]{1,0:T(8,128)(2,1)S(1)} %bitcast.22, bf16[384,1536]{1,0:T(8,128)(2,1)S(1)} %bitcast.25, ...), custom_call_target="tpu_custom_call" | custom-call | flops 6000000000 | bytes 1 | tf_op jit(solution)/shard_map/pallas_call | solution.py:300
  48.2 2.1 %collective-permute-start.10 = (bf16[2,384,512]{2,1,0:T(8,128)(2,1)S(1)}, bf16[2,384,512]{2,1,0:T(8,128)(2,1)S(1)}, u32[]{:S(2)}, u32[]{:S(2)}) collective-permute-start(bf16[2,384,512]{2,1,0:T(8,128)(2,1)S(1)} %get-tuple-element.39), channel_id=1, source_target_pairs={{0,4},{1,5},{2,6},{3,7},{4,0},{5,1},{6,2},{7,3},{8,12},{9,13},{10,... | collective-permute-start | bytes 2359304 | tf_op jit(solution)/shard_map/ppermute | solution.py:373
  50.3 3.9 %collective-permute-done.1.info.query.grad = bf16[2,400,640]{2,1,0:T(8,128)(2,1)S(1)} collective-permute-done((bf16[2,400,640]{2,1,0:T(8,128)(2,1)S(1)}, bf16[2,400,640]{2,1,0:T(8,128)(2,1)S(1)}, u32[]{:S(2)}, u32[]{:S(2)}) %collective-permute-start.1) | collective-permute-done | bytes 1024032 | tf_op jit(solution)/shard_map/ppermute | solution.py:382
  54.2 6.8 %shard_map.82 = (bf16[384,896]{1,0:T(8,128)(2,1)S(1)}, f32[2,384,384]{2,1,0:T(8,128)S(1)}, bf16[2,384,384]{2,1,0:T(8,128)(2,1)S(1)}, bf16[2,384,384]{2,1,0:T(8,128)(2,1)S(1)}, f32[8,128]{1,0:T(8,128)S(1)}) custom-call(f32[8,128]{1,0:T(8,128)S(1)} %shard_map.79.info, bf16[384,1536]{1,0:T(8,128)(2,1)S(1)} %bitcast.23, ...), custom_call_target="tpu_custom_call", output_to_operand_aliasing={{0}: (7, {})} | custom-call | flops 6000000000 | bytes 1 | tf_op jit(solution)/shard_map/pallas_call | solution.py:300
  61.1 1.5 %collective-permute-start.8 = (bf16[384,896]{1,0:T(8,128)(2,1)S(1)}, bf16[384,896]{1,0:T(8,128)(2,1)S(1)}, u32[]{:S(2)}, u32[]{:S(2)}) collective-permute-start(bf16[384,896]{1,0:T(8,128)(2,1)S(1)} %get-tuple-element.30), channel_id=1, source_target_pairs={{0,16},{16,0},{1,17},{17,1},{2,18},{18,2},{3,19},{19,3},{4,20},{20... | collective-permute-start | bytes 2064392 | tf_op jit(solution)/shard_map/ppermute | solution.py:382
  62.6 11.3 %shard_map.83 = (bf16[384,640]{1,0:T(8,128)(2,1)S(1)}, f32[2,384,640]{2,1,0:T(8,128)S(1)}, bf16[2,384,640]{2,1,0:T(8,128)(2,1)S(1)}, bf16[2,384,640]{2,1,0:T(8,128)(2,1)S(1)}, f32[8,128]{1,0:T(8,128)S(1)}) custom-call(bf16[2,400,640]{2,1,0:T(8,128)(2,1)S(1)} %collective-permute-done.1.info.query.grad, ...), custom_call_target="tpu_custom_call" | custom-call | flops 6000000000 | bytes 1 | tf_op jit(solution)/shard_map/pallas_call | solution.py:300
  73.9 0.6 collective-permute-start.9
  74.6 0.6 collective-permute-start.13
  75.1 2.4 %collective-permute-done.9 = f32[2,128]{1,0:T(2,128)S(1)} collective-permute-done((f32[2,128]{1,0:T(2,128)S(1)}, f32[2,128]{1,0:T(2,128)S(1)}, u32[]{:S(2)}, u32[]{:S(2)}) %collective-permute-start.9) | collective-permute-done | bytes 1056 | tf_op jit(solution)/shard_map/ppermute | solution.py:382
  77.6 3.5 %collective-permute-start.6 = (bf16[2,384,640]{2,1,0:T(8,128)(2,1)S(1)}, bf16[2,384,640]{2,1,0:T(8,128)(2,1)S(1)}, u32[]{:S(2)}, u32[]{:S(2)}) collective-permute-start(bf16[2,384,640]{2,1,0:T(8,128)(2,1)S(1)} %get-tuple-element.33), channel_id=1, source_target_pairs={{0,4},{1,5},{2,6},{3,7},{4,0},{5,1},{6,2},{7,3},{8,12},{9,13},{10,... | collective-permute-start | bytes 2949128 | tf_op jit(solution)/shard_map/ppermute | solution.py:373
  81.1 1.6 %shard_map.84 = bf16[2,384,512]{2,1,0:T(8,128)(2,1)S(1)} custom-call(f32[8,128]{1,0:T(8,128)S(1)} %shard_map.79.info, bf16[384,1536]{1,0:T(8,128)(2,1)S(1)} %bitcast.19, f32[2,384,512]{2,1,0:T(8,128)S(1)} %get-tuple-element.38.own, bf16[2,384,512]{2,1,0:T(8,128)(2,1)S(1)} %collective-permute-done.10.from_even, ...), custom_call_target="tpu_custom_call" | custom-call | flops 20000000000 | bytes 1 | tf_op jit(solution)/shard_map/pallas_call | solution.py:326
  82.7 0.9 collective-permute-start.12
  83.6 7.2 %collective-permute-done.13.from_even = bf16[2,384,384]{2,1,0:T(8,128)(2,1)S(1)} collective-permute-done((bf16[2,384,384]{2,1,0:T(8,128)(2,1)S(1)}, bf16[2,384,384]{2,1,0:T(8,128)(2,1)S(1)}, u32[]{:S(2)}, u32[]{:S(2)}) %collective-permute-start.13) | collective-permute-done | bytes 589856 | tf_op jit(solution)/shard_map/ppermute | solution.py:373
  90.8 1.1 shard_map.85
  91.9 1.5 %collective-permute-start.15 = (bf16[2,384,384]{2,1,0:T(8,128)(2,1)S(1)}, bf16[2,384,384]{2,1,0:T(8,128)(2,1)S(1)}, u32[]{:S(2)}, u32[]{:S(2)}) collective-permute-start(bf16[2,384,384]{2,1,0:T(8,128)(2,1)S(1)} %shard_map.85), channel_id=1, source_target_pairs={{0,16},{16,0},{1,17},{17,1},{2,18},{18,2},{3,19},{19,3},{4,20},{20... | collective-permute-start | bytes 1769480 | tf_op jit(solution)/shard_map/ppermute | solution.py:382
  93.4 1.1 collective-permute-done.16
  94.6 1.5 %collective-permute-start.17 = (f32[2,128]{1,0:T(2,128)S(1)}, f32[2,128]{1,0:T(2,128)S(1)}, u32[]{:S(2)}, u32[]{:S(2)}) collective-permute-start(f32[2,128]{1,0:T(2,128)S(1)} %add.20), channel_id=1, source_target_pairs={{0,2},{1,3},{2,0},{3,1},{4,6},{5,7},{6,4},{7,5},{8,10},{9,11},{10,... | collective-permute-start | bytes 3080 | tf_op jit(solution)/shard_map/ppermute | solution.py:389
  96.1 2.0 %collective-permute-done.17 = f32[2,128]{1,0:T(2,128)S(1)} collective-permute-done((f32[2,128]{1,0:T(2,128)S(1)}, f32[2,128]{1,0:T(2,128)S(1)}, u32[]{:S(2)}, u32[]{:S(2)}) %collective-permute-start.17) | collective-permute-done | bytes 1056 | tf_op jit(solution)/shard_map/ppermute | solution.py:389
  98.2 3.9 %collective-permute-start.18 = (f32[2,128]{1,0:T(2,128)S(1)}, f32[2,128]{1,0:T(2,128)S(1)}, u32[]{:S(2)}, u32[]{:S(2)}) collective-permute-start(f32[2,128]{1,0:T(2,128)S(1)} %add.21), channel_id=1, source_target_pairs={{0,4},{4,0},{8,12},{12,8},{1,5},{5,1},{9,13},{13,9},{2,6},{6,2},{1... | collective-permute-start | bytes 3080 | tf_op jit(solution)/shard_map/ppermute | solution.py:389
  102.1 7.5 %collective-permute-done.18 = f32[2,128]{1,0:T(2,128)S(1)} collective-permute-done((f32[2,128]{1,0:T(2,128)S(1)}, f32[2,128]{1,0:T(2,128)S(1)}, u32[]{:S(2)}, u32[]{:S(2)}) %collective-permute-start.18) | collective-permute-done | bytes 1056 | tf_op jit(solution)/shard_map/ppermute | solution.py:389
  109.6 2.1 %collective-permute-start.19 = (f32[2,128]{1,0:T(2,128)S(1)}, f32[2,128]{1,0:T(2,128)S(1)}, u32[]{:S(2)}, u32[]{:S(2)}) collective-permute-start(f32[2,128]{1,0:T(2,128)S(1)} %add.22), channel_id=1, source_target_pairs={{0,8},{4,12},{8,0},{12,4},{1,9},{5,13},{9,1},{13,5},{2,10},{6,14},... | collective-permute-start | bytes 3080 | tf_op jit(solution)/shard_map/ppermute | solution.py:389
  111.7 3.6 %collective-permute-done.15.rest_3_ = bf16[2,384,384]{2,1,0:T(8,128)(2,1)S(1)} collective-permute-done((bf16[2,384,384]{2,1,0:T(8,128)(2,1)S(1)}, bf16[2,384,384]{2,1,0:T(8,128)(2,1)S(1)}, u32[]{:S(2)}, u32[]{:S(2)}) %collective-permute-start.15) | collective-permute-done | bytes 589856 | tf_op jit(solution)/shard_map/ppermute | solution.py:382
  115.4 3.3 %shard_map.86 = bf16[3,384,1536]{2,1,0:T(8,128)(2,1)} custom-call(bf16[2,400,640]{2,1,0:T(8,128)(2,1)S(1)} %collective-permute-done.1.info.query.grad, bf16[2,384,640]{2,1,0:T(8,128)(2,1)S(1)} %collective-permute-done.key.value, f32[2,384,640]{2,1,0:T(8,128)S(1)} %get-tuple-element.32.own, bf16[2,384,640]{2,1,0:T(8,128)(2,1)S(1)} %collective-permute-done.6.from_even, ...), custom_call_target="tpu_custom_call" | custom-call | flops 1 | bytes 1 | tf_op jit(solution)/shard_map/pallas_call | solution.py:341
  118.7 0.6 multiply_bitcast_fusion
  (40 shorter events, 1.5 us)
Async XLA Ops:
  0.6 1.3 %copy-start = (bf16[1,1,1,384,1536]{4,3,2,1,0:T(8,128)(2,1)S(1)}, bf16[1,1,1,384,1536]{4,3,2,1,0:T(8,128)(2,1)}, u32[]{:S(2)}) copy-start(bf16[1,1,1,384,1536]{4,3,2,1,0:T(8,128)(2,1)} %param.8) | copy-start | bytes 3538948
  1.9 1.3 %copy-start.2 = (bf16[1,1,1,384,1536]{4,3,2,1,0:T(8,128)(2,1)S(1)}, bf16[1,1,1,384,1536]{4,3,2,1,0:T(8,128)(2,1)}, u32[]{:S(2)}) copy-start(bf16[1,1,1,384,1536]{4,3,2,1,0:T(8,128)(2,1)} %param.7) | copy-start | bytes 3538948
  3.3 6.4 %copy-start.6 = (f32[1,2,128]{2,1,0:T(2,128)S(1)}, f32[1,2,128]{2,1,0:T(2,128)}, u32[]{:S(2)}) copy-start(f32[1,2,128]{2,1,0:T(2,128)} %param.10) | copy-start | bytes 3076
  3.3 6.4 %copy-start.7 = (s32[1,1,1,3]{3,2,1,0:T(1,128)S(1)}, s32[1,1,1,3]{3,2,1,0:T(1,128)}, u32[]{:S(2)}) copy-start(s32[1,1,1,3]{3,2,1,0:T(1,128)} %param.11) | copy-start | bytes 40
  3.3 32.0 %collective-permute-start.3 = (bf16[2,384,896]{2,1,0:T(8,128)(2,1)S(1)}, bf16[2,384,896]{2,1,0:T(8,128)(2,1)S(1)}, u32[]{:S(2)}, u32[]{:S(2)}) collective-permute-start(bf16[2,384,896]{2,1,0:T(8,128)(2,1)S(1)} %shard_map.77), channel_id=1, source_target_pairs={{0,1},{1,0},{2,3},{3,2},{4,8},{5,9},{6,10},{7,11},{8,4},{9,5},{10,... | collective-permute-start | bytes 4128776 | tf_op jit(solution)/shard_map/ppermute | solution.py:373
  3.9 35.2 %collective-permute-start.2 = (bf16[2,384,896]{2,1,0:T(8,128)(2,1)S(1)}, bf16[2,384,896]{2,1,0:T(8,128)(2,1)S(1)}, u32[]{:S(2)}, u32[]{:S(2)}) collective-permute-start(bf16[2,384,896]{2,1,0:T(8,128)(2,1)S(1)} %shard_map.77), channel_id=1, source_target_pairs={{0,4},{1,5},{2,6},{3,7},{4,0},{5,1},{6,2},{7,3},{8,12},{9,13},{10,... | collective-permute-start | bytes 4128776 | tf_op jit(solution)/shard_map/ppermute | solution.py:373
  8.1 23.0 %collective-permute-start = (bf16[2,384,640]{2,1,0:T(8,128)(2,1)S(1)}, bf16[2,384,640]{2,1,0:T(8,128)(2,1)S(1)}, u32[]{:S(2)}, u32[]{:S(2)}) collective-permute-start(bf16[2,384,640]{2,1,0:T(8,128)(2,1)S(1)} %shard_map.78), channel_id=1, source_target_pairs={{0,16},{16,0},{1,17},{17,1},{2,18},{18,2},{3,19},{19,3},{4,20},{20... | collective-permute-start | bytes 2949128 | tf_op jit(solution)/shard_map/ppermute | solution.py:382
  9.7 21.4 %copy-start.4 = (bf16[1,1,1,384,1536]{4,3,2,1,0:T(8,128)(2,1)S(1)}, bf16[1,1,1,384,1536]{4,3,2,1,0:T(8,128)(2,1)}, u32[]{:S(2)}) copy-start(bf16[1,1,1,384,1536]{4,3,2,1,0:T(8,128)(2,1)} %param.6) | copy-start | bytes 3538948
  9.7 21.4 %copy-start.5 = (bf16[1,1,1,384,1536]{4,3,2,1,0:T(8,128)(2,1)S(1)}, bf16[1,1,1,384,1536]{4,3,2,1,0:T(8,128)(2,1)}, u32[]{:S(2)}) copy-start(bf16[1,1,1,384,1536]{4,3,2,1,0:T(8,128)(2,1)} %param.9) | copy-start | bytes 3538948
  31.1 7.9 %copy-start.1 = (bf16[1,1,1,384,1536]{4,3,2,1,0:T(8,128)(2,1)S(1)}, bf16[1,1,1,384,1536]{4,3,2,1,0:T(8,128)(2,1)}, u32[]{:S(2)}) copy-start(bf16[1,1,1,384,1536]{4,3,2,1,0:T(8,128)(2,1)} %param.8) | copy-start | bytes 3538948
  31.1 7.9 %copy-start.3 = (bf16[1,1,1,384,1536]{4,3,2,1,0:T(8,128)(2,1)S(1)}, bf16[1,1,1,384,1536]{4,3,2,1,0:T(8,128)(2,1)}, u32[]{:S(2)}) copy-start(bf16[1,1,1,384,1536]{4,3,2,1,0:T(8,128)(2,1)} %param.7) | copy-start | bytes 3538948
  31.3 23.0 %collective-permute-start.1 = (bf16[2,400,640]{2,1,0:T(8,128)(2,1)S(1)}, bf16[2,400,640]{2,1,0:T(8,128)(2,1)S(1)}, u32[]{:S(2)}, u32[]{:S(2)}) collective-permute-start(bf16[2,400,640]{2,1,0:T(8,128)(2,1)S(1)} %shard_map.80), channel_id=1, source_target_pairs={{0,16},{16,0},{1,17},{17,1},{2,18},{18,2},{3,19},{19,3},{4,20},{20... | collective-permute-start | bytes 3072008 | tf_op jit(solution)/shard_map/ppermute | solution.py:382
  32.8 29.8 %collective-permute-start.5 = (bf16[2,384,640]{2,1,0:T(8,128)(2,1)S(1)}, bf16[2,384,640]{2,1,0:T(8,128)(2,1)S(1)}, u32[]{:S(2)}, u32[]{:S(2)}) collective-permute-start(bf16[2,384,640]{2,1,0:T(8,128)(2,1)S(1)} %collective-permute-done.key.value), channel_id=1, source_target_pairs={{0,1},{1,0},{2,3},{3,2},{4,8},{5,9},{6,10},{7,11},{8,4},{9,5},{10,... | collective-permute-start | bytes 2949128 | tf_op jit(solution)/shard_map/ppermute | solution.py:373
  32.8 29.8 %collective-permute-start.4 = (bf16[2,384,640]{2,1,0:T(8,128)(2,1)S(1)}, bf16[2,384,640]{2,1,0:T(8,128)(2,1)S(1)}, u32[]{:S(2)}, u32[]{:S(2)}) collective-permute-start(bf16[2,384,640]{2,1,0:T(8,128)(2,1)S(1)} %collective-permute-done.key.value), channel_id=1, source_target_pairs={{0,4},{1,5},{2,6},{3,7},{4,0},{5,1},{6,2},{7,3},{8,12},{9,13},{10,... | collective-permute-start | bytes 2949128 | tf_op jit(solution)/shard_map/ppermute | solution.py:373
  48.2 32.9 %collective-permute-start.10 = (bf16[2,384,512]{2,1,0:T(8,128)(2,1)S(1)}, bf16[2,384,512]{2,1,0:T(8,128)(2,1)S(1)}, u32[]{:S(2)}, u32[]{:S(2)}) collective-permute-start(bf16[2,384,512]{2,1,0:T(8,128)(2,1)S(1)} %get-tuple-element.39), channel_id=1, source_target_pairs={{0,4},{1,5},{2,6},{3,7},{4,0},{5,1},{6,2},{7,3},{8,12},{9,13},{10,... | collective-permute-start | bytes 2359304 | tf_op jit(solution)/shard_map/ppermute | solution.py:373
  50.3 30.8 %collective-permute-start.11 = (bf16[2,384,512]{2,1,0:T(8,128)(2,1)S(1)}, bf16[2,384,512]{2,1,0:T(8,128)(2,1)S(1)}, u32[]{:S(2)}, u32[]{:S(2)}) collective-permute-start(bf16[2,384,512]{2,1,0:T(8,128)(2,1)S(1)} %get-tuple-element.40), channel_id=1, source_target_pairs={{0,1},{1,0},{2,3},{3,2},{4,8},{5,9},{6,10},{7,11},{8,4},{9,5},{10,... | collective-permute-start | bytes 2359304 | tf_op jit(solution)/shard_map/ppermute | solution.py:373
  61.1 16.5 %collective-permute-start.8 = (bf16[384,896]{1,0:T(8,128)(2,1)S(1)}, bf16[384,896]{1,0:T(8,128)(2,1)S(1)}, u32[]{:S(2)}, u32[]{:S(2)}) collective-permute-start(bf16[384,896]{1,0:T(8,128)(2,1)S(1)} %get-tuple-element.30), channel_id=1, source_target_pairs={{0,16},{16,0},{1,17},{17,1},{2,18},{18,2},{3,19},{19,3},{4,20},{20... | collective-permute-start | bytes 2064392 | tf_op jit(solution)/shard_map/ppermute | solution.py:382
  73.9 3.6 %collective-permute-start.9 = (f32[2,128]{1,0:T(2,128)S(1)}, f32[2,128]{1,0:T(2,128)S(1)}, u32[]{:S(2)}, u32[]{:S(2)}) collective-permute-start(f32[2,128]{1,0:T(2,128)S(1)} %slice.9), channel_id=1, source_target_pairs={{0,16},{16,0},{1,17},{17,1},{2,18},{18,2},{3,19},{19,3},{4,20},{20... | collective-permute-start | bytes 3080 | tf_op jit(solution)/shard_map/ppermute | solution.py:382
  74.6 16.3 %collective-permute-start.13 = (bf16[2,384,384]{2,1,0:T(8,128)(2,1)S(1)}, bf16[2,384,384]{2,1,0:T(8,128)(2,1)S(1)}, u32[]{:S(2)}, u32[]{:S(2)}) collective-permute-start(bf16[2,384,384]{2,1,0:T(8,128)(2,1)S(1)} %get-tuple-element.43), channel_id=1, source_target_pairs={{0,4},{1,5},{2,6},{3,7},{4,0},{5,1},{6,2},{7,3},{8,12},{9,13},{10,... | collective-permute-start | bytes 1769480 | tf_op jit(solution)/shard_map/ppermute | solution.py:373
  77.6 13.3 %collective-permute-start.14 = (bf16[2,384,384]{2,1,0:T(8,128)(2,1)S(1)}, bf16[2,384,384]{2,1,0:T(8,128)(2,1)S(1)}, u32[]{:S(2)}, u32[]{:S(2)}) collective-permute-start(bf16[2,384,384]{2,1,0:T(8,128)(2,1)S(1)} %get-tuple-element.44), channel_id=1, source_target_pairs={{0,1},{1,0},{2,3},{3,2},{4,8},{5,9},{6,10},{7,11},{8,4},{9,5},{10,... | collective-permute-start | bytes 1769480 | tf_op jit(solution)/shard_map/ppermute | solution.py:373
  77.6 34.2 %collective-permute-start.6 = (bf16[2,384,640]{2,1,0:T(8,128)(2,1)S(1)}, bf16[2,384,640]{2,1,0:T(8,128)(2,1)S(1)}, u32[]{:S(2)}, u32[]{:S(2)}) collective-permute-start(bf16[2,384,640]{2,1,0:T(8,128)(2,1)S(1)} %get-tuple-element.33), channel_id=1, source_target_pairs={{0,4},{1,5},{2,6},{3,7},{4,0},{5,1},{6,2},{7,3},{8,12},{9,13},{10,... | collective-permute-start | bytes 2949128 | tf_op jit(solution)/shard_map/ppermute | solution.py:373
  81.1 30.6 %collective-permute-start.7 = (bf16[2,384,640]{2,1,0:T(8,128)(2,1)S(1)}, bf16[2,384,640]{2,1,0:T(8,128)(2,1)S(1)}, u32[]{:S(2)}, u32[]{:S(2)}) collective-permute-start(bf16[2,384,640]{2,1,0:T(8,128)(2,1)S(1)} %get-tuple-element.34), channel_id=1, source_target_pairs={{0,1},{1,0},{2,3},{3,2},{4,8},{5,9},{6,10},{7,11},{8,4},{9,5},{10,... | collective-permute-start | bytes 2949128 | tf_op jit(solution)/shard_map/ppermute | solution.py:373
  82.7 32.6 %collective-permute-start.12 = (bf16[2,384,512]{2,1,0:T(8,128)(2,1)S(1)}, bf16[2,384,512]{2,1,0:T(8,128)(2,1)S(1)}, u32[]{:S(2)}, u32[]{:S(2)}) collective-permute-start(bf16[2,384,512]{2,1,0:T(8,128)(2,1)S(1)} %shard_map.84), channel_id=1, source_target_pairs={{0,16},{16,0},{1,17},{17,1},{2,18},{18,2},{3,19},{19,3},{4,20},{20... | collective-permute-start | bytes 2359304 | tf_op jit(solution)/shard_map/ppermute | solution.py:382
  91.9 23.5 %collective-permute-start.15 = (bf16[2,384,384]{2,1,0:T(8,128)(2,1)S(1)}, bf16[2,384,384]{2,1,0:T(8,128)(2,1)S(1)}, u32[]{:S(2)}, u32[]{:S(2)}) collective-permute-start(bf16[2,384,384]{2,1,0:T(8,128)(2,1)S(1)} %shard_map.85), channel_id=1, source_target_pairs={{0,16},{16,0},{1,17},{17,1},{2,18},{18,2},{3,19},{19,3},{4,20},{20... | collective-permute-start | bytes 1769480 | tf_op jit(solution)/shard_map/ppermute | solution.py:382
  93.4 1.1 collective-permute-start.16
  94.6 3.6 %collective-permute-start.17 = (f32[2,128]{1,0:T(2,128)S(1)}, f32[2,128]{1,0:T(2,128)S(1)}, u32[]{:S(2)}, u32[]{:S(2)}) collective-permute-start(f32[2,128]{1,0:T(2,128)S(1)} %add.20), channel_id=1, source_target_pairs={{0,2},{1,3},{2,0},{3,1},{4,6},{5,7},{6,4},{7,5},{8,10},{9,11},{10,... | collective-permute-start | bytes 3080 | tf_op jit(solution)/shard_map/ppermute | solution.py:389
  98.2 11.4 %collective-permute-start.18 = (f32[2,128]{1,0:T(2,128)S(1)}, f32[2,128]{1,0:T(2,128)S(1)}, u32[]{:S(2)}, u32[]{:S(2)}) collective-permute-start(f32[2,128]{1,0:T(2,128)S(1)} %add.21), channel_id=1, source_target_pairs={{0,4},{4,0},{8,12},{12,8},{1,5},{5,1},{9,13},{13,9},{2,6},{6,2},{1... | collective-permute-start | bytes 3080 | tf_op jit(solution)/shard_map/ppermute | solution.py:389
  109.6 9.1 %collective-permute-start.19 = (f32[2,128]{1,0:T(2,128)S(1)}, f32[2,128]{1,0:T(2,128)S(1)}, u32[]{:S(2)}, u32[]{:S(2)}) collective-permute-start(f32[2,128]{1,0:T(2,128)S(1)} %add.22), channel_id=1, source_target_pairs={{0,8},{4,12},{8,0},{12,4},{1,9},{5,13},{9,1},{13,5},{2,10},{6,14},... | collective-permute-start | bytes 3080 | tf_op jit(solution)/shard_map/ppermute | solution.py:389

commit v6 on v5

--- a/solution.py
+++ b/solution.py
@@ -13,7 +13,7 @@
 EPSILON = 1e-06
 ROOT_SCALE = HEAD_DIM ** (-0.5)
 EXP2_SCALE = ROOT_SCALE * math.log2(math.e)
-GROUPS = ((0, 4, False), (4, 3, False), (7, 5, True))
+GROUPS = ((0, 3, False), (3, 4, False), (7, 5, True))
 MAIN_VMEM = 20 * 1024 * 1024
 SMALL_VMEM = 12 * 1024 * 1024
 PACK_VMEM = 4 * 1024 * 1024
@@ -162,6 +162,119 @@
     gain_out[1:2, :] += key_gain_sum
 
 
+def tile_sums(key_hat, value_in, query_hat, grad_in):
+    weights = jnp.exp2(dot_nt(key_hat, query_hat) * EXP2_SCALE)
+    grad_probs = dot_nt(value_in, grad_in)
+    return weights, grad_probs
+
+
+def wide_lives(told, rows):
+    return [jnp.concatenate([told[row : row + 1]] * (rows // HEAD_DIM), axis=1) for row in (2, 3)]
+
+
+def near_is_even():
+    place = lax.rem(lax.axis_index("seq"), 4)
+    return (place == 0) | (place == 3)
+
+
+def sums_kernel(info, query, grad, key, value, pair_even, pair_odd, *rest, far_count):
+    outs = rest[-2 - far_count :]
+    told = info[...]
+    _, _, _, key_hat = normalize(key[...], told[1:2])
+    value_in = value[...]
+    rows = []
+    for query_in, grad_in in (
+        (query[...], grad[...]), (pair_even[0], pair_even[1]), (pair_odd[0], pair_odd[1])
+    ):
+        _, _, _, query_hat = normalize(query_in, told[0:1])
+        weights, grad_probs = tile_sums(key_hat, value_in, query_hat, grad_in)
+        rows.append(
+            [
+                jnp.sum(weights, axis=0, keepdims=True),
+                jnp.sum(weights * grad_probs, axis=0, keepdims=True),
+            ]
+        )
+    own, even, odd = rows
+    tail = wide_lives(told, query.shape[0])
+    blank = jnp.zeros_like(tail[0])
+    outs[0][...] = jnp.concatenate([*own, *even, *tail, blank, blank], axis=0)
+    outs[1][...] = jnp.concatenate([*own, *odd, *tail, blank, blank], axis=0)
+    near = near_is_even()
+    for index, out in enumerate(outs[2:]):
+        first, second = (even, odd) if index == 0 else (odd, even)
+        chosen = [jnp.where(near, one, two) for one, two in zip(first, second)]
+        out[...] = jnp.concatenate([*chosen, *[blank] * 6], axis=0)
+
+
+def grads_kernel(
+    info, query, grad, key, value, pair_even, pair_odd,
+    sent_even, sent_odd, from_even, from_odd, *rest, far_count,
+):
+    fars = [far[0:2, :] for far in rest[:far_count]]
+    pair_out, own_out, even_out, odd_out, gain_out = rest[-5:]
+    told = info[...]
+    near = near_is_even()
+    if far_count == 2:
+        far_even = jnp.where(near, fars[0], fars[1])
+        far_odd = jnp.where(near, fars[1], fars[0])
+    elif far_count == 1:
+        far_even = jnp.where(near, fars[0], jnp.zeros_like(fars[0]))
+        far_odd = jnp.where(near, jnp.zeros_like(fars[0]), fars[0])
+    else:
+        far_even = far_odd = jnp.zeros_like(from_even[0:2, :])
+    own_sums = (
+        sent_even[0:2, :]
+        + sent_even[4:5, :] * from_even[2:4, :]
+        + sent_even[5:6, :] * from_odd[2:4, :]
+    )
+    even_sums = (
+        from_even[0:2, :] + from_even[4:5, :] * sent_even[2:4, :] + from_even[5:6, :] * far_even
+    )
+    odd_sums = (
+        from_odd[0:2, :] + from_odd[5:6, :] * sent_odd[2:4, :] + from_odd[4:5, :] * far_odd
+    )
+    key_floats, key_scale, key_normed, key_hat = normalize(key[...], told[1:2])
+    value_in = value[...]
+    key_grad = value_grad = query_gain_sum = None
+    for query_in, grad_in, sums, live, out in (
+        (query[...], grad[...], own_sums, None, own_out),
+        (pair_even[0], pair_even[1], even_sums, from_even[4:5, :], even_out),
+        (pair_odd[0], pair_odd[1], odd_sums, from_odd[5:6, :], odd_out),
+    ):
+        _, _, query_normed, query_hat = normalize(query_in, told[0:1])
+        weights, grad_probs = tile_sums(key_hat, value_in, query_hat, grad_in)
+        inverse = 1.0 / sums[0:1]
+        deltas = sums[1:2] * inverse
+        probs = weights * (inverse if live is None else inverse * live)
+        dscores = (probs * (grad_probs - deltas)).astype(jnp.bfloat16)
+        key_part = dot_nn(dscores, query_hat)
+        value_part = dot_nn(probs.astype(jnp.bfloat16), grad_in)
+        query_part = dot_tn(key_hat, dscores).T * ROOT_SCALE
+        out[...] = query_part.astype(out.dtype)
+        gain_part = jnp.sum(query_part * query_normed, axis=0, keepdims=True)
+        key_grad = key_part if key_grad is None else key_grad + key_part
+        value_grad = value_part if value_grad is None else value_grad + value_part
+        query_gain_sum = gain_part if query_gain_sum is None else query_gain_sum + gain_part
+    key_grad = key_grad * ROOT_SCALE
+    key_back = norm_back(key_grad, key_floats, key_scale, told[1:2])
+    pair_out[0] = key_back.astype(pair_out.dtype)
+    pair_out[1] = value_grad.astype(pair_out.dtype)
+
+    @pl.when(pl.program_id(0) == 0)
+    def _():
+        gain_out[...] = jnp.zeros_like(gain_out)
+
+    gain_out[0:1, :] += query_gain_sum
+    gain_out[1:2, :] += jnp.sum(key_grad * key_normed, axis=0, keepdims=True)
+
+
+def answer_kernel(info, query, own, from_even, from_odd, out):
+    gain = info[0:1, :]
+    floats, scaled, _, _ = normalize(query[...], gain)
+    total = own[...] + from_even[...].astype(jnp.float32) + from_odd[...].astype(jnp.float32)
+    out[...] = norm_back(total, floats, scaled, gain).astype(out.dtype)
+
+
 def finished(info, key, own, from_even, from_odd):
     told = told_info(info) if len(info.shape) == 3 else info[...]
     key_gain = told[1:2]
@@ -169,12 +282,6 @@
     key_grad = own[0] + from_even[0].astype(jnp.float32) + from_odd[0].astype(jnp.float32)
     value_grad = own[1] + from_even[1].astype(jnp.float32) + from_odd[1].astype(jnp.float32)
     return norm_back(key_grad, key_floats, key_scale, key_gain), value_grad
-
-
-def finish_kernel(info, key, own, from_even, from_odd, out):
-    key_grad, value_grad = finished(info, key, own, from_even, from_odd)
-    out[0] = key_grad.astype(out.dtype)
-    out[1] = value_grad.astype(out.dtype)
 
 
 def last_kernel(info, key, own, from_even, from_odd, *rest, places, first, count):
@@ -291,47 +398,89 @@
     return pl.BlockSpec((2, 16, HEAD_DIM), lambda head: (0, below, 0))
 
 
-def main_call(
-    info, operands, pair_even, pair_odd, pair_first, count, query_grads, query_heads, query_first
-):
+def main_call(info, operands, pair_even, pair_odd, count):
     rows = pair_even.shape[1]
     lanes = count * HEAD_DIM
-    earlier = [] if query_grads is None else [query_grads]
     return pl.pallas_call(
         main_kernel,
         grid=(count,),
         in_specs=[info_block(info)]
         + [head_block(rows, first, slot) for _, first, slot in operands]
-        + [pair_block(rows, pair_first)] * 2
-        + [pl.BlockSpec(memory_space=pl.ANY)] * len(earlier),
-        out_specs=[head_block(rows, query_first)]
-        + [pair_block(rows)] * 3
-        + [whole_block((8, HEAD_DIM))],
+        + [pair_block(rows)] * 2,
+        out_specs=[head_block(rows, 0)] + [pair_block(rows)] * 3 + [whole_block((8, HEAD_DIM))],
         out_shape=[
-            jax.ShapeDtypeStruct((rows, query_heads * HEAD_DIM), jnp.bfloat16),
+            jax.ShapeDtypeStruct((rows, lanes), jnp.bfloat16),
             jax.ShapeDtypeStruct((2, rows, lanes), jnp.float32),
             jax.ShapeDtypeStruct((2, rows, lanes), jnp.bfloat16),
             jax.ShapeDtypeStruct((2, rows, lanes), jnp.bfloat16),
             jax.ShapeDtypeStruct((8, HEAD_DIM), jnp.float32),
         ],
-        input_output_aliases={7: 0} if earlier else {},
         compiler_params=pltpu.CompilerParams(vmem_limit_bytes=MAIN_VMEM),
         cost_estimate=MAIN_COST,
-    )(info, *[array for array, _, _ in operands], pair_even, pair_odd, *earlier)
-
-
-def finish_call(info, key, own, from_even, from_odd, count):
-    array, first, slot = key
-    rows = own.shape[1]
-    return pl.pallas_call(
-        finish_kernel,
+    )(info, *[array for array, _, _ in operands], pair_even, pair_odd)
+
+
+def row_block(rows, first):
+    return pl.BlockSpec((8, rows), lambda head: (first + head, 0))
+
+
+def sums_call(info, arrays, pair_even, pair_odd, first, count, heads, earlier, far_count):
+    rows = pair_even.shape[1]
+    amount = 2 + far_count
+    earlier = [] if earlier is None else earlier
+    return pl.pallas_call(
+        functools.partial(sums_kernel, far_count=far_count),
         grid=(count,),
-        in_specs=[info_block(info), head_block(rows, first, slot)] + [pair_block(rows)] * 3,
-        out_specs=pair_block(rows),
-        out_shape=jax.ShapeDtypeStruct((2, rows, count * HEAD_DIM), jnp.bfloat16),
+        in_specs=[info_block(info)]
+        + [head_block(rows, first)] * 4
+        + [pair_block(rows)] * 2
+        + [pl.BlockSpec(memory_space=pl.ANY)] * len(earlier),
+        out_specs=[row_block(rows, first)] * amount,
+        out_shape=[jax.ShapeDtypeStruct((8 * heads, rows), jnp.float32)] * amount,
+        input_output_aliases={7 + index: index for index in range(len(earlier))},
+        compiler_params=pltpu.CompilerParams(vmem_limit_bytes=MAIN_VMEM),
+        cost_estimate=MAIN_COST,
+    )(info, *arrays, pair_even, pair_odd, *earlier)
+
+
+def grads_call(info, arrays, pair_even, pair_odd, sums, first, count, heads, earlier, far_count):
+    rows = pair_even.shape[1]
+    lanes = heads * HEAD_DIM
+    earlier = [] if earlier is None else earlier
+    place = 7 + len(sums)
+    return pl.pallas_call(
+        functools.partial(grads_kernel, far_count=far_count),
+        grid=(count,),
+        in_specs=[info_block(info)]
+        + [head_block(rows, first)] * 4
+        + [pair_block(rows)] * 2
+        + [row_block(rows, first)] * len(sums)
+        + [pl.BlockSpec(memory_space=pl.ANY)] * len(earlier),
+        out_specs=[pair_block(rows)] + [head_block(rows, first)] * 3 + [whole_block((8, HEAD_DIM))],
+        out_shape=[
+            jax.ShapeDtypeStruct((2, rows, count * HEAD_DIM), jnp.bfloat16),
+            jax.ShapeDtypeStruct((rows, lanes), jnp.float32),
+            jax.ShapeDtypeStruct((rows, lanes), jnp.bfloat16),
+            jax.ShapeDtypeStruct((rows, lanes), jnp.bfloat16),
+            jax.ShapeDtypeStruct((8, HEAD_DIM), jnp.float32),
+        ],
+        input_output_aliases={place + index: 1 + index for index in range(len(earlier))},
+        compiler_params=pltpu.CompilerParams(vmem_limit_bytes=MAIN_VMEM),
+        cost_estimate=MAIN_COST,
+    )(info, *arrays, pair_even, pair_odd, *sums, *earlier)
+
+
+def answer_call(info, query, own, from_even, from_odd, first, count):
+    rows = own.shape[0]
+    return pl.pallas_call(
+        answer_kernel,
+        grid=(count,),
+        in_specs=[info_block(info), head_block(rows, first)] + [head_block(rows, 0)] * 3,
+        out_specs=head_block(rows, 0),
+        out_shape=jax.ShapeDtypeStruct((rows, count * HEAD_DIM), jnp.bfloat16),
         compiler_params=pltpu.CompilerParams(vmem_limit_bytes=SMALL_VMEM),
         cost_estimate=LONG_COST,
-    )(info, array, own, from_even, from_odd)
+    )(info, query, own, from_even, from_odd)
 
 
 def last_call(info, key, own, from_even, from_odd, pieces, places, first, count):
@@ -362,15 +511,29 @@
     return other if 0 <= other < count else tile
 
 
-def exchanged(value, parity):
-    count, width = lax.axis_size("seq"), lax.axis_size("dp")
+def far_partner(tile, base, count):
+    other = ((tile - base) ^ 2) + base if tile >= base else tile
+    return other if 0 <= other < count else tile
+
+
+def paired(value, partners):
+    width = lax.axis_size("dp")
     pairs = []
-    for tile in range(count):
-        other = partner(tile, parity, count)
+    for tile, other in enumerate(partners):
         for sample in range(width):
             moved = sample ^ 1 if other == tile and width % 2 == 0 else sample
             pairs.append((tile * width + sample, other * width + moved))
     return lax.ppermute(value, ("seq", "dp"), pairs)
+
+
+def exchanged(value, parity):
+    count = lax.axis_size("seq")
+    return paired(value, [partner(tile, parity, count) for tile in range(count)])
+
+
+def far_partners(count):
+    both = [[far_partner(tile, base, count) for tile in range(count)] for base in (0, 2)]
+    return [partners for partners in both if partners != list(range(count))]
 
 
 def after(value, *others):
@@ -396,51 +559,58 @@
     query, key, value, grad = (a[0, 0, 0] for a in (queries, keys, values, grad_out))
     rows = query.shape[0]
     seq_count = lax.axis_size("seq")
-    home_heads = sum(count for _, count, away in GROUPS if not away)
-    home_pair = pack_call(key, value, 0, home_heads)
-    away_pair = pack_call(after(key, home_pair), value, home_heads, HEADS - home_heads)
-    home_gathered = (exchanged(home_pair, 0), exchanged(home_pair, 1))
-    info = info_call(kv_tiles[0, 0, 0], after(norm_gains[0], away_pair))
+    *home, (away_first, away_count, _) = GROUPS
+    home_heads = sum(count for _, count, _ in home)
+    fars = far_partners(seq_count)
+    asks = [pack_call(query, grad, *home[0][:2])]
+    away_pair = pack_call(after(key, asks[0]), value, away_first, away_count)
+    for first, count, _ in home[1:]:
+        asks.append(pack_call(after(query, away_pair), grad, first, count))
+    asked_home = [(exchanged(ask, 0), exchanged(ask, 1)) for ask in asks]
+    info = info_call(kv_tiles[0, 0, 0], after(norm_gains[0], asks[-1]))
     away_pair = turned(away_pair, -1)
-    asked = ask_call(info, after(query, away_pair), grad, home_heads, HEADS - home_heads)
+    arrays = (query, grad, key, value)
+    asked = ask_call(info, after(query, away_pair), grad, away_first, away_count)
+    sums = None
+    for (first, count, _), ask in zip(home, asked_home):
+        told = info if sums is None else after(info, asked)
+        sums = sums_call(told, arrays, *ask, first, count, home_heads, sums, len(fars))
     asked = turned(asked, -1)
+    received = [exchanged(sums[0], 0), exchanged(sums[1], 1)]
+    received += [paired(value, partners) for value, partners in zip(sums[2:], fars)]
+    all_sums = (*sums[:2], *received)
+    away_pair = after(away_pair, *received)
     away_gathered = (exchanged(away_pair, 0), exchanged(away_pair, 1))
-    sources, parts, sums = [], [], []
-    query_grads = None
-    for first, count, away in GROUPS:
-        if away:
-            asked = after(asked, query_grads)
-            operands = [(asked, 0, 0), (asked, 0, 1), (away_pair, 0, 0), (away_pair, 0, 1)]
-            sources.append((asked, operands))
-            query_low, own, to_even, to_odd, gain = main_call(
-                *sources[-1], *away_gathered, 0, count, None, count, 0
-            )
-            sums.append(turned(gain[:2], 1))
-        else:
-            group_info = after(info, asked) if first else info
-            sources.append((group_info, [(a, first, None) for a in (query, grad, key, value)]))
-            query_grads, own, to_even, to_odd, gain = main_call(
-                *sources[-1], *home_gathered, first, count, query_grads, home_heads, first
-            )
-            sums.append(gain[:2])
-        parts.append((own, exchanged(to_even, 0), exchanged(to_odd, 1)))
-    query_grads = turned(query_grads, -1)
-    pieces = [query_grads, query_low]
-    places = [(0, 0), (0, home_heads * HEAD_DIM)]
-    for index, ((first, count, away), (group_info, operands), part) in enumerate(
-        zip(GROUPS, sources, parts)
-    ):
-        own, from_even, from_odd = part
-        if away:
-            out = last_call(
-                group_info, operands[2], own, from_even, from_odd, pieces, tuple(places), first, count
-            )
-        else:
-            own = after(own, query_grads, *(sums[-1:] if index == 0 else ()))
-            pair_low = finish_call(group_info, operands[2], own, from_even, from_odd, count)
-            pieces.append(turned(pair_low, -1))
-            places.append((slice(1, 3), first * HEAD_DIM))
-    summed = total_over(total_over(sum(sums), "dp"), "seq", out)
+    gains, pieces, places = [], [], []
+    parts = None
+    for (first, count, _), ask in zip(home, asked_home):
+        told = after(info, asked) if gains else info
+        pair_low, *parts, gain = grads_call(
+            told, arrays, *ask, all_sums, first, count, home_heads, parts, len(fars)
+        )
+        if gains:
+            pair_low = after(pair_low, *away_gathered)
+        gains.append(gain[:2])
+        pieces.append(turned(pair_low, -1))
+        places.append((slice(1, 3), first * HEAD_DIM))
+    to_even, to_odd = (after(part, *away_gathered) for part in parts[1:])
+    answer = (after(parts[0], pieces[0]), exchanged(to_even, 0), exchanged(to_odd, 1))
+    asked = after(asked, pair_low)
+    operands = [(asked, 0, 0), (asked, 0, 1), (away_pair, 0, 0), (away_pair, 0, 1)]
+    query_low, own, to_even, to_odd, gain = main_call(
+        asked, operands, *away_gathered, away_count
+    )
+    gains.append(turned(after(gain[:2], pieces[len(home) - 1]), 1))
+    returned = (exchanged(to_even, 0), exchanged(to_odd, 1))
+    pieces.append(query_low)
+    places.append((0, away_first * HEAD_DIM))
+    answer = answer_call(info, query, *answer, 0, home_heads)
+    pieces.append(turned(answer, -1))
+    places.append((0, 0))
+    out = last_call(
+        asked, operands[2], own, *returned, pieces, tuple(places), away_first, away_count
+    )
+    summed = total_over(total_over(sum(gains), "dp"), "seq", out)
     tokens = lax.axis_size("dp") * seq_count * rows * HEADS
     return (out[None, :, None, None], (summed / math.sqrt(tokens))[None])
 

time: 119 us -> 124 us (1.042)
  Pallas kernels: 34.2 us -> 38.3 us
  local copies, waits for them, and re-layouts: 2.57 us -> 4.05 us
    pallas_call x2 -> x5, Pallas kernels: 2.66 us -> 22.7 us  [the longest x2 14.3 us: grads_call(): pl.pallas_call(functools.partial(grads_kernel, far_count=far_count), grid...]
    pallas_call x3 -> x1, Pallas kernels: 27.3 us -> 11.3 us  [main_call(): pl.pallas_call(main_kernel, grid=(count,), in_specs=[info_block(info)] +...]
    ppermute x10 -> x13, waiting for transfers between devices: 10.9 us -> 21.4 us  [paired(): return lax.ppermute(value, ('seq', 'dp'), pairs)]
    ppermute x6, waiting for transfers between devices: 30.8 us -> 23.2 us  [turned(): lax.ppermute(value, 'pipe', [(i, (i + step) % count) for i in range(count)])]
    ppermute x4, waiting for transfers between devices: 10.7 us -> 6.65 us  [total_over(): other = lax.ppermute(value, axis, [(i, i ^ step) for i in range(count)])]
    ppermute x4, starting transfers between devices: 7.57 us -> 3.76 us  [total_over(): other = lax.ppermute(value, axis, [(i, i ^ step) for i in range(count)])]
    ppermute x10 -> x13, starting transfers between devices: 13.4 us -> 16.6 us  [paired(): return lax.ppermute(value, ('seq', 'dp'), pairs)]
    unnamed x16, local copies, waits for them, and re-layouts: 2.56 us -> 4.05 us
  transfers between devices with their start and end apart: 20 -> 23, of which waited for: 9 -> 10; matrix products, arithmetic and copies ran while one was open for 0% -> 0% of each run, Pallas kernels for 29% -> 31%
where the time goes in v6:
time: 124 us
  waiting for transfers between devices  51.3 us (41%)
  Pallas kernels  38.3 us (31%)
  starting transfers between devices  28.5 us (23%)
  local copies, waits for them, and re-layouts  4.05 us (3%)
    ppermute x6, waiting for transfers between devices, turned(): lax.ppermute(value, 'pipe', [(i, (i + step) % count) for i in range(count)])  23.2 us
    ppermute x13, waiting for transfers between devices, paired(): return lax.ppermute(value, ('seq', 'dp'), pairs)  21.4 us
    ppermute x13, starting transfers between devices, paired(): return lax.ppermute(value, ('seq', 'dp'), pairs)  16.6 us
    pallas_call x2, Pallas kernels, grads_call(): pl.pallas_call(functools.partial(grads_kernel, far_count=far_count), grid...  14.3 us
    pallas_call x1, Pallas kernels, main_call(): pl.pallas_call(main_kernel, grid=(count,), in_specs=[info_block(info)] +...  11.3 us
    ppermute x6, starting transfers between devices, turned(): lax.ppermute(value, 'pipe', [(i, (i + step) % count) for i in range(count)])  8.14 us
    ppermute x4, waiting for transfers between devices, total_over(): other = lax.ppermute(value, axis, [(i, i ^ step) for i in range(count)])  6.65 us
    pallas_call x2, Pallas kernels, sums_call(): pl.pallas_call(functools.partial(sums_kernel, far_count=far_count), grid=...  6.45 us
  transfers between devices with their start and end apart: 23, of which 10 were waited for; matrix products, arithmetic and copies ran while one was open for 0% of the time, Pallas kernels for 31%

profile of v6, /device:TPU:0, one launch (start us, length us, event | category | flops | bytes accessed | tf_op | source)
XLA Modules:
  0.0 123.5 jit_solution(18009704863260085518)
XLA Ops:
  0.6 1.3 %copy-done = bf16[1,1,1,384,1536]{4,3,2,1,0:T(8,128)(2,1)S(1)} copy-done((bf16[1,1,1,384,1536]{4,3,2,1,0:T(8,128)(2,1)S(1)}, bf16[1,1,1,384,1536]{4,3,2,1,0:T(8,128)(2,1)}, u32[]{:S(2)}) %copy-start) | copy-done | bytes 1179672
  1.9 1.3 %copy-done.2 = bf16[1,1,1,384,1536]{4,3,2,1,0:T(8,128)(2,1)S(1)} copy-done((bf16[1,1,1,384,1536]{4,3,2,1,0:T(8,128)(2,1)S(1)}, bf16[1,1,1,384,1536]{4,3,2,1,0:T(8,128)(2,1)}, u32[]{:S(2)}) %copy-start.2) | copy-done | bytes 1179672
  3.8 4.1 %collective-permute-start.4 = (bf16[2,384,384]{2,1,0:T(8,128)(2,1)S(1)}, bf16[2,384,384]{2,1,0:T(8,128)(2,1)S(1)}, u32[]{:S(2)}, u32[]{:S(2)}) collective-permute-start(bf16[2,384,384]{2,1,0:T(8,128)(2,1)S(1)} %shard_map.77), channel_id=1, source_target_pairs={{0,4},{1,5},{2,6},{3,7},{4,0},{5,1},{6,2},{7,3},{8,12},{9,13},{10,... | collective-permute-start | bytes 1769480 | tf_op jit(solution)/shard_map/ppermute | solution.py:526
  8.1 1.1 copy-done.1
  9.7 1.6 %collective-permute-start.2 = (bf16[2,384,512]{2,1,0:T(8,128)(2,1)S(1)}, bf16[2,384,512]{2,1,0:T(8,128)(2,1)S(1)}, u32[]{:S(2)}, u32[]{:S(2)}) collective-permute-start(bf16[2,384,512]{2,1,0:T(8,128)(2,1)S(1)} %shard_map.79), channel_id=1, source_target_pairs={{0,4},{1,5},{2,6},{3,7},{4,0},{5,1},{6,2},{7,3},{8,12},{9,13},{10,... | collective-permute-start | bytes 2359304 | tf_op jit(solution)/shard_map/ppermute | solution.py:526
  11.4 1.5 %collective-permute-start = (bf16[2,384,640]{2,1,0:T(8,128)(2,1)S(1)}, bf16[2,384,640]{2,1,0:T(8,128)(2,1)S(1)}, u32[]{:S(2)}, u32[]{:S(2)}) collective-permute-start(bf16[2,384,640]{2,1,0:T(8,128)(2,1)S(1)} %shard_map.78), channel_id=1, source_target_pairs={{0,16},{16,0},{1,17},{17,1},{2,18},{18,2},{3,19},{19,3},{4,20},{20... | collective-permute-start | bytes 2949128 | tf_op jit(solution)/shard_map/ppermute | solution.py:545
  13.5 8.7 %collective-permute-done.4.pair_even = bf16[2,384,384]{2,1,0:T(8,128)(2,1)S(1)} collective-permute-done((bf16[2,384,384]{2,1,0:T(8,128)(2,1)S(1)}, bf16[2,384,384]{2,1,0:T(8,128)(2,1)S(1)}, u32[]{:S(2)}, u32[]{:S(2)}) %collective-permute-start.4) | collective-permute-done | bytes 589856 | tf_op jit(solution)/shard_map/ppermute | solution.py:526
  22.1 2.8 %shard_map.82 = (f32[56,384]{1,0:T(8,128)S(1)}, f32[56,384]{1,0:T(8,128)S(1)}, f32[56,384]{1,0:T(8,128)S(1)}) custom-call(f32[8,128]{1,0:T(8,128)S(1)} %shard_map.80.info, bf16[384,1536]{1,0:T(8,128)(2,1)S(1)} %bitcast.20, bf16[384,1536]{1,0:T(8,128)(2,1)S(1)} %bitcast.13, bf16[384,1536]{1,0:T(8,128)(2,1)S(1)} %bitcast.27, bf16[384,1536]{1,0:T(8,128)(2,1)S(1)} %bitcast.32, ...), custom_call_target="tpu_custom_call" | custom-call | flops 6000000000 | bytes 1 | tf_op jit(solution)/shard_map/pallas_call | solution.py:431
  24.9 9.7 %collective-permute-done.key.value = bf16[2,384,640]{2,1,0:T(8,128)(2,1)S(1)} collective-permute-done((bf16[2,384,640]{2,1,0:T(8,128)(2,1)S(1)}, bf16[2,384,640]{2,1,0:T(8,128)(2,1)S(1)}, u32[]{:S(2)}, u32[]{:S(2)}) %collective-permute-start) | collective-permute-done | bytes 983072 | tf_op jit(solution)/shard_map/ppermute | solution.py:545
  34.8 1.6 %collective-permute-start.1 = (bf16[2,400,640]{2,1,0:T(8,128)(2,1)S(1)}, bf16[2,400,640]{2,1,0:T(8,128)(2,1)S(1)}, u32[]{:S(2)}, u32[]{:S(2)}) collective-permute-start(bf16[2,400,640]{2,1,0:T(8,128)(2,1)S(1)} %shard_map.81), channel_id=1, source_target_pairs={{0,16},{16,0},{1,17},{17,1},{2,18},{18,2},{3,19},{19,3},{4,20},{20... | collective-permute-start | bytes 3072008 | tf_op jit(solution)/shard_map/ppermute | solution.py:545
  36.3 1.5 %collective-permute-done.2.pair_even = bf16[2,384,512]{2,1,0:T(8,128)(2,1)S(1)} collective-permute-done((bf16[2,384,512]{2,1,0:T(8,128)(2,1)S(1)}, bf16[2,384,512]{2,1,0:T(8,128)(2,1)S(1)}, u32[]{:S(2)}, u32[]{:S(2)}) %collective-permute-start.2) | collective-permute-done | bytes 786464 | tf_op jit(solution)/shard_map/ppermute | solution.py:526
  37.8 3.7 %shard_map.83 = (f32[56,384]{1,0:T(8,128)S(1)}, f32[56,384]{1,0:T(8,128)S(1)}, f32[56,384]{1,0:T(8,128)S(1)}) custom-call(f32[8,128]{1,0:T(8,128)S(1)} %shard_map.80.info, bf16[384,1536]{1,0:T(8,128)(2,1)S(1)} %bitcast.22, bf16[384,1536]{1,0:T(8,128)(2,1)S(1)} %bitcast.15, ...), custom_call_target="tpu_custom_call", output_to_operand_aliasing={{0}: (7, {}), {1}: (8, {}), {2}: (9, {})} | custom-call | flops 6000000000 | bytes 1 | tf_op jit(solution)/shard_map/pallas_call | solution.py:431
  41.5 2.0 %collective-permute-start.8 = (f32[56,384]{1,0:T(8,128)S(1)}, f32[56,384]{1,0:T(8,128)S(1)}, u32[]{:S(2)}, u32[]{:S(2)}) collective-permute-start(f32[56,384]{1,0:T(8,128)S(1)} %get-tuple-element.48), channel_id=1, source_target_pairs={{0,8},{1,9},{2,10},{3,11},{4,12},{5,13},{6,14},{7,15},{8,0},{9,1},... | collective-permute-start | bytes 258056 | tf_op jit(solution)/shard_map/ppermute | solution.py:526
  43.6 1.8 %collective-permute-start.6 = (f32[56,384]{1,0:T(8,128)S(1)}, f32[56,384]{1,0:T(8,128)S(1)}, u32[]{:S(2)}, u32[]{:S(2)}) collective-permute-start(f32[56,384]{1,0:T(8,128)S(1)} %get-tuple-element.46.sent_even), channel_id=1, source_target_pairs={{0,4},{1,5},{2,6},{3,7},{4,0},{5,1},{6,2},{7,3},{8,12},{9,13},{10,... | collective-permute-start | bytes 258056 | tf_op jit(solution)/shard_map/ppermute | solution.py:526
  45.3 3.1 %collective-permute-done.8.rest_0_ = f32[56,384]{1,0:T(8,128)S(1)} collective-permute-done((f32[56,384]{1,0:T(8,128)S(1)}, f32[56,384]{1,0:T(8,128)S(1)}, u32[]{:S(2)}, u32[]{:S(2)}) %collective-permute-start.8) | collective-permute-done | bytes 86048 | tf_op jit(solution)/shard_map/ppermute | solution.py:526
  48.5 3.7 %collective-permute-start.9 = (bf16[2,384,640]{2,1,0:T(8,128)(2,1)S(1)}, bf16[2,384,640]{2,1,0:T(8,128)(2,1)S(1)}, u32[]{:S(2)}, u32[]{:S(2)}) collective-permute-start(bf16[2,384,640]{2,1,0:T(8,128)(2,1)S(1)} %collective-permute-done.key.value), channel_id=1, source_target_pairs={{0,4},{1,5},{2,6},{3,7},{4,0},{5,1},{6,2},{7,3},{8,12},{9,13},{10,... | collective-permute-start | bytes 2949128 | tf_op jit(solution)/shard_map/ppermute | solution.py:526
  52.2 6.1 %shard_map.84 = (bf16[2,384,384]{2,1,0:T(8,128)(2,1)S(1)}, f32[384,896]{1,0:T(8,128)S(1)}, bf16[384,896]{1,0:T(8,128)(2,1)S(1)}, bf16[384,896]{1,0:T(8,128)(2,1)S(1)}, f32[8,128]{1,0:T(8,128)S(1)}) custom-call(f32[8,128]{1,0:T(8,128)S(1)} %shard_map.80.info, bf16[384,1536]{1,0:T(8,128)(2,1)S(1)} %bitcast.23, bf16[384,1536]{1,0:T(8,128)(2,1)S(1)} %bitcast.16, ...), custom_call_target="tpu_custom_call" | custom-call | flops 6000000000 | bytes 1 | tf_op jit(solution)/shard_map/pallas_call | solution.py:451
  58.3 1.5 %collective-permute-start.13 = (bf16[2,384,384]{2,1,0:T(8,128)(2,1)S(1)}, bf16[2,384,384]{2,1,0:T(8,128)(2,1)S(1)}, u32[]{:S(2)}, u32[]{:S(2)}) collective-permute-start(bf16[2,384,384]{2,1,0:T(8,128)(2,1)S(1)} %get-tuple-element.59), channel_id=1, source_target_pairs={{0,16},{16,0},{1,17},{17,1},{2,18},{18,2},{3,19},{19,3},{4,20},{20... | collective-permute-start | bytes 1769480 | tf_op jit(solution)/shard_map/ppermute | solution.py:545
  59.9 8.2 %shard_map.85 = (bf16[2,384,512]{2,1,0:T(8,128)(2,1)S(1)}, f32[384,896]{1,0:T(8,128)S(1)}, bf16[384,896]{1,0:T(8,128)(2,1)S(1)}, bf16[384,896]{1,0:T(8,128)(2,1)S(1)}, f32[8,128]{1,0:T(8,128)S(1)}) custom-call(f32[8,128]{1,0:T(8,128)S(1)} %shard_map.80.info, ...), custom_call_target="tpu_custom_call", output_to_operand_aliasing={{1}: (12, {}), {2}: (13, {}), {3}: (14, {})} | custom-call | flops 6000000000 | bytes 1 | tf_op jit(solution)/shard_map/pallas_call | solution.py:451
  68.1 4.7 %collective-permute-done.9.pair_even = bf16[2,384,640]{2,1,0:T(8,128)(2,1)S(1)} collective-permute-done((bf16[2,384,640]{2,1,0:T(8,128)(2,1)S(1)}, bf16[2,384,640]{2,1,0:T(8,128)(2,1)S(1)}, u32[]{:S(2)}, u32[]{:S(2)}) %collective-permute-start.9) | collective-permute-done | bytes 983072 | tf_op jit(solution)/shard_map/ppermute | solution.py:526
  72.8 2.6 %collective-permute-start.15 = (bf16[384,896]{1,0:T(8,128)(2,1)S(1)}, bf16[384,896]{1,0:T(8,128)(2,1)S(1)}, u32[]{:S(2)}, u32[]{:S(2)}) collective-permute-start(bf16[384,896]{1,0:T(8,128)(2,1)S(1)} %get-tuple-element.64), channel_id=1, source_target_pairs={{0,4},{1,5},{2,6},{3,7},{4,0},{5,1},{6,2},{7,3},{8,12},{9,13},{10,... | collective-permute-start | bytes 2064392 | tf_op jit(solution)/shard_map/ppermute | solution.py:526
  75.4 1.5 %collective-permute-start.14 = (bf16[2,384,512]{2,1,0:T(8,128)(2,1)S(1)}, bf16[2,384,512]{2,1,0:T(8,128)(2,1)S(1)}, u32[]{:S(2)}, u32[]{:S(2)}) collective-permute-start(bf16[2,384,512]{2,1,0:T(8,128)(2,1)S(1)} %get-tuple-element.54), channel_id=1, source_target_pairs={{0,16},{16,0},{1,17},{17,1},{2,18},{18,2},{3,19},{19,3},{4,20},{20... | collective-permute-start | bytes 2359304 | tf_op jit(solution)/shard_map/ppermute | solution.py:545
  76.8 11.3 %shard_map.86 = (bf16[384,640]{1,0:T(8,128)(2,1)S(1)}, f32[2,384,640]{2,1,0:T(8,128)S(1)}, bf16[2,384,640]{2,1,0:T(8,128)(2,1)S(1)}, bf16[2,384,640]{2,1,0:T(8,128)(2,1)S(1)}, f32[8,128]{1,0:T(8,128)S(1)}) custom-call(bf16[2,400,640]{2,1,0:T(8,128)(2,1)S(1)} %collective-permute-done.1.info.query.grad, ...), custom_call_target="tpu_custom_call" | custom-call | flops 6000000000 | bytes 1 | tf_op jit(solution)/shard_map/pallas_call | solution.py:404
  88.3 3.3 %collective-permute-done.15.from_even = bf16[384,896]{1,0:T(8,128)(2,1)S(1)} collective-permute-done((bf16[384,896]{1,0:T(8,128)(2,1)S(1)}, bf16[384,896]{1,0:T(8,128)(2,1)S(1)}, u32[]{:S(2)}, u32[]{:S(2)}) %collective-permute-start.15) | collective-permute-done | bytes 688160 | tf_op jit(solution)/shard_map/ppermute | solution.py:526
  91.7 1.9 %shard_map.87 = bf16[384,896]{1,0:T(8,128)(2,1)S(1)} custom-call(f32[8,128]{1,0:T(8,128)S(1)} %shard_map.80.info, bf16[384,1536]{1,0:T(8,128)(2,1)S(1)} %bitcast.25, f32[384,896]{1,0:T(8,128)S(1)} %get-tuple-element.62.own, bf16[384,896]{1,0:T(8,128)(2,1)S(1)} %collective-permute-done.15.from_even, bf16[384,896]{1,0:T(8,128)(2,1)S(1)} %collective-permute-done.16.from_odd), custom_call_target="tpu_custom_call" | custom-call | flops 20000000000 | bytes 1 | tf_op jit(solution)/shard_map/pallas_call | solution.py:475
  93.6 1.5 %collective-permute-start.17 = (bf16[384,896]{1,0:T(8,128)(2,1)S(1)}, bf16[384,896]{1,0:T(8,128)(2,1)S(1)}, u32[]{:S(2)}, u32[]{:S(2)}) collective-permute-start(bf16[384,896]{1,0:T(8,128)(2,1)S(1)} %shard_map.87), channel_id=1, source_target_pairs={{0,16},{16,0},{1,17},{17,1},{2,18},{18,2},{3,19},{19,3},{4,20},{20... | collective-permute-start | bytes 2064392 | tf_op jit(solution)/shard_map/ppermute | solution.py:545
  95.7 13.5 %collective-permute-done.18 = f32[2,128]{1,0:T(2,128)S(1)} collective-permute-done((f32[2,128]{1,0:T(2,128)S(1)}, f32[2,128]{1,0:T(2,128)S(1)}, u32[]{:S(2)}, u32[]{:S(2)}) %collective-permute-start.18) | collective-permute-done | bytes 1056 | tf_op jit(solution)/shard_map/ppermute | solution.py:545
  110.3 1.5 %collective-permute-start.20 = (f32[2,128]{1,0:T(2,128)S(1)}, f32[2,128]{1,0:T(2,128)S(1)}, u32[]{:S(2)}, u32[]{:S(2)}) collective-permute-start(f32[2,128]{1,0:T(2,128)S(1)} %add.20), channel_id=1, source_target_pairs={{0,2},{1,3},{2,0},{3,1},{4,6},{5,7},{6,4},{7,5},{8,10},{9,11},{10,... | collective-permute-start | bytes 3080 | tf_op jit(solution)/shard_map/ppermute | solution.py:552
  111.8 2.1 %collective-permute-done.20 = f32[2,128]{1,0:T(2,128)S(1)} collective-permute-done((f32[2,128]{1,0:T(2,128)S(1)}, f32[2,128]{1,0:T(2,128)S(1)}, u32[]{:S(2)}, u32[]{:S(2)}) %collective-permute-start.20) | collective-permute-done | bytes 1056 | tf_op jit(solution)/shard_map/ppermute | solution.py:552
  114.0 3.4 %collective-permute-done.21 = f32[2,128]{1,0:T(2,128)S(1)} collective-permute-done((f32[2,128]{1,0:T(2,128)S(1)}, f32[2,128]{1,0:T(2,128)S(1)}, u32[]{:S(2)}, u32[]{:S(2)}) %collective-permute-start.21) | collective-permute-done | bytes 1056 | tf_op jit(solution)/shard_map/ppermute | solution.py:552
  117.5 2.1 %collective-permute-start.22 = (f32[2,128]{1,0:T(2,128)S(1)}, f32[2,128]{1,0:T(2,128)S(1)}, u32[]{:S(2)}, u32[]{:S(2)}) collective-permute-start(f32[2,128]{1,0:T(2,128)S(1)} %add.22), channel_id=1, source_target_pairs={{0,8},{4,12},{8,0},{12,4},{1,9},{5,13},{9,1},{13,5},{2,10},{6,14},... | collective-permute-start | bytes 3080 | tf_op jit(solution)/shard_map/ppermute | solution.py:552
  119.6 3.3 %shard_map.88 = bf16[3,384,1536]{2,1,0:T(8,128)(2,1)} custom-call(bf16[2,400,640]{2,1,0:T(8,128)(2,1)S(1)} %collective-permute-done.1.info.query.grad, bf16[2,384,640]{2,1,0:T(8,128)(2,1)S(1)} %collective-permute-done.key.value, f32[2,384,640]{2,1,0:T(8,128)S(1)} %get-tuple-element.56.own, bf16[2,384,640]{2,1,0:T(8,128)(2,1)S(1)} %collective-permute-done.11.from_even, ...), custom_call_target="tpu_custom_call" | custom-call | flops 1 | bytes 1 | tf_op jit(solution)/shard_map/pallas_call | solution.py:490
  (48 shorter events, 4.5 us)
Async XLA Ops:
  0.6 1.3 %copy-start = (bf16[1,1,1,384,1536]{4,3,2,1,0:T(8,128)(2,1)S(1)}, bf16[1,1,1,384,1536]{4,3,2,1,0:T(8,128)(2,1)}, u32[]{:S(2)}) copy-start(bf16[1,1,1,384,1536]{4,3,2,1,0:T(8,128)(2,1)} %param.9) | copy-start | bytes 3538948
  1.9 1.3 %copy-start.2 = (bf16[1,1,1,384,1536]{4,3,2,1,0:T(8,128)(2,1)S(1)}, bf16[1,1,1,384,1536]{4,3,2,1,0:T(8,128)(2,1)}, u32[]{:S(2)}) copy-start(bf16[1,1,1,384,1536]{4,3,2,1,0:T(8,128)(2,1)} %param.6) | copy-start | bytes 3538948
  3.2 4.8 %copy-start.4 = (bf16[1,1,1,384,1536]{4,3,2,1,0:T(8,128)(2,1)S(1)}, bf16[1,1,1,384,1536]{4,3,2,1,0:T(8,128)(2,1)}, u32[]{:S(2)}) copy-start(bf16[1,1,1,384,1536]{4,3,2,1,0:T(8,128)(2,1)} %param.7) | copy-start | bytes 3538948
  3.2 4.8 %copy-start.5 = (bf16[1,1,1,384,1536]{4,3,2,1,0:T(8,128)(2,1)S(1)}, bf16[1,1,1,384,1536]{4,3,2,1,0:T(8,128)(2,1)}, u32[]{:S(2)}) copy-start(bf16[1,1,1,384,1536]{4,3,2,1,0:T(8,128)(2,1)} %param.8) | copy-start | bytes 3538948
  3.3 10.2 %collective-permute-start.5 = (bf16[2,384,384]{2,1,0:T(8,128)(2,1)S(1)}, bf16[2,384,384]{2,1,0:T(8,128)(2,1)S(1)}, u32[]{:S(2)}, u32[]{:S(2)}) collective-permute-start(bf16[2,384,384]{2,1,0:T(8,128)(2,1)S(1)} %shard_map.77), channel_id=1, source_target_pairs={{0,1},{1,0},{2,3},{3,2},{4,8},{5,9},{6,10},{7,11},{8,4},{9,5},{10,... | collective-permute-start | bytes 1769480 | tf_op jit(solution)/shard_map/ppermute | solution.py:526
  3.8 18.3 %collective-permute-start.4 = (bf16[2,384,384]{2,1,0:T(8,128)(2,1)S(1)}, bf16[2,384,384]{2,1,0:T(8,128)(2,1)S(1)}, u32[]{:S(2)}, u32[]{:S(2)}) collective-permute-start(bf16[2,384,384]{2,1,0:T(8,128)(2,1)S(1)} %shard_map.77), channel_id=1, source_target_pairs={{0,4},{1,5},{2,6},{3,7},{4,0},{5,1},{6,2},{7,3},{8,12},{9,13},{10,... | collective-permute-start | bytes 1769480 | tf_op jit(solution)/shard_map/ppermute | solution.py:526
  7.9 1.3 %copy-start.1 = (bf16[1,1,1,384,1536]{4,3,2,1,0:T(8,128)(2,1)S(1)}, bf16[1,1,1,384,1536]{4,3,2,1,0:T(8,128)(2,1)}, u32[]{:S(2)}) copy-start(bf16[1,1,1,384,1536]{4,3,2,1,0:T(8,128)(2,1)} %param.9) | copy-start | bytes 3538948
  7.9 1.6 %copy-start.3 = (bf16[1,1,1,384,1536]{4,3,2,1,0:T(8,128)(2,1)S(1)}, bf16[1,1,1,384,1536]{4,3,2,1,0:T(8,128)(2,1)}, u32[]{:S(2)}) copy-start(bf16[1,1,1,384,1536]{4,3,2,1,0:T(8,128)(2,1)} %param.6) | copy-start | bytes 3538948
  9.6 3.3 %copy-start.6 = (f32[1,2,128]{2,1,0:T(2,128)S(1)}, f32[1,2,128]{2,1,0:T(2,128)}, u32[]{:S(2)}) copy-start(f32[1,2,128]{2,1,0:T(2,128)} %param.10) | copy-start | bytes 3076
  9.6 3.3 %copy-start.7 = (s32[1,1,1,3]{3,2,1,0:T(1,128)S(1)}, s32[1,1,1,3]{3,2,1,0:T(1,128)}, u32[]{:S(2)}) copy-start(s32[1,1,1,3]{3,2,1,0:T(1,128)} %param.11) | copy-start | bytes 40
  9.7 26.7 %collective-permute-start.3 = (bf16[2,384,512]{2,1,0:T(8,128)(2,1)S(1)}, bf16[2,384,512]{2,1,0:T(8,128)(2,1)S(1)}, u32[]{:S(2)}, u32[]{:S(2)}) collective-permute-start(bf16[2,384,512]{2,1,0:T(8,128)(2,1)S(1)} %shard_map.79), channel_id=1, source_target_pairs={{0,1},{1,0},{2,3},{3,2},{4,8},{5,9},{6,10},{7,11},{8,4},{9,5},{10,... | collective-permute-start | bytes 2359304 | tf_op jit(solution)/shard_map/ppermute | solution.py:526
  9.7 28.1 %collective-permute-start.2 = (bf16[2,384,512]{2,1,0:T(8,128)(2,1)S(1)}, bf16[2,384,512]{2,1,0:T(8,128)(2,1)S(1)}, u32[]{:S(2)}, u32[]{:S(2)}) collective-permute-start(bf16[2,384,512]{2,1,0:T(8,128)(2,1)S(1)} %shard_map.79), channel_id=1, source_target_pairs={{0,4},{1,5},{2,6},{3,7},{4,0},{5,1},{6,2},{7,3},{8,12},{9,13},{10,... | collective-permute-start | bytes 2359304 | tf_op jit(solution)/shard_map/ppermute | solution.py:526
  11.4 23.3 %collective-permute-start = (bf16[2,384,640]{2,1,0:T(8,128)(2,1)S(1)}, bf16[2,384,640]{2,1,0:T(8,128)(2,1)S(1)}, u32[]{:S(2)}, u32[]{:S(2)}) collective-permute-start(bf16[2,384,640]{2,1,0:T(8,128)(2,1)S(1)} %shard_map.78), channel_id=1, source_target_pairs={{0,16},{16,0},{1,17},{17,1},{2,18},{18,2},{3,19},{19,3},{4,20},{20... | collective-permute-start | bytes 2949128 | tf_op jit(solution)/shard_map/ppermute | solution.py:545
  34.8 25.1 %collective-permute-start.1 = (bf16[2,400,640]{2,1,0:T(8,128)(2,1)S(1)}, bf16[2,400,640]{2,1,0:T(8,128)(2,1)S(1)}, u32[]{:S(2)}, u32[]{:S(2)}) collective-permute-start(bf16[2,400,640]{2,1,0:T(8,128)(2,1)S(1)} %shard_map.81), channel_id=1, source_target_pairs={{0,16},{16,0},{1,17},{17,1},{2,18},{18,2},{3,19},{19,3},{4,20},{20... | collective-permute-start | bytes 3072008 | tf_op jit(solution)/shard_map/ppermute | solution.py:545
  41.5 6.9 %collective-permute-start.8 = (f32[56,384]{1,0:T(8,128)S(1)}, f32[56,384]{1,0:T(8,128)S(1)}, u32[]{:S(2)}, u32[]{:S(2)}) collective-permute-start(f32[56,384]{1,0:T(8,128)S(1)} %get-tuple-element.48), channel_id=1, source_target_pairs={{0,8},{1,9},{2,10},{3,11},{4,12},{5,13},{6,14},{7,15},{8,0},{9,1},... | collective-permute-start | bytes 258056 | tf_op jit(solution)/shard_map/ppermute | solution.py:526
  43.6 4.9 %collective-permute-start.6 = (f32[56,384]{1,0:T(8,128)S(1)}, f32[56,384]{1,0:T(8,128)S(1)}, u32[]{:S(2)}, u32[]{:S(2)}) collective-permute-start(f32[56,384]{1,0:T(8,128)S(1)} %get-tuple-element.46.sent_even), channel_id=1, source_target_pairs={{0,4},{1,5},{2,6},{3,7},{4,0},{5,1},{6,2},{7,3},{8,12},{9,13},{10,... | collective-permute-start | bytes 258056 | tf_op jit(solution)/shard_map/ppermute | solution.py:526
  45.3 3.2 %collective-permute-start.7 = (f32[56,384]{1,0:T(8,128)S(1)}, f32[56,384]{1,0:T(8,128)S(1)}, u32[]{:S(2)}, u32[]{:S(2)}) collective-permute-start(f32[56,384]{1,0:T(8,128)S(1)} %get-tuple-element.47.sent_odd), channel_id=1, source_target_pairs={{0,1},{1,0},{2,3},{3,2},{4,8},{5,9},{6,10},{7,11},{8,4},{9,5},{10,... | collective-permute-start | bytes 258056 | tf_op jit(solution)/shard_map/ppermute | solution.py:526
  48.5 19.6 %collective-permute-start.10 = (bf16[2,384,640]{2,1,0:T(8,128)(2,1)S(1)}, bf16[2,384,640]{2,1,0:T(8,128)(2,1)S(1)}, u32[]{:S(2)}, u32[]{:S(2)}) collective-permute-start(bf16[2,384,640]{2,1,0:T(8,128)(2,1)S(1)} %collective-permute-done.key.value), channel_id=1, source_target_pairs={{0,1},{1,0},{2,3},{3,2},{4,8},{5,9},{6,10},{7,11},{8,4},{9,5},{10,... | collective-permute-start | bytes 2949128 | tf_op jit(solution)/shard_map/ppermute | solution.py:526
  48.5 24.3 %collective-permute-start.9 = (bf16[2,384,640]{2,1,0:T(8,128)(2,1)S(1)}, bf16[2,384,640]{2,1,0:T(8,128)(2,1)S(1)}, u32[]{:S(2)}, u32[]{:S(2)}) collective-permute-start(bf16[2,384,640]{2,1,0:T(8,128)(2,1)S(1)} %collective-permute-done.key.value), channel_id=1, source_target_pairs={{0,4},{1,5},{2,6},{3,7},{4,0},{5,1},{6,2},{7,3},{8,12},{9,13},{10,... | collective-permute-start | bytes 2949128 | tf_op jit(solution)/shard_map/ppermute | solution.py:526
  58.3 17.0 %collective-permute-start.13 = (bf16[2,384,384]{2,1,0:T(8,128)(2,1)S(1)}, bf16[2,384,384]{2,1,0:T(8,128)(2,1)S(1)}, u32[]{:S(2)}, u32[]{:S(2)}) collective-permute-start(bf16[2,384,384]{2,1,0:T(8,128)(2,1)S(1)} %get-tuple-element.59), channel_id=1, source_target_pairs={{0,16},{16,0},{1,17},{17,1},{2,18},{18,2},{3,19},{19,3},{4,20},{20... | collective-permute-start | bytes 1769480 | tf_op jit(solution)/shard_map/ppermute | solution.py:545
  72.8 15.5 %collective-permute-start.16 = (bf16[384,896]{1,0:T(8,128)(2,1)S(1)}, bf16[384,896]{1,0:T(8,128)(2,1)S(1)}, u32[]{:S(2)}, u32[]{:S(2)}) collective-permute-start(bf16[384,896]{1,0:T(8,128)(2,1)S(1)} %get-tuple-element.66), channel_id=1, source_target_pairs={{0,1},{1,0},{2,3},{3,2},{4,8},{5,9},{6,10},{7,11},{8,4},{9,5},{10,... | collective-permute-start | bytes 2064392 | tf_op jit(solution)/shard_map/ppermute | solution.py:526
  72.8 18.8 %collective-permute-start.15 = (bf16[384,896]{1,0:T(8,128)(2,1)S(1)}, bf16[384,896]{1,0:T(8,128)(2,1)S(1)}, u32[]{:S(2)}, u32[]{:S(2)}) collective-permute-start(bf16[384,896]{1,0:T(8,128)(2,1)S(1)} %get-tuple-element.64), channel_id=1, source_target_pairs={{0,4},{1,5},{2,6},{3,7},{4,0},{5,1},{6,2},{7,3},{8,12},{9,13},{10,... | collective-permute-start | bytes 2064392 | tf_op jit(solution)/shard_map/ppermute | solution.py:526
  75.4 19.8 %collective-permute-start.14 = (bf16[2,384,512]{2,1,0:T(8,128)(2,1)S(1)}, bf16[2,384,512]{2,1,0:T(8,128)(2,1)S(1)}, u32[]{:S(2)}, u32[]{:S(2)}) collective-permute-start(bf16[2,384,512]{2,1,0:T(8,128)(2,1)S(1)} %get-tuple-element.54), channel_id=1, source_target_pairs={{0,16},{16,0},{1,17},{17,1},{2,18},{18,2},{3,19},{19,3},{4,20},{20... | collective-permute-start | bytes 2359304 | tf_op jit(solution)/shard_map/ppermute | solution.py:545
  88.2 31.5 %collective-permute-start.11 = (bf16[2,384,640]{2,1,0:T(8,128)(2,1)S(1)}, bf16[2,384,640]{2,1,0:T(8,128)(2,1)S(1)}, u32[]{:S(2)}, u32[]{:S(2)}) collective-permute-start(bf16[2,384,640]{2,1,0:T(8,128)(2,1)S(1)} %get-tuple-element.57), channel_id=1, source_target_pairs={{0,4},{1,5},{2,6},{3,7},{4,0},{5,1},{6,2},{7,3},{8,12},{9,13},{10,... | collective-permute-start | bytes 2949128 | tf_op jit(solution)/shard_map/ppermute | solution.py:526
  88.2 31.4 %collective-permute-start.12 = (bf16[2,384,640]{2,1,0:T(8,128)(2,1)S(1)}, bf16[2,384,640]{2,1,0:T(8,128)(2,1)S(1)}, u32[]{:S(2)}, u32[]{:S(2)}) collective-permute-start(bf16[2,384,640]{2,1,0:T(8,128)(2,1)S(1)} %get-tuple-element.58), channel_id=1, source_target_pairs={{0,1},{1,0},{2,3},{3,2},{4,8},{5,9},{6,10},{7,11},{8,4},{9,5},{10,... | collective-permute-start | bytes 2949128 | tf_op jit(solution)/shard_map/ppermute | solution.py:526
  93.6 26.0 %collective-permute-start.17 = (bf16[384,896]{1,0:T(8,128)(2,1)S(1)}, bf16[384,896]{1,0:T(8,128)(2,1)S(1)}, u32[]{:S(2)}, u32[]{:S(2)}) collective-permute-start(bf16[384,896]{1,0:T(8,128)(2,1)S(1)} %shard_map.87), channel_id=1, source_target_pairs={{0,16},{16,0},{1,17},{17,1},{2,18},{18,2},{3,19},{19,3},{4,20},{20... | collective-permute-start | bytes 2064392 | tf_op jit(solution)/shard_map/ppermute | solution.py:545
  95.1 14.1 %collective-permute-start.18 = (f32[2,128]{1,0:T(2,128)S(1)}, f32[2,128]{1,0:T(2,128)S(1)}, u32[]{:S(2)}, u32[]{:S(2)}) collective-permute-start(f32[2,128]{1,0:T(2,128)S(1)} %slice.11), channel_id=1, source_target_pairs={{0,16},{16,0},{1,17},{17,1},{2,18},{18,2},{3,19},{19,3},{4,20},{20... | collective-permute-start | bytes 3080 | tf_op jit(solution)/shard_map/ppermute | solution.py:545
  109.2 1.1 collective-permute-start.19
  110.3 3.6 %collective-permute-start.20 = (f32[2,128]{1,0:T(2,128)S(1)}, f32[2,128]{1,0:T(2,128)S(1)}, u32[]{:S(2)}, u32[]{:S(2)}) collective-permute-start(f32[2,128]{1,0:T(2,128)S(1)} %add.20), channel_id=1, source_target_pairs={{0,2},{1,3},{2,0},{3,1},{4,6},{5,7},{6,4},{7,5},{8,10},{9,11},{10,... | collective-permute-start | bytes 3080 | tf_op jit(solution)/shard_map/ppermute | solution.py:552
  113.9 3.6 %collective-permute-start.21 = (f32[2,128]{1,0:T(2,128)S(1)}, f32[2,128]{1,0:T(2,128)S(1)}, u32[]{:S(2)}, u32[]{:S(2)}) collective-permute-start(f32[2,128]{1,0:T(2,128)S(1)} %add.21), channel_id=1, source_target_pairs={{0,4},{4,0},{8,12},{12,8},{1,5},{5,1},{9,13},{13,9},{2,6},{6,2},{1... | collective-permute-start | bytes 3080 | tf_op jit(solution)/shard_map/ppermute | solution.py:552
  117.5 5.5 %collective-permute-start.22 = (f32[2,128]{1,0:T(2,128)S(1)}, f32[2,128]{1,0:T(2,128)S(1)}, u32[]{:S(2)}, u32[]{:S(2)}) collective-permute-start(f32[2,128]{1,0:T(2,128)S(1)} %add.22), channel_id=1, source_target_pairs={{0,8},{4,12},{8,0},{12,4},{1,9},{5,13},{9,1},{13,5},{2,10},{6,14},... | collective-permute-start | bytes 3080 | tf_op jit(solution)/shard_map/ppermute | solution.py:552

commit v7 on v6

--- a/solution.py
+++ b/solution.py
@@ -13,7 +13,7 @@
 EPSILON = 1e-06
 ROOT_SCALE = HEAD_DIM ** (-0.5)
 EXP2_SCALE = ROOT_SCALE * math.log2(math.e)
-GROUPS = ((0, 3, False), (3, 4, False), (7, 5, True))
+GROUPS = ((0, 3, False), (3, 3, False), (6, 6, True))
 MAIN_VMEM = 20 * 1024 * 1024
 SMALL_VMEM = 12 * 1024 * 1024
 PACK_VMEM = 4 * 1024 * 1024
@@ -346,15 +346,15 @@
     return pl.BlockSpec(shape, lambda head: (0,) * len(shape))
 
 
-def pack_params():
+def pack_params(limit):
     return dict(
         scratch_shapes=[pltpu.SemaphoreType.DMA((2,))],
-        compiler_params=pltpu.CompilerParams(vmem_limit_bytes=PACK_VMEM),
+        compiler_params=pltpu.CompilerParams(vmem_limit_bytes=limit),
         cost_estimate=COST,
     )
 
 
-def pack_call(first_in, second_in, first, count):
+def pack_call(first_in, second_in, first, count, limit=PACK_VMEM):
     rows = first_in.shape[0]
     width = count * HEAD_DIM
     return pl.pallas_call(
@@ -363,7 +363,7 @@
         in_specs=[pl.BlockSpec(memory_space=pl.ANY)] * 2,
         out_specs=whole_block((2, rows, width)),
         out_shape=jax.ShapeDtypeStruct((2, rows, width), jnp.bfloat16),
-        **pack_params(),
+        **pack_params(limit),
     )(first_in, second_in)
 
 
@@ -376,7 +376,7 @@
         in_specs=[whole_block(info.shape)] + [pl.BlockSpec(memory_space=pl.ANY)] * 2,
         out_specs=whole_block((2, rows + 16, width)),
         out_shape=jax.ShapeDtypeStruct((2, rows + 16, width), jnp.bfloat16),
-        **pack_params(),
+        **pack_params(PACK_VMEM),
     )(info, query, grad)
 
 
@@ -570,11 +570,10 @@
     info = info_call(kv_tiles[0, 0, 0], after(norm_gains[0], asks[-1]))
     away_pair = turned(away_pair, -1)
     arrays = (query, grad, key, value)
-    asked = ask_call(info, after(query, away_pair), grad, away_first, away_count)
     sums = None
     for (first, count, _), ask in zip(home, asked_home):
-        told = info if sums is None else after(info, asked)
-        sums = sums_call(told, arrays, *ask, first, count, home_heads, sums, len(fars))
+        sums = sums_call(info, arrays, *ask, first, count, home_heads, sums, len(fars))
+    asked = ask_call(info, after(query, away_pair, sums[0]), grad, away_first, away_count)
     asked = turned(asked, -1)
     received = [exchanged(sums[0], 0), exchanged(sums[1], 1)]
     received += [paired(value, partners) for value, partners in zip(sums[2:], fars)]
@@ -583,29 +582,25 @@
     away_gathered = (exchanged(away_pair, 0), exchanged(away_pair, 1))
     gains, pieces, places = [], [], []
     parts = None
-    for (first, count, _), ask in zip(home, asked_home):
-        told = after(info, asked) if gains else info
+    for (first, count, _), ask in zip(home[::-1], asked_home[::-1]):
         pair_low, *parts, gain = grads_call(
-            told, arrays, *ask, all_sums, first, count, home_heads, parts, len(fars)
+            info, arrays, *ask, all_sums, first, count, home_heads, parts, len(fars)
         )
-        if gains:
-            pair_low = after(pair_low, *away_gathered)
         gains.append(gain[:2])
         pieces.append(turned(pair_low, -1))
         places.append((slice(1, 3), first * HEAD_DIM))
-    to_even, to_odd = (after(part, *away_gathered) for part in parts[1:])
-    answer = (after(parts[0], pieces[0]), exchanged(to_even, 0), exchanged(to_odd, 1))
+    answer = (parts[0], exchanged(parts[1], 0), exchanged(parts[2], 1))
     asked = after(asked, pair_low)
     operands = [(asked, 0, 0), (asked, 0, 1), (away_pair, 0, 0), (away_pair, 0, 1)]
     query_low, own, to_even, to_odd, gain = main_call(
         asked, operands, *away_gathered, away_count
     )
-    gains.append(turned(after(gain[:2], pieces[len(home) - 1]), 1))
+    gains.append(turned(after(gain[:2], *answer[1:]), 1))
     returned = (exchanged(to_even, 0), exchanged(to_odd, 1))
     pieces.append(query_low)
     places.append((0, away_first * HEAD_DIM))
     answer = answer_call(info, query, *answer, 0, home_heads)
-    pieces.append(turned(answer, -1))
+    pieces.append(turned(after(answer, gains[-1], pieces[0]), -1))
     places.append((0, 0))
     out = last_call(
         asked, operands[2], own, *returned, pieces, tuple(places), away_first, away_count

time: 124 us -> 120 us (0.968)
  waiting for transfers between devices: 51.3 us -> 46 us
  starting transfers between devices: 28.5 us -> 31 us
    ppermute x6, waiting for transfers between devices: 23.2 us -> 11.5 us  [turned(): lax.ppermute(value, 'pipe', [(i, (i + step) % count) for i in range(count)])]
    ppermute x4, waiting for transfers between devices: 6.65 us -> 12.7 us  [total_over(): other = lax.ppermute(value, axis, [(i, i ^ step) for i in range(count)])]
    ppermute x4, starting transfers between devices: 3.76 us -> 7.22 us  [total_over(): other = lax.ppermute(value, axis, [(i, i ^ step) for i in range(count)])]
    pallas_call x1, Pallas kernels: 11.3 us -> 13.6 us  [main_call(): pl.pallas_call(main_kernel, grid=(count,), in_specs=[info_block(info)] +...]
    pallas_call x2, Pallas kernels: 14.3 us -> 12.3 us  [grads_call(): pl.pallas_call(functools.partial(grads_kernel, far_count=far_count), grid...]
  transfers between devices with their start and end apart: 23 -> 23, of which waited for: 10 -> 9; matrix products, arithmetic and copies ran while one was open for 0% -> 0% of each run, Pallas kernels for 31% -> 31%
where the time goes in v7:
time: 120 us
  waiting for transfers between devices  46 us (38%)
  Pallas kernels  37.5 us (31%)
  starting transfers between devices  31 us (26%)
  local copies, waits for them, and re-layouts  4.06 us (3%)
    ppermute x13, waiting for transfers between devices, paired(): return lax.ppermute(value, ('seq', 'dp'), pairs)  21.8 us
    ppermute x13, starting transfers between devices, paired(): return lax.ppermute(value, ('seq', 'dp'), pairs)  15.6 us
    pallas_call x1, Pallas kernels, main_call(): pl.pallas_call(main_kernel, grid=(count,), in_specs=[info_block(info)] +...  13.6 us
    ppermute x4, waiting for transfers between devices, total_over(): other = lax.ppermute(value, axis, [(i, i ^ step) for i in range(count)])  12.7 us
    pallas_call x2, Pallas kernels, grads_call(): pl.pallas_call(functools.partial(grads_kernel, far_count=far_count), grid...  12.3 us
    ppermute x6, waiting for transfers between devices, turned(): lax.ppermute(value, 'pipe', [(i, (i + step) % count) for i in range(count)])  11.5 us
    ppermute x6, starting transfers between devices, turned(): lax.ppermute(value, 'pipe', [(i, (i + step) % count) for i in range(count)])  8.14 us
    ppermute x4, starting transfers between devices, total_over(): other = lax.ppermute(value, axis, [(i, i ^ step) for i in range(count)])  7.22 us
  transfers between devices with their start and end apart: 23, of which 9 were waited for; matrix products, arithmetic and copies ran while one was open for 0% of the time, Pallas kernels for 31%

profile of v7, /device:TPU:0, one launch (start us, length us, event | category | flops | bytes accessed | tf_op | source)
XLA Modules:
  0.0 120.0 jit_solution(10660440851114869835)
XLA Ops:
  0.6 1.3 %copy-done = bf16[1,1,1,384,1536]{4,3,2,1,0:T(8,128)(2,1)S(1)} copy-done((bf16[1,1,1,384,1536]{4,3,2,1,0:T(8,128)(2,1)S(1)}, bf16[1,1,1,384,1536]{4,3,2,1,0:T(8,128)(2,1)}, u32[]{:S(2)}) %copy-start) | copy-done | bytes 1179672
  1.9 1.3 %copy-done.2 = bf16[1,1,1,384,1536]{4,3,2,1,0:T(8,128)(2,1)S(1)} copy-done((bf16[1,1,1,384,1536]{4,3,2,1,0:T(8,128)(2,1)S(1)}, bf16[1,1,1,384,1536]{4,3,2,1,0:T(8,128)(2,1)}, u32[]{:S(2)}) %copy-start.2) | copy-done | bytes 1179672
  3.8 4.1 %collective-permute-start.3 = (bf16[2,384,384]{2,1,0:T(8,128)(2,1)S(1)}, bf16[2,384,384]{2,1,0:T(8,128)(2,1)S(1)}, u32[]{:S(2)}, u32[]{:S(2)}) collective-permute-start(bf16[2,384,384]{2,1,0:T(8,128)(2,1)S(1)} %shard_map.77), channel_id=1, source_target_pairs={{0,4},{1,5},{2,6},{3,7},{4,0},{5,1},{6,2},{7,3},{8,12},{9,13},{10,... | collective-permute-start | bytes 1769480 | tf_op jit(solution)/shard_map/ppermute | solution.py:526
  8.1 1.1 copy-done.1
  9.7 1.6 %collective-permute-start.1 = (bf16[2,384,384]{2,1,0:T(8,128)(2,1)S(1)}, bf16[2,384,384]{2,1,0:T(8,128)(2,1)S(1)}, u32[]{:S(2)}, u32[]{:S(2)}) collective-permute-start(bf16[2,384,384]{2,1,0:T(8,128)(2,1)S(1)} %shard_map.79), channel_id=1, source_target_pairs={{0,4},{1,5},{2,6},{3,7},{4,0},{5,1},{6,2},{7,3},{8,12},{9,13},{10,... | collective-permute-start | bytes 1769480 | tf_op jit(solution)/shard_map/ppermute | solution.py:526
  11.4 1.5 %collective-permute-start = (bf16[2,384,768]{2,1,0:T(8,128)(2,1)S(1)}, bf16[2,384,768]{2,1,0:T(8,128)(2,1)S(1)}, u32[]{:S(2)}, u32[]{:S(2)}) collective-permute-start(bf16[2,384,768]{2,1,0:T(8,128)(2,1)S(1)} %shard_map.78), channel_id=1, source_target_pairs={{0,16},{16,0},{1,17},{17,1},{2,18},{18,2},{3,19},{19,3},{4,20},{20... | collective-permute-start | bytes 3538952 | tf_op jit(solution)/shard_map/ppermute | solution.py:545
  13.5 8.7 %collective-permute-done.3.pair_even = bf16[2,384,384]{2,1,0:T(8,128)(2,1)S(1)} collective-permute-done((bf16[2,384,384]{2,1,0:T(8,128)(2,1)S(1)}, bf16[2,384,384]{2,1,0:T(8,128)(2,1)S(1)}, u32[]{:S(2)}, u32[]{:S(2)}) %collective-permute-start.3) | collective-permute-done | bytes 589856 | tf_op jit(solution)/shard_map/ppermute | solution.py:526
  22.1 2.8 %shard_map.81 = (f32[48,384]{1,0:T(8,128)S(1)}, f32[48,384]{1,0:T(8,128)S(1)}, f32[48,384]{1,0:T(8,128)S(1)}) custom-call(f32[8,128]{1,0:T(8,128)S(1)} %shard_map.80.info, bf16[384,1536]{1,0:T(8,128)(2,1)S(1)} %bitcast.20, bf16[384,1536]{1,0:T(8,128)(2,1)S(1)} %bitcast.13, bf16[384,1536]{1,0:T(8,128)(2,1)S(1)} %bitcast.27, bf16[384,1536]{1,0:T(8,128)(2,1)S(1)} %bitcast.32, ...), custom_call_target="tpu_custom_call" | custom-call | flops 6000000000 | bytes 1 | tf_op jit(solution)/shard_map/pallas_call | solution.py:431
  24.9 8.7 %collective-permute-done.1.pair_even = bf16[2,384,384]{2,1,0:T(8,128)(2,1)S(1)} collective-permute-done((bf16[2,384,384]{2,1,0:T(8,128)(2,1)S(1)}, bf16[2,384,384]{2,1,0:T(8,128)(2,1)S(1)}, u32[]{:S(2)}, u32[]{:S(2)}) %collective-permute-start.1) | collective-permute-done | bytes 589856 | tf_op jit(solution)/shard_map/ppermute | solution.py:526
  33.6 2.8 %shard_map.82 = (f32[48,384]{1,0:T(8,128)S(1)}, f32[48,384]{1,0:T(8,128)S(1)}, f32[48,384]{1,0:T(8,128)S(1)}) custom-call(f32[8,128]{1,0:T(8,128)S(1)} %shard_map.80.info, bf16[384,1536]{1,0:T(8,128)(2,1)S(1)} %bitcast.21, bf16[384,1536]{1,0:T(8,128)(2,1)S(1)} %bitcast.14, ...), custom_call_target="tpu_custom_call", output_to_operand_aliasing={{0}: (7, {}), {1}: (8, {}), {2}: (9, {})} | custom-call | flops 6000000000 | bytes 1 | tf_op jit(solution)/shard_map/pallas_call | solution.py:431
  36.4 2.0 %collective-permute-start.8 = (f32[48,384]{1,0:T(8,128)S(1)}, f32[48,384]{1,0:T(8,128)S(1)}, u32[]{:S(2)}, u32[]{:S(2)}) collective-permute-start(f32[48,384]{1,0:T(8,128)S(1)} %get-tuple-element.41), channel_id=1, source_target_pairs={{0,8},{1,9},{2,10},{3,11},{4,12},{5,13},{6,14},{7,15},{8,0},{9,1},... | collective-permute-start | bytes 221192 | tf_op jit(solution)/shard_map/ppermute | solution.py:526
  38.4 1.8 %collective-permute-start.6 = (f32[48,384]{1,0:T(8,128)S(1)}, f32[48,384]{1,0:T(8,128)S(1)}, u32[]{:S(2)}, u32[]{:S(2)}) collective-permute-start(f32[48,384]{1,0:T(8,128)S(1)} %get-tuple-element.38.sent_even), channel_id=1, source_target_pairs={{0,4},{1,5},{2,6},{3,7},{4,0},{5,1},{6,2},{7,3},{8,12},{9,13},{10,... | collective-permute-start | bytes 221192 | tf_op jit(solution)/shard_map/ppermute | solution.py:526
  40.3 1.6 %collective-permute-start.5 = (bf16[2,400,768]{2,1,0:T(8,128)(2,1)S(1)}, bf16[2,400,768]{2,1,0:T(8,128)(2,1)S(1)}, u32[]{:S(2)}, u32[]{:S(2)}) collective-permute-start(bf16[2,400,768]{2,1,0:T(8,128)(2,1)S(1)} %shard_map.83), channel_id=1, source_target_pairs={{0,16},{16,0},{1,17},{17,1},{2,18},{18,2},{3,19},{19,3},{4,20},{20... | collective-permute-start | bytes 3686408 | tf_op jit(solution)/shard_map/ppermute | solution.py:545
  41.9 1.4 %collective-permute-done.6.from_even = f32[48,384]{1,0:T(8,128)S(1)} collective-permute-done((f32[48,384]{1,0:T(8,128)S(1)}, f32[48,384]{1,0:T(8,128)S(1)}, u32[]{:S(2)}, u32[]{:S(2)}) %collective-permute-start.6) | collective-permute-done | bytes 73760 | tf_op jit(solution)/shard_map/ppermute | solution.py:526
  43.3 3.3 %collective-permute-start.9 = (bf16[2,384,768]{2,1,0:T(8,128)(2,1)S(1)}, bf16[2,384,768]{2,1,0:T(8,128)(2,1)S(1)}, u32[]{:S(2)}, u32[]{:S(2)}) collective-permute-start(bf16[2,384,768]{2,1,0:T(8,128)(2,1)S(1)} %collective-permute-done.key.value), channel_id=1, source_target_pairs={{0,4},{1,5},{2,6},{3,7},{4,0},{5,1},{6,2},{7,3},{8,12},{9,13},{10,... | collective-permute-start | bytes 3538952 | tf_op jit(solution)/shard_map/ppermute | solution.py:526
  46.6 6.1 %shard_map.84 = (bf16[2,384,384]{2,1,0:T(8,128)(2,1)S(1)}, f32[384,768]{1,0:T(8,128)S(1)}, bf16[384,768]{1,0:T(8,128)(2,1)S(1)}, bf16[384,768]{1,0:T(8,128)(2,1)S(1)}, f32[8,128]{1,0:T(8,128)S(1)}) custom-call(f32[8,128]{1,0:T(8,128)S(1)} %shard_map.80.info, bf16[384,1536]{1,0:T(8,128)(2,1)S(1)} %bitcast.23, bf16[384,1536]{1,0:T(8,128)(2,1)S(1)} %bitcast.16, ...), custom_call_target="tpu_custom_call" | custom-call | flops 6000000000 | bytes 1 | tf_op jit(solution)/shard_map/pallas_call | solution.py:451
  52.7 6.2 %shard_map.85 = (bf16[2,384,384]{2,1,0:T(8,128)(2,1)S(1)}, f32[384,768]{1,0:T(8,128)S(1)}, bf16[384,768]{1,0:T(8,128)(2,1)S(1)}, bf16[384,768]{1,0:T(8,128)(2,1)S(1)}, f32[8,128]{1,0:T(8,128)S(1)}) custom-call(f32[8,128]{1,0:T(8,128)S(1)} %shard_map.80.info, ...), custom_call_target="tpu_custom_call", output_to_operand_aliasing={{1}: (12, {}), {2}: (13, {}), {3}: (14, {})} | custom-call | flops 6000000000 | bytes 1 | tf_op jit(solution)/shard_map/pallas_call | solution.py:451
  59.0 9.4 %collective-permute-done.5.info.query.grad = bf16[2,400,768]{2,1,0:T(8,128)(2,1)S(1)} collective-permute-done((bf16[2,400,768]{2,1,0:T(8,128)(2,1)S(1)}, bf16[2,400,768]{2,1,0:T(8,128)(2,1)S(1)}, u32[]{:S(2)}, u32[]{:S(2)}) %collective-permute-start.5) | collective-permute-done | bytes 1228832 | tf_op jit(solution)/shard_map/ppermute | solution.py:545
  68.4 1.5 %collective-permute-start.14 = (bf16[2,384,384]{2,1,0:T(8,128)(2,1)S(1)}, bf16[2,384,384]{2,1,0:T(8,128)(2,1)S(1)}, u32[]{:S(2)}, u32[]{:S(2)}) collective-permute-start(bf16[2,384,384]{2,1,0:T(8,128)(2,1)S(1)} %get-tuple-element.45), channel_id=1, source_target_pairs={{0,16},{16,0},{1,17},{17,1},{2,18},{18,2},{3,19},{19,3},{4,20},{20... | collective-permute-start | bytes 1769480 | tf_op jit(solution)/shard_map/ppermute | solution.py:545
  70.4 3.0 %collective-permute-done.9.pair_even = bf16[2,384,768]{2,1,0:T(8,128)(2,1)S(1)} collective-permute-done((bf16[2,384,768]{2,1,0:T(8,128)(2,1)S(1)}, bf16[2,384,768]{2,1,0:T(8,128)(2,1)S(1)}, u32[]{:S(2)}, u32[]{:S(2)}) %collective-permute-start.9) | collective-permute-done | bytes 1179680 | tf_op jit(solution)/shard_map/ppermute | solution.py:526
  73.5 13.6 %shard_map.86 = (bf16[384,768]{1,0:T(8,128)(2,1)S(1)}, f32[2,384,768]{2,1,0:T(8,128)S(1)}, bf16[2,384,768]{2,1,0:T(8,128)(2,1)S(1)}, bf16[2,384,768]{2,1,0:T(8,128)(2,1)S(1)}, f32[8,128]{1,0:T(8,128)S(1)}) custom-call(bf16[2,400,768]{2,1,0:T(8,128)(2,1)S(1)} %collective-permute-done.5.info.query.grad, ...), custom_call_target="tpu_custom_call" | custom-call | flops 6000000000 | bytes 1 | tf_op jit(solution)/shard_map/pallas_call | solution.py:404
  87.1 1.6 %collective-permute-start.17 = (f32[2,128]{1,0:T(2,128)S(1)}, f32[2,128]{1,0:T(2,128)S(1)}, u32[]{:S(2)}, u32[]{:S(2)}) collective-permute-start(f32[2,128]{1,0:T(2,128)S(1)} %slice.9), channel_id=1, source_target_pairs={{0,16},{16,0},{1,17},{17,1},{2,18},{18,2},{3,19},{19,3},{4,20},{20... | collective-permute-start | bytes 3080 | tf_op jit(solution)/shard_map/ppermute | solution.py:545
  88.7 2.0 %collective-permute-start.11 = (bf16[2,384,768]{2,1,0:T(8,128)(2,1)S(1)}, bf16[2,384,768]{2,1,0:T(8,128)(2,1)S(1)}, u32[]{:S(2)}, u32[]{:S(2)}) collective-permute-start(bf16[2,384,768]{2,1,0:T(8,128)(2,1)S(1)} %get-tuple-element.49), channel_id=1, source_target_pairs={{0,4},{1,5},{2,6},{3,7},{4,0},{5,1},{6,2},{7,3},{8,12},{9,13},{10,... | collective-permute-start | bytes 3538952 | tf_op jit(solution)/shard_map/ppermute | solution.py:526
  90.7 1.7 %shard_map.87 = bf16[384,768]{1,0:T(8,128)(2,1)S(1)} custom-call(f32[8,128]{1,0:T(8,128)S(1)} %shard_map.80.info, bf16[384,1536]{1,0:T(8,128)(2,1)S(1)} %bitcast.25, f32[384,768]{1,0:T(8,128)S(1)} %get-tuple-element.53.own, bf16[384,768]{1,0:T(8,128)(2,1)S(1)} %collective-permute-done.15.from_even, bf16[384,768]{1,0:T(8,128)(2,1)S(1)} %collective-permute-done.16.from_odd), custom_call_target="tpu_custom_call" | custom-call | flops 20000000000 | bytes 1 | tf_op jit(solution)/shard_map/pallas_call | solution.py:475
  92.4 2.1 %collective-permute-done.13.rest_0_ = bf16[2,384,384]{2,1,0:T(8,128)(2,1)S(1)} collective-permute-done((bf16[2,384,384]{2,1,0:T(8,128)(2,1)S(1)}, bf16[2,384,384]{2,1,0:T(8,128)(2,1)S(1)}, u32[]{:S(2)}, u32[]{:S(2)}) %collective-permute-start.13) | collective-permute-done | bytes 589856 | tf_op jit(solution)/shard_map/ppermute | solution.py:545
  94.5 1.5 %collective-permute-start.18 = (bf16[384,768]{1,0:T(8,128)(2,1)S(1)}, bf16[384,768]{1,0:T(8,128)(2,1)S(1)}, u32[]{:S(2)}, u32[]{:S(2)}) collective-permute-start(bf16[384,768]{1,0:T(8,128)(2,1)S(1)} %shard_map.87), channel_id=1, source_target_pairs={{0,16},{16,0},{1,17},{17,1},{2,18},{18,2},{3,19},{19,3},{4,20},{20... | collective-permute-start | bytes 1769480 | tf_op jit(solution)/shard_map/ppermute | solution.py:545
  97.2 1.5 %collective-permute-start.20 = (f32[2,128]{1,0:T(2,128)S(1)}, f32[2,128]{1,0:T(2,128)S(1)}, u32[]{:S(2)}, u32[]{:S(2)}) collective-permute-start(f32[2,128]{1,0:T(2,128)S(1)} %add.20), channel_id=1, source_target_pairs={{0,2},{1,3},{2,0},{3,1},{4,6},{5,7},{6,4},{7,5},{8,10},{9,11},{10,... | collective-permute-start | bytes 3080 | tf_op jit(solution)/shard_map/ppermute | solution.py:552
  98.7 2.0 %collective-permute-done.20 = f32[2,128]{1,0:T(2,128)S(1)} collective-permute-done((f32[2,128]{1,0:T(2,128)S(1)}, f32[2,128]{1,0:T(2,128)S(1)}, u32[]{:S(2)}, u32[]{:S(2)}) %collective-permute-start.20) | collective-permute-done | bytes 1056 | tf_op jit(solution)/shard_map/ppermute | solution.py:552
  100.7 2.6 %collective-permute-start.21 = (f32[2,128]{1,0:T(2,128)S(1)}, f32[2,128]{1,0:T(2,128)S(1)}, u32[]{:S(2)}, u32[]{:S(2)}) collective-permute-start(f32[2,128]{1,0:T(2,128)S(1)} %add.21), channel_id=1, source_target_pairs={{0,4},{4,0},{8,12},{12,8},{1,5},{5,1},{9,13},{13,9},{2,6},{6,2},{1... | collective-permute-start | bytes 3080 | tf_op jit(solution)/shard_map/ppermute | solution.py:552
  103.4 9.5 %collective-permute-done.21 = f32[2,128]{1,0:T(2,128)S(1)} collective-permute-done((f32[2,128]{1,0:T(2,128)S(1)}, f32[2,128]{1,0:T(2,128)S(1)}, u32[]{:S(2)}, u32[]{:S(2)}) %collective-permute-start.21) | collective-permute-done | bytes 1056 | tf_op jit(solution)/shard_map/ppermute | solution.py:552
  112.9 3.0 %collective-permute-start.22 = (f32[2,128]{1,0:T(2,128)S(1)}, f32[2,128]{1,0:T(2,128)S(1)}, u32[]{:S(2)}, u32[]{:S(2)}) collective-permute-start(f32[2,128]{1,0:T(2,128)S(1)} %add.22), channel_id=1, source_target_pairs={{0,8},{4,12},{8,0},{12,4},{1,9},{5,13},{9,1},{13,5},{2,10},{6,14},... | collective-permute-start | bytes 3080 | tf_op jit(solution)/shard_map/ppermute | solution.py:552
  116.0 3.4 %shard_map.88 = bf16[3,384,1536]{2,1,0:T(8,128)(2,1)} custom-call(bf16[2,400,768]{2,1,0:T(8,128)(2,1)S(1)} %collective-permute-done.5.info.query.grad, bf16[2,384,768]{2,1,0:T(8,128)(2,1)S(1)} %collective-permute-done.key.value, f32[2,384,768]{2,1,0:T(8,128)S(1)} %get-tuple-element.48.own, bf16[2,384,768]{2,1,0:T(8,128)(2,1)S(1)} %collective-permute-done.11.from_even, ...), custom_call_target="tpu_custom_call" | custom-call | flops 1 | bytes 1 | tf_op jit(solution)/shard_map/pallas_call | solution.py:490
  (48 shorter events, 4.4 us)
Async XLA Ops:
  0.6 1.3 %copy-start = (bf16[1,1,1,384,1536]{4,3,2,1,0:T(8,128)(2,1)S(1)}, bf16[1,1,1,384,1536]{4,3,2,1,0:T(8,128)(2,1)}, u32[]{:S(2)}) copy-start(bf16[1,1,1,384,1536]{4,3,2,1,0:T(8,128)(2,1)} %param.9) | copy-start | bytes 3538948
  1.9 1.3 %copy-start.2 = (bf16[1,1,1,384,1536]{4,3,2,1,0:T(8,128)(2,1)S(1)}, bf16[1,1,1,384,1536]{4,3,2,1,0:T(8,128)(2,1)}, u32[]{:S(2)}) copy-start(bf16[1,1,1,384,1536]{4,3,2,1,0:T(8,128)(2,1)} %param.6) | copy-start | bytes 3538948
  3.2 4.8 %copy-start.4 = (bf16[1,1,1,384,1536]{4,3,2,1,0:T(8,128)(2,1)S(1)}, bf16[1,1,1,384,1536]{4,3,2,1,0:T(8,128)(2,1)}, u32[]{:S(2)}) copy-start(bf16[1,1,1,384,1536]{4,3,2,1,0:T(8,128)(2,1)} %param.7) | copy-start | bytes 3538948
  3.2 4.8 %copy-start.5 = (bf16[1,1,1,384,1536]{4,3,2,1,0:T(8,128)(2,1)S(1)}, bf16[1,1,1,384,1536]{4,3,2,1,0:T(8,128)(2,1)}, u32[]{:S(2)}) copy-start(bf16[1,1,1,384,1536]{4,3,2,1,0:T(8,128)(2,1)} %param.8) | copy-start | bytes 3538948
  3.3 10.2 %collective-permute-start.4 = (bf16[2,384,384]{2,1,0:T(8,128)(2,1)S(1)}, bf16[2,384,384]{2,1,0:T(8,128)(2,1)S(1)}, u32[]{:S(2)}, u32[]{:S(2)}) collective-permute-start(bf16[2,384,384]{2,1,0:T(8,128)(2,1)S(1)} %shard_map.77), channel_id=1, source_target_pairs={{0,1},{1,0},{2,3},{3,2},{4,8},{5,9},{6,10},{7,11},{8,4},{9,5},{10,... | collective-permute-start | bytes 1769480 | tf_op jit(solution)/shard_map/ppermute | solution.py:526
  3.8 18.3 %collective-permute-start.3 = (bf16[2,384,384]{2,1,0:T(8,128)(2,1)S(1)}, bf16[2,384,384]{2,1,0:T(8,128)(2,1)S(1)}, u32[]{:S(2)}, u32[]{:S(2)}) collective-permute-start(bf16[2,384,384]{2,1,0:T(8,128)(2,1)S(1)} %shard_map.77), channel_id=1, source_target_pairs={{0,4},{1,5},{2,6},{3,7},{4,0},{5,1},{6,2},{7,3},{8,12},{9,13},{10,... | collective-permute-start | bytes 1769480 | tf_op jit(solution)/shard_map/ppermute | solution.py:526
  7.9 1.3 %copy-start.1 = (bf16[1,1,1,384,1536]{4,3,2,1,0:T(8,128)(2,1)S(1)}, bf16[1,1,1,384,1536]{4,3,2,1,0:T(8,128)(2,1)}, u32[]{:S(2)}) copy-start(bf16[1,1,1,384,1536]{4,3,2,1,0:T(8,128)(2,1)} %param.9) | copy-start | bytes 3538948
  7.9 1.6 %copy-start.3 = (bf16[1,1,1,384,1536]{4,3,2,1,0:T(8,128)(2,1)S(1)}, bf16[1,1,1,384,1536]{4,3,2,1,0:T(8,128)(2,1)}, u32[]{:S(2)}) copy-start(bf16[1,1,1,384,1536]{4,3,2,1,0:T(8,128)(2,1)} %param.6) | copy-start | bytes 3538948
  9.6 3.3 %copy-start.6 = (f32[1,2,128]{2,1,0:T(2,128)S(1)}, f32[1,2,128]{2,1,0:T(2,128)}, u32[]{:S(2)}) copy-start(f32[1,2,128]{2,1,0:T(2,128)} %param.10) | copy-start | bytes 3076
  9.6 3.3 %copy-start.7 = (s32[1,1,1,3]{3,2,1,0:T(1,128)S(1)}, s32[1,1,1,3]{3,2,1,0:T(1,128)}, u32[]{:S(2)}) copy-start(s32[1,1,1,3]{3,2,1,0:T(1,128)} %param.11) | copy-start | bytes 40
  9.7 15.3 %collective-permute-start.2 = (bf16[2,384,384]{2,1,0:T(8,128)(2,1)S(1)}, bf16[2,384,384]{2,1,0:T(8,128)(2,1)S(1)}, u32[]{:S(2)}, u32[]{:S(2)}) collective-permute-start(bf16[2,384,384]{2,1,0:T(8,128)(2,1)S(1)} %shard_map.79), channel_id=1, source_target_pairs={{0,1},{1,0},{2,3},{3,2},{4,8},{5,9},{6,10},{7,11},{8,4},{9,5},{10,... | collective-permute-start | bytes 1769480 | tf_op jit(solution)/shard_map/ppermute | solution.py:526
  9.7 23.9 %collective-permute-start.1 = (bf16[2,384,384]{2,1,0:T(8,128)(2,1)S(1)}, bf16[2,384,384]{2,1,0:T(8,128)(2,1)S(1)}, u32[]{:S(2)}, u32[]{:S(2)}) collective-permute-start(bf16[2,384,384]{2,1,0:T(8,128)(2,1)S(1)} %shard_map.79), channel_id=1, source_target_pairs={{0,4},{1,5},{2,6},{3,7},{4,0},{5,1},{6,2},{7,3},{8,12},{9,13},{10,... | collective-permute-start | bytes 1769480 | tf_op jit(solution)/shard_map/ppermute | solution.py:526
  11.4 28.8 %collective-permute-start = (bf16[2,384,768]{2,1,0:T(8,128)(2,1)S(1)}, bf16[2,384,768]{2,1,0:T(8,128)(2,1)S(1)}, u32[]{:S(2)}, u32[]{:S(2)}) collective-permute-start(bf16[2,384,768]{2,1,0:T(8,128)(2,1)S(1)} %shard_map.78), channel_id=1, source_target_pairs={{0,16},{16,0},{1,17},{17,1},{2,18},{18,2},{3,19},{19,3},{4,20},{20... | collective-permute-start | bytes 3538952 | tf_op jit(solution)/shard_map/ppermute | solution.py:545
  36.4 5.5 %collective-permute-start.8 = (f32[48,384]{1,0:T(8,128)S(1)}, f32[48,384]{1,0:T(8,128)S(1)}, u32[]{:S(2)}, u32[]{:S(2)}) collective-permute-start(f32[48,384]{1,0:T(8,128)S(1)} %get-tuple-element.41), channel_id=1, source_target_pairs={{0,8},{1,9},{2,10},{3,11},{4,12},{5,13},{6,14},{7,15},{8,0},{9,1},... | collective-permute-start | bytes 221192 | tf_op jit(solution)/shard_map/ppermute | solution.py:526
  38.4 3.5 %collective-permute-start.7 = (f32[48,384]{1,0:T(8,128)S(1)}, f32[48,384]{1,0:T(8,128)S(1)}, u32[]{:S(2)}, u32[]{:S(2)}) collective-permute-start(f32[48,384]{1,0:T(8,128)S(1)} %get-tuple-element.40.sent_odd), channel_id=1, source_target_pairs={{0,1},{1,0},{2,3},{3,2},{4,8},{5,9},{6,10},{7,11},{8,4},{9,5},{10,... | collective-permute-start | bytes 221192 | tf_op jit(solution)/shard_map/ppermute | solution.py:526
  38.4 4.9 %collective-permute-start.6 = (f32[48,384]{1,0:T(8,128)S(1)}, f32[48,384]{1,0:T(8,128)S(1)}, u32[]{:S(2)}, u32[]{:S(2)}) collective-permute-start(f32[48,384]{1,0:T(8,128)S(1)} %get-tuple-element.38.sent_even), channel_id=1, source_target_pairs={{0,4},{1,5},{2,6},{3,7},{4,0},{5,1},{6,2},{7,3},{8,12},{9,13},{10,... | collective-permute-start | bytes 221192 | tf_op jit(solution)/shard_map/ppermute | solution.py:526
  40.3 28.1 %collective-permute-start.5 = (bf16[2,400,768]{2,1,0:T(8,128)(2,1)S(1)}, bf16[2,400,768]{2,1,0:T(8,128)(2,1)S(1)}, u32[]{:S(2)}, u32[]{:S(2)}) collective-permute-start(bf16[2,400,768]{2,1,0:T(8,128)(2,1)S(1)} %shard_map.83), channel_id=1, source_target_pairs={{0,16},{16,0},{1,17},{17,1},{2,18},{18,2},{3,19},{19,3},{4,20},{20... | collective-permute-start | bytes 3686408 | tf_op jit(solution)/shard_map/ppermute | solution.py:545
  43.3 26.6 %collective-permute-start.10 = (bf16[2,384,768]{2,1,0:T(8,128)(2,1)S(1)}, bf16[2,384,768]{2,1,0:T(8,128)(2,1)S(1)}, u32[]{:S(2)}, u32[]{:S(2)}) collective-permute-start(bf16[2,384,768]{2,1,0:T(8,128)(2,1)S(1)} %collective-permute-done.key.value), channel_id=1, source_target_pairs={{0,1},{1,0},{2,3},{3,2},{4,8},{5,9},{6,10},{7,11},{8,4},{9,5},{10,... | collective-permute-start | bytes 3538952 | tf_op jit(solution)/shard_map/ppermute | solution.py:526
  43.3 30.2 %collective-permute-start.9 = (bf16[2,384,768]{2,1,0:T(8,128)(2,1)S(1)}, bf16[2,384,768]{2,1,0:T(8,128)(2,1)S(1)}, u32[]{:S(2)}, u32[]{:S(2)}) collective-permute-start(bf16[2,384,768]{2,1,0:T(8,128)(2,1)S(1)} %collective-permute-done.key.value), channel_id=1, source_target_pairs={{0,4},{1,5},{2,6},{3,7},{4,0},{5,1},{6,2},{7,3},{8,12},{9,13},{10,... | collective-permute-start | bytes 3538952 | tf_op jit(solution)/shard_map/ppermute | solution.py:526
  58.9 28.2 %collective-permute-start.15 = (bf16[384,768]{1,0:T(8,128)(2,1)S(1)}, bf16[384,768]{1,0:T(8,128)(2,1)S(1)}, u32[]{:S(2)}, u32[]{:S(2)}) collective-permute-start(bf16[384,768]{1,0:T(8,128)(2,1)S(1)} %get-tuple-element.54), channel_id=1, source_target_pairs={{0,4},{1,5},{2,6},{3,7},{4,0},{5,1},{6,2},{7,3},{8,12},{9,13},{10,... | collective-permute-start | bytes 1769480 | tf_op jit(solution)/shard_map/ppermute | solution.py:526
  59.0 28.1 %collective-permute-start.16 = (bf16[384,768]{1,0:T(8,128)(2,1)S(1)}, bf16[384,768]{1,0:T(8,128)(2,1)S(1)}, u32[]{:S(2)}, u32[]{:S(2)}) collective-permute-start(bf16[384,768]{1,0:T(8,128)(2,1)S(1)} %get-tuple-element.55), channel_id=1, source_target_pairs={{0,1},{1,0},{2,3},{3,2},{4,8},{5,9},{6,10},{7,11},{8,4},{9,5},{10,... | collective-permute-start | bytes 1769480 | tf_op jit(solution)/shard_map/ppermute | solution.py:526
  68.4 47.5 %collective-permute-start.14 = (bf16[2,384,384]{2,1,0:T(8,128)(2,1)S(1)}, bf16[2,384,384]{2,1,0:T(8,128)(2,1)S(1)}, u32[]{:S(2)}, u32[]{:S(2)}) collective-permute-start(bf16[2,384,384]{2,1,0:T(8,128)(2,1)S(1)} %get-tuple-element.45), channel_id=1, source_target_pairs={{0,16},{16,0},{1,17},{17,1},{2,18},{18,2},{3,19},{19,3},{4,20},{20... | collective-permute-start | bytes 1769480 | tf_op jit(solution)/shard_map/ppermute | solution.py:545
  69.9 24.6 %collective-permute-start.13 = (bf16[2,384,384]{2,1,0:T(8,128)(2,1)S(1)}, bf16[2,384,384]{2,1,0:T(8,128)(2,1)S(1)}, u32[]{:S(2)}, u32[]{:S(2)}) collective-permute-start(bf16[2,384,384]{2,1,0:T(8,128)(2,1)S(1)} %get-tuple-element.51), channel_id=1, source_target_pairs={{0,16},{16,0},{1,17},{17,1},{2,18},{18,2},{3,19},{19,3},{4,20},{20... | collective-permute-start | bytes 1769480 | tf_op jit(solution)/shard_map/ppermute | solution.py:545
  87.1 7.4 %collective-permute-start.17 = (f32[2,128]{1,0:T(2,128)S(1)}, f32[2,128]{1,0:T(2,128)S(1)}, u32[]{:S(2)}, u32[]{:S(2)}) collective-permute-start(f32[2,128]{1,0:T(2,128)S(1)} %slice.9), channel_id=1, source_target_pairs={{0,16},{16,0},{1,17},{17,1},{2,18},{18,2},{3,19},{19,3},{4,20},{20... | collective-permute-start | bytes 3080 | tf_op jit(solution)/shard_map/ppermute | solution.py:545
  88.7 27.3 %collective-permute-start.11 = (bf16[2,384,768]{2,1,0:T(8,128)(2,1)S(1)}, bf16[2,384,768]{2,1,0:T(8,128)(2,1)S(1)}, u32[]{:S(2)}, u32[]{:S(2)}) collective-permute-start(bf16[2,384,768]{2,1,0:T(8,128)(2,1)S(1)} %get-tuple-element.49), channel_id=1, source_target_pairs={{0,4},{1,5},{2,6},{3,7},{4,0},{5,1},{6,2},{7,3},{8,12},{9,13},{10,... | collective-permute-start | bytes 3538952 | tf_op jit(solution)/shard_map/ppermute | solution.py:526
  90.7 25.2 %collective-permute-start.12 = (bf16[2,384,768]{2,1,0:T(8,128)(2,1)S(1)}, bf16[2,384,768]{2,1,0:T(8,128)(2,1)S(1)}, u32[]{:S(2)}, u32[]{:S(2)}) collective-permute-start(bf16[2,384,768]{2,1,0:T(8,128)(2,1)S(1)} %get-tuple-element.50), channel_id=1, source_target_pairs={{0,1},{1,0},{2,3},{3,2},{4,8},{5,9},{6,10},{7,11},{8,4},{9,5},{10,... | collective-permute-start | bytes 3538952 | tf_op jit(solution)/shard_map/ppermute | solution.py:526
  94.5 21.4 %collective-permute-start.18 = (bf16[384,768]{1,0:T(8,128)(2,1)S(1)}, bf16[384,768]{1,0:T(8,128)(2,1)S(1)}, u32[]{:S(2)}, u32[]{:S(2)}) collective-permute-start(bf16[384,768]{1,0:T(8,128)(2,1)S(1)} %shard_map.87), channel_id=1, source_target_pairs={{0,16},{16,0},{1,17},{17,1},{2,18},{18,2},{3,19},{19,3},{4,20},{20... | collective-permute-start | bytes 1769480 | tf_op jit(solution)/shard_map/ppermute | solution.py:545
  96.0 1.1 collective-permute-start.19
  97.2 3.6 %collective-permute-start.20 = (f32[2,128]{1,0:T(2,128)S(1)}, f32[2,128]{1,0:T(2,128)S(1)}, u32[]{:S(2)}, u32[]{:S(2)}) collective-permute-start(f32[2,128]{1,0:T(2,128)S(1)} %add.20), channel_id=1, source_target_pairs={{0,2},{1,3},{2,0},{3,1},{4,6},{5,7},{6,4},{7,5},{8,10},{9,11},{10,... | collective-permute-start | bytes 3080 | tf_op jit(solution)/shard_map/ppermute | solution.py:552
  100.7 12.2 %collective-permute-start.21 = (f32[2,128]{1,0:T(2,128)S(1)}, f32[2,128]{1,0:T(2,128)S(1)}, u32[]{:S(2)}, u32[]{:S(2)}) collective-permute-start(f32[2,128]{1,0:T(2,128)S(1)} %add.21), channel_id=1, source_target_pairs={{0,4},{4,0},{8,12},{12,8},{1,5},{5,1},{9,13},{13,9},{2,6},{6,2},{1... | collective-permute-start | bytes 3080 | tf_op jit(solution)/shard_map/ppermute | solution.py:552
  112.9 6.5 %collective-permute-start.22 = (f32[2,128]{1,0:T(2,128)S(1)}, f32[2,128]{1,0:T(2,128)S(1)}, u32[]{:S(2)}, u32[]{:S(2)}) collective-permute-start(f32[2,128]{1,0:T(2,128)S(1)} %add.22), channel_id=1, source_target_pairs={{0,8},{4,12},{8,0},{12,4},{1,9},{5,13},{9,1},{13,5},{2,10},{6,14},... | collective-permute-start | bytes 3080 | tf_op jit(solution)/shard_map/ppermute | solution.py:552

commit v8 on v7

--- a/solution.py
+++ b/solution.py
@@ -13,7 +13,9 @@
 EPSILON = 1e-06
 ROOT_SCALE = HEAD_DIM ** (-0.5)
 EXP2_SCALE = ROOT_SCALE * math.log2(math.e)
-GROUPS = ((0, 3, False), (3, 3, False), (6, 6, True))
+QUERY_GROUPS = ((0, 3), (3, 2))
+KEY_GROUP = (5, 2)
+AWAY_GROUP = (7, 5)
 MAIN_VMEM = 20 * 1024 * 1024
 SMALL_VMEM = 12 * 1024 * 1024
 PACK_VMEM = 4 * 1024 * 1024
@@ -268,7 +270,7 @@
     gain_out[1:2, :] += jnp.sum(key_grad * key_normed, axis=0, keepdims=True)
 
 
-def answer_kernel(info, query, own, from_even, from_odd, out):
+def answer_kernel(info, query, own, from_even, from_odd, _, out):
     gain = info[0:1, :]
     floats, scaled, _, _ = normalize(query[...], gain)
     total = own[...] + from_even[...].astype(jnp.float32) + from_odd[...].astype(jnp.float32)
@@ -282,6 +284,12 @@
     key_grad = own[0] + from_even[0].astype(jnp.float32) + from_odd[0].astype(jnp.float32)
     value_grad = own[1] + from_even[1].astype(jnp.float32) + from_odd[1].astype(jnp.float32)
     return norm_back(key_grad, key_floats, key_scale, key_gain), value_grad
+
+
+def finish_kernel(info, key, own, from_even, from_odd, out):
+    key_grad, value_grad = finished(info, key, own, from_even, from_odd)
+    out[0] = key_grad.astype(out.dtype)
+    out[1] = value_grad.astype(out.dtype)
 
 
 def last_kernel(info, key, own, from_even, from_odd, *rest, places, first, count):
@@ -398,7 +406,7 @@
     return pl.BlockSpec((2, 16, HEAD_DIM), lambda head: (0, below, 0))
 
 
-def main_call(info, operands, pair_even, pair_odd, count):
+def main_call(info, operands, pair_even, pair_odd, count, heads, place):
     rows = pair_even.shape[1]
     lanes = count * HEAD_DIM
     return pl.pallas_call(
@@ -407,9 +415,9 @@
         in_specs=[info_block(info)]
         + [head_block(rows, first, slot) for _, first, slot in operands]
         + [pair_block(rows)] * 2,
-        out_specs=[head_block(rows, 0)] + [pair_block(rows)] * 3 + [whole_block((8, HEAD_DIM))],
+        out_specs=[head_block(rows, place)] + [pair_block(rows)] * 3 + [whole_block((8, HEAD_DIM))],
         out_shape=[
-            jax.ShapeDtypeStruct((rows, lanes), jnp.bfloat16),
+            jax.ShapeDtypeStruct((rows, heads * HEAD_DIM), jnp.bfloat16),
             jax.ShapeDtypeStruct((2, rows, lanes), jnp.float32),
             jax.ShapeDtypeStruct((2, rows, lanes), jnp.bfloat16),
             jax.ShapeDtypeStruct((2, rows, lanes), jnp.bfloat16),
@@ -418,6 +426,20 @@
         compiler_params=pltpu.CompilerParams(vmem_limit_bytes=MAIN_VMEM),
         cost_estimate=MAIN_COST,
     )(info, *[array for array, _, _ in operands], pair_even, pair_odd)
+
+
+def finish_call(info, key, own, from_even, from_odd, count):
+    array, first, slot = key
+    rows = own.shape[1]
+    return pl.pallas_call(
+        finish_kernel,
+        grid=(count,),
+        in_specs=[info_block(info), head_block(rows, first, slot)] + [pair_block(rows)] * 3,
+        out_specs=pair_block(rows),
+        out_shape=jax.ShapeDtypeStruct((2, rows, count * HEAD_DIM), jnp.bfloat16),
+        compiler_params=pltpu.CompilerParams(vmem_limit_bytes=SMALL_VMEM),
+        cost_estimate=COST,
+    )(info, array, own, from_even, from_odd)
 
 
 def row_block(rows, first):
@@ -456,31 +478,36 @@
         + [pair_block(rows)] * 2
         + [row_block(rows, first)] * len(sums)
         + [pl.BlockSpec(memory_space=pl.ANY)] * len(earlier),
-        out_specs=[pair_block(rows)] + [head_block(rows, first)] * 3 + [whole_block((8, HEAD_DIM))],
+        out_specs=[pair_block(rows, first)]
+        + [head_block(rows, first)] * 3
+        + [whole_block((8, HEAD_DIM))],
         out_shape=[
-            jax.ShapeDtypeStruct((2, rows, count * HEAD_DIM), jnp.bfloat16),
+            jax.ShapeDtypeStruct((2, rows, lanes), jnp.bfloat16),
             jax.ShapeDtypeStruct((rows, lanes), jnp.float32),
             jax.ShapeDtypeStruct((rows, lanes), jnp.bfloat16),
             jax.ShapeDtypeStruct((rows, lanes), jnp.bfloat16),
             jax.ShapeDtypeStruct((8, HEAD_DIM), jnp.float32),
         ],
-        input_output_aliases={place + index: 1 + index for index in range(len(earlier))},
+        input_output_aliases={place + index: index for index in range(len(earlier))},
         compiler_params=pltpu.CompilerParams(vmem_limit_bytes=MAIN_VMEM),
         cost_estimate=MAIN_COST,
     )(info, *arrays, pair_even, pair_odd, *sums, *earlier)
 
 
-def answer_call(info, query, own, from_even, from_odd, first, count):
-    rows = own.shape[0]
+def answer_call(info, query, own, from_even, from_odd, low):
+    rows, lanes = own.shape
     return pl.pallas_call(
         answer_kernel,
-        grid=(count,),
-        in_specs=[info_block(info), head_block(rows, first)] + [head_block(rows, 0)] * 3,
+        grid=(lanes // HEAD_DIM,),
+        in_specs=[info_block(info)]
+        + [head_block(rows, 0)] * 4
+        + [pl.BlockSpec(memory_space=pl.ANY)],
         out_specs=head_block(rows, 0),
-        out_shape=jax.ShapeDtypeStruct((rows, count * HEAD_DIM), jnp.bfloat16),
+        out_shape=jax.ShapeDtypeStruct(low.shape, low.dtype),
+        input_output_aliases={5: 0},
         compiler_params=pltpu.CompilerParams(vmem_limit_bytes=SMALL_VMEM),
         cost_estimate=LONG_COST,
-    )(info, query, own, from_even, from_odd)
+    )(info, query, own, from_even, from_odd, low)
 
 
 def last_call(info, key, own, from_even, from_odd, pieces, places, first, count):
@@ -559,49 +586,62 @@
     query, key, value, grad = (a[0, 0, 0] for a in (queries, keys, values, grad_out))
     rows = query.shape[0]
     seq_count = lax.axis_size("seq")
-    *home, (away_first, away_count, _) = GROUPS
-    home_heads = sum(count for _, count, _ in home)
+    key_first, key_count = KEY_GROUP
+    away_first, away_count = AWAY_GROUP
     fars = far_partners(seq_count)
-    asks = [pack_call(query, grad, *home[0][:2])]
+    arrays = (query, grad, key, value)
+    asks = [pack_call(query, grad, *QUERY_GROUPS[0])]
     away_pair = pack_call(after(key, asks[0]), value, away_first, away_count)
-    for first, count, _ in home[1:]:
+    for first, count in QUERY_GROUPS[1:]:
         asks.append(pack_call(after(query, away_pair), grad, first, count))
-    asked_home = [(exchanged(ask, 0), exchanged(ask, 1)) for ask in asks]
+    told_pairs = [(exchanged(ask, 0), exchanged(ask, 1)) for ask in asks]
+    key_pair = pack_call(after(key, asks[-1]), value, key_first, key_count)
+    key_pair = after(key_pair, *told_pairs[0])
+    key_pairs = (exchanged(key_pair, 0), exchanged(key_pair, 1))
     info = info_call(kv_tiles[0, 0, 0], after(norm_gains[0], asks[-1]))
     away_pair = turned(away_pair, -1)
-    arrays = (query, grad, key, value)
     sums = None
-    for (first, count, _), ask in zip(home, asked_home):
-        sums = sums_call(info, arrays, *ask, first, count, home_heads, sums, len(fars))
+    for (first, count), told in zip(QUERY_GROUPS, told_pairs):
+        sums = sums_call(info, arrays, *told, first, count, key_first, sums, len(fars))
+    received = [exchanged(sums[0], 0), exchanged(sums[1], 1)]
+    received += [
+        paired(after(value, away_pair), partners) for value, partners in zip(sums[2:], fars)
+    ]
+    all_sums = (*sums[:2], *received)
     asked = ask_call(info, after(query, away_pair, sums[0]), grad, away_first, away_count)
     asked = turned(asked, -1)
-    received = [exchanged(sums[0], 0), exchanged(sums[1], 1)]
-    received += [paired(value, partners) for value, partners in zip(sums[2:], fars)]
-    all_sums = (*sums[:2], *received)
-    away_pair = after(away_pair, *received)
-    away_gathered = (exchanged(away_pair, 0), exchanged(away_pair, 1))
-    gains, pieces, places = [], [], []
-    parts = None
-    for (first, count, _), ask in zip(home[::-1], asked_home[::-1]):
-        pair_low, *parts, gain = grads_call(
-            info, arrays, *ask, all_sums, first, count, home_heads, parts, len(fars)
+    away_sent = after(away_pair, *key_pairs)
+    away_pairs = (exchanged(away_sent, 0), exchanged(away_sent, 1))
+    gains, parts = [], None
+    for (first, count), told in zip(QUERY_GROUPS, told_pairs):
+        *parts, gain = grads_call(
+            info, arrays, *told, all_sums, first, count, key_first, parts, len(fars)
         )
         gains.append(gain[:2])
-        pieces.append(turned(pair_low, -1))
-        places.append((slice(1, 3), first * HEAD_DIM))
-    answer = (parts[0], exchanged(parts[1], 0), exchanged(parts[2], 1))
-    asked = after(asked, pair_low)
+    pair_low, own, to_even, to_odd = parts
+    pieces = [turned(pair_low, -1)]
+    places = [(slice(1, 3), 0)]
+    answer = (own, exchanged(to_even, 0), exchanged(to_odd, 1))
+    operands = [(array, key_first, None) for array in arrays]
+    low, own, to_even, to_odd, gain = main_call(
+        after(info, pair_low), operands, *key_pairs, key_count, away_first, key_first
+    )
+    gains.append(gain[:2])
+    key_answer = (own, exchanged(to_even, 0), exchanged(to_odd, 1))
     operands = [(asked, 0, 0), (asked, 0, 1), (away_pair, 0, 0), (away_pair, 0, 1)]
     query_low, own, to_even, to_odd, gain = main_call(
-        asked, operands, *away_gathered, away_count
-    )
-    gains.append(turned(after(gain[:2], *answer[1:]), 1))
+        after(asked, low), operands, *away_pairs, away_count, away_count, 0
+    )
+    gains.append(turned(after(gain[:2], *answer[1:], pieces[0]), 1))
     returned = (exchanged(to_even, 0), exchanged(to_odd, 1))
     pieces.append(query_low)
     places.append((0, away_first * HEAD_DIM))
-    answer = answer_call(info, query, *answer, 0, home_heads)
-    pieces.append(turned(after(answer, gains[-1], pieces[0]), -1))
+    low = answer_call(info, query, *answer, low)
+    pieces.append(turned(after(low, gains[-1], pieces[0]), -1))
     places.append((0, 0))
+    low = finish_call(after(info, pieces[0]), (key, key_first, None), *key_answer, key_count)
+    pieces.append(turned(low, -1))
+    places.append((slice(1, 3), key_first * HEAD_DIM))
     out = last_call(
         asked, operands[2], own, *returned, pieces, tuple(places), away_first, away_count
     )

time: 120 us -> 117 us (0.975); the launches traced: 120 us -> 115 us
  waiting for transfers between devices: 46 us -> 42.4 us
    ppermute x13 -> x17, waiting for transfers between devices: 21.8 us -> 15.3 us  [paired(): return lax.ppermute(value, ('seq', 'dp'), pairs)]
    ppermute x6, waiting for transfers between devices: 11.5 us -> 17.7 us  [turned(): lax.ppermute(value, 'pipe', [(i, (i + step) % count) for i in range(count)])]
    ppermute x4, waiting for transfers between devices: 12.7 us -> 9.45 us  [total_over(): other = lax.ppermute(value, axis, [(i, i ^ step) for i in range(count)])]
    ppermute x13 -> x17, starting transfers between devices: 15.6 us -> 18.7 us  [paired(): return lax.ppermute(value, ('seq', 'dp'), pairs)]
    ppermute x4, starting transfers between devices: 7.22 us -> 4.5 us  [total_over(): other = lax.ppermute(value, axis, [(i, i ^ step) for i in range(count)])]
    pallas_call x1 -> x2, Pallas kernels: 13.6 us -> 15.9 us  [main_call(): pl.pallas_call(main_kernel, grid=(count,), in_specs=[info_block(info)] +...]
    pallas_call x2, Pallas kernels: 12.3 us -> 10.3 us  [grads_call(): pl.pallas_call(functools.partial(grads_kernel, far_count=far_count), grid...]
  transfers between devices with their start and end apart: 23 -> 27, of which waited for: 9 -> 10; matrix products, arithmetic and copies ran while one was open for 0% -> 0% of each run, Pallas kernels for 31% -> 32%
where the time goes in v8:
time: 117 us; the launch traced here: 115 us
  waiting for transfers between devices  42.4 us (36%)
  Pallas kernels  37.5 us (32%)
  starting transfers between devices  30.4 us (26%)
  local copies, waits for them, and re-layouts  3.71 us (3%)
    ppermute x17, starting transfers between devices, paired(): return lax.ppermute(value, ('seq', 'dp'), pairs)  18.7 us
    ppermute x6, waiting for transfers between devices, turned(): lax.ppermute(value, 'pipe', [(i, (i + step) % count) for i in range(count)])  17.7 us
    pallas_call x2, Pallas kernels, main_call(): pl.pallas_call(main_kernel, grid=(count,), in_specs=[info_block(info)] +...  15.9 us
    ppermute x17, waiting for transfers between devices, paired(): return lax.ppermute(value, ('seq', 'dp'), pairs)  15.3 us
    pallas_call x2, Pallas kernels, grads_call(): pl.pallas_call(functools.partial(grads_kernel, far_count=far_count), grid...  10.3 us
    ppermute x4, waiting for transfers between devices, total_over(): other = lax.ppermute(value, axis, [(i, i ^ step) for i in range(count)])  9.45 us
    ppermute x6, starting transfers between devices, turned(): lax.ppermute(value, 'pipe', [(i, (i + step) % count) for i in range(count)])  7.22 us
    pallas_call x2, Pallas kernels, sums_call(): pl.pallas_call(functools.partial(sums_kernel, far_count=far_count), grid=...  4.62 us
  transfers between devices with their start and end apart: 27, of which 10 were waited for; matrix products, arithmetic and copies ran while one was open for 0% of the time, Pallas kernels for 32%

profile of v8, /device:TPU:0, one launch (start us, length us, event | category | flops | bytes accessed | tf_op | source)
XLA Modules:
  0.0 115.5 jit_solution(7663735026873746216)
XLA Ops:
  0.6 1.3 %copy-done.1 = bf16[1,1,1,384,1536]{4,3,2,1,0:T(8,128)(2,1)S(1)} copy-done((bf16[1,1,1,384,1536]{4,3,2,1,0:T(8,128)(2,1)S(1)}, bf16[1,1,1,384,1536]{4,3,2,1,0:T(8,128)(2,1)}, u32[]{:S(2)}) %copy-start.1) | copy-done | bytes 1179672
  1.9 1.3 %copy-done.3 = bf16[1,1,1,384,1536]{4,3,2,1,0:T(8,128)(2,1)S(1)} copy-done((bf16[1,1,1,384,1536]{4,3,2,1,0:T(8,128)(2,1)S(1)}, bf16[1,1,1,384,1536]{4,3,2,1,0:T(8,128)(2,1)}, u32[]{:S(2)}) %copy-start.3) | copy-done | bytes 1179672
  3.8 4.1 %collective-permute-start.3 = (bf16[2,384,384]{2,1,0:T(8,128)(2,1)S(1)}, bf16[2,384,384]{2,1,0:T(8,128)(2,1)S(1)}, u32[]{:S(2)}, u32[]{:S(2)}) collective-permute-start(bf16[2,384,384]{2,1,0:T(8,128)(2,1)S(1)} %shard_map.77), channel_id=1, source_target_pairs={{0,4},{1,5},{2,6},{3,7},{4,0},{5,1},{6,2},{7,3},{8,12},{9,13},{10,... | collective-permute-start | bytes 1769480 | tf_op jit(solution)/shard_map/ppermute | solution.py:553
  9.4 1.6 %collective-permute-start.1 = (bf16[2,384,256]{2,1,0:T(8,128)(2,1)S(1)}, bf16[2,384,256]{2,1,0:T(8,128)(2,1)S(1)}, u32[]{:S(2)}, u32[]{:S(2)}) collective-permute-start(bf16[2,384,256]{2,1,0:T(8,128)(2,1)S(1)} %shard_map.79), channel_id=1, source_target_pairs={{0,4},{1,5},{2,6},{3,7},{4,0},{5,1},{6,2},{7,3},{8,12},{9,13},{10,... | collective-permute-start | bytes 1179656 | tf_op jit(solution)/shard_map/ppermute | solution.py:553
  11.0 1.5 %collective-permute-start = (bf16[2,384,640]{2,1,0:T(8,128)(2,1)S(1)}, bf16[2,384,640]{2,1,0:T(8,128)(2,1)S(1)}, u32[]{:S(2)}, u32[]{:S(2)}) collective-permute-start(bf16[2,384,640]{2,1,0:T(8,128)(2,1)S(1)} %shard_map.78), channel_id=1, source_target_pairs={{0,16},{16,0},{1,17},{17,1},{2,18},{18,2},{3,19},{19,3},{4,20},{20... | collective-permute-start | bytes 2949128 | tf_op jit(solution)/shard_map/ppermute | solution.py:572
  13.1 9.0 %collective-permute-done.3.pair_even = bf16[2,384,384]{2,1,0:T(8,128)(2,1)S(1)} collective-permute-done((bf16[2,384,384]{2,1,0:T(8,128)(2,1)S(1)}, bf16[2,384,384]{2,1,0:T(8,128)(2,1)S(1)}, u32[]{:S(2)}, u32[]{:S(2)}) %collective-permute-start.3) | collective-permute-done | bytes 589856 | tf_op jit(solution)/shard_map/ppermute | solution.py:553
  22.1 2.5 %collective-permute-start.9 = (bf16[2,384,256]{2,1,0:T(8,128)(2,1)S(1)}, bf16[2,384,256]{2,1,0:T(8,128)(2,1)S(1)}, u32[]{:S(2)}, u32[]{:S(2)}) collective-permute-start(bf16[2,384,256]{2,1,0:T(8,128)(2,1)S(1)} %shard_map.86), channel_id=1, source_target_pairs={{0,4},{1,5},{2,6},{3,7},{4,0},{5,1},{6,2},{7,3},{8,12},{9,13},{10,... | collective-permute-start | bytes 1179656 | tf_op jit(solution)/shard_map/ppermute | solution.py:553
  24.6 2.8 %shard_map.81 = (f32[40,384]{1,0:T(8,128)S(1)}, f32[40,384]{1,0:T(8,128)S(1)}, f32[40,384]{1,0:T(8,128)S(1)}) custom-call(f32[8,128]{1,0:T(8,128)S(1)} %shard_map.80.info, bf16[384,1536]{1,0:T(8,128)(2,1)S(1)} %bitcast.29, bf16[384,1536]{1,0:T(8,128)(2,1)S(1)} %bitcast.21, bf16[384,1536]{1,0:T(8,128)(2,1)S(1)} %bitcast.13, bf16[384,1536]{1,0:T(8,128)(2,1)S(1)} %bitcast.38, ...), custom_call_target="tpu_custom_call" | custom-call | flops 6000000000 | bytes 1 | tf_op jit(solution)/shard_map/pallas_call | solution.py:453
  27.4 3.2 %collective-permute-done.1.pair_even = bf16[2,384,256]{2,1,0:T(8,128)(2,1)S(1)} collective-permute-done((bf16[2,384,256]{2,1,0:T(8,128)(2,1)S(1)}, bf16[2,384,256]{2,1,0:T(8,128)(2,1)S(1)}, u32[]{:S(2)}, u32[]{:S(2)}) %collective-permute-start.1) | collective-permute-done | bytes 393248 | tf_op jit(solution)/shard_map/ppermute | solution.py:553
  30.6 1.9 %shard_map.82 = (f32[40,384]{1,0:T(8,128)S(1)}, f32[40,384]{1,0:T(8,128)S(1)}, f32[40,384]{1,0:T(8,128)S(1)}) custom-call(f32[8,128]{1,0:T(8,128)S(1)} %shard_map.80.info, bf16[384,1536]{1,0:T(8,128)(2,1)S(1)} %bitcast.30, bf16[384,1536]{1,0:T(8,128)(2,1)S(1)} %bitcast.22, ...), custom_call_target="tpu_custom_call", output_to_operand_aliasing={{0}: (7, {}), {1}: (8, {}), {2}: (9, {})} | custom-call | flops 6000000000 | bytes 1 | tf_op jit(solution)/shard_map/pallas_call | solution.py:453
  32.5 2.5 %collective-permute-start.6 = (f32[40,384]{1,0:T(8,128)S(1)}, f32[40,384]{1,0:T(8,128)S(1)}, u32[]{:S(2)}, u32[]{:S(2)}) collective-permute-start(f32[40,384]{1,0:T(8,128)S(1)} %get-tuple-element.48.sent_even), channel_id=1, source_target_pairs={{0,4},{1,5},{2,6},{3,7},{4,0},{5,1},{6,2},{7,3},{8,12},{9,13},{10,... | collective-permute-start | bytes 184328 | tf_op jit(solution)/shard_map/ppermute | solution.py:553
  36.0 3.1 %collective-permute-done.9.pair_even = bf16[2,384,256]{2,1,0:T(8,128)(2,1)S(1)} collective-permute-done((bf16[2,384,256]{2,1,0:T(8,128)(2,1)S(1)}, bf16[2,384,256]{2,1,0:T(8,128)(2,1)S(1)}, u32[]{:S(2)}, u32[]{:S(2)}) %collective-permute-start.9) | collective-permute-done | bytes 393248 | tf_op jit(solution)/shard_map/ppermute | solution.py:553
  39.1 2.4 %collective-permute-start.11 = (bf16[2,384,640]{2,1,0:T(8,128)(2,1)S(1)}, bf16[2,384,640]{2,1,0:T(8,128)(2,1)S(1)}, u32[]{:S(2)}, u32[]{:S(2)}) collective-permute-start(bf16[2,384,640]{2,1,0:T(8,128)(2,1)S(1)} %collective-permute-done.key.value), channel_id=1, source_target_pairs={{0,4},{1,5},{2,6},{3,7},{4,0},{5,1},{6,2},{7,3},{8,12},{9,13},{10,... | collective-permute-start | bytes 2949128 | tf_op jit(solution)/shard_map/ppermute | solution.py:553
  41.6 1.6 %collective-permute-start.5 = (bf16[2,400,640]{2,1,0:T(8,128)(2,1)S(1)}, bf16[2,400,640]{2,1,0:T(8,128)(2,1)S(1)}, u32[]{:S(2)}, u32[]{:S(2)}) collective-permute-start(bf16[2,400,640]{2,1,0:T(8,128)(2,1)S(1)} %shard_map.83), channel_id=1, source_target_pairs={{0,16},{16,0},{1,17},{17,1},{2,18},{18,2},{3,19},{19,3},{4,20},{20... | collective-permute-start | bytes 3072008 | tf_op jit(solution)/shard_map/ppermute | solution.py:572
  43.2 6.1 %shard_map.84 = (bf16[2,384,640]{2,1,0:T(8,128)(2,1)S(1)}, f32[384,640]{1,0:T(8,128)S(1)}, bf16[384,640]{1,0:T(8,128)(2,1)S(1)}, bf16[384,640]{1,0:T(8,128)(2,1)S(1)}, f32[8,128]{1,0:T(8,128)S(1)}) custom-call(f32[8,128]{1,0:T(8,128)S(1)} %shard_map.80.info, bf16[384,1536]{1,0:T(8,128)(2,1)S(1)} %bitcast.32, bf16[384,1536]{1,0:T(8,128)(2,1)S(1)} %bitcast.24, ...), custom_call_target="tpu_custom_call" | custom-call | flops 6000000000 | bytes 1 | tf_op jit(solution)/shard_map/pallas_call | solution.py:473
  49.3 4.1 %shard_map.85 = (bf16[2,384,640]{2,1,0:T(8,128)(2,1)S(1)}, f32[384,640]{1,0:T(8,128)S(1)}, bf16[384,640]{1,0:T(8,128)(2,1)S(1)}, bf16[384,640]{1,0:T(8,128)(2,1)S(1)}, f32[8,128]{1,0:T(8,128)S(1)}) custom-call(f32[8,128]{1,0:T(8,128)S(1)} %shard_map.80.info, ...), custom_call_target="tpu_custom_call", output_to_operand_aliasing={{0}: (12, {}), {1}: (13, {}), {2}: (14, {}), {3}: (15, {})} | custom-call | flops 6000000000 | bytes 1 | tf_op jit(solution)/shard_map/pallas_call | solution.py:473
  54.4 4.5 %shard_map.87 = (bf16[384,896]{1,0:T(8,128)(2,1)S(1)}, f32[2,384,256]{2,1,0:T(8,128)S(1)}, bf16[2,384,256]{2,1,0:T(8,128)(2,1)S(1)}, bf16[2,384,256]{2,1,0:T(8,128)(2,1)S(1)}, f32[8,128]{1,0:T(8,128)S(1)}) custom-call(f32[8,128]{1,0:T(8,128)S(1)} %shard_map.80.info, bf16[384,1536]{1,0:T(8,128)(2,1)S(1)} %bitcast.34, bf16[384,1536]{1,0:T(8,128)(2,1)S(1)} %bitcast.26, ...), custom_call_target="tpu_custom_call" | custom-call | flops 6000000000 | bytes 1 | tf_op jit(solution)/shard_map/pallas_call | solution.py:412
  58.9 8.3 %collective-permute-done.5.info.query.grad = bf16[2,400,640]{2,1,0:T(8,128)(2,1)S(1)} collective-permute-done((bf16[2,400,640]{2,1,0:T(8,128)(2,1)S(1)}, bf16[2,400,640]{2,1,0:T(8,128)(2,1)S(1)}, u32[]{:S(2)}, u32[]{:S(2)}) %collective-permute-start.5) | collective-permute-done | bytes 1024032 | tf_op jit(solution)/shard_map/ppermute | solution.py:572
  67.2 1.7 %collective-permute-start.20 = (bf16[2,384,256]{2,1,0:T(8,128)(2,1)S(1)}, bf16[2,384,256]{2,1,0:T(8,128)(2,1)S(1)}, u32[]{:S(2)}, u32[]{:S(2)}) collective-permute-start(bf16[2,384,256]{2,1,0:T(8,128)(2,1)S(1)} %get-tuple-element.76), channel_id=1, source_target_pairs={{0,4},{1,5},{2,6},{3,7},{4,0},{5,1},{6,2},{7,3},{8,12},{9,13},{10,... | collective-permute-start | bytes 1179656 | tf_op jit(solution)/shard_map/ppermute | solution.py:553
  68.9 11.3 %shard_map.88 = (bf16[384,640]{1,0:T(8,128)(2,1)S(1)}, f32[2,384,640]{2,1,0:T(8,128)S(1)}, bf16[2,384,640]{2,1,0:T(8,128)(2,1)S(1)}, bf16[2,384,640]{2,1,0:T(8,128)(2,1)S(1)}, f32[8,128]{1,0:T(8,128)S(1)}) custom-call(bf16[2,400,640]{2,1,0:T(8,128)(2,1)S(1)} %collective-permute-done.5.info.query.grad, ...), custom_call_target="tpu_custom_call" | custom-call | flops 6000000000 | bytes 1 | tf_op jit(solution)/shard_map/pallas_call | solution.py:412
  80.3 1.9 %collective-permute-start.13 = (bf16[2,384,640]{2,1,0:T(8,128)(2,1)S(1)}, bf16[2,384,640]{2,1,0:T(8,128)(2,1)S(1)}, u32[]{:S(2)}, u32[]{:S(2)}) collective-permute-start(bf16[2,384,640]{2,1,0:T(8,128)(2,1)S(1)} %get-tuple-element.65), channel_id=1, source_target_pairs={{0,4},{1,5},{2,6},{3,7},{4,0},{5,1},{6,2},{7,3},{8,12},{9,13},{10,... | collective-permute-start | bytes 2949128 | tf_op jit(solution)/shard_map/ppermute | solution.py:553
  82.2 3.3 %collective-permute-done.15.rest_0_ = bf16[2,384,640]{2,1,0:T(8,128)(2,1)S(1)} collective-permute-done((bf16[2,384,640]{2,1,0:T(8,128)(2,1)S(1)}, bf16[2,384,640]{2,1,0:T(8,128)(2,1)S(1)}, u32[]{:S(2)}, u32[]{:S(2)}) %collective-permute-start.15) | collective-permute-done | bytes 983072 | tf_op jit(solution)/shard_map/ppermute | solution.py:572
  85.4 1.5 %collective-permute-start.18 = (f32[2,128]{1,0:T(2,128)S(1)}, f32[2,128]{1,0:T(2,128)S(1)}, u32[]{:S(2)}, u32[]{:S(2)}) collective-permute-start(f32[2,128]{1,0:T(2,128)S(1)} %slice.12), channel_id=1, source_target_pairs={{0,16},{16,0},{1,17},{17,1},{2,18},{18,2},{3,19},{19,3},{4,20},{20... | collective-permute-start | bytes 3080 | tf_op jit(solution)/shard_map/ppermute | solution.py:572
  86.9 1.4 %shard_map.89 = bf16[384,896]{1,0:T(8,128)(2,1)S(1)} custom-call(f32[8,128]{1,0:T(8,128)S(1)} %shard_map.80.info, bf16[384,1536]{1,0:T(8,128)(2,1)S(1)} %bitcast.35, f32[384,640]{1,0:T(8,128)S(1)} %get-tuple-element.68.own, bf16[384,640]{1,0:T(8,128)(2,1)S(1)} %collective-permute-done.16.from_even, ...), custom_call_target="tpu_custom_call", output_to_operand_aliasing={{}: (5, {})} | custom-call | flops 20000000000 | bytes 1 | tf_op jit(solution)/shard_map/pallas_call | solution.py:499
  89.0 1.5 %collective-permute-start.19 = (bf16[384,896]{1,0:T(8,128)(2,1)S(1)}, bf16[384,896]{1,0:T(8,128)(2,1)S(1)}, u32[]{:S(2)}, u32[]{:S(2)}) collective-permute-start(bf16[384,896]{1,0:T(8,128)(2,1)S(1)} %shard_map.89), channel_id=1, source_target_pairs={{0,16},{16,0},{1,17},{17,1},{2,18},{18,2},{3,19},{19,3},{4,20},{20... | collective-permute-start | bytes 2064392 | tf_op jit(solution)/shard_map/ppermute | solution.py:572
  93.0 1.5 %collective-permute-start.24 = (f32[2,128]{1,0:T(2,128)S(1)}, f32[2,128]{1,0:T(2,128)S(1)}, u32[]{:S(2)}, u32[]{:S(2)}) collective-permute-start(f32[2,128]{1,0:T(2,128)S(1)} %add.24), channel_id=1, source_target_pairs={{0,2},{1,3},{2,0},{3,1},{4,6},{5,7},{6,4},{7,5},{8,10},{9,11},{10,... | collective-permute-start | bytes 3080 | tf_op jit(solution)/shard_map/ppermute | solution.py:579
  94.5 2.0 %collective-permute-done.24 = f32[2,128]{1,0:T(2,128)S(1)} collective-permute-done((f32[2,128]{1,0:T(2,128)S(1)}, f32[2,128]{1,0:T(2,128)S(1)}, u32[]{:S(2)}, u32[]{:S(2)}) %collective-permute-start.24) | collective-permute-done | bytes 1056 | tf_op jit(solution)/shard_map/ppermute | solution.py:579
  96.5 1.7 %collective-permute-start.25 = (f32[2,128]{1,0:T(2,128)S(1)}, f32[2,128]{1,0:T(2,128)S(1)}, u32[]{:S(2)}, u32[]{:S(2)}) collective-permute-start(f32[2,128]{1,0:T(2,128)S(1)} %add.25), channel_id=1, source_target_pairs={{0,4},{4,0},{8,12},{12,8},{1,5},{5,1},{9,13},{13,9},{2,6},{6,2},{1... | collective-permute-start | bytes 3080 | tf_op jit(solution)/shard_map/ppermute | solution.py:579
  98.3 6.3 %collective-permute-done.25 = f32[2,128]{1,0:T(2,128)S(1)} collective-permute-done((f32[2,128]{1,0:T(2,128)S(1)}, f32[2,128]{1,0:T(2,128)S(1)}, u32[]{:S(2)}, u32[]{:S(2)}) %collective-permute-start.25) | collective-permute-done | bytes 1056 | tf_op jit(solution)/shard_map/ppermute | solution.py:579
  104.5 1.3 %collective-permute-start.26 = (f32[2,128]{1,0:T(2,128)S(1)}, f32[2,128]{1,0:T(2,128)S(1)}, u32[]{:S(2)}, u32[]{:S(2)}) collective-permute-start(f32[2,128]{1,0:T(2,128)S(1)} %add.26), channel_id=1, source_target_pairs={{0,8},{4,12},{8,0},{12,4},{1,9},{5,13},{9,1},{13,5},{2,10},{6,14},... | collective-permute-start | bytes 3080 | tf_op jit(solution)/shard_map/ppermute | solution.py:579
  105.8 5.4 %collective-permute-done.22.rest_3_ = bf16[2,384,256]{2,1,0:T(8,128)(2,1)S(1)} collective-permute-done((bf16[2,384,256]{2,1,0:T(8,128)(2,1)S(1)}, bf16[2,384,256]{2,1,0:T(8,128)(2,1)S(1)}, u32[]{:S(2)}, u32[]{:S(2)}) %collective-permute-start.22) | collective-permute-done | bytes 393248 | tf_op jit(solution)/shard_map/ppermute | solution.py:572
  111.3 3.6 %shard_map.91 = bf16[3,384,1536]{2,1,0:T(8,128)(2,1)} custom-call(bf16[2,400,640]{2,1,0:T(8,128)(2,1)S(1)} %collective-permute-done.5.info.query.grad, bf16[2,384,640]{2,1,0:T(8,128)(2,1)S(1)} %collective-permute-done.key.value, f32[2,384,640]{2,1,0:T(8,128)S(1)} %get-tuple-element.64.own, bf16[2,384,640]{2,1,0:T(8,128)(2,1)S(1)} %collective-permute-done.13.from_even, ...), custom_call_target="tpu_custom_call" | custom-call | flops 1 | bytes 1 | tf_op jit(solution)/shard_map/pallas_call | solution.py:517
  (59 shorter events, 8.6 us)
Async XLA Ops:
  3.2 4.8 %copy-start = (bf16[1,1,1,384,1536]{4,3,2,1,0:T(8,128)(2,1)S(1)}, bf16[1,1,1,384,1536]{4,3,2,1,0:T(8,128)(2,1)}, u32[]{:S(2)}) copy-start(bf16[1,1,1,384,1536]{4,3,2,1,0:T(8,128)(2,1)} %param.7) | copy-start | bytes 3538948
  3.2 4.8 %copy-start.5 = (bf16[1,1,1,384,1536]{4,3,2,1,0:T(8,128)(2,1)S(1)}, bf16[1,1,1,384,1536]{4,3,2,1,0:T(8,128)(2,1)}, u32[]{:S(2)}) copy-start(bf16[1,1,1,384,1536]{4,3,2,1,0:T(8,128)(2,1)} %param.8) | copy-start | bytes 3538948
  3.3 9.9 %collective-permute-start.4 = (bf16[2,384,384]{2,1,0:T(8,128)(2,1)S(1)}, bf16[2,384,384]{2,1,0:T(8,128)(2,1)S(1)}, u32[]{:S(2)}, u32[]{:S(2)}) collective-permute-start(bf16[2,384,384]{2,1,0:T(8,128)(2,1)S(1)} %shard_map.77), channel_id=1, source_target_pairs={{0,1},{1,0},{2,3},{3,2},{4,8},{5,9},{6,10},{7,11},{8,4},{9,5},{10,... | collective-permute-start | bytes 1769480 | tf_op jit(solution)/shard_map/ppermute | solution.py:553
  3.8 18.3 %collective-permute-start.3 = (bf16[2,384,384]{2,1,0:T(8,128)(2,1)S(1)}, bf16[2,384,384]{2,1,0:T(8,128)(2,1)S(1)}, u32[]{:S(2)}, u32[]{:S(2)}) collective-permute-start(bf16[2,384,384]{2,1,0:T(8,128)(2,1)S(1)} %shard_map.77), channel_id=1, source_target_pairs={{0,4},{1,5},{2,6},{3,7},{4,0},{5,1},{6,2},{7,3},{8,12},{9,13},{10,... | collective-permute-start | bytes 1769480 | tf_op jit(solution)/shard_map/ppermute | solution.py:553
  9.2 3.3 %copy-start.6 = (f32[1,2,128]{2,1,0:T(2,128)S(1)}, f32[1,2,128]{2,1,0:T(2,128)}, u32[]{:S(2)}) copy-start(f32[1,2,128]{2,1,0:T(2,128)} %param.10) | copy-start | bytes 3076
  9.2 3.3 %copy-start.7 = (s32[1,1,1,3]{3,2,1,0:T(1,128)S(1)}, s32[1,1,1,3]{3,2,1,0:T(1,128)}, u32[]{:S(2)}) copy-start(s32[1,1,1,3]{3,2,1,0:T(1,128)} %param.11) | copy-start | bytes 40
  9.3 18.1 %collective-permute-start.2 = (bf16[2,384,256]{2,1,0:T(8,128)(2,1)S(1)}, bf16[2,384,256]{2,1,0:T(8,128)(2,1)S(1)}, u32[]{:S(2)}, u32[]{:S(2)}) collective-permute-start(bf16[2,384,256]{2,1,0:T(8,128)(2,1)S(1)} %shard_map.79), channel_id=1, source_target_pairs={{0,1},{1,0},{2,3},{3,2},{4,8},{5,9},{6,10},{7,11},{8,4},{9,5},{10,... | collective-permute-start | bytes 1179656 | tf_op jit(solution)/shard_map/ppermute | solution.py:553
  9.4 21.2 %collective-permute-start.1 = (bf16[2,384,256]{2,1,0:T(8,128)(2,1)S(1)}, bf16[2,384,256]{2,1,0:T(8,128)(2,1)S(1)}, u32[]{:S(2)}, u32[]{:S(2)}) collective-permute-start(bf16[2,384,256]{2,1,0:T(8,128)(2,1)S(1)} %shard_map.79), channel_id=1, source_target_pairs={{0,4},{1,5},{2,6},{3,7},{4,0},{5,1},{6,2},{7,3},{8,12},{9,13},{10,... | collective-permute-start | bytes 1179656 | tf_op jit(solution)/shard_map/ppermute | solution.py:553
  11.0 24.0 %collective-permute-start = (bf16[2,384,640]{2,1,0:T(8,128)(2,1)S(1)}, bf16[2,384,640]{2,1,0:T(8,128)(2,1)S(1)}, u32[]{:S(2)}, u32[]{:S(2)}) collective-permute-start(bf16[2,384,640]{2,1,0:T(8,128)(2,1)S(1)} %shard_map.78), channel_id=1, source_target_pairs={{0,16},{16,0},{1,17},{17,1},{2,18},{18,2},{3,19},{19,3},{4,20},{20... | collective-permute-start | bytes 2949128 | tf_op jit(solution)/shard_map/ppermute | solution.py:572
  13.1 11.5 %copy-start.4 = (bf16[1,1,1,384,1536]{4,3,2,1,0:T(8,128)(2,1)S(1)}, bf16[1,1,1,384,1536]{4,3,2,1,0:T(8,128)(2,1)}, u32[]{:S(2)}) copy-start(bf16[1,1,1,384,1536]{4,3,2,1,0:T(8,128)(2,1)} %param.6) | copy-start | bytes 3538948
  22.1 13.9 %collective-permute-start.10 = (bf16[2,384,256]{2,1,0:T(8,128)(2,1)S(1)}, bf16[2,384,256]{2,1,0:T(8,128)(2,1)S(1)}, u32[]{:S(2)}, u32[]{:S(2)}) collective-permute-start(bf16[2,384,256]{2,1,0:T(8,128)(2,1)S(1)} %shard_map.86), channel_id=1, source_target_pairs={{0,1},{1,0},{2,3},{3,2},{4,8},{5,9},{6,10},{7,11},{8,4},{9,5},{10,... | collective-permute-start | bytes 1179656 | tf_op jit(solution)/shard_map/ppermute | solution.py:553
  22.1 17.0 %collective-permute-start.9 = (bf16[2,384,256]{2,1,0:T(8,128)(2,1)S(1)}, bf16[2,384,256]{2,1,0:T(8,128)(2,1)S(1)}, u32[]{:S(2)}, u32[]{:S(2)}) collective-permute-start(bf16[2,384,256]{2,1,0:T(8,128)(2,1)S(1)} %shard_map.86), channel_id=1, source_target_pairs={{0,4},{1,5},{2,6},{3,7},{4,0},{5,1},{6,2},{7,3},{8,12},{9,13},{10,... | collective-permute-start | bytes 1179656 | tf_op jit(solution)/shard_map/ppermute | solution.py:553
  32.4 9.2 %collective-permute-start.7 = (f32[40,384]{1,0:T(8,128)S(1)}, f32[40,384]{1,0:T(8,128)S(1)}, u32[]{:S(2)}, u32[]{:S(2)}) collective-permute-start(f32[40,384]{1,0:T(8,128)S(1)} %get-tuple-element.50.sent_odd), channel_id=1, source_target_pairs={{0,1},{1,0},{2,3},{3,2},{4,8},{5,9},{6,10},{7,11},{8,4},{9,5},{10,... | collective-permute-start | bytes 184328 | tf_op jit(solution)/shard_map/ppermute | solution.py:553
  32.5 10.6 %collective-permute-start.6 = (f32[40,384]{1,0:T(8,128)S(1)}, f32[40,384]{1,0:T(8,128)S(1)}, u32[]{:S(2)}, u32[]{:S(2)}) collective-permute-start(f32[40,384]{1,0:T(8,128)S(1)} %get-tuple-element.48.sent_even), channel_id=1, source_target_pairs={{0,4},{1,5},{2,6},{3,7},{4,0},{5,1},{6,2},{7,3},{8,12},{9,13},{10,... | collective-permute-start | bytes 184328 | tf_op jit(solution)/shard_map/ppermute | solution.py:553
  35.0 8.2 %collective-permute-start.8 = (f32[40,384]{1,0:T(8,128)S(1)}, f32[40,384]{1,0:T(8,128)S(1)}, u32[]{:S(2)}, u32[]{:S(2)}) collective-permute-start(f32[40,384]{1,0:T(8,128)S(1)} %get-tuple-element.52), channel_id=1, source_target_pairs={{0,8},{1,9},{2,10},{3,11},{4,12},{5,13},{6,14},{7,15},{8,0},{9,1},... | collective-permute-start | bytes 184328 | tf_op jit(solution)/shard_map/ppermute | solution.py:553
  39.1 28.1 %collective-permute-start.12 = (bf16[2,384,640]{2,1,0:T(8,128)(2,1)S(1)}, bf16[2,384,640]{2,1,0:T(8,128)(2,1)S(1)}, u32[]{:S(2)}, u32[]{:S(2)}) collective-permute-start(bf16[2,384,640]{2,1,0:T(8,128)(2,1)S(1)} %collective-permute-done.key.value), channel_id=1, source_target_pairs={{0,1},{1,0},{2,3},{3,2},{4,8},{5,9},{6,10},{7,11},{8,4},{9,5},{10,... | collective-permute-start | bytes 2949128 | tf_op jit(solution)/shard_map/ppermute | solution.py:553
  39.1 29.8 %collective-permute-start.11 = (bf16[2,384,640]{2,1,0:T(8,128)(2,1)S(1)}, bf16[2,384,640]{2,1,0:T(8,128)(2,1)S(1)}, u32[]{:S(2)}, u32[]{:S(2)}) collective-permute-start(bf16[2,384,640]{2,1,0:T(8,128)(2,1)S(1)} %collective-permute-done.key.value), channel_id=1, source_target_pairs={{0,4},{1,5},{2,6},{3,7},{4,0},{5,1},{6,2},{7,3},{8,12},{9,13},{10,... | collective-permute-start | bytes 2949128 | tf_op jit(solution)/shard_map/ppermute | solution.py:553
  41.6 25.6 %collective-permute-start.5 = (bf16[2,400,640]{2,1,0:T(8,128)(2,1)S(1)}, bf16[2,400,640]{2,1,0:T(8,128)(2,1)S(1)}, u32[]{:S(2)}, u32[]{:S(2)}) collective-permute-start(bf16[2,400,640]{2,1,0:T(8,128)(2,1)S(1)} %shard_map.83), channel_id=1, source_target_pairs={{0,16},{16,0},{1,17},{17,1},{2,18},{18,2},{3,19},{19,3},{4,20},{20... | collective-permute-start | bytes 3072008 | tf_op jit(solution)/shard_map/ppermute | solution.py:572
  53.4 32.0 %collective-permute-start.15 = (bf16[2,384,640]{2,1,0:T(8,128)(2,1)S(1)}, bf16[2,384,640]{2,1,0:T(8,128)(2,1)S(1)}, u32[]{:S(2)}, u32[]{:S(2)}) collective-permute-start(bf16[2,384,640]{2,1,0:T(8,128)(2,1)S(1)} %get-tuple-element.57), channel_id=1, source_target_pairs={{0,16},{16,0},{1,17},{17,1},{2,18},{18,2},{3,19},{19,3},{4,20},{20... | collective-permute-start | bytes 2949128 | tf_op jit(solution)/shard_map/ppermute | solution.py:572
  54.0 26.2 %collective-permute-start.16 = (bf16[384,640]{1,0:T(8,128)(2,1)S(1)}, bf16[384,640]{1,0:T(8,128)(2,1)S(1)}, u32[]{:S(2)}, u32[]{:S(2)}) collective-permute-start(bf16[384,640]{1,0:T(8,128)(2,1)S(1)} %get-tuple-element.69), channel_id=1, source_target_pairs={{0,4},{1,5},{2,6},{3,7},{4,0},{5,1},{6,2},{7,3},{8,12},{9,13},{10,... | collective-permute-start | bytes 1474568 | tf_op jit(solution)/shard_map/ppermute | solution.py:553
  67.2 14.9 %collective-permute-start.17 = (bf16[384,640]{1,0:T(8,128)(2,1)S(1)}, bf16[384,640]{1,0:T(8,128)(2,1)S(1)}, u32[]{:S(2)}, u32[]{:S(2)}) collective-permute-start(bf16[384,640]{1,0:T(8,128)(2,1)S(1)} %get-tuple-element.70), channel_id=1, source_target_pairs={{0,1},{1,0},{2,3},{3,2},{4,8},{5,9},{6,10},{7,11},{8,4},{9,5},{10,... | collective-permute-start | bytes 1474568 | tf_op jit(solution)/shard_map/ppermute | solution.py:553
  67.2 23.3 %collective-permute-start.20 = (bf16[2,384,256]{2,1,0:T(8,128)(2,1)S(1)}, bf16[2,384,256]{2,1,0:T(8,128)(2,1)S(1)}, u32[]{:S(2)}, u32[]{:S(2)}) collective-permute-start(bf16[2,384,256]{2,1,0:T(8,128)(2,1)S(1)} %get-tuple-element.76), channel_id=1, source_target_pairs={{0,4},{1,5},{2,6},{3,7},{4,0},{5,1},{6,2},{7,3},{8,12},{9,13},{10,... | collective-permute-start | bytes 1179656 | tf_op jit(solution)/shard_map/ppermute | solution.py:553
  68.9 21.6 %collective-permute-start.21 = (bf16[2,384,256]{2,1,0:T(8,128)(2,1)S(1)}, bf16[2,384,256]{2,1,0:T(8,128)(2,1)S(1)}, u32[]{:S(2)}, u32[]{:S(2)}) collective-permute-start(bf16[2,384,256]{2,1,0:T(8,128)(2,1)S(1)} %get-tuple-element.77), channel_id=1, source_target_pairs={{0,1},{1,0},{2,3},{3,2},{4,8},{5,9},{6,10},{7,11},{8,4},{9,5},{10,... | collective-permute-start | bytes 1179656 | tf_op jit(solution)/shard_map/ppermute | solution.py:553
  80.3 31.0 %collective-permute-start.13 = (bf16[2,384,640]{2,1,0:T(8,128)(2,1)S(1)}, bf16[2,384,640]{2,1,0:T(8,128)(2,1)S(1)}, u32[]{:S(2)}, u32[]{:S(2)}) collective-permute-start(bf16[2,384,640]{2,1,0:T(8,128)(2,1)S(1)} %get-tuple-element.65), channel_id=1, source_target_pairs={{0,4},{1,5},{2,6},{3,7},{4,0},{5,1},{6,2},{7,3},{8,12},{9,13},{10,... | collective-permute-start | bytes 2949128 | tf_op jit(solution)/shard_map/ppermute | solution.py:553
  82.2 29.1 %collective-permute-start.14 = (bf16[2,384,640]{2,1,0:T(8,128)(2,1)S(1)}, bf16[2,384,640]{2,1,0:T(8,128)(2,1)S(1)}, u32[]{:S(2)}, u32[]{:S(2)}) collective-permute-start(bf16[2,384,640]{2,1,0:T(8,128)(2,1)S(1)} %get-tuple-element.66), channel_id=1, source_target_pairs={{0,1},{1,0},{2,3},{3,2},{4,8},{5,9},{6,10},{7,11},{8,4},{9,5},{10,... | collective-permute-start | bytes 2949128 | tf_op jit(solution)/shard_map/ppermute | solution.py:553
  85.4 3.6 %collective-permute-start.18 = (f32[2,128]{1,0:T(2,128)S(1)}, f32[2,128]{1,0:T(2,128)S(1)}, u32[]{:S(2)}, u32[]{:S(2)}) collective-permute-start(f32[2,128]{1,0:T(2,128)S(1)} %slice.12), channel_id=1, source_target_pairs={{0,16},{16,0},{1,17},{17,1},{2,18},{18,2},{3,19},{19,3},{4,20},{20... | collective-permute-start | bytes 3080 | tf_op jit(solution)/shard_map/ppermute | solution.py:572
  89.0 22.3 %collective-permute-start.19 = (bf16[384,896]{1,0:T(8,128)(2,1)S(1)}, bf16[384,896]{1,0:T(8,128)(2,1)S(1)}, u32[]{:S(2)}, u32[]{:S(2)}) collective-permute-start(bf16[384,896]{1,0:T(8,128)(2,1)S(1)} %shard_map.89), channel_id=1, source_target_pairs={{0,16},{16,0},{1,17},{17,1},{2,18},{18,2},{3,19},{19,3},{4,20},{20... | collective-permute-start | bytes 2064392 | tf_op jit(solution)/shard_map/ppermute | solution.py:572
  91.2 20.0 %collective-permute-start.22 = (bf16[2,384,256]{2,1,0:T(8,128)(2,1)S(1)}, bf16[2,384,256]{2,1,0:T(8,128)(2,1)S(1)}, u32[]{:S(2)}, u32[]{:S(2)}) collective-permute-start(bf16[2,384,256]{2,1,0:T(8,128)(2,1)S(1)} %shard_map.90), channel_id=1, source_target_pairs={{0,16},{16,0},{1,17},{17,1},{2,18},{18,2},{3,19},{19,3},{4,20},{20... | collective-permute-start | bytes 1179656 | tf_op jit(solution)/shard_map/ppermute | solution.py:572
  91.8 1.1 collective-permute-start.23
  93.0 3.6 %collective-permute-start.24 = (f32[2,128]{1,0:T(2,128)S(1)}, f32[2,128]{1,0:T(2,128)S(1)}, u32[]{:S(2)}, u32[]{:S(2)}) collective-permute-start(f32[2,128]{1,0:T(2,128)S(1)} %add.24), channel_id=1, source_target_pairs={{0,2},{1,3},{2,0},{3,1},{4,6},{5,7},{6,4},{7,5},{8,10},{9,11},{10,... | collective-permute-start | bytes 3080 | tf_op jit(solution)/shard_map/ppermute | solution.py:579
  96.5 8.0 %collective-permute-start.25 = (f32[2,128]{1,0:T(2,128)S(1)}, f32[2,128]{1,0:T(2,128)S(1)}, u32[]{:S(2)}, u32[]{:S(2)}) collective-permute-start(f32[2,128]{1,0:T(2,128)S(1)} %add.25), channel_id=1, source_target_pairs={{0,4},{4,0},{8,12},{12,8},{1,5},{5,1},{9,13},{13,9},{2,6},{6,2},{1... | collective-permute-start | bytes 3080 | tf_op jit(solution)/shard_map/ppermute | solution.py:579
  104.5 10.3 %collective-permute-start.26 = (f32[2,128]{1,0:T(2,128)S(1)}, f32[2,128]{1,0:T(2,128)S(1)}, u32[]{:S(2)}, u32[]{:S(2)}) collective-permute-start(f32[2,128]{1,0:T(2,128)S(1)} %add.26), channel_id=1, source_target_pairs={{0,8},{4,12},{8,0},{12,4},{1,9},{5,13},{9,1},{13,5},{2,10},{6,14},... | collective-permute-start | bytes 3080 | tf_op jit(solution)/shard_map/ppermute | solution.py:579
  (3 other events, 3.8 us)

commit v9 on v8

--- a/solution.py
+++ b/solution.py
@@ -600,16 +600,18 @@
     key_pairs = (exchanged(key_pair, 0), exchanged(key_pair, 1))
     info = info_call(kv_tiles[0, 0, 0], after(norm_gains[0], asks[-1]))
     away_pair = turned(away_pair, -1)
+    ask_low = ask_call(info, after(query, *told_pairs[-1]), grad, away_first, away_count)
     sums = None
     for (first, count), told in zip(QUERY_GROUPS, told_pairs):
-        sums = sums_call(info, arrays, *told, first, count, key_first, sums, len(fars))
+        info_then = info if sums is None else after(info, ask_low)
+        sums = sums_call(info_then, arrays, *told, first, count, key_first, sums, len(fars))
     received = [exchanged(sums[0], 0), exchanged(sums[1], 1)]
     received += [
-        paired(after(value, away_pair), partners) for value, partners in zip(sums[2:], fars)
+        paired(after(value, *key_pairs), partners)
+        for value, partners in zip(sums[2:], fars)
     ]
     all_sums = (*sums[:2], *received)
-    asked = ask_call(info, after(query, away_pair, sums[0]), grad, away_first, away_count)
-    asked = turned(asked, -1)
+    asked = turned(ask_low, -1)
     away_sent = after(away_pair, *key_pairs)
     away_pairs = (exchanged(away_sent, 0), exchanged(away_sent, 1))
     gains, parts = [], None
@@ -624,7 +626,7 @@
     answer = (own, exchanged(to_even, 0), exchanged(to_odd, 1))
     operands = [(array, key_first, None) for array in arrays]
     low, own, to_even, to_odd, gain = main_call(
-        after(info, pair_low), operands, *key_pairs, key_count, away_first, key_first
+        after(info, pair_low, asked), operands, *key_pairs, key_count, away_first, key_first
     )
     gains.append(gain[:2])
     key_answer = (own, exchanged(to_even, 0), exchanged(to_odd, 1))
@@ -632,12 +634,12 @@
     query_low, own, to_even, to_odd, gain = main_call(
         after(asked, low), operands, *away_pairs, away_count, away_count, 0
     )
-    gains.append(turned(after(gain[:2], *answer[1:], pieces[0]), 1))
+    gains.append(turned(after(gain[:2], pieces[0]), 1))
     returned = (exchanged(to_even, 0), exchanged(to_odd, 1))
     pieces.append(query_low)
     places.append((0, away_first * HEAD_DIM))
     low = answer_call(info, query, *answer, low)
-    pieces.append(turned(after(low, gains[-1], pieces[0]), -1))
+    pieces.append(turned(after(low, gains[-1]), -1))
     places.append((0, 0))
     low = finish_call(after(info, pieces[0]), (key, key_first, None), *key_answer, key_count)
     pieces.append(turned(low, -1))

time: 117 us -> 124 us (1.060)
  waiting for transfers between devices: 42.4 us -> 51.6 us
    ppermute x17, waiting for transfers between devices: 15.3 us -> 21.9 us  [paired(): return lax.ppermute(value, ('seq', 'dp'), pairs)]
    ppermute x4, starting transfers between devices: 4.5 us -> 2.48 us  [total_over(): other = lax.ppermute(value, axis, [(i, i ^ step) for i in range(count)])]
    ppermute x4, waiting for transfers between devices: 9.45 us -> 11.1 us  [total_over(): other = lax.ppermute(value, axis, [(i, i ^ step) for i in range(count)])]
  transfers between devices with their start and end apart: 27 -> 27, of which waited for: 10 -> 10; matrix products, arithmetic and copies ran while one was open for 0% -> 0% of each run, Pallas kernels for 32% -> 30%
where the time goes in v9:
time: 124 us
  waiting for transfers between devices  51.6 us (42%)
  Pallas kernels  37.5 us (30%)
  starting transfers between devices  29.4 us (24%)
  local copies, waits for them, and re-layouts  3.71 us (3%)
    ppermute x17, waiting for transfers between devices, paired(): return lax.ppermute(value, ('seq', 'dp'), pairs)  21.9 us
    ppermute x17, starting transfers between devices, paired(): return lax.ppermute(value, ('seq', 'dp'), pairs)  18.8 us
    ppermute x6, waiting for transfers between devices, turned(): lax.ppermute(value, 'pipe', [(i, (i + step) % count) for i in range(count)])  18.6 us
    pallas_call x2, Pallas kernels, main_call(): pl.pallas_call(main_kernel, grid=(count,), in_specs=[info_block(info)] +...  15.9 us
    ppermute x4, waiting for transfers between devices, total_over(): other = lax.ppermute(value, axis, [(i, i ^ step) for i in range(count)])  11.1 us
    pallas_call x2, Pallas kernels, grads_call(): pl.pallas_call(functools.partial(grads_kernel, far_count=far_count), grid...  10.3 us
    ppermute x6, starting transfers between devices, turned(): lax.ppermute(value, 'pipe', [(i, (i + step) % count) for i in range(count)])  8.12 us
    pallas_call x2, Pallas kernels, sums_call(): pl.pallas_call(functools.partial(sums_kernel, far_count=far_count), grid=...  4.64 us
  transfers between devices with their start and end apart: 27, of which 10 were waited for; matrix products, arithmetic and copies ran while one was open for 0% of the time, Pallas kernels for 30%

profile of v9, /device:TPU:0, one launch (start us, length us, event | category | flops | bytes accessed | tf_op | source)
XLA Modules:
  0.0 123.7 jit_solution(11494292051610952854)
XLA Ops:
  0.6 1.3 %copy-done.1 = bf16[1,1,1,384,1536]{4,3,2,1,0:T(8,128)(2,1)S(1)} copy-done((bf16[1,1,1,384,1536]{4,3,2,1,0:T(8,128)(2,1)S(1)}, bf16[1,1,1,384,1536]{4,3,2,1,0:T(8,128)(2,1)}, u32[]{:S(2)}) %copy-start.1) | copy-done | bytes 1179672
  1.9 1.3 %copy-done.3 = bf16[1,1,1,384,1536]{4,3,2,1,0:T(8,128)(2,1)S(1)} copy-done((bf16[1,1,1,384,1536]{4,3,2,1,0:T(8,128)(2,1)S(1)}, bf16[1,1,1,384,1536]{4,3,2,1,0:T(8,128)(2,1)}, u32[]{:S(2)}) %copy-start.3) | copy-done | bytes 1179672
  3.8 4.1 %collective-permute-start.4 = (bf16[2,384,384]{2,1,0:T(8,128)(2,1)S(1)}, bf16[2,384,384]{2,1,0:T(8,128)(2,1)S(1)}, u32[]{:S(2)}, u32[]{:S(2)}) collective-permute-start(bf16[2,384,384]{2,1,0:T(8,128)(2,1)S(1)} %shard_map.77), channel_id=1, source_target_pairs={{0,4},{1,5},{2,6},{3,7},{4,0},{5,1},{6,2},{7,3},{8,12},{9,13},{10,... | collective-permute-start | bytes 1769480 | tf_op jit(solution)/shard_map/ppermute | solution.py:553
  8.1 1.2 copy-done.2
  9.4 1.6 %collective-permute-start = (bf16[2,384,256]{2,1,0:T(8,128)(2,1)S(1)}, bf16[2,384,256]{2,1,0:T(8,128)(2,1)S(1)}, u32[]{:S(2)}, u32[]{:S(2)}) collective-permute-start(bf16[2,384,256]{2,1,0:T(8,128)(2,1)S(1)} %shard_map.79), channel_id=1, source_target_pairs={{0,4},{1,5},{2,6},{3,7},{4,0},{5,1},{6,2},{7,3},{8,12},{9,13},{10,... | collective-permute-start | bytes 1179656 | tf_op jit(solution)/shard_map/ppermute | solution.py:553
  11.0 1.5 %collective-permute-start.3 = (bf16[2,384,640]{2,1,0:T(8,128)(2,1)S(1)}, bf16[2,384,640]{2,1,0:T(8,128)(2,1)S(1)}, u32[]{:S(2)}, u32[]{:S(2)}) collective-permute-start(bf16[2,384,640]{2,1,0:T(8,128)(2,1)S(1)} %shard_map.78), channel_id=1, source_target_pairs={{0,16},{16,0},{1,17},{17,1},{2,18},{18,2},{3,19},{19,3},{4,20},{20... | collective-permute-start | bytes 2949128 | tf_op jit(solution)/shard_map/ppermute | solution.py:572
  13.1 16.3 %collective-permute-done.pair_even = bf16[2,384,256]{2,1,0:T(8,128)(2,1)S(1)} collective-permute-done((bf16[2,384,256]{2,1,0:T(8,128)(2,1)S(1)}, bf16[2,384,256]{2,1,0:T(8,128)(2,1)S(1)}, u32[]{:S(2)}, u32[]{:S(2)}) %collective-permute-start) | collective-permute-done | bytes 393248 | tf_op jit(solution)/shard_map/ppermute | solution.py:553
  29.6 2.5 %collective-permute-start.8 = (bf16[2,384,256]{2,1,0:T(8,128)(2,1)S(1)}, bf16[2,384,256]{2,1,0:T(8,128)(2,1)S(1)}, u32[]{:S(2)}, u32[]{:S(2)}) collective-permute-start(bf16[2,384,256]{2,1,0:T(8,128)(2,1)S(1)} %shard_map.84), channel_id=1, source_target_pairs={{0,4},{1,5},{2,6},{3,7},{4,0},{5,1},{6,2},{7,3},{8,12},{9,13},{10,... | collective-permute-start | bytes 1179656 | tf_op jit(solution)/shard_map/ppermute | solution.py:553
  32.2 2.8 %shard_map.82 = (f32[40,384]{1,0:T(8,128)S(1)}, f32[40,384]{1,0:T(8,128)S(1)}, f32[40,384]{1,0:T(8,128)S(1)}) custom-call(f32[8,128]{1,0:T(8,128)S(1)} %shard_map.80.info, bf16[384,1536]{1,0:T(8,128)(2,1)S(1)} %bitcast.30, bf16[384,1536]{1,0:T(8,128)(2,1)S(1)} %bitcast.22, bf16[384,1536]{1,0:T(8,128)(2,1)S(1)} %bitcast.13, bf16[384,1536]{1,0:T(8,128)(2,1)S(1)} %bitcast.38, ...), custom_call_target="tpu_custom_call" | custom-call | flops 6000000000 | bytes 1 | tf_op jit(solution)/shard_map/pallas_call | solution.py:453
  34.9 1.9 %shard_map.83 = (f32[40,384]{1,0:T(8,128)S(1)}, f32[40,384]{1,0:T(8,128)S(1)}, f32[40,384]{1,0:T(8,128)S(1)}) custom-call(f32[8,128]{1,0:T(8,128)S(1)} %shard_map.80.info, bf16[384,1536]{1,0:T(8,128)(2,1)S(1)} %bitcast.31, bf16[384,1536]{1,0:T(8,128)(2,1)S(1)} %bitcast.23, ...), custom_call_target="tpu_custom_call", output_to_operand_aliasing={{0}: (7, {}), {1}: (8, {}), {2}: (9, {})} | custom-call | flops 6000000000 | bytes 1 | tf_op jit(solution)/shard_map/pallas_call | solution.py:453
  37.0 4.8 %collective-permute-done.8.pair_even = bf16[2,384,256]{2,1,0:T(8,128)(2,1)S(1)} collective-permute-done((bf16[2,384,256]{2,1,0:T(8,128)(2,1)S(1)}, bf16[2,384,256]{2,1,0:T(8,128)(2,1)S(1)}, u32[]{:S(2)}, u32[]{:S(2)}) %collective-permute-start.8) | collective-permute-done | bytes 393248 | tf_op jit(solution)/shard_map/ppermute | solution.py:553
  41.8 2.0 %collective-permute-start.10 = (f32[40,384]{1,0:T(8,128)S(1)}, f32[40,384]{1,0:T(8,128)S(1)}, u32[]{:S(2)}, u32[]{:S(2)}) collective-permute-start(f32[40,384]{1,0:T(8,128)S(1)} %get-tuple-element.56), channel_id=1, source_target_pairs={{0,8},{1,9},{2,10},{3,11},{4,12},{5,13},{6,14},{7,15},{8,0},{9,1},... | collective-permute-start | bytes 184328 | tf_op jit(solution)/shard_map/ppermute | solution.py:553
  43.8 1.5 %collective-permute-start.2 = (bf16[2,400,640]{2,1,0:T(8,128)(2,1)S(1)}, bf16[2,400,640]{2,1,0:T(8,128)(2,1)S(1)}, u32[]{:S(2)}, u32[]{:S(2)}) collective-permute-start(bf16[2,400,640]{2,1,0:T(8,128)(2,1)S(1)} %shard_map.81), channel_id=1, source_target_pairs={{0,16},{16,0},{1,17},{17,1},{2,18},{18,2},{3,19},{19,3},{4,20},{20... | collective-permute-start | bytes 3072008 | tf_op jit(solution)/shard_map/ppermute | solution.py:572
  45.3 1.6 %collective-permute-start.11 = (bf16[2,384,640]{2,1,0:T(8,128)(2,1)S(1)}, bf16[2,384,640]{2,1,0:T(8,128)(2,1)S(1)}, u32[]{:S(2)}, u32[]{:S(2)}) collective-permute-start(bf16[2,384,640]{2,1,0:T(8,128)(2,1)S(1)} %collective-permute-done.3.key.value), channel_id=1, source_target_pairs={{0,4},{1,5},{2,6},{3,7},{4,0},{5,1},{6,2},{7,3},{8,12},{9,13},{10,... | collective-permute-start | bytes 2949128 | tf_op jit(solution)/shard_map/ppermute | solution.py:553
  47.7 6.1 %shard_map.85 = (bf16[2,384,640]{2,1,0:T(8,128)(2,1)S(1)}, f32[384,640]{1,0:T(8,128)S(1)}, bf16[384,640]{1,0:T(8,128)(2,1)S(1)}, bf16[384,640]{1,0:T(8,128)(2,1)S(1)}, f32[8,128]{1,0:T(8,128)S(1)}) custom-call(f32[8,128]{1,0:T(8,128)S(1)} %shard_map.80.info, bf16[384,1536]{1,0:T(8,128)(2,1)S(1)} %bitcast.32, bf16[384,1536]{1,0:T(8,128)(2,1)S(1)} %bitcast.24, ...), custom_call_target="tpu_custom_call" | custom-call | flops 6000000000 | bytes 1 | tf_op jit(solution)/shard_map/pallas_call | solution.py:473
  53.8 4.1 %shard_map.86 = (bf16[2,384,640]{2,1,0:T(8,128)(2,1)S(1)}, f32[384,640]{1,0:T(8,128)S(1)}, bf16[384,640]{1,0:T(8,128)(2,1)S(1)}, bf16[384,640]{1,0:T(8,128)(2,1)S(1)}, f32[8,128]{1,0:T(8,128)S(1)}) custom-call(f32[8,128]{1,0:T(8,128)S(1)} %shard_map.80.info, ...), custom_call_target="tpu_custom_call", output_to_operand_aliasing={{0}: (12, {}), {1}: (13, {}), {2}: (14, {}), {3}: (15, {})} | custom-call | flops 6000000000 | bytes 1 | tf_op jit(solution)/shard_map/pallas_call | solution.py:473
  58.7 7.9 %collective-permute-done.2.info.query.grad = bf16[2,400,640]{2,1,0:T(8,128)(2,1)S(1)} collective-permute-done((bf16[2,400,640]{2,1,0:T(8,128)(2,1)S(1)}, bf16[2,400,640]{2,1,0:T(8,128)(2,1)S(1)}, u32[]{:S(2)}, u32[]{:S(2)}) %collective-permute-start.2) | collective-permute-done | bytes 1024032 | tf_op jit(solution)/shard_map/ppermute | solution.py:572
  66.6 1.5 %collective-permute-start.15 = (bf16[2,384,640]{2,1,0:T(8,128)(2,1)S(1)}, bf16[2,384,640]{2,1,0:T(8,128)(2,1)S(1)}, u32[]{:S(2)}, u32[]{:S(2)}) collective-permute-start(bf16[2,384,640]{2,1,0:T(8,128)(2,1)S(1)} %get-tuple-element.61), channel_id=1, source_target_pairs={{0,16},{16,0},{1,17},{17,1},{2,18},{18,2},{3,19},{19,3},{4,20},{20... | collective-permute-start | bytes 2949128 | tf_op jit(solution)/shard_map/ppermute | solution.py:572
  68.1 4.6 %shard_map.87 = (bf16[384,896]{1,0:T(8,128)(2,1)S(1)}, f32[2,384,256]{2,1,0:T(8,128)S(1)}, bf16[2,384,256]{2,1,0:T(8,128)(2,1)S(1)}, bf16[2,384,256]{2,1,0:T(8,128)(2,1)S(1)}, f32[8,128]{1,0:T(8,128)S(1)}) custom-call(f32[8,128]{1,0:T(8,128)S(1)} %shard_map.80.info, bf16[384,1536]{1,0:T(8,128)(2,1)S(1)} %bitcast.34, bf16[384,1536]{1,0:T(8,128)(2,1)S(1)} %bitcast.26, ...), custom_call_target="tpu_custom_call" | custom-call | flops 6000000000 | bytes 1 | tf_op jit(solution)/shard_map/pallas_call | solution.py:412
  72.7 2.3 %collective-permute-start.20 = (bf16[2,384,256]{2,1,0:T(8,128)(2,1)S(1)}, bf16[2,384,256]{2,1,0:T(8,128)(2,1)S(1)}, u32[]{:S(2)}, u32[]{:S(2)}) collective-permute-start(bf16[2,384,256]{2,1,0:T(8,128)(2,1)S(1)} %get-tuple-element.78), channel_id=1, source_target_pairs={{0,4},{1,5},{2,6},{3,7},{4,0},{5,1},{6,2},{7,3},{8,12},{9,13},{10,... | collective-permute-start | bytes 1179656 | tf_op jit(solution)/shard_map/ppermute | solution.py:553
  75.0 11.3 %shard_map.88 = (bf16[384,640]{1,0:T(8,128)(2,1)S(1)}, f32[2,384,640]{2,1,0:T(8,128)S(1)}, bf16[2,384,640]{2,1,0:T(8,128)(2,1)S(1)}, bf16[2,384,640]{2,1,0:T(8,128)(2,1)S(1)}, f32[8,128]{1,0:T(8,128)S(1)}) custom-call(bf16[2,400,640]{2,1,0:T(8,128)(2,1)S(1)} %collective-permute-done.2.info.query.grad, ...), custom_call_target="tpu_custom_call" | custom-call | flops 6000000000 | bytes 1 | tf_op jit(solution)/shard_map/pallas_call | solution.py:412
  86.3 1.1 collective-permute-done.15.rest_0_
  87.4 3.1 %collective-permute-start.13 = (bf16[2,384,640]{2,1,0:T(8,128)(2,1)S(1)}, bf16[2,384,640]{2,1,0:T(8,128)(2,1)S(1)}, u32[]{:S(2)}, u32[]{:S(2)}) collective-permute-start(bf16[2,384,640]{2,1,0:T(8,128)(2,1)S(1)} %get-tuple-element.67), channel_id=1, source_target_pairs={{0,4},{1,5},{2,6},{3,7},{4,0},{5,1},{6,2},{7,3},{8,12},{9,13},{10,... | collective-permute-start | bytes 2949128 | tf_op jit(solution)/shard_map/ppermute | solution.py:553
  90.5 1.6 %collective-permute-start.18 = (f32[2,128]{1,0:T(2,128)S(1)}, f32[2,128]{1,0:T(2,128)S(1)}, u32[]{:S(2)}, u32[]{:S(2)}) collective-permute-start(f32[2,128]{1,0:T(2,128)S(1)} %slice.12), channel_id=1, source_target_pairs={{0,16},{16,0},{1,17},{17,1},{2,18},{18,2},{3,19},{19,3},{4,20},{20... | collective-permute-start | bytes 3080 | tf_op jit(solution)/shard_map/ppermute | solution.py:572
  92.1 1.4 %shard_map.89 = bf16[384,896]{1,0:T(8,128)(2,1)S(1)} custom-call(f32[8,128]{1,0:T(8,128)S(1)} %shard_map.80.info, bf16[384,1536]{1,0:T(8,128)(2,1)S(1)} %bitcast.35, f32[384,640]{1,0:T(8,128)S(1)} %get-tuple-element.70.own, bf16[384,640]{1,0:T(8,128)(2,1)S(1)} %collective-permute-done.16.from_even, ...), custom_call_target="tpu_custom_call", output_to_operand_aliasing={{}: (5, {})} | custom-call | flops 20000000000 | bytes 1 | tf_op jit(solution)/shard_map/pallas_call | solution.py:499
  94.1 1.5 %collective-permute-start.19 = (bf16[384,896]{1,0:T(8,128)(2,1)S(1)}, bf16[384,896]{1,0:T(8,128)(2,1)S(1)}, u32[]{:S(2)}, u32[]{:S(2)}) collective-permute-start(bf16[384,896]{1,0:T(8,128)(2,1)S(1)} %shard_map.89), channel_id=1, source_target_pairs={{0,16},{16,0},{1,17},{17,1},{2,18},{18,2},{3,19},{19,3},{4,20},{20... | collective-permute-start | bytes 2064392 | tf_op jit(solution)/shard_map/ppermute | solution.py:572
  97.0 1.1 collective-permute-done.23
  98.1 1.5 %collective-permute-start.24 = (f32[2,128]{1,0:T(2,128)S(1)}, f32[2,128]{1,0:T(2,128)S(1)}, u32[]{:S(2)}, u32[]{:S(2)}) collective-permute-start(f32[2,128]{1,0:T(2,128)S(1)} %add.24), channel_id=1, source_target_pairs={{0,2},{1,3},{2,0},{3,1},{4,6},{5,7},{6,4},{7,5},{8,10},{9,11},{10,... | collective-permute-start | bytes 3080 | tf_op jit(solution)/shard_map/ppermute | solution.py:579
  99.6 2.0 %collective-permute-done.24 = f32[2,128]{1,0:T(2,128)S(1)} collective-permute-done((f32[2,128]{1,0:T(2,128)S(1)}, f32[2,128]{1,0:T(2,128)S(1)}, u32[]{:S(2)}, u32[]{:S(2)}) %collective-permute-start.24) | collective-permute-done | bytes 1056 | tf_op jit(solution)/shard_map/ppermute | solution.py:579
  102.6 8.0 %collective-permute-done.25 = f32[2,128]{1,0:T(2,128)S(1)} collective-permute-done((f32[2,128]{1,0:T(2,128)S(1)}, f32[2,128]{1,0:T(2,128)S(1)}, u32[]{:S(2)}, u32[]{:S(2)}) %collective-permute-start.25) | collective-permute-done | bytes 1056 | tf_op jit(solution)/shard_map/ppermute | solution.py:579
  110.6 8.9 %collective-permute-done.22.rest_3_ = bf16[2,384,256]{2,1,0:T(8,128)(2,1)S(1)} collective-permute-done((bf16[2,384,256]{2,1,0:T(8,128)(2,1)S(1)}, bf16[2,384,256]{2,1,0:T(8,128)(2,1)S(1)}, u32[]{:S(2)}, u32[]{:S(2)}) %collective-permute-start.22) | collective-permute-done | bytes 393248 | tf_op jit(solution)/shard_map/ppermute | solution.py:572
  119.5 3.6 %shard_map.91 = bf16[3,384,1536]{2,1,0:T(8,128)(2,1)} custom-call(bf16[2,400,640]{2,1,0:T(8,128)(2,1)S(1)} %collective-permute-done.2.info.query.grad, bf16[2,384,640]{2,1,0:T(8,128)(2,1)S(1)} %collective-permute-done.3.key.value, f32[2,384,640]{2,1,0:T(8,128)S(1)} %get-tuple-element.66.own, bf16[2,384,640]{2,1,0:T(8,128)(2,1)S(1)} %collective-permute-done.13.from_even, ...), custom_call_target="tpu_custom_call" | custom-call | flops 1 | bytes 1 | tf_op jit(solution)/shard_map/pallas_call | solution.py:517
  (59 shorter events, 6.9 us)
Async XLA Ops:
  3.2 4.8 %copy-start = (bf16[1,1,1,384,1536]{4,3,2,1,0:T(8,128)(2,1)S(1)}, bf16[1,1,1,384,1536]{4,3,2,1,0:T(8,128)(2,1)}, u32[]{:S(2)}) copy-start(bf16[1,1,1,384,1536]{4,3,2,1,0:T(8,128)(2,1)} %param.7) | copy-start | bytes 3538948
  3.2 4.8 %copy-start.5 = (bf16[1,1,1,384,1536]{4,3,2,1,0:T(8,128)(2,1)S(1)}, bf16[1,1,1,384,1536]{4,3,2,1,0:T(8,128)(2,1)}, u32[]{:S(2)}) copy-start(bf16[1,1,1,384,1536]{4,3,2,1,0:T(8,128)(2,1)} %param.8) | copy-start | bytes 3538948
  3.3 26.3 %collective-permute-start.5 = (bf16[2,384,384]{2,1,0:T(8,128)(2,1)S(1)}, bf16[2,384,384]{2,1,0:T(8,128)(2,1)S(1)}, u32[]{:S(2)}, u32[]{:S(2)}) collective-permute-start(bf16[2,384,384]{2,1,0:T(8,128)(2,1)S(1)} %shard_map.77), channel_id=1, source_target_pairs={{0,1},{1,0},{2,3},{3,2},{4,8},{5,9},{6,10},{7,11},{8,4},{9,5},{10,... | collective-permute-start | bytes 1769480 | tf_op jit(solution)/shard_map/ppermute | solution.py:553
  3.8 25.8 %collective-permute-start.4 = (bf16[2,384,384]{2,1,0:T(8,128)(2,1)S(1)}, bf16[2,384,384]{2,1,0:T(8,128)(2,1)S(1)}, u32[]{:S(2)}, u32[]{:S(2)}) collective-permute-start(bf16[2,384,384]{2,1,0:T(8,128)(2,1)S(1)} %shard_map.77), channel_id=1, source_target_pairs={{0,4},{1,5},{2,6},{3,7},{4,0},{5,1},{6,2},{7,3},{8,12},{9,13},{10,... | collective-permute-start | bytes 1769480 | tf_op jit(solution)/shard_map/ppermute | solution.py:553
  9.2 3.3 %copy-start.6 = (f32[1,2,128]{2,1,0:T(2,128)S(1)}, f32[1,2,128]{2,1,0:T(2,128)}, u32[]{:S(2)}) copy-start(f32[1,2,128]{2,1,0:T(2,128)} %param.10) | copy-start | bytes 3076
  9.2 3.3 %copy-start.7 = (s32[1,1,1,3]{3,2,1,0:T(1,128)S(1)}, s32[1,1,1,3]{3,2,1,0:T(1,128)}, u32[]{:S(2)}) copy-start(s32[1,1,1,3]{3,2,1,0:T(1,128)} %param.11) | copy-start | bytes 40
  9.3 3.9 %collective-permute-start.1 = (bf16[2,384,256]{2,1,0:T(8,128)(2,1)S(1)}, bf16[2,384,256]{2,1,0:T(8,128)(2,1)S(1)}, u32[]{:S(2)}, u32[]{:S(2)}) collective-permute-start(bf16[2,384,256]{2,1,0:T(8,128)(2,1)S(1)} %shard_map.79), channel_id=1, source_target_pairs={{0,1},{1,0},{2,3},{3,2},{4,8},{5,9},{6,10},{7,11},{8,4},{9,5},{10,... | collective-permute-start | bytes 1179656 | tf_op jit(solution)/shard_map/ppermute | solution.py:553
  9.4 20.1 %collective-permute-start = (bf16[2,384,256]{2,1,0:T(8,128)(2,1)S(1)}, bf16[2,384,256]{2,1,0:T(8,128)(2,1)S(1)}, u32[]{:S(2)}, u32[]{:S(2)}) collective-permute-start(bf16[2,384,256]{2,1,0:T(8,128)(2,1)S(1)} %shard_map.79), channel_id=1, source_target_pairs={{0,4},{1,5},{2,6},{3,7},{4,0},{5,1},{6,2},{7,3},{8,12},{9,13},{10,... | collective-permute-start | bytes 1179656 | tf_op jit(solution)/shard_map/ppermute | solution.py:553
  11.0 34.3 %collective-permute-start.3 = (bf16[2,384,640]{2,1,0:T(8,128)(2,1)S(1)}, bf16[2,384,640]{2,1,0:T(8,128)(2,1)S(1)}, u32[]{:S(2)}, u32[]{:S(2)}) collective-permute-start(bf16[2,384,640]{2,1,0:T(8,128)(2,1)S(1)} %shard_map.78), channel_id=1, source_target_pairs={{0,16},{16,0},{1,17},{17,1},{2,18},{18,2},{3,19},{19,3},{4,20},{20... | collective-permute-start | bytes 2949128 | tf_op jit(solution)/shard_map/ppermute | solution.py:572
  13.1 16.3 %copy-start.4 = (bf16[1,1,1,384,1536]{4,3,2,1,0:T(8,128)(2,1)S(1)}, bf16[1,1,1,384,1536]{4,3,2,1,0:T(8,128)(2,1)}, u32[]{:S(2)}) copy-start(bf16[1,1,1,384,1536]{4,3,2,1,0:T(8,128)(2,1)} %param.6) | copy-start | bytes 3538948
  29.6 7.4 %collective-permute-start.9 = (bf16[2,384,256]{2,1,0:T(8,128)(2,1)S(1)}, bf16[2,384,256]{2,1,0:T(8,128)(2,1)S(1)}, u32[]{:S(2)}, u32[]{:S(2)}) collective-permute-start(bf16[2,384,256]{2,1,0:T(8,128)(2,1)S(1)} %shard_map.84), channel_id=1, source_target_pairs={{0,1},{1,0},{2,3},{3,2},{4,8},{5,9},{6,10},{7,11},{8,4},{9,5},{10,... | collective-permute-start | bytes 1179656 | tf_op jit(solution)/shard_map/ppermute | solution.py:553
  29.6 12.2 %collective-permute-start.8 = (bf16[2,384,256]{2,1,0:T(8,128)(2,1)S(1)}, bf16[2,384,256]{2,1,0:T(8,128)(2,1)S(1)}, u32[]{:S(2)}, u32[]{:S(2)}) collective-permute-start(bf16[2,384,256]{2,1,0:T(8,128)(2,1)S(1)} %shard_map.84), channel_id=1, source_target_pairs={{0,4},{1,5},{2,6},{3,7},{4,0},{5,1},{6,2},{7,3},{8,12},{9,13},{10,... | collective-permute-start | bytes 1179656 | tf_op jit(solution)/shard_map/ppermute | solution.py:553
  36.8 8.5 %collective-permute-start.6 = (f32[40,384]{1,0:T(8,128)S(1)}, f32[40,384]{1,0:T(8,128)S(1)}, u32[]{:S(2)}, u32[]{:S(2)}) collective-permute-start(f32[40,384]{1,0:T(8,128)S(1)} %get-tuple-element.51.sent_even), channel_id=1, source_target_pairs={{0,4},{1,5},{2,6},{3,7},{4,0},{5,1},{6,2},{7,3},{8,12},{9,13},{10,... | collective-permute-start | bytes 184328 | tf_op jit(solution)/shard_map/ppermute | solution.py:553
  36.9 10.0 %collective-permute-start.7 = (f32[40,384]{1,0:T(8,128)S(1)}, f32[40,384]{1,0:T(8,128)S(1)}, u32[]{:S(2)}, u32[]{:S(2)}) collective-permute-start(f32[40,384]{1,0:T(8,128)S(1)} %get-tuple-element.52.sent_odd), channel_id=1, source_target_pairs={{0,1},{1,0},{2,3},{3,2},{4,8},{5,9},{6,10},{7,11},{8,4},{9,5},{10,... | collective-permute-start | bytes 184328 | tf_op jit(solution)/shard_map/ppermute | solution.py:553
  41.8 5.8 %collective-permute-start.10 = (f32[40,384]{1,0:T(8,128)S(1)}, f32[40,384]{1,0:T(8,128)S(1)}, u32[]{:S(2)}, u32[]{:S(2)}) collective-permute-start(f32[40,384]{1,0:T(8,128)S(1)} %get-tuple-element.56), channel_id=1, source_target_pairs={{0,8},{1,9},{2,10},{3,11},{4,12},{5,13},{6,14},{7,15},{8,0},{9,1},... | collective-permute-start | bytes 184328 | tf_op jit(solution)/shard_map/ppermute | solution.py:553
  43.8 22.8 %collective-permute-start.2 = (bf16[2,400,640]{2,1,0:T(8,128)(2,1)S(1)}, bf16[2,400,640]{2,1,0:T(8,128)(2,1)S(1)}, u32[]{:S(2)}, u32[]{:S(2)}) collective-permute-start(bf16[2,400,640]{2,1,0:T(8,128)(2,1)S(1)} %shard_map.81), channel_id=1, source_target_pairs={{0,16},{16,0},{1,17},{17,1},{2,18},{18,2},{3,19},{19,3},{4,20},{20... | collective-permute-start | bytes 3072008 | tf_op jit(solution)/shard_map/ppermute | solution.py:572
  45.3 27.4 %collective-permute-start.12 = (bf16[2,384,640]{2,1,0:T(8,128)(2,1)S(1)}, bf16[2,384,640]{2,1,0:T(8,128)(2,1)S(1)}, u32[]{:S(2)}, u32[]{:S(2)}) collective-permute-start(bf16[2,384,640]{2,1,0:T(8,128)(2,1)S(1)} %collective-permute-done.3.key.value), channel_id=1, source_target_pairs={{0,1},{1,0},{2,3},{3,2},{4,8},{5,9},{6,10},{7,11},{8,4},{9,5},{10,... | collective-permute-start | bytes 2949128 | tf_op jit(solution)/shard_map/ppermute | solution.py:553
  45.3 29.7 %collective-permute-start.11 = (bf16[2,384,640]{2,1,0:T(8,128)(2,1)S(1)}, bf16[2,384,640]{2,1,0:T(8,128)(2,1)S(1)}, u32[]{:S(2)}, u32[]{:S(2)}) collective-permute-start(bf16[2,384,640]{2,1,0:T(8,128)(2,1)S(1)} %collective-permute-done.3.key.value), channel_id=1, source_target_pairs={{0,4},{1,5},{2,6},{3,7},{4,0},{5,1},{6,2},{7,3},{8,12},{9,13},{10,... | collective-permute-start | bytes 2949128 | tf_op jit(solution)/shard_map/ppermute | solution.py:553
  57.9 32.5 %collective-permute-start.16 = (bf16[384,640]{1,0:T(8,128)(2,1)S(1)}, bf16[384,640]{1,0:T(8,128)(2,1)S(1)}, u32[]{:S(2)}, u32[]{:S(2)}) collective-permute-start(bf16[384,640]{1,0:T(8,128)(2,1)S(1)} %get-tuple-element.71), channel_id=1, source_target_pairs={{0,4},{1,5},{2,6},{3,7},{4,0},{5,1},{6,2},{7,3},{8,12},{9,13},{10,... | collective-permute-start | bytes 1474568 | tf_op jit(solution)/shard_map/ppermute | solution.py:553
  58.7 31.8 %collective-permute-start.17 = (bf16[384,640]{1,0:T(8,128)(2,1)S(1)}, bf16[384,640]{1,0:T(8,128)(2,1)S(1)}, u32[]{:S(2)}, u32[]{:S(2)}) collective-permute-start(bf16[384,640]{1,0:T(8,128)(2,1)S(1)} %get-tuple-element.72), channel_id=1, source_target_pairs={{0,1},{1,0},{2,3},{3,2},{4,8},{5,9},{6,10},{7,11},{8,4},{9,5},{10,... | collective-permute-start | bytes 1474568 | tf_op jit(solution)/shard_map/ppermute | solution.py:553
  66.6 20.8 %collective-permute-start.15 = (bf16[2,384,640]{2,1,0:T(8,128)(2,1)S(1)}, bf16[2,384,640]{2,1,0:T(8,128)(2,1)S(1)}, u32[]{:S(2)}, u32[]{:S(2)}) collective-permute-start(bf16[2,384,640]{2,1,0:T(8,128)(2,1)S(1)} %get-tuple-element.61), channel_id=1, source_target_pairs={{0,16},{16,0},{1,17},{17,1},{2,18},{18,2},{3,19},{19,3},{4,20},{20... | collective-permute-start | bytes 2949128 | tf_op jit(solution)/shard_map/ppermute | solution.py:572
  72.7 23.0 %collective-permute-start.20 = (bf16[2,384,256]{2,1,0:T(8,128)(2,1)S(1)}, bf16[2,384,256]{2,1,0:T(8,128)(2,1)S(1)}, u32[]{:S(2)}, u32[]{:S(2)}) collective-permute-start(bf16[2,384,256]{2,1,0:T(8,128)(2,1)S(1)} %get-tuple-element.78), channel_id=1, source_target_pairs={{0,4},{1,5},{2,6},{3,7},{4,0},{5,1},{6,2},{7,3},{8,12},{9,13},{10,... | collective-permute-start | bytes 1179656 | tf_op jit(solution)/shard_map/ppermute | solution.py:553
  75.0 20.7 %collective-permute-start.21 = (bf16[2,384,256]{2,1,0:T(8,128)(2,1)S(1)}, bf16[2,384,256]{2,1,0:T(8,128)(2,1)S(1)}, u32[]{:S(2)}, u32[]{:S(2)}) collective-permute-start(bf16[2,384,256]{2,1,0:T(8,128)(2,1)S(1)} %get-tuple-element.79), channel_id=1, source_target_pairs={{0,1},{1,0},{2,3},{3,2},{4,8},{5,9},{6,10},{7,11},{8,4},{9,5},{10,... | collective-permute-start | bytes 1179656 | tf_op jit(solution)/shard_map/ppermute | solution.py:553
  87.4 32.1 %collective-permute-start.13 = (bf16[2,384,640]{2,1,0:T(8,128)(2,1)S(1)}, bf16[2,384,640]{2,1,0:T(8,128)(2,1)S(1)}, u32[]{:S(2)}, u32[]{:S(2)}) collective-permute-start(bf16[2,384,640]{2,1,0:T(8,128)(2,1)S(1)} %get-tuple-element.67), channel_id=1, source_target_pairs={{0,4},{1,5},{2,6},{3,7},{4,0},{5,1},{6,2},{7,3},{8,12},{9,13},{10,... | collective-permute-start | bytes 2949128 | tf_op jit(solution)/shard_map/ppermute | solution.py:553
  90.5 29.0 %collective-permute-start.14 = (bf16[2,384,640]{2,1,0:T(8,128)(2,1)S(1)}, bf16[2,384,640]{2,1,0:T(8,128)(2,1)S(1)}, u32[]{:S(2)}, u32[]{:S(2)}) collective-permute-start(bf16[2,384,640]{2,1,0:T(8,128)(2,1)S(1)} %get-tuple-element.68), channel_id=1, source_target_pairs={{0,1},{1,0},{2,3},{3,2},{4,8},{5,9},{6,10},{7,11},{8,4},{9,5},{10,... | collective-permute-start | bytes 2949128 | tf_op jit(solution)/shard_map/ppermute | solution.py:553
  90.5 3.6 %collective-permute-start.18 = (f32[2,128]{1,0:T(2,128)S(1)}, f32[2,128]{1,0:T(2,128)S(1)}, u32[]{:S(2)}, u32[]{:S(2)}) collective-permute-start(f32[2,128]{1,0:T(2,128)S(1)} %slice.12), channel_id=1, source_target_pairs={{0,16},{16,0},{1,17},{17,1},{2,18},{18,2},{3,19},{19,3},{4,20},{20... | collective-permute-start | bytes 3080 | tf_op jit(solution)/shard_map/ppermute | solution.py:572
  94.1 25.4 %collective-permute-start.19 = (bf16[384,896]{1,0:T(8,128)(2,1)S(1)}, bf16[384,896]{1,0:T(8,128)(2,1)S(1)}, u32[]{:S(2)}, u32[]{:S(2)}) collective-permute-start(bf16[384,896]{1,0:T(8,128)(2,1)S(1)} %shard_map.89), channel_id=1, source_target_pairs={{0,16},{16,0},{1,17},{17,1},{2,18},{18,2},{3,19},{19,3},{4,20},{20... | collective-permute-start | bytes 2064392 | tf_op jit(solution)/shard_map/ppermute | solution.py:572
  96.4 23.1 %collective-permute-start.22 = (bf16[2,384,256]{2,1,0:T(8,128)(2,1)S(1)}, bf16[2,384,256]{2,1,0:T(8,128)(2,1)S(1)}, u32[]{:S(2)}, u32[]{:S(2)}) collective-permute-start(bf16[2,384,256]{2,1,0:T(8,128)(2,1)S(1)} %shard_map.90), channel_id=1, source_target_pairs={{0,16},{16,0},{1,17},{17,1},{2,18},{18,2},{3,19},{19,3},{4,20},{20... | collective-permute-start | bytes 1179656 | tf_op jit(solution)/shard_map/ppermute | solution.py:572
  97.0 1.1 collective-permute-start.23
  98.1 3.6 %collective-permute-start.24 = (f32[2,128]{1,0:T(2,128)S(1)}, f32[2,128]{1,0:T(2,128)S(1)}, u32[]{:S(2)}, u32[]{:S(2)}) collective-permute-start(f32[2,128]{1,0:T(2,128)S(1)} %add.24), channel_id=1, source_target_pairs={{0,2},{1,3},{2,0},{3,1},{4,6},{5,7},{6,4},{7,5},{8,10},{9,11},{10,... | collective-permute-start | bytes 3080 | tf_op jit(solution)/shard_map/ppermute | solution.py:579
  101.7 8.9 %collective-permute-start.25 = (f32[2,128]{1,0:T(2,128)S(1)}, f32[2,128]{1,0:T(2,128)S(1)}, u32[]{:S(2)}, u32[]{:S(2)}) collective-permute-start(f32[2,128]{1,0:T(2,128)S(1)} %add.25), channel_id=1, source_target_pairs={{0,4},{4,0},{8,12},{12,8},{1,5},{5,1},{9,13},{13,9},{2,6},{6,2},{1... | collective-permute-start | bytes 3080 | tf_op jit(solution)/shard_map/ppermute | solution.py:579
  110.6 12.5 %collective-permute-start.26 = (f32[2,128]{1,0:T(2,128)S(1)}, f32[2,128]{1,0:T(2,128)S(1)}, u32[]{:S(2)}, u32[]{:S(2)}) collective-permute-start(f32[2,128]{1,0:T(2,128)S(1)} %add.26), channel_id=1, source_target_pairs={{0,8},{4,12},{8,0},{12,4},{1,9},{5,13},{9,1},{13,5},{2,10},{6,14},... | collective-permute-start | bytes 3080 | tf_op jit(solution)/shard_map/ppermute | solution.py:579
  (3 other events, 3.8 us)

commit v10 on v8

--- a/solution.py
+++ b/solution.py
@@ -490,7 +490,7 @@
         ],
         input_output_aliases={place + index: index for index in range(len(earlier))},
         compiler_params=pltpu.CompilerParams(vmem_limit_bytes=MAIN_VMEM),
-        cost_estimate=MAIN_COST,
+        cost_estimate=COST,
     )(info, *arrays, pair_even, pair_odd, *sums, *earlier)
 
 
@@ -605,12 +605,12 @@
         sums = sums_call(info, arrays, *told, first, count, key_first, sums, len(fars))
     received = [exchanged(sums[0], 0), exchanged(sums[1], 1)]
     received += [
-        paired(after(value, away_pair), partners) for value, partners in zip(sums[2:], fars)
+        paired(value, partners) for value, partners in zip(sums[2:], fars)
     ]
     all_sums = (*sums[:2], *received)
     asked = ask_call(info, after(query, away_pair, sums[0]), grad, away_first, away_count)
     asked = turned(asked, -1)
-    away_sent = after(away_pair, *key_pairs)
+    away_sent = after(away_pair, *key_pairs, *received)
     away_pairs = (exchanged(away_sent, 0), exchanged(away_sent, 1))
     gains, parts = [], None
     for (first, count), told in zip(QUERY_GROUPS, told_pairs):
@@ -632,12 +632,12 @@
     query_low, own, to_even, to_odd, gain = main_call(
         after(asked, low), operands, *away_pairs, away_count, away_count, 0
     )
-    gains.append(turned(after(gain[:2], *answer[1:], pieces[0]), 1))
     returned = (exchanged(to_even, 0), exchanged(to_odd, 1))
     pieces.append(query_low)
     places.append((0, away_first * HEAD_DIM))
     low = answer_call(info, query, *answer, low)
-    pieces.append(turned(after(low, gains[-1], pieces[0]), -1))
+    gains.append(turned(after(gain[:2], low, pieces[0]), 1))
+    pieces.append(turned(after(low, gains[-1]), -1))
     places.append((0, 0))
     low = finish_call(after(info, pieces[0]), (key, key_first, None), *key_answer, key_count)
     pieces.append(turned(low, -1))

time: 117 us -> 117 us (level)
  starting transfers between devices: 30.4 us -> 32.3 us
    ppermute x6, waiting for transfers between devices: 17.7 us -> 12 us  [turned(): lax.ppermute(value, 'pipe', [(i, (i + step) % count) for i in range(count)])]
    ppermute x4, waiting for transfers between devices: 9.45 us -> 12.9 us  [total_over(): other = lax.ppermute(value, axis, [(i, i ^ step) for i in range(count)])]
    ppermute x17, waiting for transfers between devices: 15.3 us -> 16.5 us  [paired(): return lax.ppermute(value, ('seq', 'dp'), pairs)]
where the time goes in v10:
time: 117 us; the launch traced here: 116 us
  waiting for transfers between devices  41.4 us (35%)
  Pallas kernels  37.5 us (32%)
  starting transfers between devices  32.3 us (28%)
  local copies, waits for them, and re-layouts  3.71 us (3%)
    ppermute x17, starting transfers between devices, paired(): return lax.ppermute(value, ('seq', 'dp'), pairs)  19.4 us
    ppermute x17, waiting for transfers between devices, paired(): return lax.ppermute(value, ('seq', 'dp'), pairs)  16.5 us
    pallas_call x2, Pallas kernels, main_call(): pl.pallas_call(main_kernel, grid=(count,), in_specs=[info_block(info)] +...  15.9 us
    ppermute x4, waiting for transfers between devices, total_over(): other = lax.ppermute(value, axis, [(i, i ^ step) for i in range(count)])  12.9 us
    ppermute x6, waiting for transfers between devices, turned(): lax.ppermute(value, 'pipe', [(i, (i + step) % count) for i in range(count)])  12 us
    pallas_call x2, Pallas kernels, grads_call(): pl.pallas_call(functools.partial(grads_kernel, far_count=far_count), grid...  10.3 us
    ppermute x6, starting transfers between devices, turned(): lax.ppermute(value, 'pipe', [(i, (i + step) % count) for i in range(count)])  7.31 us
    ppermute x4, starting transfers between devices, total_over(): other = lax.ppermute(value, axis, [(i, i ^ step) for i in range(count)])  5.58 us
  transfers between devices with their start and end apart: 27, of which 10 were waited for; matrix products, arithmetic and copies ran while one was open for 0% of the time, Pallas kernels for 32%

profile of v10, /device:TPU:0, one launch (start us, length us, event | category | flops | bytes accessed | tf_op | source)
XLA Modules:
  0.0 116.4 jit_solution(17907047138098471511)
XLA Ops:
  1.9 1.3 %copy-done.3 = bf16[1,1,1,384,1536]{4,3,2,1,0:T(8,128)(2,1)S(1)} copy-done((bf16[1,1,1,384,1536]{4,3,2,1,0:T(8,128)(2,1)S(1)}, bf16[1,1,1,384,1536]{4,3,2,1,0:T(8,128)(2,1)}, u32[]{:S(2)}) %copy-start.3) | copy-done | bytes 1179672
  3.8 4.1 %collective-permute-start.3 = (bf16[2,384,384]{2,1,0:T(8,128)(2,1)S(1)}, bf16[2,384,384]{2,1,0:T(8,128)(2,1)S(1)}, u32[]{:S(2)}, u32[]{:S(2)}) collective-permute-start(bf16[2,384,384]{2,1,0:T(8,128)(2,1)S(1)} %shard_map.77), channel_id=1, source_target_pairs={{0,4},{1,5},{2,6},{3,7},{4,0},{5,1},{6,2},{7,3},{8,12},{9,13},{10,... | collective-permute-start | bytes 1769480 | tf_op jit(solution)/shard_map/ppermute | solution.py:553
  9.4 1.6 %collective-permute-start.1 = (bf16[2,384,256]{2,1,0:T(8,128)(2,1)S(1)}, bf16[2,384,256]{2,1,0:T(8,128)(2,1)S(1)}, u32[]{:S(2)}, u32[]{:S(2)}) collective-permute-start(bf16[2,384,256]{2,1,0:T(8,128)(2,1)S(1)} %shard_map.79), channel_id=1, source_target_pairs={{0,4},{1,5},{2,6},{3,7},{4,0},{5,1},{6,2},{7,3},{8,12},{9,13},{10,... | collective-permute-start | bytes 1179656 | tf_op jit(solution)/shard_map/ppermute | solution.py:553
  11.0 1.5 %collective-permute-start = (bf16[2,384,640]{2,1,0:T(8,128)(2,1)S(1)}, bf16[2,384,640]{2,1,0:T(8,128)(2,1)S(1)}, u32[]{:S(2)}, u32[]{:S(2)}) collective-permute-start(bf16[2,384,640]{2,1,0:T(8,128)(2,1)S(1)} %shard_map.78), channel_id=1, source_target_pairs={{0,16},{16,0},{1,17},{17,1},{2,18},{18,2},{3,19},{19,3},{4,20},{20... | collective-permute-start | bytes 2949128 | tf_op jit(solution)/shard_map/ppermute | solution.py:572
  13.1 9.0 %collective-permute-done.3.pair_even = bf16[2,384,384]{2,1,0:T(8,128)(2,1)S(1)} collective-permute-done((bf16[2,384,384]{2,1,0:T(8,128)(2,1)S(1)}, bf16[2,384,384]{2,1,0:T(8,128)(2,1)S(1)}, u32[]{:S(2)}, u32[]{:S(2)}) %collective-permute-start.3) | collective-permute-done | bytes 589856 | tf_op jit(solution)/shard_map/ppermute | solution.py:553
  22.1 2.5 %collective-permute-start.9 = (bf16[2,384,256]{2,1,0:T(8,128)(2,1)S(1)}, bf16[2,384,256]{2,1,0:T(8,128)(2,1)S(1)}, u32[]{:S(2)}, u32[]{:S(2)}) collective-permute-start(bf16[2,384,256]{2,1,0:T(8,128)(2,1)S(1)} %shard_map.86), channel_id=1, source_target_pairs={{0,4},{1,5},{2,6},{3,7},{4,0},{5,1},{6,2},{7,3},{8,12},{9,13},{10,... | collective-permute-start | bytes 1179656 | tf_op jit(solution)/shard_map/ppermute | solution.py:553
  24.6 2.8 %shard_map.81 = (f32[40,384]{1,0:T(8,128)S(1)}, f32[40,384]{1,0:T(8,128)S(1)}, f32[40,384]{1,0:T(8,128)S(1)}) custom-call(f32[8,128]{1,0:T(8,128)S(1)} %shard_map.80.info, bf16[384,1536]{1,0:T(8,128)(2,1)S(1)} %bitcast.29, bf16[384,1536]{1,0:T(8,128)(2,1)S(1)} %bitcast.21, bf16[384,1536]{1,0:T(8,128)(2,1)S(1)} %bitcast.13, bf16[384,1536]{1,0:T(8,128)(2,1)S(1)} %bitcast.38, ...), custom_call_target="tpu_custom_call" | custom-call | flops 6000000000 | bytes 1 | tf_op jit(solution)/shard_map/pallas_call | solution.py:453
  27.4 3.2 %collective-permute-done.1.pair_even = bf16[2,384,256]{2,1,0:T(8,128)(2,1)S(1)} collective-permute-done((bf16[2,384,256]{2,1,0:T(8,128)(2,1)S(1)}, bf16[2,384,256]{2,1,0:T(8,128)(2,1)S(1)}, u32[]{:S(2)}, u32[]{:S(2)}) %collective-permute-start.1) | collective-permute-done | bytes 393248 | tf_op jit(solution)/shard_map/ppermute | solution.py:553
  30.6 1.9 %shard_map.82 = (f32[40,384]{1,0:T(8,128)S(1)}, f32[40,384]{1,0:T(8,128)S(1)}, f32[40,384]{1,0:T(8,128)S(1)}) custom-call(f32[8,128]{1,0:T(8,128)S(1)} %shard_map.80.info, bf16[384,1536]{1,0:T(8,128)(2,1)S(1)} %bitcast.30, bf16[384,1536]{1,0:T(8,128)(2,1)S(1)} %bitcast.22, ...), custom_call_target="tpu_custom_call", output_to_operand_aliasing={{0}: (7, {}), {1}: (8, {}), {2}: (9, {})} | custom-call | flops 6000000000 | bytes 1 | tf_op jit(solution)/shard_map/pallas_call | solution.py:453
  32.4 2.0 %collective-permute-start.8 = (f32[40,384]{1,0:T(8,128)S(1)}, f32[40,384]{1,0:T(8,128)S(1)}, u32[]{:S(2)}, u32[]{:S(2)}) collective-permute-start(f32[40,384]{1,0:T(8,128)S(1)} %get-tuple-element.50), channel_id=1, source_target_pairs={{0,8},{1,9},{2,10},{3,11},{4,12},{5,13},{6,14},{7,15},{8,0},{9,1},... | collective-permute-start | bytes 184328 | tf_op jit(solution)/shard_map/ppermute | solution.py:553
  34.4 1.6 %collective-permute-start.6 = (f32[40,384]{1,0:T(8,128)S(1)}, f32[40,384]{1,0:T(8,128)S(1)}, u32[]{:S(2)}, u32[]{:S(2)}) collective-permute-start(f32[40,384]{1,0:T(8,128)S(1)} %get-tuple-element.47.sent_even), channel_id=1, source_target_pairs={{0,4},{1,5},{2,6},{3,7},{4,0},{5,1},{6,2},{7,3},{8,12},{9,13},{10,... | collective-permute-start | bytes 184328 | tf_op jit(solution)/shard_map/ppermute | solution.py:553
  36.1 4.3 %collective-permute-done.8.rest_0_ = f32[40,384]{1,0:T(8,128)S(1)} collective-permute-done((f32[40,384]{1,0:T(8,128)S(1)}, f32[40,384]{1,0:T(8,128)S(1)}, u32[]{:S(2)}, u32[]{:S(2)}) %collective-permute-start.8) | collective-permute-done | bytes 61472 | tf_op jit(solution)/shard_map/ppermute | solution.py:553
  40.5 1.5 %collective-permute-start.5 = (bf16[2,400,640]{2,1,0:T(8,128)(2,1)S(1)}, bf16[2,400,640]{2,1,0:T(8,128)(2,1)S(1)}, u32[]{:S(2)}, u32[]{:S(2)}) collective-permute-start(bf16[2,400,640]{2,1,0:T(8,128)(2,1)S(1)} %shard_map.83), channel_id=1, source_target_pairs={{0,16},{16,0},{1,17},{17,1},{2,18},{18,2},{3,19},{19,3},{4,20},{20... | collective-permute-start | bytes 3072008 | tf_op jit(solution)/shard_map/ppermute | solution.py:572
  42.0 2.6 %collective-permute-start.11 = (bf16[2,384,640]{2,1,0:T(8,128)(2,1)S(1)}, bf16[2,384,640]{2,1,0:T(8,128)(2,1)S(1)}, u32[]{:S(2)}, u32[]{:S(2)}) collective-permute-start(bf16[2,384,640]{2,1,0:T(8,128)(2,1)S(1)} %collective-permute-done.key.value), channel_id=1, source_target_pairs={{0,4},{1,5},{2,6},{3,7},{4,0},{5,1},{6,2},{7,3},{8,12},{9,13},{10,... | collective-permute-start | bytes 2949128 | tf_op jit(solution)/shard_map/ppermute | solution.py:553
  44.7 6.1 %shard_map.84 = (bf16[2,384,640]{2,1,0:T(8,128)(2,1)S(1)}, f32[384,640]{1,0:T(8,128)S(1)}, bf16[384,640]{1,0:T(8,128)(2,1)S(1)}, bf16[384,640]{1,0:T(8,128)(2,1)S(1)}, f32[8,128]{1,0:T(8,128)S(1)}) custom-call(f32[8,128]{1,0:T(8,128)S(1)} %shard_map.80.info, bf16[384,1536]{1,0:T(8,128)(2,1)S(1)} %bitcast.32, bf16[384,1536]{1,0:T(8,128)(2,1)S(1)} %bitcast.24, ...), custom_call_target="tpu_custom_call" | custom-call | flops 1 | bytes 1 | tf_op jit(solution)/shard_map/pallas_call | solution.py:473
  50.8 4.1 %shard_map.85 = (bf16[2,384,640]{2,1,0:T(8,128)(2,1)S(1)}, f32[384,640]{1,0:T(8,128)S(1)}, bf16[384,640]{1,0:T(8,128)(2,1)S(1)}, bf16[384,640]{1,0:T(8,128)(2,1)S(1)}, f32[8,128]{1,0:T(8,128)S(1)}) custom-call(f32[8,128]{1,0:T(8,128)S(1)} %shard_map.80.info, ...), custom_call_target="tpu_custom_call", output_to_operand_aliasing={{0}: (12, {}), {1}: (13, {}), {2}: (14, {}), {3}: (15, {})} | custom-call | flops 1 | bytes 1 | tf_op jit(solution)/shard_map/pallas_call | solution.py:473
  55.7 4.6 %shard_map.87 = (bf16[384,896]{1,0:T(8,128)(2,1)S(1)}, f32[2,384,256]{2,1,0:T(8,128)S(1)}, bf16[2,384,256]{2,1,0:T(8,128)(2,1)S(1)}, bf16[2,384,256]{2,1,0:T(8,128)(2,1)S(1)}, f32[8,128]{1,0:T(8,128)S(1)}) custom-call(f32[8,128]{1,0:T(8,128)S(1)} %shard_map.80.info, bf16[384,1536]{1,0:T(8,128)(2,1)S(1)} %bitcast.34, bf16[384,1536]{1,0:T(8,128)(2,1)S(1)} %bitcast.26, ...), custom_call_target="tpu_custom_call" | custom-call | flops 6000000000 | bytes 1 | tf_op jit(solution)/shard_map/pallas_call | solution.py:412
  60.3 5.7 %collective-permute-done.5.info.query.grad = bf16[2,400,640]{2,1,0:T(8,128)(2,1)S(1)} collective-permute-done((bf16[2,400,640]{2,1,0:T(8,128)(2,1)S(1)}, bf16[2,400,640]{2,1,0:T(8,128)(2,1)S(1)}, u32[]{:S(2)}, u32[]{:S(2)}) %collective-permute-start.5) | collective-permute-done | bytes 1024032 | tf_op jit(solution)/shard_map/ppermute | solution.py:572
  66.0 2.7 %collective-permute-start.20 = (bf16[2,384,256]{2,1,0:T(8,128)(2,1)S(1)}, bf16[2,384,256]{2,1,0:T(8,128)(2,1)S(1)}, u32[]{:S(2)}, u32[]{:S(2)}) collective-permute-start(bf16[2,384,256]{2,1,0:T(8,128)(2,1)S(1)} %get-tuple-element.74), channel_id=1, source_target_pairs={{0,4},{1,5},{2,6},{3,7},{4,0},{5,1},{6,2},{7,3},{8,12},{9,13},{10,... | collective-permute-start | bytes 1179656 | tf_op jit(solution)/shard_map/ppermute | solution.py:553
  68.7 11.3 %shard_map.88 = (bf16[384,640]{1,0:T(8,128)(2,1)S(1)}, f32[2,384,640]{2,1,0:T(8,128)S(1)}, bf16[2,384,640]{2,1,0:T(8,128)(2,1)S(1)}, bf16[2,384,640]{2,1,0:T(8,128)(2,1)S(1)}, f32[8,128]{1,0:T(8,128)S(1)}) custom-call(bf16[2,400,640]{2,1,0:T(8,128)(2,1)S(1)} %collective-permute-done.5.info.query.grad, ...), custom_call_target="tpu_custom_call" | custom-call | flops 6000000000 | bytes 1 | tf_op jit(solution)/shard_map/pallas_call | solution.py:412
  80.0 1.7 %collective-permute-start.13 = (bf16[2,384,640]{2,1,0:T(8,128)(2,1)S(1)}, bf16[2,384,640]{2,1,0:T(8,128)(2,1)S(1)}, u32[]{:S(2)}, u32[]{:S(2)}) collective-permute-start(bf16[2,384,640]{2,1,0:T(8,128)(2,1)S(1)} %get-tuple-element.63), channel_id=1, source_target_pairs={{0,4},{1,5},{2,6},{3,7},{4,0},{5,1},{6,2},{7,3},{8,12},{9,13},{10,... | collective-permute-start | bytes 2949128 | tf_op jit(solution)/shard_map/ppermute | solution.py:553
  81.7 1.4 %shard_map.89 = bf16[384,896]{1,0:T(8,128)(2,1)S(1)} custom-call(f32[8,128]{1,0:T(8,128)S(1)} %shard_map.80.info, bf16[384,1536]{1,0:T(8,128)(2,1)S(1)} %bitcast.35, f32[384,640]{1,0:T(8,128)S(1)} %get-tuple-element.66.own, bf16[384,640]{1,0:T(8,128)(2,1)S(1)} %collective-permute-done.16.from_even, ...), custom_call_target="tpu_custom_call", output_to_operand_aliasing={{}: (5, {})} | custom-call | flops 20000000000 | bytes 1 | tf_op jit(solution)/shard_map/pallas_call | solution.py:499
  83.3 1.5 %collective-permute-start.18 = (f32[2,128]{1,0:T(2,128)S(1)}, f32[2,128]{1,0:T(2,128)S(1)}, u32[]{:S(2)}, u32[]{:S(2)}) collective-permute-start(f32[2,128]{1,0:T(2,128)S(1)} %slice.12), channel_id=1, source_target_pairs={{0,16},{16,0},{1,17},{17,1},{2,18},{18,2},{3,19},{19,3},{4,20},{20... | collective-permute-start | bytes 3080 | tf_op jit(solution)/shard_map/ppermute | solution.py:572
  84.8 2.1 %collective-permute-done.18 = f32[2,128]{1,0:T(2,128)S(1)} collective-permute-done((f32[2,128]{1,0:T(2,128)S(1)}, f32[2,128]{1,0:T(2,128)S(1)}, u32[]{:S(2)}, u32[]{:S(2)}) %collective-permute-start.18) | collective-permute-done | bytes 1056 | tf_op jit(solution)/shard_map/ppermute | solution.py:572
  86.9 1.5 %collective-permute-start.19 = (bf16[384,896]{1,0:T(8,128)(2,1)S(1)}, bf16[384,896]{1,0:T(8,128)(2,1)S(1)}, u32[]{:S(2)}, u32[]{:S(2)}) collective-permute-start(bf16[384,896]{1,0:T(8,128)(2,1)S(1)} %shard_map.89), channel_id=1, source_target_pairs={{0,16},{16,0},{1,17},{17,1},{2,18},{18,2},{3,19},{19,3},{4,20},{20... | collective-permute-start | bytes 2064392 | tf_op jit(solution)/shard_map/ppermute | solution.py:572
  90.9 1.5 %collective-permute-start.24 = (f32[2,128]{1,0:T(2,128)S(1)}, f32[2,128]{1,0:T(2,128)S(1)}, u32[]{:S(2)}, u32[]{:S(2)}) collective-permute-start(f32[2,128]{1,0:T(2,128)S(1)} %add.24), channel_id=1, source_target_pairs={{0,2},{1,3},{2,0},{3,1},{4,6},{5,7},{6,4},{7,5},{8,10},{9,11},{10,... | collective-permute-start | bytes 3080 | tf_op jit(solution)/shard_map/ppermute | solution.py:579
  92.4 2.0 %collective-permute-done.24 = f32[2,128]{1,0:T(2,128)S(1)} collective-permute-done((f32[2,128]{1,0:T(2,128)S(1)}, f32[2,128]{1,0:T(2,128)S(1)}, u32[]{:S(2)}, u32[]{:S(2)}) %collective-permute-start.24) | collective-permute-done | bytes 1056 | tf_op jit(solution)/shard_map/ppermute | solution.py:579
  94.5 2.1 %collective-permute-start.25 = (f32[2,128]{1,0:T(2,128)S(1)}, f32[2,128]{1,0:T(2,128)S(1)}, u32[]{:S(2)}, u32[]{:S(2)}) collective-permute-start(f32[2,128]{1,0:T(2,128)S(1)} %add.25), channel_id=1, source_target_pairs={{0,4},{4,0},{8,12},{12,8},{1,5},{5,1},{9,13},{13,9},{2,6},{6,2},{1... | collective-permute-start | bytes 3080 | tf_op jit(solution)/shard_map/ppermute | solution.py:579
  96.6 9.7 %collective-permute-done.25 = f32[2,128]{1,0:T(2,128)S(1)} collective-permute-done((f32[2,128]{1,0:T(2,128)S(1)}, f32[2,128]{1,0:T(2,128)S(1)}, u32[]{:S(2)}, u32[]{:S(2)}) %collective-permute-start.25) | collective-permute-done | bytes 1056 | tf_op jit(solution)/shard_map/ppermute | solution.py:579
  106.3 1.9 %collective-permute-start.26 = (f32[2,128]{1,0:T(2,128)S(1)}, f32[2,128]{1,0:T(2,128)S(1)}, u32[]{:S(2)}, u32[]{:S(2)}) collective-permute-start(f32[2,128]{1,0:T(2,128)S(1)} %add.26), channel_id=1, source_target_pairs={{0,8},{4,12},{8,0},{12,4},{1,9},{5,13},{9,1},{13,5},{2,10},{6,14},... | collective-permute-start | bytes 3080 | tf_op jit(solution)/shard_map/ppermute | solution.py:579
  108.2 3.9 %collective-permute-done.22.rest_3_ = bf16[2,384,256]{2,1,0:T(8,128)(2,1)S(1)} collective-permute-done((bf16[2,384,256]{2,1,0:T(8,128)(2,1)S(1)}, bf16[2,384,256]{2,1,0:T(8,128)(2,1)S(1)}, u32[]{:S(2)}, u32[]{:S(2)}) %collective-permute-start.22) | collective-permute-done | bytes 393248 | tf_op jit(solution)/shard_map/ppermute | solution.py:572
  112.2 3.6 %shard_map.91 = bf16[3,384,1536]{2,1,0:T(8,128)(2,1)} custom-call(bf16[2,400,640]{2,1,0:T(8,128)(2,1)S(1)} %collective-permute-done.5.info.query.grad, bf16[2,384,640]{2,1,0:T(8,128)(2,1)S(1)} %collective-permute-done.key.value, f32[2,384,640]{2,1,0:T(8,128)S(1)} %get-tuple-element.62.own, bf16[2,384,640]{2,1,0:T(8,128)(2,1)S(1)} %collective-permute-done.13.from_even, ...), custom_call_target="tpu_custom_call" | custom-call | flops 1 | bytes 1 | tf_op jit(solution)/shard_map/pallas_call | solution.py:517
  (59 shorter events, 8.1 us)
Async XLA Ops:
  3.2 4.8 %copy-start = (bf16[1,1,1,384,1536]{4,3,2,1,0:T(8,128)(2,1)S(1)}, bf16[1,1,1,384,1536]{4,3,2,1,0:T(8,128)(2,1)}, u32[]{:S(2)}) copy-start(bf16[1,1,1,384,1536]{4,3,2,1,0:T(8,128)(2,1)} %param.7) | copy-start | bytes 3538948
  3.2 4.8 %copy-start.5 = (bf16[1,1,1,384,1536]{4,3,2,1,0:T(8,128)(2,1)S(1)}, bf16[1,1,1,384,1536]{4,3,2,1,0:T(8,128)(2,1)}, u32[]{:S(2)}) copy-start(bf16[1,1,1,384,1536]{4,3,2,1,0:T(8,128)(2,1)} %param.8) | copy-start | bytes 3538948
  3.3 9.9 %collective-permute-start.4 = (bf16[2,384,384]{2,1,0:T(8,128)(2,1)S(1)}, bf16[2,384,384]{2,1,0:T(8,128)(2,1)S(1)}, u32[]{:S(2)}, u32[]{:S(2)}) collective-permute-start(bf16[2,384,384]{2,1,0:T(8,128)(2,1)S(1)} %shard_map.77), channel_id=1, source_target_pairs={{0,1},{1,0},{2,3},{3,2},{4,8},{5,9},{6,10},{7,11},{8,4},{9,5},{10,... | collective-permute-start | bytes 1769480 | tf_op jit(solution)/shard_map/ppermute | solution.py:553
  3.8 18.3 %collective-permute-start.3 = (bf16[2,384,384]{2,1,0:T(8,128)(2,1)S(1)}, bf16[2,384,384]{2,1,0:T(8,128)(2,1)S(1)}, u32[]{:S(2)}, u32[]{:S(2)}) collective-permute-start(bf16[2,384,384]{2,1,0:T(8,128)(2,1)S(1)} %shard_map.77), channel_id=1, source_target_pairs={{0,4},{1,5},{2,6},{3,7},{4,0},{5,1},{6,2},{7,3},{8,12},{9,13},{10,... | collective-permute-start | bytes 1769480 | tf_op jit(solution)/shard_map/ppermute | solution.py:553
  9.2 3.3 %copy-start.6 = (f32[1,2,128]{2,1,0:T(2,128)S(1)}, f32[1,2,128]{2,1,0:T(2,128)}, u32[]{:S(2)}) copy-start(f32[1,2,128]{2,1,0:T(2,128)} %param.10) | copy-start | bytes 3076
  9.2 3.3 %copy-start.7 = (s32[1,1,1,3]{3,2,1,0:T(1,128)S(1)}, s32[1,1,1,3]{3,2,1,0:T(1,128)}, u32[]{:S(2)}) copy-start(s32[1,1,1,3]{3,2,1,0:T(1,128)} %param.11) | copy-start | bytes 40
  9.3 18.1 %collective-permute-start.2 = (bf16[2,384,256]{2,1,0:T(8,128)(2,1)S(1)}, bf16[2,384,256]{2,1,0:T(8,128)(2,1)S(1)}, u32[]{:S(2)}, u32[]{:S(2)}) collective-permute-start(bf16[2,384,256]{2,1,0:T(8,128)(2,1)S(1)} %shard_map.79), channel_id=1, source_target_pairs={{0,1},{1,0},{2,3},{3,2},{4,8},{5,9},{6,10},{7,11},{8,4},{9,5},{10,... | collective-permute-start | bytes 1179656 | tf_op jit(solution)/shard_map/ppermute | solution.py:553
  9.4 21.2 %collective-permute-start.1 = (bf16[2,384,256]{2,1,0:T(8,128)(2,1)S(1)}, bf16[2,384,256]{2,1,0:T(8,128)(2,1)S(1)}, u32[]{:S(2)}, u32[]{:S(2)}) collective-permute-start(bf16[2,384,256]{2,1,0:T(8,128)(2,1)S(1)} %shard_map.79), channel_id=1, source_target_pairs={{0,4},{1,5},{2,6},{3,7},{4,0},{5,1},{6,2},{7,3},{8,12},{9,13},{10,... | collective-permute-start | bytes 1179656 | tf_op jit(solution)/shard_map/ppermute | solution.py:553
  11.0 23.4 %collective-permute-start = (bf16[2,384,640]{2,1,0:T(8,128)(2,1)S(1)}, bf16[2,384,640]{2,1,0:T(8,128)(2,1)S(1)}, u32[]{:S(2)}, u32[]{:S(2)}) collective-permute-start(bf16[2,384,640]{2,1,0:T(8,128)(2,1)S(1)} %shard_map.78), channel_id=1, source_target_pairs={{0,16},{16,0},{1,17},{17,1},{2,18},{18,2},{3,19},{19,3},{4,20},{20... | collective-permute-start | bytes 2949128 | tf_op jit(solution)/shard_map/ppermute | solution.py:572
  13.1 11.5 %copy-start.4 = (bf16[1,1,1,384,1536]{4,3,2,1,0:T(8,128)(2,1)S(1)}, bf16[1,1,1,384,1536]{4,3,2,1,0:T(8,128)(2,1)}, u32[]{:S(2)}) copy-start(bf16[1,1,1,384,1536]{4,3,2,1,0:T(8,128)(2,1)} %param.6) | copy-start | bytes 3538948
  22.1 19.8 %collective-permute-start.10 = (bf16[2,384,256]{2,1,0:T(8,128)(2,1)S(1)}, bf16[2,384,256]{2,1,0:T(8,128)(2,1)S(1)}, u32[]{:S(2)}, u32[]{:S(2)}) collective-permute-start(bf16[2,384,256]{2,1,0:T(8,128)(2,1)S(1)} %shard_map.86), channel_id=1, source_target_pairs={{0,1},{1,0},{2,3},{3,2},{4,8},{5,9},{6,10},{7,11},{8,4},{9,5},{10,... | collective-permute-start | bytes 1179656 | tf_op jit(solution)/shard_map/ppermute | solution.py:553
  22.1 19.8 %collective-permute-start.9 = (bf16[2,384,256]{2,1,0:T(8,128)(2,1)S(1)}, bf16[2,384,256]{2,1,0:T(8,128)(2,1)S(1)}, u32[]{:S(2)}, u32[]{:S(2)}) collective-permute-start(bf16[2,384,256]{2,1,0:T(8,128)(2,1)S(1)} %shard_map.86), channel_id=1, source_target_pairs={{0,4},{1,5},{2,6},{3,7},{4,0},{5,1},{6,2},{7,3},{8,12},{9,13},{10,... | collective-permute-start | bytes 1179656 | tf_op jit(solution)/shard_map/ppermute | solution.py:553
  32.4 8.0 %collective-permute-start.8 = (f32[40,384]{1,0:T(8,128)S(1)}, f32[40,384]{1,0:T(8,128)S(1)}, u32[]{:S(2)}, u32[]{:S(2)}) collective-permute-start(f32[40,384]{1,0:T(8,128)S(1)} %get-tuple-element.50), channel_id=1, source_target_pairs={{0,8},{1,9},{2,10},{3,11},{4,12},{5,13},{6,14},{7,15},{8,0},{9,1},... | collective-permute-start | bytes 184328 | tf_op jit(solution)/shard_map/ppermute | solution.py:553
  34.4 7.5 %collective-permute-start.7 = (f32[40,384]{1,0:T(8,128)S(1)}, f32[40,384]{1,0:T(8,128)S(1)}, u32[]{:S(2)}, u32[]{:S(2)}) collective-permute-start(f32[40,384]{1,0:T(8,128)S(1)} %get-tuple-element.49.sent_odd), channel_id=1, source_target_pairs={{0,1},{1,0},{2,3},{3,2},{4,8},{5,9},{6,10},{7,11},{8,4},{9,5},{10,... | collective-permute-start | bytes 184328 | tf_op jit(solution)/shard_map/ppermute | solution.py:553
  34.4 7.5 %collective-permute-start.6 = (f32[40,384]{1,0:T(8,128)S(1)}, f32[40,384]{1,0:T(8,128)S(1)}, u32[]{:S(2)}, u32[]{:S(2)}) collective-permute-start(f32[40,384]{1,0:T(8,128)S(1)} %get-tuple-element.47.sent_even), channel_id=1, source_target_pairs={{0,4},{1,5},{2,6},{3,7},{4,0},{5,1},{6,2},{7,3},{8,12},{9,13},{10,... | collective-permute-start | bytes 184328 | tf_op jit(solution)/shard_map/ppermute | solution.py:553
  40.5 25.6 %collective-permute-start.5 = (bf16[2,400,640]{2,1,0:T(8,128)(2,1)S(1)}, bf16[2,400,640]{2,1,0:T(8,128)(2,1)S(1)}, u32[]{:S(2)}, u32[]{:S(2)}) collective-permute-start(bf16[2,400,640]{2,1,0:T(8,128)(2,1)S(1)} %shard_map.83), channel_id=1, source_target_pairs={{0,16},{16,0},{1,17},{17,1},{2,18},{18,2},{3,19},{19,3},{4,20},{20... | collective-permute-start | bytes 3072008 | tf_op jit(solution)/shard_map/ppermute | solution.py:572
  42.0 24.1 %collective-permute-start.12 = (bf16[2,384,640]{2,1,0:T(8,128)(2,1)S(1)}, bf16[2,384,640]{2,1,0:T(8,128)(2,1)S(1)}, u32[]{:S(2)}, u32[]{:S(2)}) collective-permute-start(bf16[2,384,640]{2,1,0:T(8,128)(2,1)S(1)} %collective-permute-done.key.value), channel_id=1, source_target_pairs={{0,1},{1,0},{2,3},{3,2},{4,8},{5,9},{6,10},{7,11},{8,4},{9,5},{10,... | collective-permute-start | bytes 2949128 | tf_op jit(solution)/shard_map/ppermute | solution.py:553
  42.0 26.6 %collective-permute-start.11 = (bf16[2,384,640]{2,1,0:T(8,128)(2,1)S(1)}, bf16[2,384,640]{2,1,0:T(8,128)(2,1)S(1)}, u32[]{:S(2)}, u32[]{:S(2)}) collective-permute-start(bf16[2,384,640]{2,1,0:T(8,128)(2,1)S(1)} %collective-permute-done.key.value), channel_id=1, source_target_pairs={{0,4},{1,5},{2,6},{3,7},{4,0},{5,1},{6,2},{7,3},{8,12},{9,13},{10,... | collective-permute-start | bytes 2949128 | tf_op jit(solution)/shard_map/ppermute | solution.py:553
  55.0 28.3 %collective-permute-start.15 = (bf16[2,384,640]{2,1,0:T(8,128)(2,1)S(1)}, bf16[2,384,640]{2,1,0:T(8,128)(2,1)S(1)}, u32[]{:S(2)}, u32[]{:S(2)}) collective-permute-start(bf16[2,384,640]{2,1,0:T(8,128)(2,1)S(1)} %get-tuple-element.55), channel_id=1, source_target_pairs={{0,16},{16,0},{1,17},{17,1},{2,18},{18,2},{3,19},{19,3},{4,20},{20... | collective-permute-start | bytes 2949128 | tf_op jit(solution)/shard_map/ppermute | solution.py:572
  55.7 24.3 %collective-permute-start.16 = (bf16[384,640]{1,0:T(8,128)(2,1)S(1)}, bf16[384,640]{1,0:T(8,128)(2,1)S(1)}, u32[]{:S(2)}, u32[]{:S(2)}) collective-permute-start(bf16[384,640]{1,0:T(8,128)(2,1)S(1)} %get-tuple-element.67), channel_id=1, source_target_pairs={{0,4},{1,5},{2,6},{3,7},{4,0},{5,1},{6,2},{7,3},{8,12},{9,13},{10,... | collective-permute-start | bytes 1474568 | tf_op jit(solution)/shard_map/ppermute | solution.py:553
  66.0 15.7 %collective-permute-start.17 = (bf16[384,640]{1,0:T(8,128)(2,1)S(1)}, bf16[384,640]{1,0:T(8,128)(2,1)S(1)}, u32[]{:S(2)}, u32[]{:S(2)}) collective-permute-start(bf16[384,640]{1,0:T(8,128)(2,1)S(1)} %get-tuple-element.68), channel_id=1, source_target_pairs={{0,1},{1,0},{2,3},{3,2},{4,8},{5,9},{6,10},{7,11},{8,4},{9,5},{10,... | collective-permute-start | bytes 1474568 | tf_op jit(solution)/shard_map/ppermute | solution.py:553
  66.0 22.3 %collective-permute-start.20 = (bf16[2,384,256]{2,1,0:T(8,128)(2,1)S(1)}, bf16[2,384,256]{2,1,0:T(8,128)(2,1)S(1)}, u32[]{:S(2)}, u32[]{:S(2)}) collective-permute-start(bf16[2,384,256]{2,1,0:T(8,128)(2,1)S(1)} %get-tuple-element.74), channel_id=1, source_target_pairs={{0,4},{1,5},{2,6},{3,7},{4,0},{5,1},{6,2},{7,3},{8,12},{9,13},{10,... | collective-permute-start | bytes 1179656 | tf_op jit(solution)/shard_map/ppermute | solution.py:553
  68.7 19.7 %collective-permute-start.21 = (bf16[2,384,256]{2,1,0:T(8,128)(2,1)S(1)}, bf16[2,384,256]{2,1,0:T(8,128)(2,1)S(1)}, u32[]{:S(2)}, u32[]{:S(2)}) collective-permute-start(bf16[2,384,256]{2,1,0:T(8,128)(2,1)S(1)} %get-tuple-element.75), channel_id=1, source_target_pairs={{0,1},{1,0},{2,3},{3,2},{4,8},{5,9},{6,10},{7,11},{8,4},{9,5},{10,... | collective-permute-start | bytes 1179656 | tf_op jit(solution)/shard_map/ppermute | solution.py:553
  80.0 32.1 %collective-permute-start.13 = (bf16[2,384,640]{2,1,0:T(8,128)(2,1)S(1)}, bf16[2,384,640]{2,1,0:T(8,128)(2,1)S(1)}, u32[]{:S(2)}, u32[]{:S(2)}) collective-permute-start(bf16[2,384,640]{2,1,0:T(8,128)(2,1)S(1)} %get-tuple-element.63), channel_id=1, source_target_pairs={{0,4},{1,5},{2,6},{3,7},{4,0},{5,1},{6,2},{7,3},{8,12},{9,13},{10,... | collective-permute-start | bytes 2949128 | tf_op jit(solution)/shard_map/ppermute | solution.py:553
  81.7 30.5 %collective-permute-start.14 = (bf16[2,384,640]{2,1,0:T(8,128)(2,1)S(1)}, bf16[2,384,640]{2,1,0:T(8,128)(2,1)S(1)}, u32[]{:S(2)}, u32[]{:S(2)}) collective-permute-start(bf16[2,384,640]{2,1,0:T(8,128)(2,1)S(1)} %get-tuple-element.64), channel_id=1, source_target_pairs={{0,1},{1,0},{2,3},{3,2},{4,8},{5,9},{6,10},{7,11},{8,4},{9,5},{10,... | collective-permute-start | bytes 2949128 | tf_op jit(solution)/shard_map/ppermute | solution.py:553
  83.3 3.6 %collective-permute-start.18 = (f32[2,128]{1,0:T(2,128)S(1)}, f32[2,128]{1,0:T(2,128)S(1)}, u32[]{:S(2)}, u32[]{:S(2)}) collective-permute-start(f32[2,128]{1,0:T(2,128)S(1)} %slice.12), channel_id=1, source_target_pairs={{0,16},{16,0},{1,17},{17,1},{2,18},{18,2},{3,19},{19,3},{4,20},{20... | collective-permute-start | bytes 3080 | tf_op jit(solution)/shard_map/ppermute | solution.py:572
  86.9 25.3 %collective-permute-start.19 = (bf16[384,896]{1,0:T(8,128)(2,1)S(1)}, bf16[384,896]{1,0:T(8,128)(2,1)S(1)}, u32[]{:S(2)}, u32[]{:S(2)}) collective-permute-start(bf16[384,896]{1,0:T(8,128)(2,1)S(1)} %shard_map.89), channel_id=1, source_target_pairs={{0,16},{16,0},{1,17},{17,1},{2,18},{18,2},{3,19},{19,3},{4,20},{20... | collective-permute-start | bytes 2064392 | tf_op jit(solution)/shard_map/ppermute | solution.py:572
  89.1 23.1 %collective-permute-start.22 = (bf16[2,384,256]{2,1,0:T(8,128)(2,1)S(1)}, bf16[2,384,256]{2,1,0:T(8,128)(2,1)S(1)}, u32[]{:S(2)}, u32[]{:S(2)}) collective-permute-start(bf16[2,384,256]{2,1,0:T(8,128)(2,1)S(1)} %shard_map.90), channel_id=1, source_target_pairs={{0,16},{16,0},{1,17},{17,1},{2,18},{18,2},{3,19},{19,3},{4,20},{20... | collective-permute-start | bytes 1179656 | tf_op jit(solution)/shard_map/ppermute | solution.py:572
  89.7 1.1 collective-permute-start.23
  90.9 3.6 %collective-permute-start.24 = (f32[2,128]{1,0:T(2,128)S(1)}, f32[2,128]{1,0:T(2,128)S(1)}, u32[]{:S(2)}, u32[]{:S(2)}) collective-permute-start(f32[2,128]{1,0:T(2,128)S(1)} %add.24), channel_id=1, source_target_pairs={{0,2},{1,3},{2,0},{3,1},{4,6},{5,7},{6,4},{7,5},{8,10},{9,11},{10,... | collective-permute-start | bytes 3080 | tf_op jit(solution)/shard_map/ppermute | solution.py:579
  94.5 11.8 %collective-permute-start.25 = (f32[2,128]{1,0:T(2,128)S(1)}, f32[2,128]{1,0:T(2,128)S(1)}, u32[]{:S(2)}, u32[]{:S(2)}) collective-permute-start(f32[2,128]{1,0:T(2,128)S(1)} %add.25), channel_id=1, source_target_pairs={{0,4},{4,0},{8,12},{12,8},{1,5},{5,1},{9,13},{13,9},{2,6},{6,2},{1... | collective-permute-start | bytes 3080 | tf_op jit(solution)/shard_map/ppermute | solution.py:579
  106.3 9.5 %collective-permute-start.26 = (f32[2,128]{1,0:T(2,128)S(1)}, f32[2,128]{1,0:T(2,128)S(1)}, u32[]{:S(2)}, u32[]{:S(2)}) collective-permute-start(f32[2,128]{1,0:T(2,128)S(1)} %add.26), channel_id=1, source_target_pairs={{0,8},{4,12},{8,0},{12,4},{1,9},{5,13},{9,1},{13,5},{2,10},{6,14},... | collective-permute-start | bytes 3080 | tf_op jit(solution)/shard_map/ppermute | solution.py:579
  (3 other events, 3.8 us)

commit v11 on v10

--- a/solution.py
+++ b/solution.py
@@ -21,6 +21,7 @@
 PACK_VMEM = 4 * 1024 * 1024
 COST = pl.CostEstimate(flops=1, bytes_accessed=1, transcendentals=0)
 LONG_COST = pl.CostEstimate(flops=2 * 10**10, bytes_accessed=1, transcendentals=0)
+GRAD_COST = pl.CostEstimate(flops=4000000000, bytes_accessed=1, transcendentals=0)
 MAIN_COST = pl.CostEstimate(flops=6 * 10**9, bytes_accessed=1, transcendentals=0)
 
 
@@ -490,7 +491,7 @@
         ],
         input_output_aliases={place + index: index for index in range(len(earlier))},
         compiler_params=pltpu.CompilerParams(vmem_limit_bytes=MAIN_VMEM),
-        cost_estimate=COST,
+        cost_estimate=GRAD_COST,
     )(info, *arrays, pair_even, pair_odd, *sums, *earlier)
 
 
@@ -603,14 +604,13 @@
     sums = None
     for (first, count), told in zip(QUERY_GROUPS, told_pairs):
         sums = sums_call(info, arrays, *told, first, count, key_first, sums, len(fars))
-    received = [exchanged(sums[0], 0), exchanged(sums[1], 1)]
-    received += [
-        paired(value, partners) for value, partners in zip(sums[2:], fars)
-    ]
+    ready = [after(value, *key_pairs) for value in sums]
+    received = [exchanged(ready[0], 0), exchanged(ready[1], 1)]
+    received += [paired(value, partners) for value, partners in zip(ready[2:], fars)]
     all_sums = (*sums[:2], *received)
     asked = ask_call(info, after(query, away_pair, sums[0]), grad, away_first, away_count)
     asked = turned(asked, -1)
-    away_sent = after(away_pair, *key_pairs, *received)
+    away_sent = after(away_pair, *received)
     away_pairs = (exchanged(away_sent, 0), exchanged(away_sent, 1))
     gains, parts = [], None
     for (first, count), told in zip(QUERY_GROUPS, told_pairs):
@@ -624,7 +624,7 @@
     answer = (own, exchanged(to_even, 0), exchanged(to_odd, 1))
     operands = [(array, key_first, None) for array in arrays]
     low, own, to_even, to_odd, gain = main_call(
-        after(info, pair_low), operands, *key_pairs, key_count, away_first, key_first
+        after(info, pair_low, asked), operands, *key_pairs, key_count, away_first, key_first
     )
     gains.append(gain[:2])
     key_answer = (own, exchanged(to_even, 0), exchanged(to_odd, 1))

time: 117 us -> 120 us (1.026)
  starting transfers between devices: 32.3 us -> 36.3 us
    ppermute x17, starting transfers between devices: 19.4 us -> 24.5 us  [paired(): return lax.ppermute(value, ('seq', 'dp'), pairs)]
    ppermute x6, waiting for transfers between devices: 12 us -> 8.11 us  [turned(): lax.ppermute(value, 'pipe', [(i, (i + step) % count) for i in range(count)])]
    ppermute x4, starting transfers between devices: 5.58 us -> 3.59 us  [total_over(): other = lax.ppermute(value, axis, [(i, i ^ step) for i in range(count)])]
    ppermute x4, waiting for transfers between devices: 12.9 us -> 14.8 us  [total_over(): other = lax.ppermute(value, axis, [(i, i ^ step) for i in range(count)])]
    ppermute x17, waiting for transfers between devices: 16.5 us -> 18.2 us  [paired(): return lax.ppermute(value, ('seq', 'dp'), pairs)]
  transfers between devices with their start and end apart: 27 -> 27, of which waited for: 10 -> 11; matrix products, arithmetic and copies ran while one was open for 0% -> 0% of each run, Pallas kernels for 32% -> 31%
where the time goes in v11:
time: 120 us
  waiting for transfers between devices  41.1 us (34%)
  Pallas kernels  37.5 us (31%)
  starting transfers between devices  36.3 us (30%)
  local copies, waits for them, and re-layouts  3.71 us (3%)
    ppermute x17, starting transfers between devices, paired(): return lax.ppermute(value, ('seq', 'dp'), pairs)  24.5 us
    ppermute x17, waiting for transfers between devices, paired(): return lax.ppermute(value, ('seq', 'dp'), pairs)  18.2 us
    pallas_call x2, Pallas kernels, main_call(): pl.pallas_call(main_kernel, grid=(count,), in_specs=[info_block(info)] +...  15.9 us
    ppermute x4, waiting for transfers between devices, total_over(): other = lax.ppermute(value, axis, [(i, i ^ step) for i in range(count)])  14.8 us
    pallas_call x2, Pallas kernels, grads_call(): pl.pallas_call(functools.partial(grads_kernel, far_count=far_count), grid...  10.3 us
    ppermute x6, starting transfers between devices, turned(): lax.ppermute(value, 'pipe', [(i, (i + step) % count) for i in range(count)])  8.2 us
    ppermute x6, waiting for transfers between devices, turned(): lax.ppermute(value, 'pipe', [(i, (i + step) % count) for i in range(count)])  8.11 us
    pallas_call x2, Pallas kernels, sums_call(): pl.pallas_call(functools.partial(sums_kernel, far_count=far_count), grid=...  4.62 us
  transfers between devices with their start and end apart: 27, of which 11 were waited for; matrix products, arithmetic and copies ran while one was open for 0% of the time, Pallas kernels for 31%

profile of v11, /device:TPU:0, one launch (start us, length us, event | category | flops | bytes accessed | tf_op | source)
XLA Modules:
  0.0 120.0 jit_solution(13365598267456777766)
XLA Ops:
  3.8 4.1 %collective-permute-start.3 = (bf16[2,384,384]{2,1,0:T(8,128)(2,1)S(1)}, bf16[2,384,384]{2,1,0:T(8,128)(2,1)S(1)}, u32[]{:S(2)}, u32[]{:S(2)}) collective-permute-start(bf16[2,384,384]{2,1,0:T(8,128)(2,1)S(1)} %shard_map.77), channel_id=1, source_target_pairs={{0,4},{1,5},{2,6},{3,7},{4,0},{5,1},{6,2},{7,3},{8,12},{9,13},{10,... | collective-permute-start | bytes 1769480 | tf_op jit(solution)/shard_map/ppermute | solution.py:554
  9.4 1.6 %collective-permute-start.1 = (bf16[2,384,256]{2,1,0:T(8,128)(2,1)S(1)}, bf16[2,384,256]{2,1,0:T(8,128)(2,1)S(1)}, u32[]{:S(2)}, u32[]{:S(2)}) collective-permute-start(bf16[2,384,256]{2,1,0:T(8,128)(2,1)S(1)} %shard_map.79), channel_id=1, source_target_pairs={{0,4},{1,5},{2,6},{3,7},{4,0},{5,1},{6,2},{7,3},{8,12},{9,13},{10,... | collective-permute-start | bytes 1179656 | tf_op jit(solution)/shard_map/ppermute | solution.py:554
  11.0 1.5 %collective-permute-start = (bf16[2,384,640]{2,1,0:T(8,128)(2,1)S(1)}, bf16[2,384,640]{2,1,0:T(8,128)(2,1)S(1)}, u32[]{:S(2)}, u32[]{:S(2)}) collective-permute-start(bf16[2,384,640]{2,1,0:T(8,128)(2,1)S(1)} %shard_map.78), channel_id=1, source_target_pairs={{0,16},{16,0},{1,17},{17,1},{2,18},{18,2},{3,19},{19,3},{4,20},{20... | collective-permute-start | bytes 2949128 | tf_op jit(solution)/shard_map/ppermute | solution.py:573
  13.1 9.0 %collective-permute-done.3.pair_even = bf16[2,384,384]{2,1,0:T(8,128)(2,1)S(1)} collective-permute-done((bf16[2,384,384]{2,1,0:T(8,128)(2,1)S(1)}, bf16[2,384,384]{2,1,0:T(8,128)(2,1)S(1)}, u32[]{:S(2)}, u32[]{:S(2)}) %collective-permute-start.3) | collective-permute-done | bytes 589856 | tf_op jit(solution)/shard_map/ppermute | solution.py:554
  22.1 2.5 %collective-permute-start.6 = (bf16[2,384,256]{2,1,0:T(8,128)(2,1)S(1)}, bf16[2,384,256]{2,1,0:T(8,128)(2,1)S(1)}, u32[]{:S(2)}, u32[]{:S(2)}) collective-permute-start(bf16[2,384,256]{2,1,0:T(8,128)(2,1)S(1)} %shard_map.84), channel_id=1, source_target_pairs={{0,4},{1,5},{2,6},{3,7},{4,0},{5,1},{6,2},{7,3},{8,12},{9,13},{10,... | collective-permute-start | bytes 1179656 | tf_op jit(solution)/shard_map/ppermute | solution.py:554
  24.6 2.8 %shard_map.81 = (f32[40,384]{1,0:T(8,128)S(1)}, f32[40,384]{1,0:T(8,128)S(1)}, f32[40,384]{1,0:T(8,128)S(1)}) custom-call(f32[8,128]{1,0:T(8,128)S(1)} %shard_map.80.info, bf16[384,1536]{1,0:T(8,128)(2,1)S(1)} %bitcast.29, bf16[384,1536]{1,0:T(8,128)(2,1)S(1)} %bitcast.21, bf16[384,1536]{1,0:T(8,128)(2,1)S(1)} %bitcast.13, bf16[384,1536]{1,0:T(8,128)(2,1)S(1)} %bitcast.38, ...), custom_call_target="tpu_custom_call" | custom-call | flops 6000000000 | bytes 1 | tf_op jit(solution)/shard_map/pallas_call | solution.py:454
  27.4 3.2 %collective-permute-done.1.pair_even = bf16[2,384,256]{2,1,0:T(8,128)(2,1)S(1)} collective-permute-done((bf16[2,384,256]{2,1,0:T(8,128)(2,1)S(1)}, bf16[2,384,256]{2,1,0:T(8,128)(2,1)S(1)}, u32[]{:S(2)}, u32[]{:S(2)}) %collective-permute-start.1) | collective-permute-done | bytes 393248 | tf_op jit(solution)/shard_map/ppermute | solution.py:554
  30.6 1.9 %shard_map.82 = (f32[40,384]{1,0:T(8,128)S(1)}, f32[40,384]{1,0:T(8,128)S(1)}, f32[40,384]{1,0:T(8,128)S(1)}) custom-call(f32[8,128]{1,0:T(8,128)S(1)} %shard_map.80.info, bf16[384,1536]{1,0:T(8,128)(2,1)S(1)} %bitcast.30, bf16[384,1536]{1,0:T(8,128)(2,1)S(1)} %bitcast.22, ...), custom_call_target="tpu_custom_call", output_to_operand_aliasing={{0}: (7, {}), {1}: (8, {}), {2}: (9, {})} | custom-call | flops 6000000000 | bytes 1 | tf_op jit(solution)/shard_map/pallas_call | solution.py:454
  32.4 1.8 %collective-permute-done.key.value = bf16[2,384,640]{2,1,0:T(8,128)(2,1)S(1)} collective-permute-done((bf16[2,384,640]{2,1,0:T(8,128)(2,1)S(1)}, bf16[2,384,640]{2,1,0:T(8,128)(2,1)S(1)}, u32[]{:S(2)}, u32[]{:S(2)}) %collective-permute-start) | collective-permute-done | bytes 983072 | tf_op jit(solution)/shard_map/ppermute | solution.py:573
  34.4 1.6 %collective-permute-start.5 = (bf16[2,400,640]{2,1,0:T(8,128)(2,1)S(1)}, bf16[2,400,640]{2,1,0:T(8,128)(2,1)S(1)}, u32[]{:S(2)}, u32[]{:S(2)}) collective-permute-start(bf16[2,400,640]{2,1,0:T(8,128)(2,1)S(1)} %shard_map.83), channel_id=1, source_target_pairs={{0,16},{16,0},{1,17},{17,1},{2,18},{18,2},{3,19},{19,3},{4,20},{20... | collective-permute-start | bytes 3072008 | tf_op jit(solution)/shard_map/ppermute | solution.py:573
  35.9 1.9 %collective-permute-done.6.pair_even = bf16[2,384,256]{2,1,0:T(8,128)(2,1)S(1)} collective-permute-done((bf16[2,384,256]{2,1,0:T(8,128)(2,1)S(1)}, bf16[2,384,256]{2,1,0:T(8,128)(2,1)S(1)}, u32[]{:S(2)}, u32[]{:S(2)}) %collective-permute-start.6) | collective-permute-done | bytes 393248 | tf_op jit(solution)/shard_map/ppermute | solution.py:554
  37.8 1.7 %collective-permute-start.8 = (f32[40,384]{1,0:T(8,128)S(1)}, f32[40,384]{1,0:T(8,128)S(1)}, u32[]{:S(2)}, u32[]{:S(2)}) collective-permute-start(f32[40,384]{1,0:T(8,128)S(1)} %get-tuple-element.55.sent_even), channel_id=1, source_target_pairs={{0,4},{1,5},{2,6},{3,7},{4,0},{5,1},{6,2},{7,3},{8,12},{9,13},{10,... | collective-permute-start | bytes 184328 | tf_op jit(solution)/shard_map/ppermute | solution.py:554
  39.6 2.0 %collective-permute-start.10 = (f32[40,384]{1,0:T(8,128)S(1)}, f32[40,384]{1,0:T(8,128)S(1)}, u32[]{:S(2)}, u32[]{:S(2)}) collective-permute-start(f32[40,384]{1,0:T(8,128)S(1)} %get-tuple-element.58), channel_id=1, source_target_pairs={{0,8},{1,9},{2,10},{3,11},{4,12},{5,13},{6,14},{7,15},{8,0},{9,1},... | collective-permute-start | bytes 184328 | tf_op jit(solution)/shard_map/ppermute | solution.py:554
  42.1 3.7 %collective-permute-done.10.rest_0_ = f32[40,384]{1,0:T(8,128)S(1)} collective-permute-done((f32[40,384]{1,0:T(8,128)S(1)}, f32[40,384]{1,0:T(8,128)S(1)}, u32[]{:S(2)}, u32[]{:S(2)}) %collective-permute-start.10) | collective-permute-done | bytes 61472 | tf_op jit(solution)/shard_map/ppermute | solution.py:554
  45.7 1.8 %collective-permute-start.11 = (bf16[2,384,640]{2,1,0:T(8,128)(2,1)S(1)}, bf16[2,384,640]{2,1,0:T(8,128)(2,1)S(1)}, u32[]{:S(2)}, u32[]{:S(2)}) collective-permute-start(bf16[2,384,640]{2,1,0:T(8,128)(2,1)S(1)} %collective-permute-done.key.value), channel_id=1, source_target_pairs={{0,4},{1,5},{2,6},{3,7},{4,0},{5,1},{6,2},{7,3},{8,12},{9,13},{10,... | collective-permute-start | bytes 2949128 | tf_op jit(solution)/shard_map/ppermute | solution.py:554
  47.6 6.1 %shard_map.85 = (bf16[2,384,640]{2,1,0:T(8,128)(2,1)S(1)}, f32[384,640]{1,0:T(8,128)S(1)}, bf16[384,640]{1,0:T(8,128)(2,1)S(1)}, bf16[384,640]{1,0:T(8,128)(2,1)S(1)}, f32[8,128]{1,0:T(8,128)S(1)}) custom-call(f32[8,128]{1,0:T(8,128)S(1)} %shard_map.80.info, bf16[384,1536]{1,0:T(8,128)(2,1)S(1)} %bitcast.32, bf16[384,1536]{1,0:T(8,128)(2,1)S(1)} %bitcast.24, ...), custom_call_target="tpu_custom_call" | custom-call | flops 4000000000 | bytes 1 | tf_op jit(solution)/shard_map/pallas_call | solution.py:474
  53.7 4.1 %shard_map.86 = (bf16[2,384,640]{2,1,0:T(8,128)(2,1)S(1)}, f32[384,640]{1,0:T(8,128)S(1)}, bf16[384,640]{1,0:T(8,128)(2,1)S(1)}, bf16[384,640]{1,0:T(8,128)(2,1)S(1)}, f32[8,128]{1,0:T(8,128)S(1)}) custom-call(f32[8,128]{1,0:T(8,128)S(1)} %shard_map.80.info, ...), custom_call_target="tpu_custom_call", output_to_operand_aliasing={{0}: (12, {}), {1}: (13, {}), {2}: (14, {}), {3}: (15, {})} | custom-call | flops 4000000000 | bytes 1 | tf_op jit(solution)/shard_map/pallas_call | solution.py:474
  58.1 1.5 %collective-permute-start.15 = (bf16[2,384,640]{2,1,0:T(8,128)(2,1)S(1)}, bf16[2,384,640]{2,1,0:T(8,128)(2,1)S(1)}, u32[]{:S(2)}, u32[]{:S(2)}) collective-permute-start(bf16[2,384,640]{2,1,0:T(8,128)(2,1)S(1)} %get-tuple-element.63), channel_id=1, source_target_pairs={{0,16},{16,0},{1,17},{17,1},{2,18},{18,2},{3,19},{19,3},{4,20},{20... | collective-permute-start | bytes 2949128 | tf_op jit(solution)/shard_map/ppermute | solution.py:573
  59.6 4.6 %shard_map.87 = (bf16[384,896]{1,0:T(8,128)(2,1)S(1)}, f32[2,384,256]{2,1,0:T(8,128)S(1)}, bf16[2,384,256]{2,1,0:T(8,128)(2,1)S(1)}, bf16[2,384,256]{2,1,0:T(8,128)(2,1)S(1)}, f32[8,128]{1,0:T(8,128)S(1)}) custom-call(f32[8,128]{1,0:T(8,128)S(1)} %shard_map.80.info, bf16[384,1536]{1,0:T(8,128)(2,1)S(1)} %bitcast.34, bf16[384,1536]{1,0:T(8,128)(2,1)S(1)} %bitcast.26, ...), custom_call_target="tpu_custom_call" | custom-call | flops 6000000000 | bytes 1 | tf_op jit(solution)/shard_map/pallas_call | solution.py:413
  64.2 7.7 %collective-permute-start.20 = (bf16[2,384,256]{2,1,0:T(8,128)(2,1)S(1)}, bf16[2,384,256]{2,1,0:T(8,128)(2,1)S(1)}, u32[]{:S(2)}, u32[]{:S(2)}) collective-permute-start(bf16[2,384,256]{2,1,0:T(8,128)(2,1)S(1)} %get-tuple-element.80), channel_id=1, source_target_pairs={{0,4},{1,5},{2,6},{3,7},{4,0},{5,1},{6,2},{7,3},{8,12},{9,13},{10,... | collective-permute-start | bytes 1179656 | tf_op jit(solution)/shard_map/ppermute | solution.py:554
  71.9 11.3 %shard_map.88 = (bf16[384,640]{1,0:T(8,128)(2,1)S(1)}, f32[2,384,640]{2,1,0:T(8,128)S(1)}, bf16[2,384,640]{2,1,0:T(8,128)(2,1)S(1)}, bf16[2,384,640]{2,1,0:T(8,128)(2,1)S(1)}, f32[8,128]{1,0:T(8,128)S(1)}) custom-call(bf16[2,400,640]{2,1,0:T(8,128)(2,1)S(1)} %collective-permute-done.5.info.query.grad, ...), custom_call_target="tpu_custom_call" | custom-call | flops 6000000000 | bytes 1 | tf_op jit(solution)/shard_map/pallas_call | solution.py:413
  83.3 2.1 %collective-permute-start.13 = (bf16[2,384,640]{2,1,0:T(8,128)(2,1)S(1)}, bf16[2,384,640]{2,1,0:T(8,128)(2,1)S(1)}, u32[]{:S(2)}, u32[]{:S(2)}) collective-permute-start(bf16[2,384,640]{2,1,0:T(8,128)(2,1)S(1)} %get-tuple-element.69), channel_id=1, source_target_pairs={{0,4},{1,5},{2,6},{3,7},{4,0},{5,1},{6,2},{7,3},{8,12},{9,13},{10,... | collective-permute-start | bytes 2949128 | tf_op jit(solution)/shard_map/ppermute | solution.py:554
  85.4 1.4 %shard_map.89 = bf16[384,896]{1,0:T(8,128)(2,1)S(1)} custom-call(f32[8,128]{1,0:T(8,128)S(1)} %shard_map.80.info, bf16[384,1536]{1,0:T(8,128)(2,1)S(1)} %bitcast.35, f32[384,640]{1,0:T(8,128)S(1)} %get-tuple-element.72.own, bf16[384,640]{1,0:T(8,128)(2,1)S(1)} %collective-permute-done.16.from_even, ...), custom_call_target="tpu_custom_call", output_to_operand_aliasing={{}: (5, {})} | custom-call | flops 20000000000 | bytes 1 | tf_op jit(solution)/shard_map/pallas_call | solution.py:500
  86.8 1.6 %collective-permute-start.18 = (f32[2,128]{1,0:T(2,128)S(1)}, f32[2,128]{1,0:T(2,128)S(1)}, u32[]{:S(2)}, u32[]{:S(2)}) collective-permute-start(f32[2,128]{1,0:T(2,128)S(1)} %slice.12), channel_id=1, source_target_pairs={{0,16},{16,0},{1,17},{17,1},{2,18},{18,2},{3,19},{19,3},{4,20},{20... | collective-permute-start | bytes 3080 | tf_op jit(solution)/shard_map/ppermute | solution.py:573
  88.4 2.1 %collective-permute-done.18 = f32[2,128]{1,0:T(2,128)S(1)} collective-permute-done((f32[2,128]{1,0:T(2,128)S(1)}, f32[2,128]{1,0:T(2,128)S(1)}, u32[]{:S(2)}, u32[]{:S(2)}) %collective-permute-start.18) | collective-permute-done | bytes 1056 | tf_op jit(solution)/shard_map/ppermute | solution.py:573
  90.4 1.5 %collective-permute-start.19 = (bf16[384,896]{1,0:T(8,128)(2,1)S(1)}, bf16[384,896]{1,0:T(8,128)(2,1)S(1)}, u32[]{:S(2)}, u32[]{:S(2)}) collective-permute-start(bf16[384,896]{1,0:T(8,128)(2,1)S(1)} %shard_map.89), channel_id=1, source_target_pairs={{0,16},{16,0},{1,17},{17,1},{2,18},{18,2},{3,19},{19,3},{4,20},{20... | collective-permute-start | bytes 2064392 | tf_op jit(solution)/shard_map/ppermute | solution.py:573
  94.4 1.5 %collective-permute-start.24 = (f32[2,128]{1,0:T(2,128)S(1)}, f32[2,128]{1,0:T(2,128)S(1)}, u32[]{:S(2)}, u32[]{:S(2)}) collective-permute-start(f32[2,128]{1,0:T(2,128)S(1)} %add.24), channel_id=1, source_target_pairs={{0,2},{1,3},{2,0},{3,1},{4,6},{5,7},{6,4},{7,5},{8,10},{9,11},{10,... | collective-permute-start | bytes 3080 | tf_op jit(solution)/shard_map/ppermute | solution.py:580
  95.9 2.0 %collective-permute-done.24 = f32[2,128]{1,0:T(2,128)S(1)} collective-permute-done((f32[2,128]{1,0:T(2,128)S(1)}, f32[2,128]{1,0:T(2,128)S(1)}, u32[]{:S(2)}, u32[]{:S(2)}) %collective-permute-start.24) | collective-permute-done | bytes 1056 | tf_op jit(solution)/shard_map/ppermute | solution.py:580
  98.4 11.6 %collective-permute-done.25 = f32[2,128]{1,0:T(2,128)S(1)} collective-permute-done((f32[2,128]{1,0:T(2,128)S(1)}, f32[2,128]{1,0:T(2,128)S(1)}, u32[]{:S(2)}, u32[]{:S(2)}) %collective-permute-start.25) | collective-permute-done | bytes 1056 | tf_op jit(solution)/shard_map/ppermute | solution.py:580
  110.0 1.6 %collective-permute-start.26 = (f32[2,128]{1,0:T(2,128)S(1)}, f32[2,128]{1,0:T(2,128)S(1)}, u32[]{:S(2)}, u32[]{:S(2)}) collective-permute-start(f32[2,128]{1,0:T(2,128)S(1)} %add.26), channel_id=1, source_target_pairs={{0,8},{4,12},{8,0},{12,4},{1,9},{5,13},{9,1},{13,5},{2,10},{6,14},... | collective-permute-start | bytes 3080 | tf_op jit(solution)/shard_map/ppermute | solution.py:580
  111.6 4.2 %collective-permute-done.22.rest_3_ = bf16[2,384,256]{2,1,0:T(8,128)(2,1)S(1)} collective-permute-done((bf16[2,384,256]{2,1,0:T(8,128)(2,1)S(1)}, bf16[2,384,256]{2,1,0:T(8,128)(2,1)S(1)}, u32[]{:S(2)}, u32[]{:S(2)}) %collective-permute-start.22) | collective-permute-done | bytes 393248 | tf_op jit(solution)/shard_map/ppermute | solution.py:573
  115.8 3.6 %shard_map.91 = bf16[3,384,1536]{2,1,0:T(8,128)(2,1)} custom-call(bf16[2,400,640]{2,1,0:T(8,128)(2,1)S(1)} %collective-permute-done.5.info.query.grad, bf16[2,384,640]{2,1,0:T(8,128)(2,1)S(1)} %collective-permute-done.key.value, f32[2,384,640]{2,1,0:T(8,128)S(1)} %get-tuple-element.68.own, bf16[2,384,640]{2,1,0:T(8,128)(2,1)S(1)} %collective-permute-done.13.from_even, ...), custom_call_target="tpu_custom_call" | custom-call | flops 1 | bytes 1 | tf_op jit(solution)/shard_map/pallas_call | solution.py:518
  (59 shorter events, 9.5 us)
Async XLA Ops:
  3.2 4.8 %copy-start = (bf16[1,1,1,384,1536]{4,3,2,1,0:T(8,128)(2,1)S(1)}, bf16[1,1,1,384,1536]{4,3,2,1,0:T(8,128)(2,1)}, u32[]{:S(2)}) copy-start(bf16[1,1,1,384,1536]{4,3,2,1,0:T(8,128)(2,1)} %param.7) | copy-start | bytes 3538948
  3.2 4.8 %copy-start.5 = (bf16[1,1,1,384,1536]{4,3,2,1,0:T(8,128)(2,1)S(1)}, bf16[1,1,1,384,1536]{4,3,2,1,0:T(8,128)(2,1)}, u32[]{:S(2)}) copy-start(bf16[1,1,1,384,1536]{4,3,2,1,0:T(8,128)(2,1)} %param.8) | copy-start | bytes 3538948
  3.3 9.9 %collective-permute-start.4 = (bf16[2,384,384]{2,1,0:T(8,128)(2,1)S(1)}, bf16[2,384,384]{2,1,0:T(8,128)(2,1)S(1)}, u32[]{:S(2)}, u32[]{:S(2)}) collective-permute-start(bf16[2,384,384]{2,1,0:T(8,128)(2,1)S(1)} %shard_map.77), channel_id=1, source_target_pairs={{0,1},{1,0},{2,3},{3,2},{4,8},{5,9},{6,10},{7,11},{8,4},{9,5},{10,... | collective-permute-start | bytes 1769480 | tf_op jit(solution)/shard_map/ppermute | solution.py:554
  3.8 18.3 %collective-permute-start.3 = (bf16[2,384,384]{2,1,0:T(8,128)(2,1)S(1)}, bf16[2,384,384]{2,1,0:T(8,128)(2,1)S(1)}, u32[]{:S(2)}, u32[]{:S(2)}) collective-permute-start(bf16[2,384,384]{2,1,0:T(8,128)(2,1)S(1)} %shard_map.77), channel_id=1, source_target_pairs={{0,4},{1,5},{2,6},{3,7},{4,0},{5,1},{6,2},{7,3},{8,12},{9,13},{10,... | collective-permute-start | bytes 1769480 | tf_op jit(solution)/shard_map/ppermute | solution.py:554
  9.2 3.3 %copy-start.6 = (f32[1,2,128]{2,1,0:T(2,128)S(1)}, f32[1,2,128]{2,1,0:T(2,128)}, u32[]{:S(2)}) copy-start(f32[1,2,128]{2,1,0:T(2,128)} %param.10) | copy-start | bytes 3076
  9.2 3.3 %copy-start.7 = (s32[1,1,1,3]{3,2,1,0:T(1,128)S(1)}, s32[1,1,1,3]{3,2,1,0:T(1,128)}, u32[]{:S(2)}) copy-start(s32[1,1,1,3]{3,2,1,0:T(1,128)} %param.11) | copy-start | bytes 40
  9.3 18.1 %collective-permute-start.2 = (bf16[2,384,256]{2,1,0:T(8,128)(2,1)S(1)}, bf16[2,384,256]{2,1,0:T(8,128)(2,1)S(1)}, u32[]{:S(2)}, u32[]{:S(2)}) collective-permute-start(bf16[2,384,256]{2,1,0:T(8,128)(2,1)S(1)} %shard_map.79), channel_id=1, source_target_pairs={{0,1},{1,0},{2,3},{3,2},{4,8},{5,9},{6,10},{7,11},{8,4},{9,5},{10,... | collective-permute-start | bytes 1179656 | tf_op jit(solution)/shard_map/ppermute | solution.py:554
  9.4 21.2 %collective-permute-start.1 = (bf16[2,384,256]{2,1,0:T(8,128)(2,1)S(1)}, bf16[2,384,256]{2,1,0:T(8,128)(2,1)S(1)}, u32[]{:S(2)}, u32[]{:S(2)}) collective-permute-start(bf16[2,384,256]{2,1,0:T(8,128)(2,1)S(1)} %shard_map.79), channel_id=1, source_target_pairs={{0,4},{1,5},{2,6},{3,7},{4,0},{5,1},{6,2},{7,3},{8,12},{9,13},{10,... | collective-permute-start | bytes 1179656 | tf_op jit(solution)/shard_map/ppermute | solution.py:554
  11.0 23.3 %collective-permute-start = (bf16[2,384,640]{2,1,0:T(8,128)(2,1)S(1)}, bf16[2,384,640]{2,1,0:T(8,128)(2,1)S(1)}, u32[]{:S(2)}, u32[]{:S(2)}) collective-permute-start(bf16[2,384,640]{2,1,0:T(8,128)(2,1)S(1)} %shard_map.78), channel_id=1, source_target_pairs={{0,16},{16,0},{1,17},{17,1},{2,18},{18,2},{3,19},{19,3},{4,20},{20... | collective-permute-start | bytes 2949128 | tf_op jit(solution)/shard_map/ppermute | solution.py:573
  13.1 11.5 %copy-start.4 = (bf16[1,1,1,384,1536]{4,3,2,1,0:T(8,128)(2,1)S(1)}, bf16[1,1,1,384,1536]{4,3,2,1,0:T(8,128)(2,1)}, u32[]{:S(2)}) copy-start(bf16[1,1,1,384,1536]{4,3,2,1,0:T(8,128)(2,1)} %param.6) | copy-start | bytes 3538948
  22.1 13.8 %collective-permute-start.7 = (bf16[2,384,256]{2,1,0:T(8,128)(2,1)S(1)}, bf16[2,384,256]{2,1,0:T(8,128)(2,1)S(1)}, u32[]{:S(2)}, u32[]{:S(2)}) collective-permute-start(bf16[2,384,256]{2,1,0:T(8,128)(2,1)S(1)} %shard_map.84), channel_id=1, source_target_pairs={{0,1},{1,0},{2,3},{3,2},{4,8},{5,9},{6,10},{7,11},{8,4},{9,5},{10,... | collective-permute-start | bytes 1179656 | tf_op jit(solution)/shard_map/ppermute | solution.py:554
  22.1 15.7 %collective-permute-start.6 = (bf16[2,384,256]{2,1,0:T(8,128)(2,1)S(1)}, bf16[2,384,256]{2,1,0:T(8,128)(2,1)S(1)}, u32[]{:S(2)}, u32[]{:S(2)}) collective-permute-start(bf16[2,384,256]{2,1,0:T(8,128)(2,1)S(1)} %shard_map.84), channel_id=1, source_target_pairs={{0,4},{1,5},{2,6},{3,7},{4,0},{5,1},{6,2},{7,3},{8,12},{9,13},{10,... | collective-permute-start | bytes 1179656 | tf_op jit(solution)/shard_map/ppermute | solution.py:554
  34.4 23.7 %collective-permute-start.5 = (bf16[2,400,640]{2,1,0:T(8,128)(2,1)S(1)}, bf16[2,400,640]{2,1,0:T(8,128)(2,1)S(1)}, u32[]{:S(2)}, u32[]{:S(2)}) collective-permute-start(bf16[2,400,640]{2,1,0:T(8,128)(2,1)S(1)} %shard_map.83), channel_id=1, source_target_pairs={{0,16},{16,0},{1,17},{17,1},{2,18},{18,2},{3,19},{19,3},{4,20},{20... | collective-permute-start | bytes 3072008 | tf_op jit(solution)/shard_map/ppermute | solution.py:573
  37.8 4.2 %collective-permute-start.8 = (f32[40,384]{1,0:T(8,128)S(1)}, f32[40,384]{1,0:T(8,128)S(1)}, u32[]{:S(2)}, u32[]{:S(2)}) collective-permute-start(f32[40,384]{1,0:T(8,128)S(1)} %get-tuple-element.55.sent_even), channel_id=1, source_target_pairs={{0,4},{1,5},{2,6},{3,7},{4,0},{5,1},{6,2},{7,3},{8,12},{9,13},{10,... | collective-permute-start | bytes 184328 | tf_op jit(solution)/shard_map/ppermute | solution.py:554
  39.6 2.5 %collective-permute-start.9 = (f32[40,384]{1,0:T(8,128)S(1)}, f32[40,384]{1,0:T(8,128)S(1)}, u32[]{:S(2)}, u32[]{:S(2)}) collective-permute-start(f32[40,384]{1,0:T(8,128)S(1)} %get-tuple-element.56.sent_odd), channel_id=1, source_target_pairs={{0,1},{1,0},{2,3},{3,2},{4,8},{5,9},{6,10},{7,11},{8,4},{9,5},{10,... | collective-permute-start | bytes 184328 | tf_op jit(solution)/shard_map/ppermute | solution.py:554
  39.6 6.2 %collective-permute-start.10 = (f32[40,384]{1,0:T(8,128)S(1)}, f32[40,384]{1,0:T(8,128)S(1)}, u32[]{:S(2)}, u32[]{:S(2)}) collective-permute-start(f32[40,384]{1,0:T(8,128)S(1)} %get-tuple-element.58), channel_id=1, source_target_pairs={{0,8},{1,9},{2,10},{3,11},{4,12},{5,13},{6,14},{7,15},{8,0},{9,1},... | collective-permute-start | bytes 184328 | tf_op jit(solution)/shard_map/ppermute | solution.py:554
  45.7 18.5 %collective-permute-start.12 = (bf16[2,384,640]{2,1,0:T(8,128)(2,1)S(1)}, bf16[2,384,640]{2,1,0:T(8,128)(2,1)S(1)}, u32[]{:S(2)}, u32[]{:S(2)}) collective-permute-start(bf16[2,384,640]{2,1,0:T(8,128)(2,1)S(1)} %collective-permute-done.key.value), channel_id=1, source_target_pairs={{0,1},{1,0},{2,3},{3,2},{4,8},{5,9},{6,10},{7,11},{8,4},{9,5},{10,... | collective-permute-start | bytes 2949128 | tf_op jit(solution)/shard_map/ppermute | solution.py:554
  45.7 26.2 %collective-permute-start.11 = (bf16[2,384,640]{2,1,0:T(8,128)(2,1)S(1)}, bf16[2,384,640]{2,1,0:T(8,128)(2,1)S(1)}, u32[]{:S(2)}, u32[]{:S(2)}) collective-permute-start(bf16[2,384,640]{2,1,0:T(8,128)(2,1)S(1)} %collective-permute-done.key.value), channel_id=1, source_target_pairs={{0,4},{1,5},{2,6},{3,7},{4,0},{5,1},{6,2},{7,3},{8,12},{9,13},{10,... | collective-permute-start | bytes 2949128 | tf_op jit(solution)/shard_map/ppermute | solution.py:554
  57.9 25.4 %collective-permute-start.16 = (bf16[384,640]{1,0:T(8,128)(2,1)S(1)}, bf16[384,640]{1,0:T(8,128)(2,1)S(1)}, u32[]{:S(2)}, u32[]{:S(2)}) collective-permute-start(bf16[384,640]{1,0:T(8,128)(2,1)S(1)} %get-tuple-element.73), channel_id=1, source_target_pairs={{0,4},{1,5},{2,6},{3,7},{4,0},{5,1},{6,2},{7,3},{8,12},{9,13},{10,... | collective-permute-start | bytes 1474568 | tf_op jit(solution)/shard_map/ppermute | solution.py:554
  58.1 27.3 %collective-permute-start.17 = (bf16[384,640]{1,0:T(8,128)(2,1)S(1)}, bf16[384,640]{1,0:T(8,128)(2,1)S(1)}, u32[]{:S(2)}, u32[]{:S(2)}) collective-permute-start(bf16[384,640]{1,0:T(8,128)(2,1)S(1)} %get-tuple-element.74), channel_id=1, source_target_pairs={{0,1},{1,0},{2,3},{3,2},{4,8},{5,9},{6,10},{7,11},{8,4},{9,5},{10,... | collective-permute-start | bytes 1474568 | tf_op jit(solution)/shard_map/ppermute | solution.py:554
  58.1 28.7 %collective-permute-start.15 = (bf16[2,384,640]{2,1,0:T(8,128)(2,1)S(1)}, bf16[2,384,640]{2,1,0:T(8,128)(2,1)S(1)}, u32[]{:S(2)}, u32[]{:S(2)}) collective-permute-start(bf16[2,384,640]{2,1,0:T(8,128)(2,1)S(1)} %get-tuple-element.63), channel_id=1, source_target_pairs={{0,16},{16,0},{1,17},{17,1},{2,18},{18,2},{3,19},{19,3},{4,20},{20... | collective-permute-start | bytes 2949128 | tf_op jit(solution)/shard_map/ppermute | solution.py:573
  64.2 27.7 %collective-permute-start.20 = (bf16[2,384,256]{2,1,0:T(8,128)(2,1)S(1)}, bf16[2,384,256]{2,1,0:T(8,128)(2,1)S(1)}, u32[]{:S(2)}, u32[]{:S(2)}) collective-permute-start(bf16[2,384,256]{2,1,0:T(8,128)(2,1)S(1)} %get-tuple-element.80), channel_id=1, source_target_pairs={{0,4},{1,5},{2,6},{3,7},{4,0},{5,1},{6,2},{7,3},{8,12},{9,13},{10,... | collective-permute-start | bytes 1179656 | tf_op jit(solution)/shard_map/ppermute | solution.py:554
  71.9 20.0 %collective-permute-start.21 = (bf16[2,384,256]{2,1,0:T(8,128)(2,1)S(1)}, bf16[2,384,256]{2,1,0:T(8,128)(2,1)S(1)}, u32[]{:S(2)}, u32[]{:S(2)}) collective-permute-start(bf16[2,384,256]{2,1,0:T(8,128)(2,1)S(1)} %get-tuple-element.81), channel_id=1, source_target_pairs={{0,1},{1,0},{2,3},{3,2},{4,8},{5,9},{6,10},{7,11},{8,4},{9,5},{10,... | collective-permute-start | bytes 1179656 | tf_op jit(solution)/shard_map/ppermute | solution.py:554
  83.3 32.6 %collective-permute-start.13 = (bf16[2,384,640]{2,1,0:T(8,128)(2,1)S(1)}, bf16[2,384,640]{2,1,0:T(8,128)(2,1)S(1)}, u32[]{:S(2)}, u32[]{:S(2)}) collective-permute-start(bf16[2,384,640]{2,1,0:T(8,128)(2,1)S(1)} %get-tuple-element.69), channel_id=1, source_target_pairs={{0,4},{1,5},{2,6},{3,7},{4,0},{5,1},{6,2},{7,3},{8,12},{9,13},{10,... | collective-permute-start | bytes 2949128 | tf_op jit(solution)/shard_map/ppermute | solution.py:554
  85.4 30.5 %collective-permute-start.14 = (bf16[2,384,640]{2,1,0:T(8,128)(2,1)S(1)}, bf16[2,384,640]{2,1,0:T(8,128)(2,1)S(1)}, u32[]{:S(2)}, u32[]{:S(2)}) collective-permute-start(bf16[2,384,640]{2,1,0:T(8,128)(2,1)S(1)} %get-tuple-element.70), channel_id=1, source_target_pairs={{0,1},{1,0},{2,3},{3,2},{4,8},{5,9},{6,10},{7,11},{8,4},{9,5},{10,... | collective-permute-start | bytes 2949128 | tf_op jit(solution)/shard_map/ppermute | solution.py:554
  86.8 3.6 %collective-permute-start.18 = (f32[2,128]{1,0:T(2,128)S(1)}, f32[2,128]{1,0:T(2,128)S(1)}, u32[]{:S(2)}, u32[]{:S(2)}) collective-permute-start(f32[2,128]{1,0:T(2,128)S(1)} %slice.12), channel_id=1, source_target_pairs={{0,16},{16,0},{1,17},{17,1},{2,18},{18,2},{3,19},{19,3},{4,20},{20... | collective-permute-start | bytes 3080 | tf_op jit(solution)/shard_map/ppermute | solution.py:573
  90.4 21.2 %collective-permute-start.19 = (bf16[384,896]{1,0:T(8,128)(2,1)S(1)}, bf16[384,896]{1,0:T(8,128)(2,1)S(1)}, u32[]{:S(2)}, u32[]{:S(2)}) collective-permute-start(bf16[384,896]{1,0:T(8,128)(2,1)S(1)} %shard_map.89), channel_id=1, source_target_pairs={{0,16},{16,0},{1,17},{17,1},{2,18},{18,2},{3,19},{19,3},{4,20},{20... | collective-permute-start | bytes 2064392 | tf_op jit(solution)/shard_map/ppermute | solution.py:573
  92.7 23.2 %collective-permute-start.22 = (bf16[2,384,256]{2,1,0:T(8,128)(2,1)S(1)}, bf16[2,384,256]{2,1,0:T(8,128)(2,1)S(1)}, u32[]{:S(2)}, u32[]{:S(2)}) collective-permute-start(bf16[2,384,256]{2,1,0:T(8,128)(2,1)S(1)} %shard_map.90), channel_id=1, source_target_pairs={{0,16},{16,0},{1,17},{17,1},{2,18},{18,2},{3,19},{19,3},{4,20},{20... | collective-permute-start | bytes 1179656 | tf_op jit(solution)/shard_map/ppermute | solution.py:573
  93.3 1.1 collective-permute-start.23
  94.4 3.6 %collective-permute-start.24 = (f32[2,128]{1,0:T(2,128)S(1)}, f32[2,128]{1,0:T(2,128)S(1)}, u32[]{:S(2)}, u32[]{:S(2)}) collective-permute-start(f32[2,128]{1,0:T(2,128)S(1)} %add.24), channel_id=1, source_target_pairs={{0,2},{1,3},{2,0},{3,1},{4,6},{5,7},{6,4},{7,5},{8,10},{9,11},{10,... | collective-permute-start | bytes 3080 | tf_op jit(solution)/shard_map/ppermute | solution.py:580
  98.0 12.0 %collective-permute-start.25 = (f32[2,128]{1,0:T(2,128)S(1)}, f32[2,128]{1,0:T(2,128)S(1)}, u32[]{:S(2)}, u32[]{:S(2)}) collective-permute-start(f32[2,128]{1,0:T(2,128)S(1)} %add.25), channel_id=1, source_target_pairs={{0,4},{4,0},{8,12},{12,8},{1,5},{5,1},{9,13},{13,9},{2,6},{6,2},{1... | collective-permute-start | bytes 3080 | tf_op jit(solution)/shard_map/ppermute | solution.py:580
  110.0 9.5 %collective-permute-start.26 = (f32[2,128]{1,0:T(2,128)S(1)}, f32[2,128]{1,0:T(2,128)S(1)}, u32[]{:S(2)}, u32[]{:S(2)}) collective-permute-start(f32[2,128]{1,0:T(2,128)S(1)} %add.26), channel_id=1, source_target_pairs={{0,8},{4,12},{8,0},{12,4},{1,9},{5,13},{9,1},{13,5},{2,10},{6,14},... | collective-permute-start | bytes 3080 | tf_op jit(solution)/shard_map/ppermute | solution.py:580
  (3 other events, 3.8 us)

commit v12 on v11

--- a/solution.py
+++ b/solution.py
@@ -604,7 +604,7 @@
     sums = None
     for (first, count), told in zip(QUERY_GROUPS, told_pairs):
         sums = sums_call(info, arrays, *told, first, count, key_first, sums, len(fars))
-    ready = [after(value, *key_pairs) for value in sums]
+    ready = [*sums[:2], *[after(value, *key_pairs) for value in sums[2:]]]
     received = [exchanged(ready[0], 0), exchanged(ready[1], 1)]
     received += [paired(value, partners) for value, partners in zip(ready[2:], fars)]
     all_sums = (*sums[:2], *received)
@@ -635,8 +635,8 @@
     returned = (exchanged(to_even, 0), exchanged(to_odd, 1))
     pieces.append(query_low)
     places.append((0, away_first * HEAD_DIM))
+    gains.append(turned(after(gain[:2], pieces[0]), 1))
     low = answer_call(info, query, *answer, low)
-    gains.append(turned(after(gain[:2], low, pieces[0]), 1))
     pieces.append(turned(after(low, gains[-1]), -1))
     places.append((0, 0))
     low = finish_call(after(info, pieces[0]), (key, key_first, None), *key_answer, key_count)

time: 120 us -> 117 us (0.975)
  waiting for transfers between devices: 41.1 us -> 37.4 us
    ppermute x6, waiting for transfers between devices: 8.11 us -> 4.71 us  [turned(): lax.ppermute(value, 'pipe', [(i, (i + step) % count) for i in range(count)])]
    ppermute x4, starting transfers between devices: 3.59 us -> 5.68 us  [total_over(): other = lax.ppermute(value, axis, [(i, i ^ step) for i in range(count)])]
    ppermute x17, starting transfers between devices: 24.5 us -> 22.8 us  [paired(): return lax.ppermute(value, ('seq', 'dp'), pairs)]
  transfers between devices with their start and end apart: 27 -> 27, of which waited for: 11 -> 11; matrix products, arithmetic and copies ran while one was open for 0% -> 0% of each run, Pallas kernels for 31% -> 32%
where the time goes in v12:
time: 117 us
  Pallas kernels  37.4 us (32%)
  waiting for transfers between devices  37.4 us (32%)
  starting transfers between devices  36.9 us (32%)
  local copies, waits for them, and re-layouts  3.71 us (3%)
    ppermute x17, starting transfers between devices, paired(): return lax.ppermute(value, ('seq', 'dp'), pairs)  22.8 us
    ppermute x17, waiting for transfers between devices, paired(): return lax.ppermute(value, ('seq', 'dp'), pairs)  17.6 us
    pallas_call x2, Pallas kernels, main_call(): pl.pallas_call(main_kernel, grid=(count,), in_specs=[info_block(info)] +...  15.9 us
    ppermute x4, waiting for transfers between devices, total_over(): other = lax.ppermute(value, axis, [(i, i ^ step) for i in range(count)])  15.1 us
    pallas_call x2, Pallas kernels, grads_call(): pl.pallas_call(functools.partial(grads_kernel, far_count=far_count), grid...  10.3 us
    ppermute x6, starting transfers between devices, turned(): lax.ppermute(value, 'pipe', [(i, (i + step) % count) for i in range(count)])  8.41 us
    ppermute x4, starting transfers between devices, total_over(): other = lax.ppermute(value, axis, [(i, i ^ step) for i in range(count)])  5.68 us
    ppermute x6, waiting for transfers between devices, turned(): lax.ppermute(value, 'pipe', [(i, (i + step) % count) for i in range(count)])  4.71 us
  transfers between devices with their start and end apart: 27, of which 11 were waited for; matrix products, arithmetic and copies ran while one was open for 0% of the time, Pallas kernels for 32%

profile of v12, /device:TPU:0, one launch (start us, length us, event | category | flops | bytes accessed | tf_op | source)
XLA Modules:
  0.0 116.9 jit_solution(2160641272874552484)
XLA Ops:
  0.6 1.3 %copy-done.1 = bf16[1,1,1,384,1536]{4,3,2,1,0:T(8,128)(2,1)S(1)} copy-done((bf16[1,1,1,384,1536]{4,3,2,1,0:T(8,128)(2,1)S(1)}, bf16[1,1,1,384,1536]{4,3,2,1,0:T(8,128)(2,1)}, u32[]{:S(2)}) %copy-start.1) | copy-done | bytes 1179672
  1.9 1.3 %copy-done.3 = bf16[1,1,1,384,1536]{4,3,2,1,0:T(8,128)(2,1)S(1)} copy-done((bf16[1,1,1,384,1536]{4,3,2,1,0:T(8,128)(2,1)S(1)}, bf16[1,1,1,384,1536]{4,3,2,1,0:T(8,128)(2,1)}, u32[]{:S(2)}) %copy-start.3) | copy-done | bytes 1179672
  3.8 4.1 %collective-permute-start.3 = (bf16[2,384,384]{2,1,0:T(8,128)(2,1)S(1)}, bf16[2,384,384]{2,1,0:T(8,128)(2,1)S(1)}, u32[]{:S(2)}, u32[]{:S(2)}) collective-permute-start(bf16[2,384,384]{2,1,0:T(8,128)(2,1)S(1)} %shard_map.77), channel_id=1, source_target_pairs={{0,4},{1,5},{2,6},{3,7},{4,0},{5,1},{6,2},{7,3},{8,12},{9,13},{10,... | collective-permute-start | bytes 1769480 | tf_op jit(solution)/shard_map/ppermute | solution.py:554
  9.4 1.6 %collective-permute-start.1 = (bf16[2,384,256]{2,1,0:T(8,128)(2,1)S(1)}, bf16[2,384,256]{2,1,0:T(8,128)(2,1)S(1)}, u32[]{:S(2)}, u32[]{:S(2)}) collective-permute-start(bf16[2,384,256]{2,1,0:T(8,128)(2,1)S(1)} %shard_map.79), channel_id=1, source_target_pairs={{0,4},{1,5},{2,6},{3,7},{4,0},{5,1},{6,2},{7,3},{8,12},{9,13},{10,... | collective-permute-start | bytes 1179656 | tf_op jit(solution)/shard_map/ppermute | solution.py:554
  11.0 1.5 %collective-permute-start = (bf16[2,384,640]{2,1,0:T(8,128)(2,1)S(1)}, bf16[2,384,640]{2,1,0:T(8,128)(2,1)S(1)}, u32[]{:S(2)}, u32[]{:S(2)}) collective-permute-start(bf16[2,384,640]{2,1,0:T(8,128)(2,1)S(1)} %shard_map.78), channel_id=1, source_target_pairs={{0,16},{16,0},{1,17},{17,1},{2,18},{18,2},{3,19},{19,3},{4,20},{20... | collective-permute-start | bytes 2949128 | tf_op jit(solution)/shard_map/ppermute | solution.py:573
  13.1 9.0 %collective-permute-done.3.pair_even = bf16[2,384,384]{2,1,0:T(8,128)(2,1)S(1)} collective-permute-done((bf16[2,384,384]{2,1,0:T(8,128)(2,1)S(1)}, bf16[2,384,384]{2,1,0:T(8,128)(2,1)S(1)}, u32[]{:S(2)}, u32[]{:S(2)}) %collective-permute-start.3) | collective-permute-done | bytes 589856 | tf_op jit(solution)/shard_map/ppermute | solution.py:554
  22.1 2.5 %collective-permute-start.8 = (bf16[2,384,256]{2,1,0:T(8,128)(2,1)S(1)}, bf16[2,384,256]{2,1,0:T(8,128)(2,1)S(1)}, u32[]{:S(2)}, u32[]{:S(2)}) collective-permute-start(bf16[2,384,256]{2,1,0:T(8,128)(2,1)S(1)} %shard_map.84), channel_id=1, source_target_pairs={{0,4},{1,5},{2,6},{3,7},{4,0},{5,1},{6,2},{7,3},{8,12},{9,13},{10,... | collective-permute-start | bytes 1179656 | tf_op jit(solution)/shard_map/ppermute | solution.py:554
  24.6 2.8 %shard_map.81 = (f32[40,384]{1,0:T(8,128)S(1)}, f32[40,384]{1,0:T(8,128)S(1)}, f32[40,384]{1,0:T(8,128)S(1)}) custom-call(f32[8,128]{1,0:T(8,128)S(1)} %shard_map.80.info, bf16[384,1536]{1,0:T(8,128)(2,1)S(1)} %bitcast.29, bf16[384,1536]{1,0:T(8,128)(2,1)S(1)} %bitcast.21, bf16[384,1536]{1,0:T(8,128)(2,1)S(1)} %bitcast.13, bf16[384,1536]{1,0:T(8,128)(2,1)S(1)} %bitcast.38, ...), custom_call_target="tpu_custom_call" | custom-call | flops 6000000000 | bytes 1 | tf_op jit(solution)/shard_map/pallas_call | solution.py:454
  27.4 3.2 %collective-permute-done.1.pair_even = bf16[2,384,256]{2,1,0:T(8,128)(2,1)S(1)} collective-permute-done((bf16[2,384,256]{2,1,0:T(8,128)(2,1)S(1)}, bf16[2,384,256]{2,1,0:T(8,128)(2,1)S(1)}, u32[]{:S(2)}, u32[]{:S(2)}) %collective-permute-start.1) | collective-permute-done | bytes 393248 | tf_op jit(solution)/shard_map/ppermute | solution.py:554
  30.6 1.9 %shard_map.82 = (f32[40,384]{1,0:T(8,128)S(1)}, f32[40,384]{1,0:T(8,128)S(1)}, f32[40,384]{1,0:T(8,128)S(1)}) custom-call(f32[8,128]{1,0:T(8,128)S(1)} %shard_map.80.info, bf16[384,1536]{1,0:T(8,128)(2,1)S(1)} %bitcast.30, bf16[384,1536]{1,0:T(8,128)(2,1)S(1)} %bitcast.22, ...), custom_call_target="tpu_custom_call", output_to_operand_aliasing={{0}: (7, {}), {1}: (8, {}), {2}: (9, {})} | custom-call | flops 6000000000 | bytes 1 | tf_op jit(solution)/shard_map/pallas_call | solution.py:454
  32.4 1.8 %collective-permute-done.key.value = bf16[2,384,640]{2,1,0:T(8,128)(2,1)S(1)} collective-permute-done((bf16[2,384,640]{2,1,0:T(8,128)(2,1)S(1)}, bf16[2,384,640]{2,1,0:T(8,128)(2,1)S(1)}, u32[]{:S(2)}, u32[]{:S(2)}) %collective-permute-start) | collective-permute-done | bytes 983072 | tf_op jit(solution)/shard_map/ppermute | solution.py:573
  34.4 1.6 %collective-permute-start.5 = (bf16[2,400,640]{2,1,0:T(8,128)(2,1)S(1)}, bf16[2,400,640]{2,1,0:T(8,128)(2,1)S(1)}, u32[]{:S(2)}, u32[]{:S(2)}) collective-permute-start(bf16[2,400,640]{2,1,0:T(8,128)(2,1)S(1)} %shard_map.83), channel_id=1, source_target_pairs={{0,16},{16,0},{1,17},{17,1},{2,18},{18,2},{3,19},{19,3},{4,20},{20... | collective-permute-start | bytes 3072008 | tf_op jit(solution)/shard_map/ppermute | solution.py:573
  37.0 1.5 %collective-permute-done.8.pair_even = bf16[2,384,256]{2,1,0:T(8,128)(2,1)S(1)} collective-permute-done((bf16[2,384,256]{2,1,0:T(8,128)(2,1)S(1)}, bf16[2,384,256]{2,1,0:T(8,128)(2,1)S(1)}, u32[]{:S(2)}, u32[]{:S(2)}) %collective-permute-start.8) | collective-permute-done | bytes 393248 | tf_op jit(solution)/shard_map/ppermute | solution.py:554
  38.5 2.0 %collective-permute-start.10 = (f32[40,384]{1,0:T(8,128)S(1)}, f32[40,384]{1,0:T(8,128)S(1)}, u32[]{:S(2)}, u32[]{:S(2)}) collective-permute-start(f32[40,384]{1,0:T(8,128)S(1)} %get-tuple-element.54), channel_id=1, source_target_pairs={{0,8},{1,9},{2,10},{3,11},{4,12},{5,13},{6,14},{7,15},{8,0},{9,1},... | collective-permute-start | bytes 184328 | tf_op jit(solution)/shard_map/ppermute | solution.py:554
  40.5 3.1 %collective-permute-done.10.rest_0_ = f32[40,384]{1,0:T(8,128)S(1)} collective-permute-done((f32[40,384]{1,0:T(8,128)S(1)}, f32[40,384]{1,0:T(8,128)S(1)}, u32[]{:S(2)}, u32[]{:S(2)}) %collective-permute-start.10) | collective-permute-done | bytes 61472 | tf_op jit(solution)/shard_map/ppermute | solution.py:554
  43.6 2.6 %collective-permute-start.11 = (bf16[2,384,640]{2,1,0:T(8,128)(2,1)S(1)}, bf16[2,384,640]{2,1,0:T(8,128)(2,1)S(1)}, u32[]{:S(2)}, u32[]{:S(2)}) collective-permute-start(bf16[2,384,640]{2,1,0:T(8,128)(2,1)S(1)} %collective-permute-done.key.value), channel_id=1, source_target_pairs={{0,4},{1,5},{2,6},{3,7},{4,0},{5,1},{6,2},{7,3},{8,12},{9,13},{10,... | collective-permute-start | bytes 2949128 | tf_op jit(solution)/shard_map/ppermute | solution.py:554
  46.2 6.1 %shard_map.85 = (bf16[2,384,640]{2,1,0:T(8,128)(2,1)S(1)}, f32[384,640]{1,0:T(8,128)S(1)}, bf16[384,640]{1,0:T(8,128)(2,1)S(1)}, bf16[384,640]{1,0:T(8,128)(2,1)S(1)}, f32[8,128]{1,0:T(8,128)S(1)}) custom-call(f32[8,128]{1,0:T(8,128)S(1)} %shard_map.80.info, bf16[384,1536]{1,0:T(8,128)(2,1)S(1)} %bitcast.32, bf16[384,1536]{1,0:T(8,128)(2,1)S(1)} %bitcast.24, ...), custom_call_target="tpu_custom_call" | custom-call | flops 4000000000 | bytes 1 | tf_op jit(solution)/shard_map/pallas_call | solution.py:474
  52.3 4.1 %shard_map.86 = (bf16[2,384,640]{2,1,0:T(8,128)(2,1)S(1)}, f32[384,640]{1,0:T(8,128)S(1)}, bf16[384,640]{1,0:T(8,128)(2,1)S(1)}, bf16[384,640]{1,0:T(8,128)(2,1)S(1)}, f32[8,128]{1,0:T(8,128)S(1)}) custom-call(f32[8,128]{1,0:T(8,128)S(1)} %shard_map.80.info, ...), custom_call_target="tpu_custom_call", output_to_operand_aliasing={{0}: (12, {}), {1}: (13, {}), {2}: (14, {}), {3}: (15, {})} | custom-call | flops 4000000000 | bytes 1 | tf_op jit(solution)/shard_map/pallas_call | solution.py:474
  57.7 1.5 %collective-permute-start.15 = (bf16[2,384,640]{2,1,0:T(8,128)(2,1)S(1)}, bf16[2,384,640]{2,1,0:T(8,128)(2,1)S(1)}, u32[]{:S(2)}, u32[]{:S(2)}) collective-permute-start(bf16[2,384,640]{2,1,0:T(8,128)(2,1)S(1)} %get-tuple-element.59), channel_id=1, source_target_pairs={{0,16},{16,0},{1,17},{17,1},{2,18},{18,2},{3,19},{19,3},{4,20},{20... | collective-permute-start | bytes 2949128 | tf_op jit(solution)/shard_map/ppermute | solution.py:573
  59.2 4.5 %shard_map.87 = (bf16[384,896]{1,0:T(8,128)(2,1)S(1)}, f32[2,384,256]{2,1,0:T(8,128)S(1)}, bf16[2,384,256]{2,1,0:T(8,128)(2,1)S(1)}, bf16[2,384,256]{2,1,0:T(8,128)(2,1)S(1)}, f32[8,128]{1,0:T(8,128)S(1)}) custom-call(f32[8,128]{1,0:T(8,128)S(1)} %shard_map.80.info, bf16[384,1536]{1,0:T(8,128)(2,1)S(1)} %bitcast.34, bf16[384,1536]{1,0:T(8,128)(2,1)S(1)} %bitcast.26, ...), custom_call_target="tpu_custom_call" | custom-call | flops 6000000000 | bytes 1 | tf_op jit(solution)/shard_map/pallas_call | solution.py:413
  63.7 6.3 %collective-permute-start.20 = (bf16[2,384,256]{2,1,0:T(8,128)(2,1)S(1)}, bf16[2,384,256]{2,1,0:T(8,128)(2,1)S(1)}, u32[]{:S(2)}, u32[]{:S(2)}) collective-permute-start(bf16[2,384,256]{2,1,0:T(8,128)(2,1)S(1)} %get-tuple-element.76), channel_id=1, source_target_pairs={{0,4},{1,5},{2,6},{3,7},{4,0},{5,1},{6,2},{7,3},{8,12},{9,13},{10,... | collective-permute-start | bytes 1179656 | tf_op jit(solution)/shard_map/ppermute | solution.py:554
  70.1 11.3 %shard_map.88 = (bf16[384,640]{1,0:T(8,128)(2,1)S(1)}, f32[2,384,640]{2,1,0:T(8,128)S(1)}, bf16[2,384,640]{2,1,0:T(8,128)(2,1)S(1)}, bf16[2,384,640]{2,1,0:T(8,128)(2,1)S(1)}, f32[8,128]{1,0:T(8,128)S(1)}) custom-call(bf16[2,400,640]{2,1,0:T(8,128)(2,1)S(1)} %collective-permute-done.5.info.query.grad, ...), custom_call_target="tpu_custom_call" | custom-call | flops 6000000000 | bytes 1 | tf_op jit(solution)/shard_map/pallas_call | solution.py:413
  81.4 1.6 %collective-permute-start.18 = (f32[2,128]{1,0:T(2,128)S(1)}, f32[2,128]{1,0:T(2,128)S(1)}, u32[]{:S(2)}, u32[]{:S(2)}) collective-permute-start(f32[2,128]{1,0:T(2,128)S(1)} %slice.12), channel_id=1, source_target_pairs={{0,16},{16,0},{1,17},{17,1},{2,18},{18,2},{3,19},{19,3},{4,20},{20... | collective-permute-start | bytes 3080 | tf_op jit(solution)/shard_map/ppermute | solution.py:573
  83.0 1.9 %collective-permute-start.13 = (bf16[2,384,640]{2,1,0:T(8,128)(2,1)S(1)}, bf16[2,384,640]{2,1,0:T(8,128)(2,1)S(1)}, u32[]{:S(2)}, u32[]{:S(2)}) collective-permute-start(bf16[2,384,640]{2,1,0:T(8,128)(2,1)S(1)} %get-tuple-element.65), channel_id=1, source_target_pairs={{0,4},{1,5},{2,6},{3,7},{4,0},{5,1},{6,2},{7,3},{8,12},{9,13},{10,... | collective-permute-start | bytes 2949128 | tf_op jit(solution)/shard_map/ppermute | solution.py:554
  84.9 1.4 %shard_map.89 = bf16[384,896]{1,0:T(8,128)(2,1)S(1)} custom-call(f32[8,128]{1,0:T(8,128)S(1)} %shard_map.80.info, bf16[384,1536]{1,0:T(8,128)(2,1)S(1)} %bitcast.35, f32[384,640]{1,0:T(8,128)S(1)} %get-tuple-element.68.own, bf16[384,640]{1,0:T(8,128)(2,1)S(1)} %collective-permute-done.16.from_even, ...), custom_call_target="tpu_custom_call", output_to_operand_aliasing={{}: (5, {})} | custom-call | flops 20000000000 | bytes 1 | tf_op jit(solution)/shard_map/pallas_call | solution.py:500
  88.3 1.7 %collective-permute-start.22 = (bf16[2,384,256]{2,1,0:T(8,128)(2,1)S(1)}, bf16[2,384,256]{2,1,0:T(8,128)(2,1)S(1)}, u32[]{:S(2)}, u32[]{:S(2)}) collective-permute-start(bf16[2,384,256]{2,1,0:T(8,128)(2,1)S(1)} %shard_map.90), channel_id=1, source_target_pairs={{0,16},{16,0},{1,17},{17,1},{2,18},{18,2},{3,19},{19,3},{4,20},{20... | collective-permute-start | bytes 1179656 | tf_op jit(solution)/shard_map/ppermute | solution.py:573
  91.2 1.5 %collective-permute-start.24 = (f32[2,128]{1,0:T(2,128)S(1)}, f32[2,128]{1,0:T(2,128)S(1)}, u32[]{:S(2)}, u32[]{:S(2)}) collective-permute-start(f32[2,128]{1,0:T(2,128)S(1)} %add.24), channel_id=1, source_target_pairs={{0,2},{1,3},{2,0},{3,1},{4,6},{5,7},{6,4},{7,5},{8,10},{9,11},{10,... | collective-permute-start | bytes 3080 | tf_op jit(solution)/shard_map/ppermute | solution.py:580
  92.7 2.0 %collective-permute-done.24 = f32[2,128]{1,0:T(2,128)S(1)} collective-permute-done((f32[2,128]{1,0:T(2,128)S(1)}, f32[2,128]{1,0:T(2,128)S(1)}, u32[]{:S(2)}, u32[]{:S(2)}) %collective-permute-start.24) | collective-permute-done | bytes 1056 | tf_op jit(solution)/shard_map/ppermute | solution.py:580
  96.0 11.9 %collective-permute-done.25 = f32[2,128]{1,0:T(2,128)S(1)} collective-permute-done((f32[2,128]{1,0:T(2,128)S(1)}, f32[2,128]{1,0:T(2,128)S(1)}, u32[]{:S(2)}, u32[]{:S(2)}) %collective-permute-start.25) | collective-permute-done | bytes 1056 | tf_op jit(solution)/shard_map/ppermute | solution.py:580
  107.9 3.0 %collective-permute-start.26 = (f32[2,128]{1,0:T(2,128)S(1)}, f32[2,128]{1,0:T(2,128)S(1)}, u32[]{:S(2)}, u32[]{:S(2)}) collective-permute-start(f32[2,128]{1,0:T(2,128)S(1)} %add.26), channel_id=1, source_target_pairs={{0,8},{4,12},{8,0},{12,4},{1,9},{5,13},{9,1},{13,5},{2,10},{6,14},... | collective-permute-start | bytes 3080 | tf_op jit(solution)/shard_map/ppermute | solution.py:580
  110.8 1.8 %collective-permute-done.22.rest_3_ = bf16[2,384,256]{2,1,0:T(8,128)(2,1)S(1)} collective-permute-done((bf16[2,384,256]{2,1,0:T(8,128)(2,1)S(1)}, bf16[2,384,256]{2,1,0:T(8,128)(2,1)S(1)}, u32[]{:S(2)}, u32[]{:S(2)}) %collective-permute-start.22) | collective-permute-done | bytes 393248 | tf_op jit(solution)/shard_map/ppermute | solution.py:573
  112.7 3.6 %shard_map.91 = bf16[3,384,1536]{2,1,0:T(8,128)(2,1)} custom-call(bf16[2,400,640]{2,1,0:T(8,128)(2,1)S(1)} %collective-permute-done.5.info.query.grad, bf16[2,384,640]{2,1,0:T(8,128)(2,1)S(1)} %collective-permute-done.key.value, f32[2,384,640]{2,1,0:T(8,128)S(1)} %get-tuple-element.64.own, bf16[2,384,640]{2,1,0:T(8,128)(2,1)S(1)} %collective-permute-done.13.from_even, ...), custom_call_target="tpu_custom_call" | custom-call | flops 1 | bytes 1 | tf_op jit(solution)/shard_map/pallas_call | solution.py:518
  (59 shorter events, 9.9 us)
Async XLA Ops:
  3.2 4.8 %copy-start = (bf16[1,1,1,384,1536]{4,3,2,1,0:T(8,128)(2,1)S(1)}, bf16[1,1,1,384,1536]{4,3,2,1,0:T(8,128)(2,1)}, u32[]{:S(2)}) copy-start(bf16[1,1,1,384,1536]{4,3,2,1,0:T(8,128)(2,1)} %param.7) | copy-start | bytes 3538948
  3.2 4.8 %copy-start.5 = (bf16[1,1,1,384,1536]{4,3,2,1,0:T(8,128)(2,1)S(1)}, bf16[1,1,1,384,1536]{4,3,2,1,0:T(8,128)(2,1)}, u32[]{:S(2)}) copy-start(bf16[1,1,1,384,1536]{4,3,2,1,0:T(8,128)(2,1)} %param.8) | copy-start | bytes 3538948
  3.3 9.9 %collective-permute-start.4 = (bf16[2,384,384]{2,1,0:T(8,128)(2,1)S(1)}, bf16[2,384,384]{2,1,0:T(8,128)(2,1)S(1)}, u32[]{:S(2)}, u32[]{:S(2)}) collective-permute-start(bf16[2,384,384]{2,1,0:T(8,128)(2,1)S(1)} %shard_map.77), channel_id=1, source_target_pairs={{0,1},{1,0},{2,3},{3,2},{4,8},{5,9},{6,10},{7,11},{8,4},{9,5},{10,... | collective-permute-start | bytes 1769480 | tf_op jit(solution)/shard_map/ppermute | solution.py:554
  3.8 18.3 %collective-permute-start.3 = (bf16[2,384,384]{2,1,0:T(8,128)(2,1)S(1)}, bf16[2,384,384]{2,1,0:T(8,128)(2,1)S(1)}, u32[]{:S(2)}, u32[]{:S(2)}) collective-permute-start(bf16[2,384,384]{2,1,0:T(8,128)(2,1)S(1)} %shard_map.77), channel_id=1, source_target_pairs={{0,4},{1,5},{2,6},{3,7},{4,0},{5,1},{6,2},{7,3},{8,12},{9,13},{10,... | collective-permute-start | bytes 1769480 | tf_op jit(solution)/shard_map/ppermute | solution.py:554
  9.2 3.3 %copy-start.6 = (f32[1,2,128]{2,1,0:T(2,128)S(1)}, f32[1,2,128]{2,1,0:T(2,128)}, u32[]{:S(2)}) copy-start(f32[1,2,128]{2,1,0:T(2,128)} %param.10) | copy-start | bytes 3076
  9.2 3.3 %copy-start.7 = (s32[1,1,1,3]{3,2,1,0:T(1,128)S(1)}, s32[1,1,1,3]{3,2,1,0:T(1,128)}, u32[]{:S(2)}) copy-start(s32[1,1,1,3]{3,2,1,0:T(1,128)} %param.11) | copy-start | bytes 40
  9.3 18.1 %collective-permute-start.2 = (bf16[2,384,256]{2,1,0:T(8,128)(2,1)S(1)}, bf16[2,384,256]{2,1,0:T(8,128)(2,1)S(1)}, u32[]{:S(2)}, u32[]{:S(2)}) collective-permute-start(bf16[2,384,256]{2,1,0:T(8,128)(2,1)S(1)} %shard_map.79), channel_id=1, source_target_pairs={{0,1},{1,0},{2,3},{3,2},{4,8},{5,9},{6,10},{7,11},{8,4},{9,5},{10,... | collective-permute-start | bytes 1179656 | tf_op jit(solution)/shard_map/ppermute | solution.py:554
  9.4 21.2 %collective-permute-start.1 = (bf16[2,384,256]{2,1,0:T(8,128)(2,1)S(1)}, bf16[2,384,256]{2,1,0:T(8,128)(2,1)S(1)}, u32[]{:S(2)}, u32[]{:S(2)}) collective-permute-start(bf16[2,384,256]{2,1,0:T(8,128)(2,1)S(1)} %shard_map.79), channel_id=1, source_target_pairs={{0,4},{1,5},{2,6},{3,7},{4,0},{5,1},{6,2},{7,3},{8,12},{9,13},{10,... | collective-permute-start | bytes 1179656 | tf_op jit(solution)/shard_map/ppermute | solution.py:554
  11.0 23.3 %collective-permute-start = (bf16[2,384,640]{2,1,0:T(8,128)(2,1)S(1)}, bf16[2,384,640]{2,1,0:T(8,128)(2,1)S(1)}, u32[]{:S(2)}, u32[]{:S(2)}) collective-permute-start(bf16[2,384,640]{2,1,0:T(8,128)(2,1)S(1)} %shard_map.78), channel_id=1, source_target_pairs={{0,16},{16,0},{1,17},{17,1},{2,18},{18,2},{3,19},{19,3},{4,20},{20... | collective-permute-start | bytes 2949128 | tf_op jit(solution)/shard_map/ppermute | solution.py:573
  13.1 11.5 %copy-start.4 = (bf16[1,1,1,384,1536]{4,3,2,1,0:T(8,128)(2,1)S(1)}, bf16[1,1,1,384,1536]{4,3,2,1,0:T(8,128)(2,1)}, u32[]{:S(2)}) copy-start(bf16[1,1,1,384,1536]{4,3,2,1,0:T(8,128)(2,1)} %param.6) | copy-start | bytes 3538948
  22.1 14.8 %collective-permute-start.9 = (bf16[2,384,256]{2,1,0:T(8,128)(2,1)S(1)}, bf16[2,384,256]{2,1,0:T(8,128)(2,1)S(1)}, u32[]{:S(2)}, u32[]{:S(2)}) collective-permute-start(bf16[2,384,256]{2,1,0:T(8,128)(2,1)S(1)} %shard_map.84), channel_id=1, source_target_pairs={{0,1},{1,0},{2,3},{3,2},{4,8},{5,9},{6,10},{7,11},{8,4},{9,5},{10,... | collective-permute-start | bytes 1179656 | tf_op jit(solution)/shard_map/ppermute | solution.py:554
  22.1 16.4 %collective-permute-start.8 = (bf16[2,384,256]{2,1,0:T(8,128)(2,1)S(1)}, bf16[2,384,256]{2,1,0:T(8,128)(2,1)S(1)}, u32[]{:S(2)}, u32[]{:S(2)}) collective-permute-start(bf16[2,384,256]{2,1,0:T(8,128)(2,1)S(1)} %shard_map.84), channel_id=1, source_target_pairs={{0,4},{1,5},{2,6},{3,7},{4,0},{5,1},{6,2},{7,3},{8,12},{9,13},{10,... | collective-permute-start | bytes 1179656 | tf_op jit(solution)/shard_map/ppermute | solution.py:554
  34.4 23.3 %collective-permute-start.5 = (bf16[2,400,640]{2,1,0:T(8,128)(2,1)S(1)}, bf16[2,400,640]{2,1,0:T(8,128)(2,1)S(1)}, u32[]{:S(2)}, u32[]{:S(2)}) collective-permute-start(bf16[2,400,640]{2,1,0:T(8,128)(2,1)S(1)} %shard_map.83), channel_id=1, source_target_pairs={{0,16},{16,0},{1,17},{17,1},{2,18},{18,2},{3,19},{19,3},{4,20},{20... | collective-permute-start | bytes 3072008 | tf_op jit(solution)/shard_map/ppermute | solution.py:573
  35.9 4.5 %collective-permute-start.6 = (f32[40,384]{1,0:T(8,128)S(1)}, f32[40,384]{1,0:T(8,128)S(1)}, u32[]{:S(2)}, u32[]{:S(2)}) collective-permute-start(f32[40,384]{1,0:T(8,128)S(1)} %get-tuple-element.48.sent_even), channel_id=1, source_target_pairs={{0,4},{1,5},{2,6},{3,7},{4,0},{5,1},{6,2},{7,3},{8,12},{9,13},{10,... | collective-permute-start | bytes 184328 | tf_op jit(solution)/shard_map/ppermute | solution.py:554
  37.0 3.5 %collective-permute-start.7 = (f32[40,384]{1,0:T(8,128)S(1)}, f32[40,384]{1,0:T(8,128)S(1)}, u32[]{:S(2)}, u32[]{:S(2)}) collective-permute-start(f32[40,384]{1,0:T(8,128)S(1)} %get-tuple-element.50.sent_odd), channel_id=1, source_target_pairs={{0,1},{1,0},{2,3},{3,2},{4,8},{5,9},{6,10},{7,11},{8,4},{9,5},{10,... | collective-permute-start | bytes 184328 | tf_op jit(solution)/shard_map/ppermute | solution.py:554
  38.5 5.1 %collective-permute-start.10 = (f32[40,384]{1,0:T(8,128)S(1)}, f32[40,384]{1,0:T(8,128)S(1)}, u32[]{:S(2)}, u32[]{:S(2)}) collective-permute-start(f32[40,384]{1,0:T(8,128)S(1)} %get-tuple-element.54), channel_id=1, source_target_pairs={{0,8},{1,9},{2,10},{3,11},{4,12},{5,13},{6,14},{7,15},{8,0},{9,1},... | collective-permute-start | bytes 184328 | tf_op jit(solution)/shard_map/ppermute | solution.py:554
  43.6 20.1 %collective-permute-start.12 = (bf16[2,384,640]{2,1,0:T(8,128)(2,1)S(1)}, bf16[2,384,640]{2,1,0:T(8,128)(2,1)S(1)}, u32[]{:S(2)}, u32[]{:S(2)}) collective-permute-start(bf16[2,384,640]{2,1,0:T(8,128)(2,1)S(1)} %collective-permute-done.key.value), channel_id=1, source_target_pairs={{0,1},{1,0},{2,3},{3,2},{4,8},{5,9},{6,10},{7,11},{8,4},{9,5},{10,... | collective-permute-start | bytes 2949128 | tf_op jit(solution)/shard_map/ppermute | solution.py:554
  43.6 26.4 %collective-permute-start.11 = (bf16[2,384,640]{2,1,0:T(8,128)(2,1)S(1)}, bf16[2,384,640]{2,1,0:T(8,128)(2,1)S(1)}, u32[]{:S(2)}, u32[]{:S(2)}) collective-permute-start(bf16[2,384,640]{2,1,0:T(8,128)(2,1)S(1)} %collective-permute-done.key.value), channel_id=1, source_target_pairs={{0,4},{1,5},{2,6},{3,7},{4,0},{5,1},{6,2},{7,3},{8,12},{9,13},{10,... | collective-permute-start | bytes 2949128 | tf_op jit(solution)/shard_map/ppermute | solution.py:554
  56.5 26.5 %collective-permute-start.16 = (bf16[384,640]{1,0:T(8,128)(2,1)S(1)}, bf16[384,640]{1,0:T(8,128)(2,1)S(1)}, u32[]{:S(2)}, u32[]{:S(2)}) collective-permute-start(bf16[384,640]{1,0:T(8,128)(2,1)S(1)} %get-tuple-element.69), channel_id=1, source_target_pairs={{0,4},{1,5},{2,6},{3,7},{4,0},{5,1},{6,2},{7,3},{8,12},{9,13},{10,... | collective-permute-start | bytes 1474568 | tf_op jit(solution)/shard_map/ppermute | solution.py:554
  56.6 28.4 %collective-permute-start.17 = (bf16[384,640]{1,0:T(8,128)(2,1)S(1)}, bf16[384,640]{1,0:T(8,128)(2,1)S(1)}, u32[]{:S(2)}, u32[]{:S(2)}) collective-permute-start(bf16[384,640]{1,0:T(8,128)(2,1)S(1)} %get-tuple-element.70), channel_id=1, source_target_pairs={{0,1},{1,0},{2,3},{3,2},{4,8},{5,9},{6,10},{7,11},{8,4},{9,5},{10,... | collective-permute-start | bytes 1474568 | tf_op jit(solution)/shard_map/ppermute | solution.py:554
  57.7 23.7 %collective-permute-start.15 = (bf16[2,384,640]{2,1,0:T(8,128)(2,1)S(1)}, bf16[2,384,640]{2,1,0:T(8,128)(2,1)S(1)}, u32[]{:S(2)}, u32[]{:S(2)}) collective-permute-start(bf16[2,384,640]{2,1,0:T(8,128)(2,1)S(1)} %get-tuple-element.59), channel_id=1, source_target_pairs={{0,16},{16,0},{1,17},{17,1},{2,18},{18,2},{3,19},{19,3},{4,20},{20... | collective-permute-start | bytes 2949128 | tf_op jit(solution)/shard_map/ppermute | solution.py:573
  63.7 23.9 %collective-permute-start.20 = (bf16[2,384,256]{2,1,0:T(8,128)(2,1)S(1)}, bf16[2,384,256]{2,1,0:T(8,128)(2,1)S(1)}, u32[]{:S(2)}, u32[]{:S(2)}) collective-permute-start(bf16[2,384,256]{2,1,0:T(8,128)(2,1)S(1)} %get-tuple-element.76), channel_id=1, source_target_pairs={{0,4},{1,5},{2,6},{3,7},{4,0},{5,1},{6,2},{7,3},{8,12},{9,13},{10,... | collective-permute-start | bytes 1179656 | tf_op jit(solution)/shard_map/ppermute | solution.py:554
  70.1 17.6 %collective-permute-start.21 = (bf16[2,384,256]{2,1,0:T(8,128)(2,1)S(1)}, bf16[2,384,256]{2,1,0:T(8,128)(2,1)S(1)}, u32[]{:S(2)}, u32[]{:S(2)}) collective-permute-start(bf16[2,384,256]{2,1,0:T(8,128)(2,1)S(1)} %get-tuple-element.77), channel_id=1, source_target_pairs={{0,1},{1,0},{2,3},{3,2},{4,8},{5,9},{6,10},{7,11},{8,4},{9,5},{10,... | collective-permute-start | bytes 1179656 | tf_op jit(solution)/shard_map/ppermute | solution.py:554
  81.4 4.9 %collective-permute-start.18 = (f32[2,128]{1,0:T(2,128)S(1)}, f32[2,128]{1,0:T(2,128)S(1)}, u32[]{:S(2)}, u32[]{:S(2)}) collective-permute-start(f32[2,128]{1,0:T(2,128)S(1)} %slice.12), channel_id=1, source_target_pairs={{0,16},{16,0},{1,17},{17,1},{2,18},{18,2},{3,19},{19,3},{4,20},{20... | collective-permute-start | bytes 3080 | tf_op jit(solution)/shard_map/ppermute | solution.py:573
  83.0 29.7 %collective-permute-start.13 = (bf16[2,384,640]{2,1,0:T(8,128)(2,1)S(1)}, bf16[2,384,640]{2,1,0:T(8,128)(2,1)S(1)}, u32[]{:S(2)}, u32[]{:S(2)}) collective-permute-start(bf16[2,384,640]{2,1,0:T(8,128)(2,1)S(1)} %get-tuple-element.65), channel_id=1, source_target_pairs={{0,4},{1,5},{2,6},{3,7},{4,0},{5,1},{6,2},{7,3},{8,12},{9,13},{10,... | collective-permute-start | bytes 2949128 | tf_op jit(solution)/shard_map/ppermute | solution.py:554
  84.9 27.8 %collective-permute-start.14 = (bf16[2,384,640]{2,1,0:T(8,128)(2,1)S(1)}, bf16[2,384,640]{2,1,0:T(8,128)(2,1)S(1)}, u32[]{:S(2)}, u32[]{:S(2)}) collective-permute-start(bf16[2,384,640]{2,1,0:T(8,128)(2,1)S(1)} %get-tuple-element.66), channel_id=1, source_target_pairs={{0,1},{1,0},{2,3},{3,2},{4,8},{5,9},{6,10},{7,11},{8,4},{9,5},{10,... | collective-permute-start | bytes 2949128 | tf_op jit(solution)/shard_map/ppermute | solution.py:554
  86.3 24.5 %collective-permute-start.19 = (bf16[384,896]{1,0:T(8,128)(2,1)S(1)}, bf16[384,896]{1,0:T(8,128)(2,1)S(1)}, u32[]{:S(2)}, u32[]{:S(2)}) collective-permute-start(bf16[384,896]{1,0:T(8,128)(2,1)S(1)} %shard_map.89), channel_id=1, source_target_pairs={{0,16},{16,0},{1,17},{17,1},{2,18},{18,2},{3,19},{19,3},{4,20},{20... | collective-permute-start | bytes 2064392 | tf_op jit(solution)/shard_map/ppermute | solution.py:573
  88.3 24.3 %collective-permute-start.22 = (bf16[2,384,256]{2,1,0:T(8,128)(2,1)S(1)}, bf16[2,384,256]{2,1,0:T(8,128)(2,1)S(1)}, u32[]{:S(2)}, u32[]{:S(2)}) collective-permute-start(bf16[2,384,256]{2,1,0:T(8,128)(2,1)S(1)} %shard_map.90), channel_id=1, source_target_pairs={{0,16},{16,0},{1,17},{17,1},{2,18},{18,2},{3,19},{19,3},{4,20},{20... | collective-permute-start | bytes 1179656 | tf_op jit(solution)/shard_map/ppermute | solution.py:573
  90.1 1.1 collective-permute-start.23
  91.2 3.6 %collective-permute-start.24 = (f32[2,128]{1,0:T(2,128)S(1)}, f32[2,128]{1,0:T(2,128)S(1)}, u32[]{:S(2)}, u32[]{:S(2)}) collective-permute-start(f32[2,128]{1,0:T(2,128)S(1)} %add.24), channel_id=1, source_target_pairs={{0,2},{1,3},{2,0},{3,1},{4,6},{5,7},{6,4},{7,5},{8,10},{9,11},{10,... | collective-permute-start | bytes 3080 | tf_op jit(solution)/shard_map/ppermute | solution.py:580
  94.8 13.1 %collective-permute-start.25 = (f32[2,128]{1,0:T(2,128)S(1)}, f32[2,128]{1,0:T(2,128)S(1)}, u32[]{:S(2)}, u32[]{:S(2)}) collective-permute-start(f32[2,128]{1,0:T(2,128)S(1)} %add.25), channel_id=1, source_target_pairs={{0,4},{4,0},{8,12},{12,8},{1,5},{5,1},{9,13},{13,9},{2,6},{6,2},{1... | collective-permute-start | bytes 3080 | tf_op jit(solution)/shard_map/ppermute | solution.py:580
  107.9 8.4 %collective-permute-start.26 = (f32[2,128]{1,0:T(2,128)S(1)}, f32[2,128]{1,0:T(2,128)S(1)}, u32[]{:S(2)}, u32[]{:S(2)}) collective-permute-start(f32[2,128]{1,0:T(2,128)S(1)} %add.26), channel_id=1, source_target_pairs={{0,8},{4,12},{8,0},{12,4},{1,9},{5,13},{9,1},{13,5},{2,10},{6,14},... | collective-permute-start | bytes 3080 | tf_op jit(solution)/shard_map/ppermute | solution.py:580
  (3 other events, 3.8 us)

commit v13 on v12

--- a/solution.py
+++ b/solution.py
@@ -13,8 +13,8 @@
 EPSILON = 1e-06
 ROOT_SCALE = HEAD_DIM ** (-0.5)
 EXP2_SCALE = ROOT_SCALE * math.log2(math.e)
-QUERY_GROUPS = ((0, 3), (3, 2))
-KEY_GROUP = (5, 2)
+QUERY_GROUPS = ((0, 4), (4, 2))
+KEY_GROUP = (6, 1)
 AWAY_GROUP = (7, 5)
 MAIN_VMEM = 20 * 1024 * 1024
 SMALL_VMEM = 12 * 1024 * 1024
@@ -636,12 +636,12 @@
     pieces.append(query_low)
     places.append((0, away_first * HEAD_DIM))
     gains.append(turned(after(gain[:2], pieces[0]), 1))
+    key_low = finish_call(after(info, pieces[0]), (key, key_first, None), *key_answer, key_count)
+    pieces.append(turned(key_low, -1))
+    places.append((slice(1, 3), key_first * HEAD_DIM))
     low = answer_call(info, query, *answer, low)
-    pieces.append(turned(after(low, gains[-1]), -1))
+    pieces.append(turned(after(low, gains[-1], key_low), -1))
     places.append((0, 0))
-    low = finish_call(after(info, pieces[0]), (key, key_first, None), *key_answer, key_count)
-    pieces.append(turned(low, -1))
-    places.append((slice(1, 3), key_first * HEAD_DIM))
     out = last_call(
         asked, operands[2], own, *returned, pieces, tuple(places), away_first, away_count
     )

time: 117 us -> 119 us (1.017)
  waiting for transfers between devices: 37.4 us -> 40.1 us
    ppermute x17, waiting for transfers between devices: 17.6 us -> 20.9 us  [paired(): return lax.ppermute(value, ('seq', 'dp'), pairs)]
    ppermute x4, waiting for transfers between devices: 15.1 us -> 12.5 us  [total_over(): other = lax.ppermute(value, axis, [(i, i ^ step) for i in range(count)])]
    pallas_call x2, Pallas kernels: 15.9 us -> 13.3 us  [main_call(): pl.pallas_call(main_kernel, grid=(count,), in_specs=[info_block(info)] +...]
    ppermute x6, starting transfers between devices: 8.41 us -> 6.26 us  [turned(): lax.ppermute(value, 'pipe', [(i, (i + step) % count) for i in range(count)])]
    pallas_call x2, Pallas kernels: 10.3 us -> 12.3 us  [grads_call(): pl.pallas_call(functools.partial(grads_kernel, far_count=far_count), grid...]
    ppermute x6, waiting for transfers between devices: 4.71 us -> 6.64 us  [turned(): lax.ppermute(value, 'pipe', [(i, (i + step) % count) for i in range(count)])]
  transfers between devices with their start and end apart: 27 -> 27, of which waited for: 11 -> 10; matrix products, arithmetic and copies ran while one was open for 0% -> 0% of each run, Pallas kernels for 32% -> 32%
where the time goes in v13:
time: 119 us
  waiting for transfers between devices  40.1 us (34%)
  Pallas kernels  37.7 us (32%)
  starting transfers between devices  35.9 us (30%)
  local copies, waits for them, and re-layouts  3.71 us (3%)
    ppermute x17, starting transfers between devices, paired(): return lax.ppermute(value, ('seq', 'dp'), pairs)  23.9 us
    ppermute x17, waiting for transfers between devices, paired(): return lax.ppermute(value, ('seq', 'dp'), pairs)  20.9 us
    pallas_call x2, Pallas kernels, main_call(): pl.pallas_call(main_kernel, grid=(count,), in_specs=[info_block(info)] +...  13.3 us
    ppermute x4, waiting for transfers between devices, total_over(): other = lax.ppermute(value, axis, [(i, i ^ step) for i in range(count)])  12.5 us
    pallas_call x2, Pallas kernels, grads_call(): pl.pallas_call(functools.partial(grads_kernel, far_count=far_count), grid...  12.3 us
    ppermute x6, waiting for transfers between devices, turned(): lax.ppermute(value, 'pipe', [(i, (i + step) % count) for i in range(count)])  6.64 us
    ppermute x6, starting transfers between devices, turned(): lax.ppermute(value, 'pipe', [(i, (i + step) % count) for i in range(count)])  6.26 us
    ppermute x4, starting transfers between devices, total_over(): other = lax.ppermute(value, axis, [(i, i ^ step) for i in range(count)])  5.76 us
  transfers between devices with their start and end apart: 27, of which 10 were waited for; matrix products, arithmetic and copies ran while one was open for 0% of the time, Pallas kernels for 32%

profile of v13, /device:TPU:0, one launch (start us, length us, event | category | flops | bytes accessed | tf_op | source)
XLA Modules:
  0.0 118.8 jit_solution(14471210439122409572)
XLA Ops:
  0.6 1.3 %copy-done.1 = bf16[1,1,1,384,1536]{4,3,2,1,0:T(8,128)(2,1)S(1)} copy-done((bf16[1,1,1,384,1536]{4,3,2,1,0:T(8,128)(2,1)S(1)}, bf16[1,1,1,384,1536]{4,3,2,1,0:T(8,128)(2,1)}, u32[]{:S(2)}) %copy-start.1) | copy-done | bytes 1179672
  1.9 1.3 %copy-done.3 = bf16[1,1,1,384,1536]{4,3,2,1,0:T(8,128)(2,1)S(1)} copy-done((bf16[1,1,1,384,1536]{4,3,2,1,0:T(8,128)(2,1)S(1)}, bf16[1,1,1,384,1536]{4,3,2,1,0:T(8,128)(2,1)}, u32[]{:S(2)}) %copy-start.3) | copy-done | bytes 1179672
  3.8 4.1 %collective-permute-start.3 = (bf16[2,384,512]{2,1,0:T(8,128)(2,1)S(1)}, bf16[2,384,512]{2,1,0:T(8,128)(2,1)S(1)}, u32[]{:S(2)}, u32[]{:S(2)}) collective-permute-start(bf16[2,384,512]{2,1,0:T(8,128)(2,1)S(1)} %shard_map.77), channel_id=1, source_target_pairs={{0,4},{1,5},{2,6},{3,7},{4,0},{5,1},{6,2},{7,3},{8,12},{9,13},{10,... | collective-permute-start | bytes 2359304 | tf_op jit(solution)/shard_map/ppermute | solution.py:554
  8.1 1.2 copy-done.2
  9.3 1.6 %collective-permute-start.1 = (bf16[2,384,256]{2,1,0:T(8,128)(2,1)S(1)}, bf16[2,384,256]{2,1,0:T(8,128)(2,1)S(1)}, u32[]{:S(2)}, u32[]{:S(2)}) collective-permute-start(bf16[2,384,256]{2,1,0:T(8,128)(2,1)S(1)} %shard_map.79), channel_id=1, source_target_pairs={{0,4},{1,5},{2,6},{3,7},{4,0},{5,1},{6,2},{7,3},{8,12},{9,13},{10,... | collective-permute-start | bytes 1179656 | tf_op jit(solution)/shard_map/ppermute | solution.py:554
  11.0 1.5 %collective-permute-start = (bf16[2,384,640]{2,1,0:T(8,128)(2,1)S(1)}, bf16[2,384,640]{2,1,0:T(8,128)(2,1)S(1)}, u32[]{:S(2)}, u32[]{:S(2)}) collective-permute-start(bf16[2,384,640]{2,1,0:T(8,128)(2,1)S(1)} %shard_map.78), channel_id=1, source_target_pairs={{0,16},{16,0},{1,17},{17,1},{2,18},{18,2},{3,19},{19,3},{4,20},{20... | collective-permute-start | bytes 2949128 | tf_op jit(solution)/shard_map/ppermute | solution.py:573
  13.1 13.2 %collective-permute-done.3.pair_even = bf16[2,384,512]{2,1,0:T(8,128)(2,1)S(1)} collective-permute-done((bf16[2,384,512]{2,1,0:T(8,128)(2,1)S(1)}, bf16[2,384,512]{2,1,0:T(8,128)(2,1)S(1)}, u32[]{:S(2)}, u32[]{:S(2)}) %collective-permute-start.3) | collective-permute-done | bytes 786464 | tf_op jit(solution)/shard_map/ppermute | solution.py:554
  26.3 2.5 %collective-permute-start.8 = (bf16[2,384,128]{2,1,0:T(8,128)(2,1)S(1)}, bf16[2,384,128]{2,1,0:T(8,128)(2,1)S(1)}, u32[]{:S(2)}, u32[]{:S(2)}) collective-permute-start(bf16[2,384,128]{2,1,0:T(8,128)(2,1)S(1)} %shard_map.84), channel_id=1, source_target_pairs={{0,4},{1,5},{2,6},{3,7},{4,0},{5,1},{6,2},{7,3},{8,12},{9,13},{10,... | collective-permute-start | bytes 589832 | tf_op jit(solution)/shard_map/ppermute | solution.py:554
  28.8 3.7 %shard_map.81 = (f32[48,384]{1,0:T(8,128)S(1)}, f32[48,384]{1,0:T(8,128)S(1)}, f32[48,384]{1,0:T(8,128)S(1)}) custom-call(f32[8,128]{1,0:T(8,128)S(1)} %shard_map.80.info, bf16[384,1536]{1,0:T(8,128)(2,1)S(1)} %bitcast.29, bf16[384,1536]{1,0:T(8,128)(2,1)S(1)} %bitcast.21, bf16[384,1536]{1,0:T(8,128)(2,1)S(1)} %bitcast.13, bf16[384,1536]{1,0:T(8,128)(2,1)S(1)} %bitcast.38, ...), custom_call_target="tpu_custom_call" | custom-call | flops 6000000000 | bytes 1 | tf_op jit(solution)/shard_map/pallas_call | solution.py:454
  32.5 2.3 %collective-permute-done.1.pair_even = bf16[2,384,256]{2,1,0:T(8,128)(2,1)S(1)} collective-permute-done((bf16[2,384,256]{2,1,0:T(8,128)(2,1)S(1)}, bf16[2,384,256]{2,1,0:T(8,128)(2,1)S(1)}, u32[]{:S(2)}, u32[]{:S(2)}) %collective-permute-start.1) | collective-permute-done | bytes 393248 | tf_op jit(solution)/shard_map/ppermute | solution.py:554
  34.8 1.9 %shard_map.82 = (f32[48,384]{1,0:T(8,128)S(1)}, f32[48,384]{1,0:T(8,128)S(1)}, f32[48,384]{1,0:T(8,128)S(1)}) custom-call(f32[8,128]{1,0:T(8,128)S(1)} %shard_map.80.info, bf16[384,1536]{1,0:T(8,128)(2,1)S(1)} %bitcast.30, bf16[384,1536]{1,0:T(8,128)(2,1)S(1)} %bitcast.22, ...), custom_call_target="tpu_custom_call", output_to_operand_aliasing={{0}: (7, {}), {1}: (8, {}), {2}: (9, {})} | custom-call | flops 6000000000 | bytes 1 | tf_op jit(solution)/shard_map/pallas_call | solution.py:454
  36.8 1.5 %collective-permute-start.5 = (bf16[2,400,640]{2,1,0:T(8,128)(2,1)S(1)}, bf16[2,400,640]{2,1,0:T(8,128)(2,1)S(1)}, u32[]{:S(2)}, u32[]{:S(2)}) collective-permute-start(bf16[2,400,640]{2,1,0:T(8,128)(2,1)S(1)} %shard_map.83), channel_id=1, source_target_pairs={{0,16},{16,0},{1,17},{17,1},{2,18},{18,2},{3,19},{19,3},{4,20},{20... | collective-permute-start | bytes 3072008 | tf_op jit(solution)/shard_map/ppermute | solution.py:573
  38.3 2.1 %collective-permute-start.6 = (f32[48,384]{1,0:T(8,128)S(1)}, f32[48,384]{1,0:T(8,128)S(1)}, u32[]{:S(2)}, u32[]{:S(2)}) collective-permute-start(f32[48,384]{1,0:T(8,128)S(1)} %get-tuple-element.48.sent_even), channel_id=1, source_target_pairs={{0,4},{1,5},{2,6},{3,7},{4,0},{5,1},{6,2},{7,3},{8,12},{9,13},{10,... | collective-permute-start | bytes 221192 | tf_op jit(solution)/shard_map/ppermute | solution.py:554
  40.4 1.5 %collective-permute-start.10 = (f32[48,384]{1,0:T(8,128)S(1)}, f32[48,384]{1,0:T(8,128)S(1)}, u32[]{:S(2)}, u32[]{:S(2)}) collective-permute-start(f32[48,384]{1,0:T(8,128)S(1)} %get-tuple-element.54), channel_id=1, source_target_pairs={{0,8},{1,9},{2,10},{3,11},{4,12},{5,13},{6,14},{7,15},{8,0},{9,1},... | collective-permute-start | bytes 221192 | tf_op jit(solution)/shard_map/ppermute | solution.py:554
  42.9 4.4 %collective-permute-done.10.rest_0_ = f32[48,384]{1,0:T(8,128)S(1)} collective-permute-done((f32[48,384]{1,0:T(8,128)S(1)}, f32[48,384]{1,0:T(8,128)S(1)}, u32[]{:S(2)}, u32[]{:S(2)}) %collective-permute-start.10) | collective-permute-done | bytes 73760 | tf_op jit(solution)/shard_map/ppermute | solution.py:554
  47.3 1.1 collective-permute-start.11
  48.4 8.2 %shard_map.85 = (bf16[2,384,768]{2,1,0:T(8,128)(2,1)S(1)}, f32[384,768]{1,0:T(8,128)S(1)}, bf16[384,768]{1,0:T(8,128)(2,1)S(1)}, bf16[384,768]{1,0:T(8,128)(2,1)S(1)}, f32[8,128]{1,0:T(8,128)S(1)}) custom-call(f32[8,128]{1,0:T(8,128)S(1)} %shard_map.80.info, bf16[384,1536]{1,0:T(8,128)(2,1)S(1)} %bitcast.32, bf16[384,1536]{1,0:T(8,128)(2,1)S(1)} %bitcast.24, ...), custom_call_target="tpu_custom_call" | custom-call | flops 4000000000 | bytes 1 | tf_op jit(solution)/shard_map/pallas_call | solution.py:474
  56.6 4.1 %shard_map.86 = (bf16[2,384,768]{2,1,0:T(8,128)(2,1)S(1)}, f32[384,768]{1,0:T(8,128)S(1)}, bf16[384,768]{1,0:T(8,128)(2,1)S(1)}, bf16[384,768]{1,0:T(8,128)(2,1)S(1)}, f32[8,128]{1,0:T(8,128)S(1)}) custom-call(f32[8,128]{1,0:T(8,128)S(1)} %shard_map.80.info, ...), custom_call_target="tpu_custom_call", output_to_operand_aliasing={{0}: (12, {}), {1}: (13, {}), {2}: (14, {}), {3}: (15, {})} | custom-call | flops 4000000000 | bytes 1 | tf_op jit(solution)/shard_map/pallas_call | solution.py:474
  62.2 2.0 %shard_map.87 = (bf16[384,896]{1,0:T(8,128)(2,1)S(1)}, f32[2,384,128]{2,1,0:T(8,128)S(1)}, bf16[2,384,128]{2,1,0:T(8,128)(2,1)S(1)}, bf16[2,384,128]{2,1,0:T(8,128)(2,1)S(1)}, f32[8,128]{1,0:T(8,128)S(1)}) custom-call(f32[8,128]{1,0:T(8,128)S(1)} %shard_map.80.info, bf16[384,1536]{1,0:T(8,128)(2,1)S(1)} %bitcast.34, bf16[384,1536]{1,0:T(8,128)(2,1)S(1)} %bitcast.26, ...), custom_call_target="tpu_custom_call" | custom-call | flops 6000000000 | bytes 1 | tf_op jit(solution)/shard_map/pallas_call | solution.py:413
  64.2 7.7 %collective-permute-start.16 = (bf16[2,384,128]{2,1,0:T(8,128)(2,1)S(1)}, bf16[2,384,128]{2,1,0:T(8,128)(2,1)S(1)}, u32[]{:S(2)}, u32[]{:S(2)}) collective-permute-start(bf16[2,384,128]{2,1,0:T(8,128)(2,1)S(1)} %get-tuple-element.70), channel_id=1, source_target_pairs={{0,4},{1,5},{2,6},{3,7},{4,0},{5,1},{6,2},{7,3},{8,12},{9,13},{10,... | collective-permute-start | bytes 589832 | tf_op jit(solution)/shard_map/ppermute | solution.py:554
  72.0 11.3 %shard_map.88 = (bf16[384,640]{1,0:T(8,128)(2,1)S(1)}, f32[2,384,640]{2,1,0:T(8,128)S(1)}, bf16[2,384,640]{2,1,0:T(8,128)(2,1)S(1)}, bf16[2,384,640]{2,1,0:T(8,128)(2,1)S(1)}, f32[8,128]{1,0:T(8,128)S(1)}) custom-call(bf16[2,400,640]{2,1,0:T(8,128)(2,1)S(1)} %collective-permute-done.5.info.query.grad, ...), custom_call_target="tpu_custom_call" | custom-call | flops 6000000000 | bytes 1 | tf_op jit(solution)/shard_map/pallas_call | solution.py:413
  83.3 4.7 %collective-permute-done.15.rest_0_ = bf16[2,384,768]{2,1,0:T(8,128)(2,1)S(1)} collective-permute-done((bf16[2,384,768]{2,1,0:T(8,128)(2,1)S(1)}, bf16[2,384,768]{2,1,0:T(8,128)(2,1)S(1)}, u32[]{:S(2)}, u32[]{:S(2)}) %collective-permute-start.15) | collective-permute-done | bytes 1179680 | tf_op jit(solution)/shard_map/ppermute | solution.py:573
  88.0 1.7 %collective-permute-start.13 = (bf16[2,384,640]{2,1,0:T(8,128)(2,1)S(1)}, bf16[2,384,640]{2,1,0:T(8,128)(2,1)S(1)}, u32[]{:S(2)}, u32[]{:S(2)}) collective-permute-start(bf16[2,384,640]{2,1,0:T(8,128)(2,1)S(1)} %get-tuple-element.65), channel_id=1, source_target_pairs={{0,4},{1,5},{2,6},{3,7},{4,0},{5,1},{6,2},{7,3},{8,12},{9,13},{10,... | collective-permute-start | bytes 2949128 | tf_op jit(solution)/shard_map/ppermute | solution.py:554
  90.4 1.7 %shard_map.90 = bf16[384,896]{1,0:T(8,128)(2,1)S(1)} custom-call(f32[8,128]{1,0:T(8,128)S(1)} %shard_map.80.info, bf16[384,1536]{1,0:T(8,128)(2,1)S(1)} %bitcast.35, f32[384,768]{1,0:T(8,128)S(1)} %get-tuple-element.72.own, bf16[384,768]{1,0:T(8,128)(2,1)S(1)} %collective-permute-done.19.from_even, ...), custom_call_target="tpu_custom_call", output_to_operand_aliasing={{}: (5, {})} | custom-call | flops 20000000000 | bytes 1 | tf_op jit(solution)/shard_map/pallas_call | solution.py:500
  94.0 1.5 %collective-permute-start.18 = (bf16[2,384,128]{2,1,0:T(8,128)(2,1)S(1)}, bf16[2,384,128]{2,1,0:T(8,128)(2,1)S(1)}, u32[]{:S(2)}, u32[]{:S(2)}) collective-permute-start(bf16[2,384,128]{2,1,0:T(8,128)(2,1)S(1)} %shard_map.89), channel_id=1, source_target_pairs={{0,16},{16,0},{1,17},{17,1},{2,18},{18,2},{3,19},{19,3},{4,20},{20... | collective-permute-start | bytes 589832 | tf_op jit(solution)/shard_map/ppermute | solution.py:573
  95.5 1.1 collective-permute-done.23
  96.6 1.5 %collective-permute-start.24 = (f32[2,128]{1,0:T(2,128)S(1)}, f32[2,128]{1,0:T(2,128)S(1)}, u32[]{:S(2)}, u32[]{:S(2)}) collective-permute-start(f32[2,128]{1,0:T(2,128)S(1)} %add.24), channel_id=1, source_target_pairs={{0,2},{1,3},{2,0},{3,1},{4,6},{5,7},{6,4},{7,5},{8,10},{9,11},{10,... | collective-permute-start | bytes 3080 | tf_op jit(solution)/shard_map/ppermute | solution.py:580
  98.1 2.0 %collective-permute-done.24 = f32[2,128]{1,0:T(2,128)S(1)} collective-permute-done((f32[2,128]{1,0:T(2,128)S(1)}, f32[2,128]{1,0:T(2,128)S(1)}, u32[]{:S(2)}, u32[]{:S(2)}) %collective-permute-start.24) | collective-permute-done | bytes 1056 | tf_op jit(solution)/shard_map/ppermute | solution.py:580
  100.2 1.6 %collective-permute-start.25 = (f32[2,128]{1,0:T(2,128)S(1)}, f32[2,128]{1,0:T(2,128)S(1)}, u32[]{:S(2)}, u32[]{:S(2)}) collective-permute-start(f32[2,128]{1,0:T(2,128)S(1)} %add.25), channel_id=1, source_target_pairs={{0,4},{4,0},{8,12},{12,8},{1,5},{5,1},{9,13},{13,9},{2,6},{6,2},{1... | collective-permute-start | bytes 3080 | tf_op jit(solution)/shard_map/ppermute | solution.py:580
  101.8 9.4 %collective-permute-done.25 = f32[2,128]{1,0:T(2,128)S(1)} collective-permute-done((f32[2,128]{1,0:T(2,128)S(1)}, f32[2,128]{1,0:T(2,128)S(1)}, u32[]{:S(2)}, u32[]{:S(2)}) %collective-permute-start.25) | collective-permute-done | bytes 1056 | tf_op jit(solution)/shard_map/ppermute | solution.py:580
  111.2 2.6 %collective-permute-start.26 = (f32[2,128]{1,0:T(2,128)S(1)}, f32[2,128]{1,0:T(2,128)S(1)}, u32[]{:S(2)}, u32[]{:S(2)}) collective-permute-start(f32[2,128]{1,0:T(2,128)S(1)} %add.26), channel_id=1, source_target_pairs={{0,8},{4,12},{8,0},{12,4},{1,9},{5,13},{9,1},{13,5},{2,10},{6,14},... | collective-permute-start | bytes 3080 | tf_op jit(solution)/shard_map/ppermute | solution.py:580
  114.6 3.7 %shard_map.91 = bf16[3,384,1536]{2,1,0:T(8,128)(2,1)} custom-call(bf16[2,400,640]{2,1,0:T(8,128)(2,1)S(1)} %collective-permute-done.5.info.query.grad, bf16[2,384,640]{2,1,0:T(8,128)(2,1)S(1)} %collective-permute-done.key.value, f32[2,384,640]{2,1,0:T(8,128)S(1)} %get-tuple-element.64.own, bf16[2,384,640]{2,1,0:T(8,128)(2,1)S(1)} %collective-permute-done.13.from_even, ...), custom_call_target="tpu_custom_call" | custom-call | flops 1 | bytes 1 | tf_op jit(solution)/shard_map/pallas_call | solution.py:518
  (59 shorter events, 8.0 us)
Async XLA Ops:
  3.2 4.8 %copy-start = (bf16[1,1,1,384,1536]{4,3,2,1,0:T(8,128)(2,1)S(1)}, bf16[1,1,1,384,1536]{4,3,2,1,0:T(8,128)(2,1)}, u32[]{:S(2)}) copy-start(bf16[1,1,1,384,1536]{4,3,2,1,0:T(8,128)(2,1)} %param.7) | copy-start | bytes 3538948
  3.2 4.8 %copy-start.5 = (bf16[1,1,1,384,1536]{4,3,2,1,0:T(8,128)(2,1)S(1)}, bf16[1,1,1,384,1536]{4,3,2,1,0:T(8,128)(2,1)}, u32[]{:S(2)}) copy-start(bf16[1,1,1,384,1536]{4,3,2,1,0:T(8,128)(2,1)} %param.8) | copy-start | bytes 3538948
  3.3 9.9 %collective-permute-start.4 = (bf16[2,384,512]{2,1,0:T(8,128)(2,1)S(1)}, bf16[2,384,512]{2,1,0:T(8,128)(2,1)S(1)}, u32[]{:S(2)}, u32[]{:S(2)}) collective-permute-start(bf16[2,384,512]{2,1,0:T(8,128)(2,1)S(1)} %shard_map.77), channel_id=1, source_target_pairs={{0,1},{1,0},{2,3},{3,2},{4,8},{5,9},{6,10},{7,11},{8,4},{9,5},{10,... | collective-permute-start | bytes 2359304 | tf_op jit(solution)/shard_map/ppermute | solution.py:554
  3.8 22.6 %collective-permute-start.3 = (bf16[2,384,512]{2,1,0:T(8,128)(2,1)S(1)}, bf16[2,384,512]{2,1,0:T(8,128)(2,1)S(1)}, u32[]{:S(2)}, u32[]{:S(2)}) collective-permute-start(bf16[2,384,512]{2,1,0:T(8,128)(2,1)S(1)} %shard_map.77), channel_id=1, source_target_pairs={{0,4},{1,5},{2,6},{3,7},{4,0},{5,1},{6,2},{7,3},{8,12},{9,13},{10,... | collective-permute-start | bytes 2359304 | tf_op jit(solution)/shard_map/ppermute | solution.py:554
  9.2 3.3 %copy-start.6 = (f32[1,2,128]{2,1,0:T(2,128)S(1)}, f32[1,2,128]{2,1,0:T(2,128)}, u32[]{:S(2)}) copy-start(f32[1,2,128]{2,1,0:T(2,128)} %param.10) | copy-start | bytes 3076
  9.2 3.3 %copy-start.7 = (s32[1,1,1,3]{3,2,1,0:T(1,128)S(1)}, s32[1,1,1,3]{3,2,1,0:T(1,128)}, u32[]{:S(2)}) copy-start(s32[1,1,1,3]{3,2,1,0:T(1,128)} %param.11) | copy-start | bytes 40
  9.3 23.2 %collective-permute-start.2 = (bf16[2,384,256]{2,1,0:T(8,128)(2,1)S(1)}, bf16[2,384,256]{2,1,0:T(8,128)(2,1)S(1)}, u32[]{:S(2)}, u32[]{:S(2)}) collective-permute-start(bf16[2,384,256]{2,1,0:T(8,128)(2,1)S(1)} %shard_map.79), channel_id=1, source_target_pairs={{0,1},{1,0},{2,3},{3,2},{4,8},{5,9},{6,10},{7,11},{8,4},{9,5},{10,... | collective-permute-start | bytes 1179656 | tf_op jit(solution)/shard_map/ppermute | solution.py:554
  9.3 25.4 %collective-permute-start.1 = (bf16[2,384,256]{2,1,0:T(8,128)(2,1)S(1)}, bf16[2,384,256]{2,1,0:T(8,128)(2,1)S(1)}, u32[]{:S(2)}, u32[]{:S(2)}) collective-permute-start(bf16[2,384,256]{2,1,0:T(8,128)(2,1)S(1)} %shard_map.79), channel_id=1, source_target_pairs={{0,4},{1,5},{2,6},{3,7},{4,0},{5,1},{6,2},{7,3},{8,12},{9,13},{10,... | collective-permute-start | bytes 1179656 | tf_op jit(solution)/shard_map/ppermute | solution.py:554
  11.0 25.7 %collective-permute-start = (bf16[2,384,640]{2,1,0:T(8,128)(2,1)S(1)}, bf16[2,384,640]{2,1,0:T(8,128)(2,1)S(1)}, u32[]{:S(2)}, u32[]{:S(2)}) collective-permute-start(bf16[2,384,640]{2,1,0:T(8,128)(2,1)S(1)} %shard_map.78), channel_id=1, source_target_pairs={{0,16},{16,0},{1,17},{17,1},{2,18},{18,2},{3,19},{19,3},{4,20},{20... | collective-permute-start | bytes 2949128 | tf_op jit(solution)/shard_map/ppermute | solution.py:573
  13.1 15.8 %copy-start.4 = (bf16[1,1,1,384,1536]{4,3,2,1,0:T(8,128)(2,1)S(1)}, bf16[1,1,1,384,1536]{4,3,2,1,0:T(8,128)(2,1)}, u32[]{:S(2)}) copy-start(bf16[1,1,1,384,1536]{4,3,2,1,0:T(8,128)(2,1)} %param.6) | copy-start | bytes 3538948
  26.3 14.1 %collective-permute-start.9 = (bf16[2,384,128]{2,1,0:T(8,128)(2,1)S(1)}, bf16[2,384,128]{2,1,0:T(8,128)(2,1)S(1)}, u32[]{:S(2)}, u32[]{:S(2)}) collective-permute-start(bf16[2,384,128]{2,1,0:T(8,128)(2,1)S(1)} %shard_map.84), channel_id=1, source_target_pairs={{0,1},{1,0},{2,3},{3,2},{4,8},{5,9},{6,10},{7,11},{8,4},{9,5},{10,... | collective-permute-start | bytes 589832 | tf_op jit(solution)/shard_map/ppermute | solution.py:554
  26.3 14.1 %collective-permute-start.8 = (bf16[2,384,128]{2,1,0:T(8,128)(2,1)S(1)}, bf16[2,384,128]{2,1,0:T(8,128)(2,1)S(1)}, u32[]{:S(2)}, u32[]{:S(2)}) collective-permute-start(bf16[2,384,128]{2,1,0:T(8,128)(2,1)S(1)} %shard_map.84), channel_id=1, source_target_pairs={{0,4},{1,5},{2,6},{3,7},{4,0},{5,1},{6,2},{7,3},{8,12},{9,13},{10,... | collective-permute-start | bytes 589832 | tf_op jit(solution)/shard_map/ppermute | solution.py:554
  36.8 25.4 %collective-permute-start.5 = (bf16[2,400,640]{2,1,0:T(8,128)(2,1)S(1)}, bf16[2,400,640]{2,1,0:T(8,128)(2,1)S(1)}, u32[]{:S(2)}, u32[]{:S(2)}) collective-permute-start(bf16[2,400,640]{2,1,0:T(8,128)(2,1)S(1)} %shard_map.83), channel_id=1, source_target_pairs={{0,16},{16,0},{1,17},{17,1},{2,18},{18,2},{3,19},{19,3},{4,20},{20... | collective-permute-start | bytes 3072008 | tf_op jit(solution)/shard_map/ppermute | solution.py:573
  38.3 4.6 %collective-permute-start.6 = (f32[48,384]{1,0:T(8,128)S(1)}, f32[48,384]{1,0:T(8,128)S(1)}, u32[]{:S(2)}, u32[]{:S(2)}) collective-permute-start(f32[48,384]{1,0:T(8,128)S(1)} %get-tuple-element.48.sent_even), channel_id=1, source_target_pairs={{0,4},{1,5},{2,6},{3,7},{4,0},{5,1},{6,2},{7,3},{8,12},{9,13},{10,... | collective-permute-start | bytes 221192 | tf_op jit(solution)/shard_map/ppermute | solution.py:554
  40.4 1.5 %collective-permute-start.7 = (f32[48,384]{1,0:T(8,128)S(1)}, f32[48,384]{1,0:T(8,128)S(1)}, u32[]{:S(2)}, u32[]{:S(2)}) collective-permute-start(f32[48,384]{1,0:T(8,128)S(1)} %get-tuple-element.50.sent_odd), channel_id=1, source_target_pairs={{0,1},{1,0},{2,3},{3,2},{4,8},{5,9},{6,10},{7,11},{8,4},{9,5},{10,... | collective-permute-start | bytes 221192 | tf_op jit(solution)/shard_map/ppermute | solution.py:554
  40.4 6.9 %collective-permute-start.10 = (f32[48,384]{1,0:T(8,128)S(1)}, f32[48,384]{1,0:T(8,128)S(1)}, u32[]{:S(2)}, u32[]{:S(2)}) collective-permute-start(f32[48,384]{1,0:T(8,128)S(1)} %get-tuple-element.54), channel_id=1, source_target_pairs={{0,8},{1,9},{2,10},{3,11},{4,12},{5,13},{6,14},{7,15},{8,0},{9,1},... | collective-permute-start | bytes 221192 | tf_op jit(solution)/shard_map/ppermute | solution.py:554
  47.3 17.0 %collective-permute-start.12 = (bf16[2,384,640]{2,1,0:T(8,128)(2,1)S(1)}, bf16[2,384,640]{2,1,0:T(8,128)(2,1)S(1)}, u32[]{:S(2)}, u32[]{:S(2)}) collective-permute-start(bf16[2,384,640]{2,1,0:T(8,128)(2,1)S(1)} %collective-permute-done.key.value), channel_id=1, source_target_pairs={{0,1},{1,0},{2,3},{3,2},{4,8},{5,9},{6,10},{7,11},{8,4},{9,5},{10,... | collective-permute-start | bytes 2949128 | tf_op jit(solution)/shard_map/ppermute | solution.py:554
  47.3 24.7 %collective-permute-start.11 = (bf16[2,384,640]{2,1,0:T(8,128)(2,1)S(1)}, bf16[2,384,640]{2,1,0:T(8,128)(2,1)S(1)}, u32[]{:S(2)}, u32[]{:S(2)}) collective-permute-start(bf16[2,384,640]{2,1,0:T(8,128)(2,1)S(1)} %collective-permute-done.key.value), channel_id=1, source_target_pairs={{0,4},{1,5},{2,6},{3,7},{4,0},{5,1},{6,2},{7,3},{8,12},{9,13},{10,... | collective-permute-start | bytes 2949128 | tf_op jit(solution)/shard_map/ppermute | solution.py:554
  60.7 27.3 %collective-permute-start.15 = (bf16[2,384,768]{2,1,0:T(8,128)(2,1)S(1)}, bf16[2,384,768]{2,1,0:T(8,128)(2,1)S(1)}, u32[]{:S(2)}, u32[]{:S(2)}) collective-permute-start(bf16[2,384,768]{2,1,0:T(8,128)(2,1)S(1)} %get-tuple-element.59), channel_id=1, source_target_pairs={{0,16},{16,0},{1,17},{17,1},{2,18},{18,2},{3,19},{19,3},{4,20},{20... | collective-permute-start | bytes 3538952 | tf_op jit(solution)/shard_map/ppermute | solution.py:573
  61.3 28.4 %collective-permute-start.19 = (bf16[384,768]{1,0:T(8,128)(2,1)S(1)}, bf16[384,768]{1,0:T(8,128)(2,1)S(1)}, u32[]{:S(2)}, u32[]{:S(2)}) collective-permute-start(bf16[384,768]{1,0:T(8,128)(2,1)S(1)} %get-tuple-element.73), channel_id=1, source_target_pairs={{0,4},{1,5},{2,6},{3,7},{4,0},{5,1},{6,2},{7,3},{8,12},{9,13},{10,... | collective-permute-start | bytes 1769480 | tf_op jit(solution)/shard_map/ppermute | solution.py:554
  62.2 27.6 %collective-permute-start.20 = (bf16[384,768]{1,0:T(8,128)(2,1)S(1)}, bf16[384,768]{1,0:T(8,128)(2,1)S(1)}, u32[]{:S(2)}, u32[]{:S(2)}) collective-permute-start(bf16[384,768]{1,0:T(8,128)(2,1)S(1)} %get-tuple-element.74), channel_id=1, source_target_pairs={{0,1},{1,0},{2,3},{3,2},{4,8},{5,9},{6,10},{7,11},{8,4},{9,5},{10,... | collective-permute-start | bytes 1769480 | tf_op jit(solution)/shard_map/ppermute | solution.py:554
  64.2 27.8 %collective-permute-start.16 = (bf16[2,384,128]{2,1,0:T(8,128)(2,1)S(1)}, bf16[2,384,128]{2,1,0:T(8,128)(2,1)S(1)}, u32[]{:S(2)}, u32[]{:S(2)}) collective-permute-start(bf16[2,384,128]{2,1,0:T(8,128)(2,1)S(1)} %get-tuple-element.70), channel_id=1, source_target_pairs={{0,4},{1,5},{2,6},{3,7},{4,0},{5,1},{6,2},{7,3},{8,12},{9,13},{10,... | collective-permute-start | bytes 589832 | tf_op jit(solution)/shard_map/ppermute | solution.py:554
  72.0 20.1 %collective-permute-start.17 = (bf16[2,384,128]{2,1,0:T(8,128)(2,1)S(1)}, bf16[2,384,128]{2,1,0:T(8,128)(2,1)S(1)}, u32[]{:S(2)}, u32[]{:S(2)}) collective-permute-start(bf16[2,384,128]{2,1,0:T(8,128)(2,1)S(1)} %get-tuple-element.71), channel_id=1, source_target_pairs={{0,1},{1,0},{2,3},{3,2},{4,8},{5,9},{6,10},{7,11},{8,4},{9,5},{10,... | collective-permute-start | bytes 589832 | tf_op jit(solution)/shard_map/ppermute | solution.py:554
  88.0 26.5 %collective-permute-start.13 = (bf16[2,384,640]{2,1,0:T(8,128)(2,1)S(1)}, bf16[2,384,640]{2,1,0:T(8,128)(2,1)S(1)}, u32[]{:S(2)}, u32[]{:S(2)}) collective-permute-start(bf16[2,384,640]{2,1,0:T(8,128)(2,1)S(1)} %get-tuple-element.65), channel_id=1, source_target_pairs={{0,4},{1,5},{2,6},{3,7},{4,0},{5,1},{6,2},{7,3},{8,12},{9,13},{10,... | collective-permute-start | bytes 2949128 | tf_op jit(solution)/shard_map/ppermute | solution.py:554
  89.8 24.8 %collective-permute-start.14 = (bf16[2,384,640]{2,1,0:T(8,128)(2,1)S(1)}, bf16[2,384,640]{2,1,0:T(8,128)(2,1)S(1)}, u32[]{:S(2)}, u32[]{:S(2)}) collective-permute-start(bf16[2,384,640]{2,1,0:T(8,128)(2,1)S(1)} %get-tuple-element.66), channel_id=1, source_target_pairs={{0,1},{1,0},{2,3},{3,2},{4,8},{5,9},{6,10},{7,11},{8,4},{9,5},{10,... | collective-permute-start | bytes 2949128 | tf_op jit(solution)/shard_map/ppermute | solution.py:554
  89.8 3.6 %collective-permute-start.21 = (f32[2,128]{1,0:T(2,128)S(1)}, f32[2,128]{1,0:T(2,128)S(1)}, u32[]{:S(2)}, u32[]{:S(2)}) collective-permute-start(f32[2,128]{1,0:T(2,128)S(1)} %slice.12), channel_id=1, source_target_pairs={{0,16},{16,0},{1,17},{17,1},{2,18},{18,2},{3,19},{19,3},{4,20},{20... | collective-permute-start | bytes 3080 | tf_op jit(solution)/shard_map/ppermute | solution.py:573
  93.4 21.1 %collective-permute-start.22 = (bf16[384,896]{1,0:T(8,128)(2,1)S(1)}, bf16[384,896]{1,0:T(8,128)(2,1)S(1)}, u32[]{:S(2)}, u32[]{:S(2)}) collective-permute-start(bf16[384,896]{1,0:T(8,128)(2,1)S(1)} %shard_map.90), channel_id=1, source_target_pairs={{0,16},{16,0},{1,17},{17,1},{2,18},{18,2},{3,19},{19,3},{4,20},{20... | collective-permute-start | bytes 2064392 | tf_op jit(solution)/shard_map/ppermute | solution.py:573
  94.0 20.6 %collective-permute-start.18 = (bf16[2,384,128]{2,1,0:T(8,128)(2,1)S(1)}, bf16[2,384,128]{2,1,0:T(8,128)(2,1)S(1)}, u32[]{:S(2)}, u32[]{:S(2)}) collective-permute-start(bf16[2,384,128]{2,1,0:T(8,128)(2,1)S(1)} %shard_map.89), channel_id=1, source_target_pairs={{0,16},{16,0},{1,17},{17,1},{2,18},{18,2},{3,19},{19,3},{4,20},{20... | collective-permute-start | bytes 589832 | tf_op jit(solution)/shard_map/ppermute | solution.py:573
  95.5 1.1 collective-permute-start.23
  96.6 3.6 %collective-permute-start.24 = (f32[2,128]{1,0:T(2,128)S(1)}, f32[2,128]{1,0:T(2,128)S(1)}, u32[]{:S(2)}, u32[]{:S(2)}) collective-permute-start(f32[2,128]{1,0:T(2,128)S(1)} %add.24), channel_id=1, source_target_pairs={{0,2},{1,3},{2,0},{3,1},{4,6},{5,7},{6,4},{7,5},{8,10},{9,11},{10,... | collective-permute-start | bytes 3080 | tf_op jit(solution)/shard_map/ppermute | solution.py:580
  100.2 11.0 %collective-permute-start.25 = (f32[2,128]{1,0:T(2,128)S(1)}, f32[2,128]{1,0:T(2,128)S(1)}, u32[]{:S(2)}, u32[]{:S(2)}) collective-permute-start(f32[2,128]{1,0:T(2,128)S(1)} %add.25), channel_id=1, source_target_pairs={{0,4},{4,0},{8,12},{12,8},{1,5},{5,1},{9,13},{13,9},{2,6},{6,2},{1... | collective-permute-start | bytes 3080 | tf_op jit(solution)/shard_map/ppermute | solution.py:580
  111.2 7.1 %collective-permute-start.26 = (f32[2,128]{1,0:T(2,128)S(1)}, f32[2,128]{1,0:T(2,128)S(1)}, u32[]{:S(2)}, u32[]{:S(2)}) collective-permute-start(f32[2,128]{1,0:T(2,128)S(1)} %add.26), channel_id=1, source_target_pairs={{0,8},{4,12},{8,0},{12,4},{1,9},{5,13},{9,1},{13,5},{2,10},{6,14},... | collective-permute-start | bytes 3080 | tf_op jit(solution)/shard_map/ppermute | solution.py:580
  (3 other events, 3.8 us)

commit v14 on v10

--- a/solution.py
+++ b/solution.py
@@ -292,10 +292,33 @@
     out[1] = value_grad.astype(out.dtype)
 
 
+def place_kernel(*refs, places):
+    amount = len(places)
+    pieces, out, staged = refs[:amount], refs[amount], refs[amount + 1 : -2]
+    load_sems, store_sems = refs[-2:]
+    loads = [
+        pltpu.make_async_copy(piece, stage, load_sems.at[slot])
+        for slot, (piece, stage) in enumerate(zip(pieces, staged))
+    ]
+    stores = [
+        pltpu.make_async_copy(
+            stage, out.at[planes, :, start : start + stage.shape[-1]], store_sems.at[slot]
+        )
+        for slot, (stage, (planes, start)) in enumerate(zip(staged, places))
+    ]
+    for load in loads:
+        load.start()
+    for load, store in zip(loads, stores):
+        load.wait()
+        store.start()
+    for store in stores:
+        store.wait()
+
+
 def last_kernel(info, key, own, from_even, from_odd, *rest, places, first, count):
     amount = len(places)
-    pieces, (out, held) = rest[:amount], rest[amount : amount + 2]
-    staged, (load_sems, store_sems) = rest[amount + 2 : -2], rest[-2:]
+    pieces, (_, out, held) = rest[:amount], rest[amount : amount + 3]
+    staged, (load_sems, store_sems) = rest[amount + 3 : -2], rest[-2:]
     head = pl.program_id(0)
     loads = [
         pltpu.make_async_copy(piece, stage, load_sems.at[slot])
@@ -510,7 +533,25 @@
     )(info, query, own, from_even, from_odd, low)
 
 
-def last_call(info, key, own, from_even, from_odd, pieces, places, first, count):
+def place_call(pieces, places):
+    rows = pieces[0].shape[-2]
+    anywhere = pl.BlockSpec(memory_space=pl.ANY)
+    return pl.pallas_call(
+        functools.partial(place_kernel, places=places),
+        in_specs=[anywhere] * len(pieces),
+        out_specs=anywhere,
+        out_shape=jax.ShapeDtypeStruct((3, rows, HEADS * HEAD_DIM), jnp.bfloat16),
+        scratch_shapes=[
+            *[pltpu.VMEM(piece.shape, piece.dtype) for piece in pieces],
+            pltpu.SemaphoreType.DMA((len(pieces),)),
+            pltpu.SemaphoreType.DMA((len(pieces),)),
+        ],
+        compiler_params=pltpu.CompilerParams(vmem_limit_bytes=SMALL_VMEM),
+        cost_estimate=COST,
+    )(*pieces)
+
+
+def last_call(info, key, own, from_even, from_odd, pieces, places, placed, first, count):
     array, offset, slot = key
     rows = own.shape[1]
     anywhere = pl.BlockSpec(memory_space=pl.ANY)
@@ -519,9 +560,10 @@
         grid=(count,),
         in_specs=[info_block(info), head_block(rows, offset, slot)]
         + [pair_block(rows)] * 3
-        + [anywhere] * len(pieces),
+        + [anywhere] * (len(pieces) + 1),
         out_specs=anywhere,
         out_shape=jax.ShapeDtypeStruct((3, rows, HEADS * HEAD_DIM), jnp.bfloat16),
+        input_output_aliases={5 + len(pieces): 0},
         scratch_shapes=[
             pltpu.VMEM((count, 2, rows, HEAD_DIM), jnp.bfloat16),
             *[pltpu.VMEM(piece.shape, piece.dtype) for piece in pieces],
@@ -530,7 +572,7 @@
         ],
         compiler_params=pltpu.CompilerParams(vmem_limit_bytes=SMALL_VMEM),
         cost_estimate=COST,
-    )(info, array, own, from_even, from_odd, *pieces)
+    )(info, array, own, from_even, from_odd, *pieces, placed)
 
 
 def partner(tile, parity, count):
@@ -576,9 +618,9 @@
     count = lax.axis_size(axis)
     step = 1
     while step < count:
-        other = lax.ppermute(value, axis, [(i, i ^ step) for i in range(count)])
+        sent = after(value, *late) if 2 * step >= count else value
+        value = value + lax.ppermute(sent, axis, [(i, i ^ step) for i in range(count)])
         step *= 2
-        value = value + (other if step < count else after(other, *late))
     return value
 
 
@@ -642,10 +684,12 @@
     low = finish_call(after(info, pieces[0]), (key, key_first, None), *key_answer, key_count)
     pieces.append(turned(low, -1))
     places.append((slice(1, 3), key_first * HEAD_DIM))
+    placed = place_call(pieces[:2], tuple(places[:2]))
     out = last_call(
-        asked, operands[2], own, *returned, pieces, tuple(places), away_first, away_count
-    )
-    summed = total_over(total_over(sum(gains), "dp"), "seq", out)
+        asked, operands[2], own, *returned, pieces[2:], tuple(places[2:]), placed,
+        away_first, away_count,
+    )
+    summed = total_over(total_over(sum(gains), "dp"), "seq", placed)
     tokens = lax.axis_size("dp") * seq_count * rows * HEADS
     return (out[None, :, None, None], (summed / math.sqrt(tokens))[None])
 

time: 117 us -> 115 us (0.983)
  waiting for transfers between devices: 41.4 us -> 39.1 us
    ppermute x6, waiting for transfers between devices: 12 us -> 8.87 us  [turned(): lax.ppermute(value, 'pipe', [(i, (i + step) % count) for i in range(count)])]
    pallas_call x0 -> x1, Pallas kernels: none -> 1.75 us  [place_call(): pl.pallas_call(functools.partial(place_kernel, places=places), in_specs=[...]
  transfers between devices with their start and end apart: 27 -> 27, of which waited for: 10 -> 11; matrix products, arithmetic and copies ran while one was open for 0% -> 1% of each run, Pallas kernels for 32% -> 31%
where the time goes in v14:
time: 115 us
  waiting for transfers between devices  39.1 us (34%)
  Pallas kernels  38.5 us (33%)
  starting transfers between devices  32.3 us (28%)
  local copies, waits for them, and re-layouts  3.71 us (3%)
    ppermute x17, starting transfers between devices, paired(): return lax.ppermute(value, ('seq', 'dp'), pairs)  19.4 us
    ppermute x17, waiting for transfers between devices, paired(): return lax.ppermute(value, ('seq', 'dp'), pairs)  16.5 us
    pallas_call x2, Pallas kernels, main_call(): pl.pallas_call(main_kernel, grid=(count,), in_specs=[info_block(info)] +...  15.9 us
    ppermute x4, waiting for transfers between devices, total_over(): lax.ppermute(sent, axis, [(i, i ^ step) for i in range(count)])  13.7 us
    pallas_call x2, Pallas kernels, grads_call(): pl.pallas_call(functools.partial(grads_kernel, far_count=far_count), grid...  10.3 us
    ppermute x6, waiting for transfers between devices, turned(): lax.ppermute(value, 'pipe', [(i, (i + step) % count) for i in range(count)])  8.87 us
    ppermute x6, starting transfers between devices, turned(): lax.ppermute(value, 'pipe', [(i, (i + step) % count) for i in range(count)])  7.31 us
    ppermute x4, starting transfers between devices, total_over(): lax.ppermute(sent, axis, [(i, i ^ step) for i in range(count)])  5.58 us
  transfers between devices with their start and end apart: 27, of which 11 were waited for; matrix products, arithmetic and copies ran while one was open for 1% of the time, Pallas kernels for 31%

profile of v14, /device:TPU:0, one launch (start us, length us, event | category | flops | bytes accessed | tf_op | source)
XLA Modules:
  0.0 115.1 jit_solution(13652757204279200072)
XLA Ops:
  3.8 4.1 %collective-permute-start.3 = (bf16[2,384,384]{2,1,0:T(8,128)(2,1)S(1)}, bf16[2,384,384]{2,1,0:T(8,128)(2,1)S(1)}, u32[]{:S(2)}, u32[]{:S(2)}) collective-permute-start(bf16[2,384,384]{2,1,0:T(8,128)(2,1)S(1)} %shard_map.77), channel_id=1, source_target_pairs={{0,4},{1,5},{2,6},{3,7},{4,0},{5,1},{6,2},{7,3},{8,12},{9,13},{10,... | collective-permute-start | bytes 1769480 | tf_op jit(solution)/shard_map/ppermute | solution.py:595
  9.4 1.6 %collective-permute-start.1 = (bf16[2,384,256]{2,1,0:T(8,128)(2,1)S(1)}, bf16[2,384,256]{2,1,0:T(8,128)(2,1)S(1)}, u32[]{:S(2)}, u32[]{:S(2)}) collective-permute-start(bf16[2,384,256]{2,1,0:T(8,128)(2,1)S(1)} %shard_map.79), channel_id=1, source_target_pairs={{0,4},{1,5},{2,6},{3,7},{4,0},{5,1},{6,2},{7,3},{8,12},{9,13},{10,... | collective-permute-start | bytes 1179656 | tf_op jit(solution)/shard_map/ppermute | solution.py:595
  11.0 1.5 %collective-permute-start = (bf16[2,384,640]{2,1,0:T(8,128)(2,1)S(1)}, bf16[2,384,640]{2,1,0:T(8,128)(2,1)S(1)}, u32[]{:S(2)}, u32[]{:S(2)}) collective-permute-start(bf16[2,384,640]{2,1,0:T(8,128)(2,1)S(1)} %shard_map.78), channel_id=1, source_target_pairs={{0,16},{16,0},{1,17},{17,1},{2,18},{18,2},{3,19},{19,3},{4,20},{20... | collective-permute-start | bytes 2949128 | tf_op jit(solution)/shard_map/ppermute | solution.py:614
  13.1 9.0 %collective-permute-done.3.pair_even = bf16[2,384,384]{2,1,0:T(8,128)(2,1)S(1)} collective-permute-done((bf16[2,384,384]{2,1,0:T(8,128)(2,1)S(1)}, bf16[2,384,384]{2,1,0:T(8,128)(2,1)S(1)}, u32[]{:S(2)}, u32[]{:S(2)}) %collective-permute-start.3) | collective-permute-done | bytes 589856 | tf_op jit(solution)/shard_map/ppermute | solution.py:595
  22.1 2.5 %collective-permute-start.9 = (bf16[2,384,256]{2,1,0:T(8,128)(2,1)S(1)}, bf16[2,384,256]{2,1,0:T(8,128)(2,1)S(1)}, u32[]{:S(2)}, u32[]{:S(2)}) collective-permute-start(bf16[2,384,256]{2,1,0:T(8,128)(2,1)S(1)} %shard_map.86), channel_id=1, source_target_pairs={{0,4},{1,5},{2,6},{3,7},{4,0},{5,1},{6,2},{7,3},{8,12},{9,13},{10,... | collective-permute-start | bytes 1179656 | tf_op jit(solution)/shard_map/ppermute | solution.py:595
  24.6 2.8 %shard_map.81 = (f32[40,384]{1,0:T(8,128)S(1)}, f32[40,384]{1,0:T(8,128)S(1)}, f32[40,384]{1,0:T(8,128)S(1)}) custom-call(f32[8,128]{1,0:T(8,128)S(1)} %shard_map.80.info, bf16[384,1536]{1,0:T(8,128)(2,1)S(1)} %bitcast.29, bf16[384,1536]{1,0:T(8,128)(2,1)S(1)} %bitcast.21, bf16[384,1536]{1,0:T(8,128)(2,1)S(1)} %bitcast.13, bf16[384,1536]{1,0:T(8,128)(2,1)S(1)} %bitcast.38, ...), custom_call_target="tpu_custom_call" | custom-call | flops 6000000000 | bytes 1 | tf_op jit(solution)/shard_map/pallas_call | solution.py:476
  27.4 3.2 %collective-permute-done.1.pair_even = bf16[2,384,256]{2,1,0:T(8,128)(2,1)S(1)} collective-permute-done((bf16[2,384,256]{2,1,0:T(8,128)(2,1)S(1)}, bf16[2,384,256]{2,1,0:T(8,128)(2,1)S(1)}, u32[]{:S(2)}, u32[]{:S(2)}) %collective-permute-start.1) | collective-permute-done | bytes 393248 | tf_op jit(solution)/shard_map/ppermute | solution.py:595
  30.6 1.9 %shard_map.82 = (f32[40,384]{1,0:T(8,128)S(1)}, f32[40,384]{1,0:T(8,128)S(1)}, f32[40,384]{1,0:T(8,128)S(1)}) custom-call(f32[8,128]{1,0:T(8,128)S(1)} %shard_map.80.info, bf16[384,1536]{1,0:T(8,128)(2,1)S(1)} %bitcast.30, bf16[384,1536]{1,0:T(8,128)(2,1)S(1)} %bitcast.22, ...), custom_call_target="tpu_custom_call", output_to_operand_aliasing={{0}: (7, {}), {1}: (8, {}), {2}: (9, {})} | custom-call | flops 6000000000 | bytes 1 | tf_op jit(solution)/shard_map/pallas_call | solution.py:476
  32.4 2.0 %collective-permute-start.8 = (f32[40,384]{1,0:T(8,128)S(1)}, f32[40,384]{1,0:T(8,128)S(1)}, u32[]{:S(2)}, u32[]{:S(2)}) collective-permute-start(f32[40,384]{1,0:T(8,128)S(1)} %get-tuple-element.50), channel_id=1, source_target_pairs={{0,8},{1,9},{2,10},{3,11},{4,12},{5,13},{6,14},{7,15},{8,0},{9,1},... | collective-permute-start | bytes 184328 | tf_op jit(solution)/shard_map/ppermute | solution.py:595
  34.4 1.6 %collective-permute-start.6 = (f32[40,384]{1,0:T(8,128)S(1)}, f32[40,384]{1,0:T(8,128)S(1)}, u32[]{:S(2)}, u32[]{:S(2)}) collective-permute-start(f32[40,384]{1,0:T(8,128)S(1)} %get-tuple-element.47.sent_even), channel_id=1, source_target_pairs={{0,4},{1,5},{2,6},{3,7},{4,0},{5,1},{6,2},{7,3},{8,12},{9,13},{10,... | collective-permute-start | bytes 184328 | tf_op jit(solution)/shard_map/ppermute | solution.py:595
  36.1 4.3 %collective-permute-done.8.rest_0_ = f32[40,384]{1,0:T(8,128)S(1)} collective-permute-done((f32[40,384]{1,0:T(8,128)S(1)}, f32[40,384]{1,0:T(8,128)S(1)}, u32[]{:S(2)}, u32[]{:S(2)}) %collective-permute-start.8) | collective-permute-done | bytes 61472 | tf_op jit(solution)/shard_map/ppermute | solution.py:595
  40.5 1.5 %collective-permute-start.5 = (bf16[2,400,640]{2,1,0:T(8,128)(2,1)S(1)}, bf16[2,400,640]{2,1,0:T(8,128)(2,1)S(1)}, u32[]{:S(2)}, u32[]{:S(2)}) collective-permute-start(bf16[2,400,640]{2,1,0:T(8,128)(2,1)S(1)} %shard_map.83), channel_id=1, source_target_pairs={{0,16},{16,0},{1,17},{17,1},{2,18},{18,2},{3,19},{19,3},{4,20},{20... | collective-permute-start | bytes 3072008 | tf_op jit(solution)/shard_map/ppermute | solution.py:614
  42.0 2.6 %collective-permute-start.11 = (bf16[2,384,640]{2,1,0:T(8,128)(2,1)S(1)}, bf16[2,384,640]{2,1,0:T(8,128)(2,1)S(1)}, u32[]{:S(2)}, u32[]{:S(2)}) collective-permute-start(bf16[2,384,640]{2,1,0:T(8,128)(2,1)S(1)} %collective-permute-done.key.value), channel_id=1, source_target_pairs={{0,4},{1,5},{2,6},{3,7},{4,0},{5,1},{6,2},{7,3},{8,12},{9,13},{10,... | collective-permute-start | bytes 2949128 | tf_op jit(solution)/shard_map/ppermute | solution.py:595
  44.7 6.1 %shard_map.84 = (bf16[2,384,640]{2,1,0:T(8,128)(2,1)S(1)}, f32[384,640]{1,0:T(8,128)S(1)}, bf16[384,640]{1,0:T(8,128)(2,1)S(1)}, bf16[384,640]{1,0:T(8,128)(2,1)S(1)}, f32[8,128]{1,0:T(8,128)S(1)}) custom-call(f32[8,128]{1,0:T(8,128)S(1)} %shard_map.80.info, bf16[384,1536]{1,0:T(8,128)(2,1)S(1)} %bitcast.32, bf16[384,1536]{1,0:T(8,128)(2,1)S(1)} %bitcast.24, ...), custom_call_target="tpu_custom_call" | custom-call | flops 1 | bytes 1 | tf_op jit(solution)/shard_map/pallas_call | solution.py:496
  50.8 4.1 %shard_map.85 = (bf16[2,384,640]{2,1,0:T(8,128)(2,1)S(1)}, f32[384,640]{1,0:T(8,128)S(1)}, bf16[384,640]{1,0:T(8,128)(2,1)S(1)}, bf16[384,640]{1,0:T(8,128)(2,1)S(1)}, f32[8,128]{1,0:T(8,128)S(1)}) custom-call(f32[8,128]{1,0:T(8,128)S(1)} %shard_map.80.info, ...), custom_call_target="tpu_custom_call", output_to_operand_aliasing={{0}: (12, {}), {1}: (13, {}), {2}: (14, {}), {3}: (15, {})} | custom-call | flops 1 | bytes 1 | tf_op jit(solution)/shard_map/pallas_call | solution.py:496
  55.7 4.6 %shard_map.87 = (bf16[384,896]{1,0:T(8,128)(2,1)S(1)}, f32[2,384,256]{2,1,0:T(8,128)S(1)}, bf16[2,384,256]{2,1,0:T(8,128)(2,1)S(1)}, bf16[2,384,256]{2,1,0:T(8,128)(2,1)S(1)}, f32[8,128]{1,0:T(8,128)S(1)}) custom-call(f32[8,128]{1,0:T(8,128)S(1)} %shard_map.80.info, bf16[384,1536]{1,0:T(8,128)(2,1)S(1)} %bitcast.34, bf16[384,1536]{1,0:T(8,128)(2,1)S(1)} %bitcast.26, ...), custom_call_target="tpu_custom_call" | custom-call | flops 6000000000 | bytes 1 | tf_op jit(solution)/shard_map/pallas_call | solution.py:435
  60.3 5.7 %collective-permute-done.5.info.query.grad = bf16[2,400,640]{2,1,0:T(8,128)(2,1)S(1)} collective-permute-done((bf16[2,400,640]{2,1,0:T(8,128)(2,1)S(1)}, bf16[2,400,640]{2,1,0:T(8,128)(2,1)S(1)}, u32[]{:S(2)}, u32[]{:S(2)}) %collective-permute-start.5) | collective-permute-done | bytes 1024032 | tf_op jit(solution)/shard_map/ppermute | solution.py:614
  66.0 2.7 %collective-permute-start.20 = (bf16[2,384,256]{2,1,0:T(8,128)(2,1)S(1)}, bf16[2,384,256]{2,1,0:T(8,128)(2,1)S(1)}, u32[]{:S(2)}, u32[]{:S(2)}) collective-permute-start(bf16[2,384,256]{2,1,0:T(8,128)(2,1)S(1)} %get-tuple-element.73), channel_id=1, source_target_pairs={{0,4},{1,5},{2,6},{3,7},{4,0},{5,1},{6,2},{7,3},{8,12},{9,13},{10,... | collective-permute-start | bytes 1179656 | tf_op jit(solution)/shard_map/ppermute | solution.py:595
  68.7 11.3 %shard_map.88 = (bf16[384,640]{1,0:T(8,128)(2,1)S(1)}, f32[2,384,640]{2,1,0:T(8,128)S(1)}, bf16[2,384,640]{2,1,0:T(8,128)(2,1)S(1)}, bf16[2,384,640]{2,1,0:T(8,128)(2,1)S(1)}, f32[8,128]{1,0:T(8,128)S(1)}) custom-call(bf16[2,400,640]{2,1,0:T(8,128)(2,1)S(1)} %collective-permute-done.5.info.query.grad, ...), custom_call_target="tpu_custom_call" | custom-call | flops 6000000000 | bytes 1 | tf_op jit(solution)/shard_map/pallas_call | solution.py:435
  80.0 1.7 %collective-permute-start.13 = (bf16[2,384,640]{2,1,0:T(8,128)(2,1)S(1)}, bf16[2,384,640]{2,1,0:T(8,128)(2,1)S(1)}, u32[]{:S(2)}, u32[]{:S(2)}) collective-permute-start(bf16[2,384,640]{2,1,0:T(8,128)(2,1)S(1)} %get-tuple-element.63), channel_id=1, source_target_pairs={{0,4},{1,5},{2,6},{3,7},{4,0},{5,1},{6,2},{7,3},{8,12},{9,13},{10,... | collective-permute-start | bytes 2949128 | tf_op jit(solution)/shard_map/ppermute | solution.py:595
  81.7 1.4 %shard_map.89 = bf16[384,896]{1,0:T(8,128)(2,1)S(1)} custom-call(f32[8,128]{1,0:T(8,128)S(1)} %shard_map.80.info, bf16[384,1536]{1,0:T(8,128)(2,1)S(1)} %bitcast.35, f32[384,640]{1,0:T(8,128)S(1)} %get-tuple-element.65.own, bf16[384,640]{1,0:T(8,128)(2,1)S(1)} %collective-permute-done.15.from_even, ...), custom_call_target="tpu_custom_call", output_to_operand_aliasing={{}: (5, {})} | custom-call | flops 20000000000 | bytes 1 | tf_op jit(solution)/shard_map/pallas_call | solution.py:522
  83.3 1.5 %collective-permute-start.18 = (f32[2,128]{1,0:T(2,128)S(1)}, f32[2,128]{1,0:T(2,128)S(1)}, u32[]{:S(2)}, u32[]{:S(2)}) collective-permute-start(f32[2,128]{1,0:T(2,128)S(1)} %slice.12), channel_id=1, source_target_pairs={{0,16},{16,0},{1,17},{17,1},{2,18},{18,2},{3,19},{19,3},{4,20},{20... | collective-permute-start | bytes 3080 | tf_op jit(solution)/shard_map/ppermute | solution.py:614
  84.8 2.1 %collective-permute-done.18 = f32[2,128]{1,0:T(2,128)S(1)} collective-permute-done((f32[2,128]{1,0:T(2,128)S(1)}, f32[2,128]{1,0:T(2,128)S(1)}, u32[]{:S(2)}, u32[]{:S(2)}) %collective-permute-start.18) | collective-permute-done | bytes 1056 | tf_op jit(solution)/shard_map/ppermute | solution.py:614
  86.9 1.5 %collective-permute-start.19 = (bf16[384,896]{1,0:T(8,128)(2,1)S(1)}, bf16[384,896]{1,0:T(8,128)(2,1)S(1)}, u32[]{:S(2)}, u32[]{:S(2)}) collective-permute-start(bf16[384,896]{1,0:T(8,128)(2,1)S(1)} %shard_map.89), channel_id=1, source_target_pairs={{0,16},{16,0},{1,17},{17,1},{2,18},{18,2},{3,19},{19,3},{4,20},{20... | collective-permute-start | bytes 2064392 | tf_op jit(solution)/shard_map/ppermute | solution.py:614
  90.9 1.5 %collective-permute-start.24 = (f32[2,128]{1,0:T(2,128)S(1)}, f32[2,128]{1,0:T(2,128)S(1)}, u32[]{:S(2)}, u32[]{:S(2)}) collective-permute-start(f32[2,128]{1,0:T(2,128)S(1)} %add.24), channel_id=1, source_target_pairs={{0,2},{1,3},{2,0},{3,1},{4,6},{5,7},{6,4},{7,5},{8,10},{9,11},{10,... | collective-permute-start | bytes 3080 | tf_op jit(solution)/shard_map/ppermute | solution.py:622
  92.4 2.0 %collective-permute-done.24 = f32[2,128]{1,0:T(2,128)S(1)} collective-permute-done((f32[2,128]{1,0:T(2,128)S(1)}, f32[2,128]{1,0:T(2,128)S(1)}, u32[]{:S(2)}, u32[]{:S(2)}) %collective-permute-start.24) | collective-permute-done | bytes 1056 | tf_op jit(solution)/shard_map/ppermute | solution.py:622
  94.5 2.1 %collective-permute-start.25 = (f32[2,128]{1,0:T(2,128)S(1)}, f32[2,128]{1,0:T(2,128)S(1)}, u32[]{:S(2)}, u32[]{:S(2)}) collective-permute-start(f32[2,128]{1,0:T(2,128)S(1)} %add.25), channel_id=1, source_target_pairs={{0,4},{4,0},{8,12},{12,8},{1,5},{5,1},{9,13},{13,9},{2,6},{6,2},{1... | collective-permute-start | bytes 3080 | tf_op jit(solution)/shard_map/ppermute | solution.py:622
  96.6 1.8 %shard_map.91.rest_2_ = bf16[3,384,1536]{2,1,0:T(8,128)(2,1)} custom-call(bf16[2,384,640]{2,1,0:T(8,128)(2,1)S(1)} %collective-permute-done.17.refs_0_, bf16[384,640]{1,0:T(8,128)(2,1)S(1)} %get-tuple-element.75.refs_1_), custom_call_target="tpu_custom_call" | custom-call | flops 1 | bytes 1 | tf_op jit(solution)/shard_map/pallas_call | solution.py:539
  98.3 8.0 %collective-permute-done.25 = f32[2,128]{1,0:T(2,128)S(1)} collective-permute-done((f32[2,128]{1,0:T(2,128)S(1)}, f32[2,128]{1,0:T(2,128)S(1)}, u32[]{:S(2)}, u32[]{:S(2)}) %collective-permute-start.25) | collective-permute-done | bytes 1056 | tf_op jit(solution)/shard_map/ppermute | solution.py:622
  106.3 1.9 %collective-permute-start.26 = (f32[2,128]{1,0:T(2,128)S(1)}, f32[2,128]{1,0:T(2,128)S(1)}, u32[]{:S(2)}, u32[]{:S(2)}) collective-permute-start(f32[2,128]{1,0:T(2,128)S(1)} %add.26), channel_id=1, source_target_pairs={{0,8},{4,12},{8,0},{12,4},{1,9},{5,13},{9,1},{13,5},{2,10},{6,14},... | collective-permute-start | bytes 3080 | tf_op jit(solution)/shard_map/ppermute | solution.py:622
  108.2 2.5 %collective-permute-done.26 = f32[2,128]{1,0:T(2,128)S(1)} collective-permute-done((f32[2,128]{1,0:T(2,128)S(1)}, f32[2,128]{1,0:T(2,128)S(1)}, u32[]{:S(2)}, u32[]{:S(2)}) %collective-permute-start.26) | collective-permute-done | bytes 1056 | tf_op jit(solution)/shard_map/ppermute | solution.py:622
  112.2 2.9 %shard_map.92 = bf16[3,384,1536]{2,1,0:T(8,128)(2,1)} custom-call(bf16[2,400,640]{2,1,0:T(8,128)(2,1)S(1)} %collective-permute-done.5.info.query.grad, bf16[2,384,640]{2,1,0:T(8,128)(2,1)S(1)} %collective-permute-done.key.value, f32[2,384,640]{2,1,0:T(8,128)S(1)} %get-tuple-element.62.own, ...), custom_call_target="tpu_custom_call", output_to_operand_aliasing={{}: (7, {})} | custom-call | flops 1 | bytes 1 | tf_op jit(solution)/shard_map/pallas_call | solution.py:558
  (60 shorter events, 10.2 us)
Async XLA Ops:
  3.2 4.8 %copy-start = (bf16[1,1,1,384,1536]{4,3,2,1,0:T(8,128)(2,1)S(1)}, bf16[1,1,1,384,1536]{4,3,2,1,0:T(8,128)(2,1)}, u32[]{:S(2)}) copy-start(bf16[1,1,1,384,1536]{4,3,2,1,0:T(8,128)(2,1)} %param.7) | copy-start | bytes 3538948
  3.2 4.8 %copy-start.5 = (bf16[1,1,1,384,1536]{4,3,2,1,0:T(8,128)(2,1)S(1)}, bf16[1,1,1,384,1536]{4,3,2,1,0:T(8,128)(2,1)}, u32[]{:S(2)}) copy-start(bf16[1,1,1,384,1536]{4,3,2,1,0:T(8,128)(2,1)} %param.8) | copy-start | bytes 3538948
  3.3 9.9 %collective-permute-start.4 = (bf16[2,384,384]{2,1,0:T(8,128)(2,1)S(1)}, bf16[2,384,384]{2,1,0:T(8,128)(2,1)S(1)}, u32[]{:S(2)}, u32[]{:S(2)}) collective-permute-start(bf16[2,384,384]{2,1,0:T(8,128)(2,1)S(1)} %shard_map.77), channel_id=1, source_target_pairs={{0,1},{1,0},{2,3},{3,2},{4,8},{5,9},{6,10},{7,11},{8,4},{9,5},{10,... | collective-permute-start | bytes 1769480 | tf_op jit(solution)/shard_map/ppermute | solution.py:595
  3.8 18.3 %collective-permute-start.3 = (bf16[2,384,384]{2,1,0:T(8,128)(2,1)S(1)}, bf16[2,384,384]{2,1,0:T(8,128)(2,1)S(1)}, u32[]{:S(2)}, u32[]{:S(2)}) collective-permute-start(bf16[2,384,384]{2,1,0:T(8,128)(2,1)S(1)} %shard_map.77), channel_id=1, source_target_pairs={{0,4},{1,5},{2,6},{3,7},{4,0},{5,1},{6,2},{7,3},{8,12},{9,13},{10,... | collective-permute-start | bytes 1769480 | tf_op jit(solution)/shard_map/ppermute | solution.py:595
  9.2 3.3 %copy-start.6 = (f32[1,2,128]{2,1,0:T(2,128)S(1)}, f32[1,2,128]{2,1,0:T(2,128)}, u32[]{:S(2)}) copy-start(f32[1,2,128]{2,1,0:T(2,128)} %param.10) | copy-start | bytes 3076
  9.2 3.3 %copy-start.7 = (s32[1,1,1,3]{3,2,1,0:T(1,128)S(1)}, s32[1,1,1,3]{3,2,1,0:T(1,128)}, u32[]{:S(2)}) copy-start(s32[1,1,1,3]{3,2,1,0:T(1,128)} %param.11) | copy-start | bytes 40
  9.3 18.1 %collective-permute-start.2 = (bf16[2,384,256]{2,1,0:T(8,128)(2,1)S(1)}, bf16[2,384,256]{2,1,0:T(8,128)(2,1)S(1)}, u32[]{:S(2)}, u32[]{:S(2)}) collective-permute-start(bf16[2,384,256]{2,1,0:T(8,128)(2,1)S(1)} %shard_map.79), channel_id=1, source_target_pairs={{0,1},{1,0},{2,3},{3,2},{4,8},{5,9},{6,10},{7,11},{8,4},{9,5},{10,... | collective-permute-start | bytes 1179656 | tf_op jit(solution)/shard_map/ppermute | solution.py:595
  9.4 21.2 %collective-permute-start.1 = (bf16[2,384,256]{2,1,0:T(8,128)(2,1)S(1)}, bf16[2,384,256]{2,1,0:T(8,128)(2,1)S(1)}, u32[]{:S(2)}, u32[]{:S(2)}) collective-permute-start(bf16[2,384,256]{2,1,0:T(8,128)(2,1)S(1)} %shard_map.79), channel_id=1, source_target_pairs={{0,4},{1,5},{2,6},{3,7},{4,0},{5,1},{6,2},{7,3},{8,12},{9,13},{10,... | collective-permute-start | bytes 1179656 | tf_op jit(solution)/shard_map/ppermute | solution.py:595
  11.0 23.4 %collective-permute-start = (bf16[2,384,640]{2,1,0:T(8,128)(2,1)S(1)}, bf16[2,384,640]{2,1,0:T(8,128)(2,1)S(1)}, u32[]{:S(2)}, u32[]{:S(2)}) collective-permute-start(bf16[2,384,640]{2,1,0:T(8,128)(2,1)S(1)} %shard_map.78), channel_id=1, source_target_pairs={{0,16},{16,0},{1,17},{17,1},{2,18},{18,2},{3,19},{19,3},{4,20},{20... | collective-permute-start | bytes 2949128 | tf_op jit(solution)/shard_map/ppermute | solution.py:614
  13.1 11.5 %copy-start.4 = (bf16[1,1,1,384,1536]{4,3,2,1,0:T(8,128)(2,1)S(1)}, bf16[1,1,1,384,1536]{4,3,2,1,0:T(8,128)(2,1)}, u32[]{:S(2)}) copy-start(bf16[1,1,1,384,1536]{4,3,2,1,0:T(8,128)(2,1)} %param.6) | copy-start | bytes 3538948
  22.1 19.8 %collective-permute-start.10 = (bf16[2,384,256]{2,1,0:T(8,128)(2,1)S(1)}, bf16[2,384,256]{2,1,0:T(8,128)(2,1)S(1)}, u32[]{:S(2)}, u32[]{:S(2)}) collective-permute-start(bf16[2,384,256]{2,1,0:T(8,128)(2,1)S(1)} %shard_map.86), channel_id=1, source_target_pairs={{0,1},{1,0},{2,3},{3,2},{4,8},{5,9},{6,10},{7,11},{8,4},{9,5},{10,... | collective-permute-start | bytes 1179656 | tf_op jit(solution)/shard_map/ppermute | solution.py:595
  22.1 19.8 %collective-permute-start.9 = (bf16[2,384,256]{2,1,0:T(8,128)(2,1)S(1)}, bf16[2,384,256]{2,1,0:T(8,128)(2,1)S(1)}, u32[]{:S(2)}, u32[]{:S(2)}) collective-permute-start(bf16[2,384,256]{2,1,0:T(8,128)(2,1)S(1)} %shard_map.86), channel_id=1, source_target_pairs={{0,4},{1,5},{2,6},{3,7},{4,0},{5,1},{6,2},{7,3},{8,12},{9,13},{10,... | collective-permute-start | bytes 1179656 | tf_op jit(solution)/shard_map/ppermute | solution.py:595
  32.4 8.0 %collective-permute-start.8 = (f32[40,384]{1,0:T(8,128)S(1)}, f32[40,384]{1,0:T(8,128)S(1)}, u32[]{:S(2)}, u32[]{:S(2)}) collective-permute-start(f32[40,384]{1,0:T(8,128)S(1)} %get-tuple-element.50), channel_id=1, source_target_pairs={{0,8},{1,9},{2,10},{3,11},{4,12},{5,13},{6,14},{7,15},{8,0},{9,1},... | collective-permute-start | bytes 184328 | tf_op jit(solution)/shard_map/ppermute | solution.py:595
  34.4 7.5 %collective-permute-start.7 = (f32[40,384]{1,0:T(8,128)S(1)}, f32[40,384]{1,0:T(8,128)S(1)}, u32[]{:S(2)}, u32[]{:S(2)}) collective-permute-start(f32[40,384]{1,0:T(8,128)S(1)} %get-tuple-element.49.sent_odd), channel_id=1, source_target_pairs={{0,1},{1,0},{2,3},{3,2},{4,8},{5,9},{6,10},{7,11},{8,4},{9,5},{10,... | collective-permute-start | bytes 184328 | tf_op jit(solution)/shard_map/ppermute | solution.py:595
  34.4 7.5 %collective-permute-start.6 = (f32[40,384]{1,0:T(8,128)S(1)}, f32[40,384]{1,0:T(8,128)S(1)}, u32[]{:S(2)}, u32[]{:S(2)}) collective-permute-start(f32[40,384]{1,0:T(8,128)S(1)} %get-tuple-element.47.sent_even), channel_id=1, source_target_pairs={{0,4},{1,5},{2,6},{3,7},{4,0},{5,1},{6,2},{7,3},{8,12},{9,13},{10,... | collective-permute-start | bytes 184328 | tf_op jit(solution)/shard_map/ppermute | solution.py:595
  40.5 25.6 %collective-permute-start.5 = (bf16[2,400,640]{2,1,0:T(8,128)(2,1)S(1)}, bf16[2,400,640]{2,1,0:T(8,128)(2,1)S(1)}, u32[]{:S(2)}, u32[]{:S(2)}) collective-permute-start(bf16[2,400,640]{2,1,0:T(8,128)(2,1)S(1)} %shard_map.83), channel_id=1, source_target_pairs={{0,16},{16,0},{1,17},{17,1},{2,18},{18,2},{3,19},{19,3},{4,20},{20... | collective-permute-start | bytes 3072008 | tf_op jit(solution)/shard_map/ppermute | solution.py:614
  42.0 24.1 %collective-permute-start.12 = (bf16[2,384,640]{2,1,0:T(8,128)(2,1)S(1)}, bf16[2,384,640]{2,1,0:T(8,128)(2,1)S(1)}, u32[]{:S(2)}, u32[]{:S(2)}) collective-permute-start(bf16[2,384,640]{2,1,0:T(8,128)(2,1)S(1)} %collective-permute-done.key.value), channel_id=1, source_target_pairs={{0,1},{1,0},{2,3},{3,2},{4,8},{5,9},{6,10},{7,11},{8,4},{9,5},{10,... | collective-permute-start | bytes 2949128 | tf_op jit(solution)/shard_map/ppermute | solution.py:595
  42.0 26.6 %collective-permute-start.11 = (bf16[2,384,640]{2,1,0:T(8,128)(2,1)S(1)}, bf16[2,384,640]{2,1,0:T(8,128)(2,1)S(1)}, u32[]{:S(2)}, u32[]{:S(2)}) collective-permute-start(bf16[2,384,640]{2,1,0:T(8,128)(2,1)S(1)} %collective-permute-done.key.value), channel_id=1, source_target_pairs={{0,4},{1,5},{2,6},{3,7},{4,0},{5,1},{6,2},{7,3},{8,12},{9,13},{10,... | collective-permute-start | bytes 2949128 | tf_op jit(solution)/shard_map/ppermute | solution.py:595
  55.0 28.3 %collective-permute-start.17 = (bf16[2,384,640]{2,1,0:T(8,128)(2,1)S(1)}, bf16[2,384,640]{2,1,0:T(8,128)(2,1)S(1)}, u32[]{:S(2)}, u32[]{:S(2)}) collective-permute-start(bf16[2,384,640]{2,1,0:T(8,128)(2,1)S(1)} %get-tuple-element.55), channel_id=1, source_target_pairs={{0,16},{16,0},{1,17},{17,1},{2,18},{18,2},{3,19},{19,3},{4,20},{20... | collective-permute-start | bytes 2949128 | tf_op jit(solution)/shard_map/ppermute | solution.py:614
  55.7 24.3 %collective-permute-start.15 = (bf16[384,640]{1,0:T(8,128)(2,1)S(1)}, bf16[384,640]{1,0:T(8,128)(2,1)S(1)}, u32[]{:S(2)}, u32[]{:S(2)}) collective-permute-start(bf16[384,640]{1,0:T(8,128)(2,1)S(1)} %get-tuple-element.66), channel_id=1, source_target_pairs={{0,4},{1,5},{2,6},{3,7},{4,0},{5,1},{6,2},{7,3},{8,12},{9,13},{10,... | collective-permute-start | bytes 1474568 | tf_op jit(solution)/shard_map/ppermute | solution.py:595
  66.0 15.7 %collective-permute-start.16 = (bf16[384,640]{1,0:T(8,128)(2,1)S(1)}, bf16[384,640]{1,0:T(8,128)(2,1)S(1)}, u32[]{:S(2)}, u32[]{:S(2)}) collective-permute-start(bf16[384,640]{1,0:T(8,128)(2,1)S(1)} %get-tuple-element.67), channel_id=1, source_target_pairs={{0,1},{1,0},{2,3},{3,2},{4,8},{5,9},{6,10},{7,11},{8,4},{9,5},{10,... | collective-permute-start | bytes 1474568 | tf_op jit(solution)/shard_map/ppermute | solution.py:595
  66.0 22.3 %collective-permute-start.20 = (bf16[2,384,256]{2,1,0:T(8,128)(2,1)S(1)}, bf16[2,384,256]{2,1,0:T(8,128)(2,1)S(1)}, u32[]{:S(2)}, u32[]{:S(2)}) collective-permute-start(bf16[2,384,256]{2,1,0:T(8,128)(2,1)S(1)} %get-tuple-element.73), channel_id=1, source_target_pairs={{0,4},{1,5},{2,6},{3,7},{4,0},{5,1},{6,2},{7,3},{8,12},{9,13},{10,... | collective-permute-start | bytes 1179656 | tf_op jit(solution)/shard_map/ppermute | solution.py:595
  68.7 19.7 %collective-permute-start.21 = (bf16[2,384,256]{2,1,0:T(8,128)(2,1)S(1)}, bf16[2,384,256]{2,1,0:T(8,128)(2,1)S(1)}, u32[]{:S(2)}, u32[]{:S(2)}) collective-permute-start(bf16[2,384,256]{2,1,0:T(8,128)(2,1)S(1)} %get-tuple-element.74), channel_id=1, source_target_pairs={{0,1},{1,0},{2,3},{3,2},{4,8},{5,9},{6,10},{7,11},{8,4},{9,5},{10,... | collective-permute-start | bytes 1179656 | tf_op jit(solution)/shard_map/ppermute | solution.py:595
  80.0 32.1 %collective-permute-start.13 = (bf16[2,384,640]{2,1,0:T(8,128)(2,1)S(1)}, bf16[2,384,640]{2,1,0:T(8,128)(2,1)S(1)}, u32[]{:S(2)}, u32[]{:S(2)}) collective-permute-start(bf16[2,384,640]{2,1,0:T(8,128)(2,1)S(1)} %get-tuple-element.63), channel_id=1, source_target_pairs={{0,4},{1,5},{2,6},{3,7},{4,0},{5,1},{6,2},{7,3},{8,12},{9,13},{10,... | collective-permute-start | bytes 2949128 | tf_op jit(solution)/shard_map/ppermute | solution.py:595
  81.7 30.5 %collective-permute-start.14 = (bf16[2,384,640]{2,1,0:T(8,128)(2,1)S(1)}, bf16[2,384,640]{2,1,0:T(8,128)(2,1)S(1)}, u32[]{:S(2)}, u32[]{:S(2)}) collective-permute-start(bf16[2,384,640]{2,1,0:T(8,128)(2,1)S(1)} %get-tuple-element.64), channel_id=1, source_target_pairs={{0,1},{1,0},{2,3},{3,2},{4,8},{5,9},{6,10},{7,11},{8,4},{9,5},{10,... | collective-permute-start | bytes 2949128 | tf_op jit(solution)/shard_map/ppermute | solution.py:595
  83.3 3.6 %collective-permute-start.18 = (f32[2,128]{1,0:T(2,128)S(1)}, f32[2,128]{1,0:T(2,128)S(1)}, u32[]{:S(2)}, u32[]{:S(2)}) collective-permute-start(f32[2,128]{1,0:T(2,128)S(1)} %slice.12), channel_id=1, source_target_pairs={{0,16},{16,0},{1,17},{17,1},{2,18},{18,2},{3,19},{19,3},{4,20},{20... | collective-permute-start | bytes 3080 | tf_op jit(solution)/shard_map/ppermute | solution.py:614
  86.9 25.3 %collective-permute-start.19 = (bf16[384,896]{1,0:T(8,128)(2,1)S(1)}, bf16[384,896]{1,0:T(8,128)(2,1)S(1)}, u32[]{:S(2)}, u32[]{:S(2)}) collective-permute-start(bf16[384,896]{1,0:T(8,128)(2,1)S(1)} %shard_map.89), channel_id=1, source_target_pairs={{0,16},{16,0},{1,17},{17,1},{2,18},{18,2},{3,19},{19,3},{4,20},{20... | collective-permute-start | bytes 2064392 | tf_op jit(solution)/shard_map/ppermute | solution.py:614
  89.1 23.1 %collective-permute-start.22 = (bf16[2,384,256]{2,1,0:T(8,128)(2,1)S(1)}, bf16[2,384,256]{2,1,0:T(8,128)(2,1)S(1)}, u32[]{:S(2)}, u32[]{:S(2)}) collective-permute-start(bf16[2,384,256]{2,1,0:T(8,128)(2,1)S(1)} %shard_map.90), channel_id=1, source_target_pairs={{0,16},{16,0},{1,17},{17,1},{2,18},{18,2},{3,19},{19,3},{4,20},{20... | collective-permute-start | bytes 1179656 | tf_op jit(solution)/shard_map/ppermute | solution.py:614
  89.7 1.1 collective-permute-start.23
  90.9 3.6 %collective-permute-start.24 = (f32[2,128]{1,0:T(2,128)S(1)}, f32[2,128]{1,0:T(2,128)S(1)}, u32[]{:S(2)}, u32[]{:S(2)}) collective-permute-start(f32[2,128]{1,0:T(2,128)S(1)} %add.24), channel_id=1, source_target_pairs={{0,2},{1,3},{2,0},{3,1},{4,6},{5,7},{6,4},{7,5},{8,10},{9,11},{10,... | collective-permute-start | bytes 3080 | tf_op jit(solution)/shard_map/ppermute | solution.py:622
  94.5 11.8 %collective-permute-start.25 = (f32[2,128]{1,0:T(2,128)S(1)}, f32[2,128]{1,0:T(2,128)S(1)}, u32[]{:S(2)}, u32[]{:S(2)}) collective-permute-start(f32[2,128]{1,0:T(2,128)S(1)} %add.25), channel_id=1, source_target_pairs={{0,4},{4,0},{8,12},{12,8},{1,5},{5,1},{9,13},{13,9},{2,6},{6,2},{1... | collective-permute-start | bytes 3080 | tf_op jit(solution)/shard_map/ppermute | solution.py:622
  106.3 4.5 %collective-permute-start.26 = (f32[2,128]{1,0:T(2,128)S(1)}, f32[2,128]{1,0:T(2,128)S(1)}, u32[]{:S(2)}, u32[]{:S(2)}) collective-permute-start(f32[2,128]{1,0:T(2,128)S(1)} %add.26), channel_id=1, source_target_pairs={{0,8},{4,12},{8,0},{12,4},{1,9},{5,13},{9,1},{13,5},{2,10},{6,14},... | collective-permute-start | bytes 3080 | tf_op jit(solution)/shard_map/ppermute | solution.py:622
  (3 other events, 3.8 us)

commit v15 on v14

--- a/solution.py
+++ b/solution.py
@@ -21,6 +21,7 @@
 PACK_VMEM = 4 * 1024 * 1024
 COST = pl.CostEstimate(flops=1, bytes_accessed=1, transcendentals=0)
 LONG_COST = pl.CostEstimate(flops=2 * 10**10, bytes_accessed=1, transcendentals=0)
+GRAD_COST = pl.CostEstimate(flops=4000000000, bytes_accessed=1, transcendentals=0)
 MAIN_COST = pl.CostEstimate(flops=6 * 10**9, bytes_accessed=1, transcendentals=0)
 
 
@@ -513,7 +514,7 @@
         ],
         input_output_aliases={place + index: index for index in range(len(earlier))},
         compiler_params=pltpu.CompilerParams(vmem_limit_bytes=MAIN_VMEM),
-        cost_estimate=COST,
+        cost_estimate=GRAD_COST,
     )(info, *arrays, pair_even, pair_odd, *sums, *earlier)
 
 
@@ -645,14 +646,13 @@
     sums = None
     for (first, count), told in zip(QUERY_GROUPS, told_pairs):
         sums = sums_call(info, arrays, *told, first, count, key_first, sums, len(fars))
-    received = [exchanged(sums[0], 0), exchanged(sums[1], 1)]
-    received += [
-        paired(value, partners) for value, partners in zip(sums[2:], fars)
-    ]
+    ready = [*sums[:2], *[after(value, *key_pairs) for value in sums[2:]]]
+    received = [exchanged(ready[0], 0), exchanged(ready[1], 1)]
+    received += [paired(value, partners) for value, partners in zip(ready[2:], fars)]
     all_sums = (*sums[:2], *received)
     asked = ask_call(info, after(query, away_pair, sums[0]), grad, away_first, away_count)
     asked = turned(asked, -1)
-    away_sent = after(away_pair, *key_pairs, *received)
+    away_sent = after(away_pair, *received)
     away_pairs = (exchanged(away_sent, 0), exchanged(away_sent, 1))
     gains, parts = [], None
     for (first, count), told in zip(QUERY_GROUPS, told_pairs):
@@ -666,7 +666,7 @@
     answer = (own, exchanged(to_even, 0), exchanged(to_odd, 1))
     operands = [(array, key_first, None) for array in arrays]
     low, own, to_even, to_odd, gain = main_call(
-        after(info, pair_low), operands, *key_pairs, key_count, away_first, key_first
+        after(info, pair_low, asked), operands, *key_pairs, key_count, away_first, key_first
     )
     gains.append(gain[:2])
     key_answer = (own, exchanged(to_even, 0), exchanged(to_odd, 1))
@@ -677,8 +677,8 @@
     returned = (exchanged(to_even, 0), exchanged(to_odd, 1))
     pieces.append(query_low)
     places.append((0, away_first * HEAD_DIM))
+    gains.append(turned(after(gain[:2], pieces[0]), 1))
     low = answer_call(info, query, *answer, low)
-    gains.append(turned(after(gain[:2], low, pieces[0]), 1))
     pieces.append(turned(after(low, gains[-1]), -1))
     places.append((0, 0))
     low = finish_call(after(info, pieces[0]), (key, key_first, None), *key_answer, key_count)

time: 115 us -> 116 us (level)
  starting transfers between devices: 32.3 us -> 36.9 us
  waiting for transfers between devices: 39.1 us -> 35.3 us
    ppermute x6, waiting for transfers between devices: 8.87 us -> 2.89 us  [turned(): lax.ppermute(value, 'pipe', [(i, (i + step) % count) for i in range(count)])]
    ppermute x17, starting transfers between devices: 19.4 us -> 22.8 us  [paired(): return lax.ppermute(value, ('seq', 'dp'), pairs)]
    ppermute x4, waiting for transfers between devices: 13.7 us -> 14.9 us  [total_over(): lax.ppermute(sent, axis, [(i, i ^ step) for i in range(count)])]
where the time goes in v15:
time: 116 us
  Pallas kernels  38.5 us (33%)
  starting transfers between devices  36.9 us (32%)
  waiting for transfers between devices  35.3 us (30%)
  local copies, waits for them, and re-layouts  3.71 us (3%)
    ppermute x17, starting transfers between devices, paired(): return lax.ppermute(value, ('seq', 'dp'), pairs)  22.8 us
    ppermute x17, waiting for transfers between devices, paired(): return lax.ppermute(value, ('seq', 'dp'), pairs)  17.6 us
    pallas_call x2, Pallas kernels, main_call(): pl.pallas_call(main_kernel, grid=(count,), in_specs=[info_block(info)] +...  15.9 us
    ppermute x4, waiting for transfers between devices, total_over(): lax.ppermute(sent, axis, [(i, i ^ step) for i in range(count)])  14.9 us
    pallas_call x2, Pallas kernels, grads_call(): pl.pallas_call(functools.partial(grads_kernel, far_count=far_count), grid...  10.3 us
    ppermute x6, starting transfers between devices, turned(): lax.ppermute(value, 'pipe', [(i, (i + step) % count) for i in range(count)])  8.41 us
    ppermute x4, starting transfers between devices, total_over(): lax.ppermute(sent, axis, [(i, i ^ step) for i in range(count)])  5.68 us
    pallas_call x2, Pallas kernels, sums_call(): pl.pallas_call(functools.partial(sums_kernel, far_count=far_count), grid=...  4.62 us
  transfers between devices with their start and end apart: 27, of which 11 were waited for; matrix products, arithmetic and copies ran while one was open for 1% of the time, Pallas kernels for 31%

profile of v15, /device:TPU:0, one launch (start us, length us, event | category | flops | bytes accessed | tf_op | source)
XLA Modules:
  0.0 115.9 jit_solution(5148676742717269698)
XLA Ops:
  1.9 1.3 %copy-done.3 = bf16[1,1,1,384,1536]{4,3,2,1,0:T(8,128)(2,1)S(1)} copy-done((bf16[1,1,1,384,1536]{4,3,2,1,0:T(8,128)(2,1)S(1)}, bf16[1,1,1,384,1536]{4,3,2,1,0:T(8,128)(2,1)}, u32[]{:S(2)}) %copy-start.3) | copy-done | bytes 1179672
  3.8 4.1 %collective-permute-start.3 = (bf16[2,384,384]{2,1,0:T(8,128)(2,1)S(1)}, bf16[2,384,384]{2,1,0:T(8,128)(2,1)S(1)}, u32[]{:S(2)}, u32[]{:S(2)}) collective-permute-start(bf16[2,384,384]{2,1,0:T(8,128)(2,1)S(1)} %shard_map.77), channel_id=1, source_target_pairs={{0,4},{1,5},{2,6},{3,7},{4,0},{5,1},{6,2},{7,3},{8,12},{9,13},{10,... | collective-permute-start | bytes 1769480 | tf_op jit(solution)/shard_map/ppermute | solution.py:596
  9.4 1.6 %collective-permute-start.1 = (bf16[2,384,256]{2,1,0:T(8,128)(2,1)S(1)}, bf16[2,384,256]{2,1,0:T(8,128)(2,1)S(1)}, u32[]{:S(2)}, u32[]{:S(2)}) collective-permute-start(bf16[2,384,256]{2,1,0:T(8,128)(2,1)S(1)} %shard_map.79), channel_id=1, source_target_pairs={{0,4},{1,5},{2,6},{3,7},{4,0},{5,1},{6,2},{7,3},{8,12},{9,13},{10,... | collective-permute-start | bytes 1179656 | tf_op jit(solution)/shard_map/ppermute | solution.py:596
  11.0 1.5 %collective-permute-start = (bf16[2,384,640]{2,1,0:T(8,128)(2,1)S(1)}, bf16[2,384,640]{2,1,0:T(8,128)(2,1)S(1)}, u32[]{:S(2)}, u32[]{:S(2)}) collective-permute-start(bf16[2,384,640]{2,1,0:T(8,128)(2,1)S(1)} %shard_map.78), channel_id=1, source_target_pairs={{0,16},{16,0},{1,17},{17,1},{2,18},{18,2},{3,19},{19,3},{4,20},{20... | collective-permute-start | bytes 2949128 | tf_op jit(solution)/shard_map/ppermute | solution.py:615
  13.1 9.0 %collective-permute-done.3.pair_even = bf16[2,384,384]{2,1,0:T(8,128)(2,1)S(1)} collective-permute-done((bf16[2,384,384]{2,1,0:T(8,128)(2,1)S(1)}, bf16[2,384,384]{2,1,0:T(8,128)(2,1)S(1)}, u32[]{:S(2)}, u32[]{:S(2)}) %collective-permute-start.3) | collective-permute-done | bytes 589856 | tf_op jit(solution)/shard_map/ppermute | solution.py:596
  22.1 2.5 %collective-permute-start.8 = (bf16[2,384,256]{2,1,0:T(8,128)(2,1)S(1)}, bf16[2,384,256]{2,1,0:T(8,128)(2,1)S(1)}, u32[]{:S(2)}, u32[]{:S(2)}) collective-permute-start(bf16[2,384,256]{2,1,0:T(8,128)(2,1)S(1)} %shard_map.84), channel_id=1, source_target_pairs={{0,4},{1,5},{2,6},{3,7},{4,0},{5,1},{6,2},{7,3},{8,12},{9,13},{10,... | collective-permute-start | bytes 1179656 | tf_op jit(solution)/shard_map/ppermute | solution.py:596
  24.6 2.8 %shard_map.81 = (f32[40,384]{1,0:T(8,128)S(1)}, f32[40,384]{1,0:T(8,128)S(1)}, f32[40,384]{1,0:T(8,128)S(1)}) custom-call(f32[8,128]{1,0:T(8,128)S(1)} %shard_map.80.info, bf16[384,1536]{1,0:T(8,128)(2,1)S(1)} %bitcast.29, bf16[384,1536]{1,0:T(8,128)(2,1)S(1)} %bitcast.21, bf16[384,1536]{1,0:T(8,128)(2,1)S(1)} %bitcast.13, bf16[384,1536]{1,0:T(8,128)(2,1)S(1)} %bitcast.38, ...), custom_call_target="tpu_custom_call" | custom-call | flops 6000000000 | bytes 1 | tf_op jit(solution)/shard_map/pallas_call | solution.py:477
  27.4 3.2 %collective-permute-done.1.pair_even = bf16[2,384,256]{2,1,0:T(8,128)(2,1)S(1)} collective-permute-done((bf16[2,384,256]{2,1,0:T(8,128)(2,1)S(1)}, bf16[2,384,256]{2,1,0:T(8,128)(2,1)S(1)}, u32[]{:S(2)}, u32[]{:S(2)}) %collective-permute-start.1) | collective-permute-done | bytes 393248 | tf_op jit(solution)/shard_map/ppermute | solution.py:596
  30.6 1.9 %shard_map.82 = (f32[40,384]{1,0:T(8,128)S(1)}, f32[40,384]{1,0:T(8,128)S(1)}, f32[40,384]{1,0:T(8,128)S(1)}) custom-call(f32[8,128]{1,0:T(8,128)S(1)} %shard_map.80.info, bf16[384,1536]{1,0:T(8,128)(2,1)S(1)} %bitcast.30, bf16[384,1536]{1,0:T(8,128)(2,1)S(1)} %bitcast.22, ...), custom_call_target="tpu_custom_call", output_to_operand_aliasing={{0}: (7, {}), {1}: (8, {}), {2}: (9, {})} | custom-call | flops 6000000000 | bytes 1 | tf_op jit(solution)/shard_map/pallas_call | solution.py:477
  32.4 1.8 %collective-permute-done.key.value = bf16[2,384,640]{2,1,0:T(8,128)(2,1)S(1)} collective-permute-done((bf16[2,384,640]{2,1,0:T(8,128)(2,1)S(1)}, bf16[2,384,640]{2,1,0:T(8,128)(2,1)S(1)}, u32[]{:S(2)}, u32[]{:S(2)}) %collective-permute-start) | collective-permute-done | bytes 983072 | tf_op jit(solution)/shard_map/ppermute | solution.py:615
  34.4 1.6 %collective-permute-start.5 = (bf16[2,400,640]{2,1,0:T(8,128)(2,1)S(1)}, bf16[2,400,640]{2,1,0:T(8,128)(2,1)S(1)}, u32[]{:S(2)}, u32[]{:S(2)}) collective-permute-start(bf16[2,400,640]{2,1,0:T(8,128)(2,1)S(1)} %shard_map.83), channel_id=1, source_target_pairs={{0,16},{16,0},{1,17},{17,1},{2,18},{18,2},{3,19},{19,3},{4,20},{20... | collective-permute-start | bytes 3072008 | tf_op jit(solution)/shard_map/ppermute | solution.py:615
  37.0 1.5 %collective-permute-done.8.pair_even = bf16[2,384,256]{2,1,0:T(8,128)(2,1)S(1)} collective-permute-done((bf16[2,384,256]{2,1,0:T(8,128)(2,1)S(1)}, bf16[2,384,256]{2,1,0:T(8,128)(2,1)S(1)}, u32[]{:S(2)}, u32[]{:S(2)}) %collective-permute-start.8) | collective-permute-done | bytes 393248 | tf_op jit(solution)/shard_map/ppermute | solution.py:596
  38.5 2.0 %collective-permute-start.10 = (f32[40,384]{1,0:T(8,128)S(1)}, f32[40,384]{1,0:T(8,128)S(1)}, u32[]{:S(2)}, u32[]{:S(2)}) collective-permute-start(f32[40,384]{1,0:T(8,128)S(1)} %get-tuple-element.54), channel_id=1, source_target_pairs={{0,8},{1,9},{2,10},{3,11},{4,12},{5,13},{6,14},{7,15},{8,0},{9,1},... | collective-permute-start | bytes 184328 | tf_op jit(solution)/shard_map/ppermute | solution.py:596
  40.5 3.1 %collective-permute-done.10.rest_0_ = f32[40,384]{1,0:T(8,128)S(1)} collective-permute-done((f32[40,384]{1,0:T(8,128)S(1)}, f32[40,384]{1,0:T(8,128)S(1)}, u32[]{:S(2)}, u32[]{:S(2)}) %collective-permute-start.10) | collective-permute-done | bytes 61472 | tf_op jit(solution)/shard_map/ppermute | solution.py:596
  43.6 2.6 %collective-permute-start.11 = (bf16[2,384,640]{2,1,0:T(8,128)(2,1)S(1)}, bf16[2,384,640]{2,1,0:T(8,128)(2,1)S(1)}, u32[]{:S(2)}, u32[]{:S(2)}) collective-permute-start(bf16[2,384,640]{2,1,0:T(8,128)(2,1)S(1)} %collective-permute-done.key.value), channel_id=1, source_target_pairs={{0,4},{1,5},{2,6},{3,7},{4,0},{5,1},{6,2},{7,3},{8,12},{9,13},{10,... | collective-permute-start | bytes 2949128 | tf_op jit(solution)/shard_map/ppermute | solution.py:596
  46.2 6.1 %shard_map.85 = (bf16[2,384,640]{2,1,0:T(8,128)(2,1)S(1)}, f32[384,640]{1,0:T(8,128)S(1)}, bf16[384,640]{1,0:T(8,128)(2,1)S(1)}, bf16[384,640]{1,0:T(8,128)(2,1)S(1)}, f32[8,128]{1,0:T(8,128)S(1)}) custom-call(f32[8,128]{1,0:T(8,128)S(1)} %shard_map.80.info, bf16[384,1536]{1,0:T(8,128)(2,1)S(1)} %bitcast.32, bf16[384,1536]{1,0:T(8,128)(2,1)S(1)} %bitcast.24, ...), custom_call_target="tpu_custom_call" | custom-call | flops 4000000000 | bytes 1 | tf_op jit(solution)/shard_map/pallas_call | solution.py:497
  52.3 4.1 %shard_map.86 = (bf16[2,384,640]{2,1,0:T(8,128)(2,1)S(1)}, f32[384,640]{1,0:T(8,128)S(1)}, bf16[384,640]{1,0:T(8,128)(2,1)S(1)}, bf16[384,640]{1,0:T(8,128)(2,1)S(1)}, f32[8,128]{1,0:T(8,128)S(1)}) custom-call(f32[8,128]{1,0:T(8,128)S(1)} %shard_map.80.info, ...), custom_call_target="tpu_custom_call", output_to_operand_aliasing={{0}: (12, {}), {1}: (13, {}), {2}: (14, {}), {3}: (15, {})} | custom-call | flops 4000000000 | bytes 1 | tf_op jit(solution)/shard_map/pallas_call | solution.py:497
  57.7 1.5 %collective-permute-start.17 = (bf16[2,384,640]{2,1,0:T(8,128)(2,1)S(1)}, bf16[2,384,640]{2,1,0:T(8,128)(2,1)S(1)}, u32[]{:S(2)}, u32[]{:S(2)}) collective-permute-start(bf16[2,384,640]{2,1,0:T(8,128)(2,1)S(1)} %get-tuple-element.59), channel_id=1, source_target_pairs={{0,16},{16,0},{1,17},{17,1},{2,18},{18,2},{3,19},{19,3},{4,20},{20... | collective-permute-start | bytes 2949128 | tf_op jit(solution)/shard_map/ppermute | solution.py:615
  59.2 4.5 %shard_map.87 = (bf16[384,896]{1,0:T(8,128)(2,1)S(1)}, f32[2,384,256]{2,1,0:T(8,128)S(1)}, bf16[2,384,256]{2,1,0:T(8,128)(2,1)S(1)}, bf16[2,384,256]{2,1,0:T(8,128)(2,1)S(1)}, f32[8,128]{1,0:T(8,128)S(1)}) custom-call(f32[8,128]{1,0:T(8,128)S(1)} %shard_map.80.info, bf16[384,1536]{1,0:T(8,128)(2,1)S(1)} %bitcast.34, bf16[384,1536]{1,0:T(8,128)(2,1)S(1)} %bitcast.26, ...), custom_call_target="tpu_custom_call" | custom-call | flops 6000000000 | bytes 1 | tf_op jit(solution)/shard_map/pallas_call | solution.py:436
  63.7 6.3 %collective-permute-start.20 = (bf16[2,384,256]{2,1,0:T(8,128)(2,1)S(1)}, bf16[2,384,256]{2,1,0:T(8,128)(2,1)S(1)}, u32[]{:S(2)}, u32[]{:S(2)}) collective-permute-start(bf16[2,384,256]{2,1,0:T(8,128)(2,1)S(1)} %get-tuple-element.75), channel_id=1, source_target_pairs={{0,4},{1,5},{2,6},{3,7},{4,0},{5,1},{6,2},{7,3},{8,12},{9,13},{10,... | collective-permute-start | bytes 1179656 | tf_op jit(solution)/shard_map/ppermute | solution.py:596
  70.1 11.3 %shard_map.88 = (bf16[384,640]{1,0:T(8,128)(2,1)S(1)}, f32[2,384,640]{2,1,0:T(8,128)S(1)}, bf16[2,384,640]{2,1,0:T(8,128)(2,1)S(1)}, bf16[2,384,640]{2,1,0:T(8,128)(2,1)S(1)}, f32[8,128]{1,0:T(8,128)S(1)}) custom-call(bf16[2,400,640]{2,1,0:T(8,128)(2,1)S(1)} %collective-permute-done.5.info.query.grad, ...), custom_call_target="tpu_custom_call" | custom-call | flops 6000000000 | bytes 1 | tf_op jit(solution)/shard_map/pallas_call | solution.py:436
  81.4 1.6 %collective-permute-start.18 = (f32[2,128]{1,0:T(2,128)S(1)}, f32[2,128]{1,0:T(2,128)S(1)}, u32[]{:S(2)}, u32[]{:S(2)}) collective-permute-start(f32[2,128]{1,0:T(2,128)S(1)} %slice.12), channel_id=1, source_target_pairs={{0,16},{16,0},{1,17},{17,1},{2,18},{18,2},{3,19},{19,3},{4,20},{20... | collective-permute-start | bytes 3080 | tf_op jit(solution)/shard_map/ppermute | solution.py:615
  83.0 1.9 %collective-permute-start.13 = (bf16[2,384,640]{2,1,0:T(8,128)(2,1)S(1)}, bf16[2,384,640]{2,1,0:T(8,128)(2,1)S(1)}, u32[]{:S(2)}, u32[]{:S(2)}) collective-permute-start(bf16[2,384,640]{2,1,0:T(8,128)(2,1)S(1)} %get-tuple-element.65), channel_id=1, source_target_pairs={{0,4},{1,5},{2,6},{3,7},{4,0},{5,1},{6,2},{7,3},{8,12},{9,13},{10,... | collective-permute-start | bytes 2949128 | tf_op jit(solution)/shard_map/ppermute | solution.py:596
  84.9 1.4 %shard_map.89 = bf16[384,896]{1,0:T(8,128)(2,1)S(1)} custom-call(f32[8,128]{1,0:T(8,128)S(1)} %shard_map.80.info, bf16[384,1536]{1,0:T(8,128)(2,1)S(1)} %bitcast.35, f32[384,640]{1,0:T(8,128)S(1)} %get-tuple-element.67.own, bf16[384,640]{1,0:T(8,128)(2,1)S(1)} %collective-permute-done.15.from_even, ...), custom_call_target="tpu_custom_call", output_to_operand_aliasing={{}: (5, {})} | custom-call | flops 20000000000 | bytes 1 | tf_op jit(solution)/shard_map/pallas_call | solution.py:523
  88.3 1.7 %collective-permute-start.22 = (bf16[2,384,256]{2,1,0:T(8,128)(2,1)S(1)}, bf16[2,384,256]{2,1,0:T(8,128)(2,1)S(1)}, u32[]{:S(2)}, u32[]{:S(2)}) collective-permute-start(bf16[2,384,256]{2,1,0:T(8,128)(2,1)S(1)} %shard_map.90), channel_id=1, source_target_pairs={{0,16},{16,0},{1,17},{17,1},{2,18},{18,2},{3,19},{19,3},{4,20},{20... | collective-permute-start | bytes 1179656 | tf_op jit(solution)/shard_map/ppermute | solution.py:615
  91.2 1.5 %collective-permute-start.24 = (f32[2,128]{1,0:T(2,128)S(1)}, f32[2,128]{1,0:T(2,128)S(1)}, u32[]{:S(2)}, u32[]{:S(2)}) collective-permute-start(f32[2,128]{1,0:T(2,128)S(1)} %add.24), channel_id=1, source_target_pairs={{0,2},{1,3},{2,0},{3,1},{4,6},{5,7},{6,4},{7,5},{8,10},{9,11},{10,... | collective-permute-start | bytes 3080 | tf_op jit(solution)/shard_map/ppermute | solution.py:623
  92.7 2.0 %collective-permute-done.24 = f32[2,128]{1,0:T(2,128)S(1)} collective-permute-done((f32[2,128]{1,0:T(2,128)S(1)}, f32[2,128]{1,0:T(2,128)S(1)}, u32[]{:S(2)}, u32[]{:S(2)}) %collective-permute-start.24) | collective-permute-done | bytes 1056 | tf_op jit(solution)/shard_map/ppermute | solution.py:623
  96.0 1.8 %shard_map.91.rest_2_ = bf16[3,384,1536]{2,1,0:T(8,128)(2,1)} custom-call(bf16[2,384,640]{2,1,0:T(8,128)(2,1)S(1)} %collective-permute-done.17.refs_0_, bf16[384,640]{1,0:T(8,128)(2,1)S(1)} %get-tuple-element.77.refs_1_), custom_call_target="tpu_custom_call" | custom-call | flops 1 | bytes 1 | tf_op jit(solution)/shard_map/pallas_call | solution.py:540
  97.7 10.1 %collective-permute-done.25 = f32[2,128]{1,0:T(2,128)S(1)} collective-permute-done((f32[2,128]{1,0:T(2,128)S(1)}, f32[2,128]{1,0:T(2,128)S(1)}, u32[]{:S(2)}, u32[]{:S(2)}) %collective-permute-start.25) | collective-permute-done | bytes 1056 | tf_op jit(solution)/shard_map/ppermute | solution.py:623
  107.9 3.0 %collective-permute-start.26 = (f32[2,128]{1,0:T(2,128)S(1)}, f32[2,128]{1,0:T(2,128)S(1)}, u32[]{:S(2)}, u32[]{:S(2)}) collective-permute-start(f32[2,128]{1,0:T(2,128)S(1)} %add.26), channel_id=1, source_target_pairs={{0,8},{4,12},{8,0},{12,4},{1,9},{5,13},{9,1},{13,5},{2,10},{6,14},... | collective-permute-start | bytes 3080 | tf_op jit(solution)/shard_map/ppermute | solution.py:623
  110.8 1.5 %collective-permute-done.26 = f32[2,128]{1,0:T(2,128)S(1)} collective-permute-done((f32[2,128]{1,0:T(2,128)S(1)}, f32[2,128]{1,0:T(2,128)S(1)}, u32[]{:S(2)}, u32[]{:S(2)}) %collective-permute-start.26) | collective-permute-done | bytes 1056 | tf_op jit(solution)/shard_map/ppermute | solution.py:623
  113.0 2.9 %shard_map.92 = bf16[3,384,1536]{2,1,0:T(8,128)(2,1)} custom-call(bf16[2,400,640]{2,1,0:T(8,128)(2,1)S(1)} %collective-permute-done.5.info.query.grad, bf16[2,384,640]{2,1,0:T(8,128)(2,1)S(1)} %collective-permute-done.key.value, f32[2,384,640]{2,1,0:T(8,128)S(1)} %get-tuple-element.64.own, ...), custom_call_target="tpu_custom_call", output_to_operand_aliasing={{}: (7, {})} | custom-call | flops 1 | bytes 1 | tf_op jit(solution)/shard_map/pallas_call | solution.py:559
  (60 shorter events, 11.2 us)
Async XLA Ops:
  3.2 4.8 %copy-start = (bf16[1,1,1,384,1536]{4,3,2,1,0:T(8,128)(2,1)S(1)}, bf16[1,1,1,384,1536]{4,3,2,1,0:T(8,128)(2,1)}, u32[]{:S(2)}) copy-start(bf16[1,1,1,384,1536]{4,3,2,1,0:T(8,128)(2,1)} %param.7) | copy-start | bytes 3538948
  3.2 4.8 %copy-start.5 = (bf16[1,1,1,384,1536]{4,3,2,1,0:T(8,128)(2,1)S(1)}, bf16[1,1,1,384,1536]{4,3,2,1,0:T(8,128)(2,1)}, u32[]{:S(2)}) copy-start(bf16[1,1,1,384,1536]{4,3,2,1,0:T(8,128)(2,1)} %param.8) | copy-start | bytes 3538948
  3.3 9.9 %collective-permute-start.4 = (bf16[2,384,384]{2,1,0:T(8,128)(2,1)S(1)}, bf16[2,384,384]{2,1,0:T(8,128)(2,1)S(1)}, u32[]{:S(2)}, u32[]{:S(2)}) collective-permute-start(bf16[2,384,384]{2,1,0:T(8,128)(2,1)S(1)} %shard_map.77), channel_id=1, source_target_pairs={{0,1},{1,0},{2,3},{3,2},{4,8},{5,9},{6,10},{7,11},{8,4},{9,5},{10,... | collective-permute-start | bytes 1769480 | tf_op jit(solution)/shard_map/ppermute | solution.py:596
  3.8 18.3 %collective-permute-start.3 = (bf16[2,384,384]{2,1,0:T(8,128)(2,1)S(1)}, bf16[2,384,384]{2,1,0:T(8,128)(2,1)S(1)}, u32[]{:S(2)}, u32[]{:S(2)}) collective-permute-start(bf16[2,384,384]{2,1,0:T(8,128)(2,1)S(1)} %shard_map.77), channel_id=1, source_target_pairs={{0,4},{1,5},{2,6},{3,7},{4,0},{5,1},{6,2},{7,3},{8,12},{9,13},{10,... | collective-permute-start | bytes 1769480 | tf_op jit(solution)/shard_map/ppermute | solution.py:596
  9.2 3.3 %copy-start.6 = (f32[1,2,128]{2,1,0:T(2,128)S(1)}, f32[1,2,128]{2,1,0:T(2,128)}, u32[]{:S(2)}) copy-start(f32[1,2,128]{2,1,0:T(2,128)} %param.10) | copy-start | bytes 3076
  9.2 3.3 %copy-start.7 = (s32[1,1,1,3]{3,2,1,0:T(1,128)S(1)}, s32[1,1,1,3]{3,2,1,0:T(1,128)}, u32[]{:S(2)}) copy-start(s32[1,1,1,3]{3,2,1,0:T(1,128)} %param.11) | copy-start | bytes 40
  9.3 18.1 %collective-permute-start.2 = (bf16[2,384,256]{2,1,0:T(8,128)(2,1)S(1)}, bf16[2,384,256]{2,1,0:T(8,128)(2,1)S(1)}, u32[]{:S(2)}, u32[]{:S(2)}) collective-permute-start(bf16[2,384,256]{2,1,0:T(8,128)(2,1)S(1)} %shard_map.79), channel_id=1, source_target_pairs={{0,1},{1,0},{2,3},{3,2},{4,8},{5,9},{6,10},{7,11},{8,4},{9,5},{10,... | collective-permute-start | bytes 1179656 | tf_op jit(solution)/shard_map/ppermute | solution.py:596
  9.4 21.2 %collective-permute-start.1 = (bf16[2,384,256]{2,1,0:T(8,128)(2,1)S(1)}, bf16[2,384,256]{2,1,0:T(8,128)(2,1)S(1)}, u32[]{:S(2)}, u32[]{:S(2)}) collective-permute-start(bf16[2,384,256]{2,1,0:T(8,128)(2,1)S(1)} %shard_map.79), channel_id=1, source_target_pairs={{0,4},{1,5},{2,6},{3,7},{4,0},{5,1},{6,2},{7,3},{8,12},{9,13},{10,... | collective-permute-start | bytes 1179656 | tf_op jit(solution)/shard_map/ppermute | solution.py:596
  11.0 23.3 %collective-permute-start = (bf16[2,384,640]{2,1,0:T(8,128)(2,1)S(1)}, bf16[2,384,640]{2,1,0:T(8,128)(2,1)S(1)}, u32[]{:S(2)}, u32[]{:S(2)}) collective-permute-start(bf16[2,384,640]{2,1,0:T(8,128)(2,1)S(1)} %shard_map.78), channel_id=1, source_target_pairs={{0,16},{16,0},{1,17},{17,1},{2,18},{18,2},{3,19},{19,3},{4,20},{20... | collective-permute-start | bytes 2949128 | tf_op jit(solution)/shard_map/ppermute | solution.py:615
  13.1 11.5 %copy-start.4 = (bf16[1,1,1,384,1536]{4,3,2,1,0:T(8,128)(2,1)S(1)}, bf16[1,1,1,384,1536]{4,3,2,1,0:T(8,128)(2,1)}, u32[]{:S(2)}) copy-start(bf16[1,1,1,384,1536]{4,3,2,1,0:T(8,128)(2,1)} %param.6) | copy-start | bytes 3538948
  22.1 14.8 %collective-permute-start.9 = (bf16[2,384,256]{2,1,0:T(8,128)(2,1)S(1)}, bf16[2,384,256]{2,1,0:T(8,128)(2,1)S(1)}, u32[]{:S(2)}, u32[]{:S(2)}) collective-permute-start(bf16[2,384,256]{2,1,0:T(8,128)(2,1)S(1)} %shard_map.84), channel_id=1, source_target_pairs={{0,1},{1,0},{2,3},{3,2},{4,8},{5,9},{6,10},{7,11},{8,4},{9,5},{10,... | collective-permute-start | bytes 1179656 | tf_op jit(solution)/shard_map/ppermute | solution.py:596
  22.1 16.4 %collective-permute-start.8 = (bf16[2,384,256]{2,1,0:T(8,128)(2,1)S(1)}, bf16[2,384,256]{2,1,0:T(8,128)(2,1)S(1)}, u32[]{:S(2)}, u32[]{:S(2)}) collective-permute-start(bf16[2,384,256]{2,1,0:T(8,128)(2,1)S(1)} %shard_map.84), channel_id=1, source_target_pairs={{0,4},{1,5},{2,6},{3,7},{4,0},{5,1},{6,2},{7,3},{8,12},{9,13},{10,... | collective-permute-start | bytes 1179656 | tf_op jit(solution)/shard_map/ppermute | solution.py:596
  34.4 23.3 %collective-permute-start.5 = (bf16[2,400,640]{2,1,0:T(8,128)(2,1)S(1)}, bf16[2,400,640]{2,1,0:T(8,128)(2,1)S(1)}, u32[]{:S(2)}, u32[]{:S(2)}) collective-permute-start(bf16[2,400,640]{2,1,0:T(8,128)(2,1)S(1)} %shard_map.83), channel_id=1, source_target_pairs={{0,16},{16,0},{1,17},{17,1},{2,18},{18,2},{3,19},{19,3},{4,20},{20... | collective-permute-start | bytes 3072008 | tf_op jit(solution)/shard_map/ppermute | solution.py:615
  35.9 4.5 %collective-permute-start.6 = (f32[40,384]{1,0:T(8,128)S(1)}, f32[40,384]{1,0:T(8,128)S(1)}, u32[]{:S(2)}, u32[]{:S(2)}) collective-permute-start(f32[40,384]{1,0:T(8,128)S(1)} %get-tuple-element.48.sent_even), channel_id=1, source_target_pairs={{0,4},{1,5},{2,6},{3,7},{4,0},{5,1},{6,2},{7,3},{8,12},{9,13},{10,... | collective-permute-start | bytes 184328 | tf_op jit(solution)/shard_map/ppermute | solution.py:596
  37.0 3.5 %collective-permute-start.7 = (f32[40,384]{1,0:T(8,128)S(1)}, f32[40,384]{1,0:T(8,128)S(1)}, u32[]{:S(2)}, u32[]{:S(2)}) collective-permute-start(f32[40,384]{1,0:T(8,128)S(1)} %get-tuple-element.50.sent_odd), channel_id=1, source_target_pairs={{0,1},{1,0},{2,3},{3,2},{4,8},{5,9},{6,10},{7,11},{8,4},{9,5},{10,... | collective-permute-start | bytes 184328 | tf_op jit(solution)/shard_map/ppermute | solution.py:596
  38.5 5.1 %collective-permute-start.10 = (f32[40,384]{1,0:T(8,128)S(1)}, f32[40,384]{1,0:T(8,128)S(1)}, u32[]{:S(2)}, u32[]{:S(2)}) collective-permute-start(f32[40,384]{1,0:T(8,128)S(1)} %get-tuple-element.54), channel_id=1, source_target_pairs={{0,8},{1,9},{2,10},{3,11},{4,12},{5,13},{6,14},{7,15},{8,0},{9,1},... | collective-permute-start | bytes 184328 | tf_op jit(solution)/shard_map/ppermute | solution.py:596
  43.6 20.1 %collective-permute-start.12 = (bf16[2,384,640]{2,1,0:T(8,128)(2,1)S(1)}, bf16[2,384,640]{2,1,0:T(8,128)(2,1)S(1)}, u32[]{:S(2)}, u32[]{:S(2)}) collective-permute-start(bf16[2,384,640]{2,1,0:T(8,128)(2,1)S(1)} %collective-permute-done.key.value), channel_id=1, source_target_pairs={{0,1},{1,0},{2,3},{3,2},{4,8},{5,9},{6,10},{7,11},{8,4},{9,5},{10,... | collective-permute-start | bytes 2949128 | tf_op jit(solution)/shard_map/ppermute | solution.py:596
  43.6 26.4 %collective-permute-start.11 = (bf16[2,384,640]{2,1,0:T(8,128)(2,1)S(1)}, bf16[2,384,640]{2,1,0:T(8,128)(2,1)S(1)}, u32[]{:S(2)}, u32[]{:S(2)}) collective-permute-start(bf16[2,384,640]{2,1,0:T(8,128)(2,1)S(1)} %collective-permute-done.key.value), channel_id=1, source_target_pairs={{0,4},{1,5},{2,6},{3,7},{4,0},{5,1},{6,2},{7,3},{8,12},{9,13},{10,... | collective-permute-start | bytes 2949128 | tf_op jit(solution)/shard_map/ppermute | solution.py:596
  56.5 26.5 %collective-permute-start.15 = (bf16[384,640]{1,0:T(8,128)(2,1)S(1)}, bf16[384,640]{1,0:T(8,128)(2,1)S(1)}, u32[]{:S(2)}, u32[]{:S(2)}) collective-permute-start(bf16[384,640]{1,0:T(8,128)(2,1)S(1)} %get-tuple-element.68), channel_id=1, source_target_pairs={{0,4},{1,5},{2,6},{3,7},{4,0},{5,1},{6,2},{7,3},{8,12},{9,13},{10,... | collective-permute-start | bytes 1474568 | tf_op jit(solution)/shard_map/ppermute | solution.py:596
  56.6 28.4 %collective-permute-start.16 = (bf16[384,640]{1,0:T(8,128)(2,1)S(1)}, bf16[384,640]{1,0:T(8,128)(2,1)S(1)}, u32[]{:S(2)}, u32[]{:S(2)}) collective-permute-start(bf16[384,640]{1,0:T(8,128)(2,1)S(1)} %get-tuple-element.69), channel_id=1, source_target_pairs={{0,1},{1,0},{2,3},{3,2},{4,8},{5,9},{6,10},{7,11},{8,4},{9,5},{10,... | collective-permute-start | bytes 1474568 | tf_op jit(solution)/shard_map/ppermute | solution.py:596
  57.7 23.7 %collective-permute-start.17 = (bf16[2,384,640]{2,1,0:T(8,128)(2,1)S(1)}, bf16[2,384,640]{2,1,0:T(8,128)(2,1)S(1)}, u32[]{:S(2)}, u32[]{:S(2)}) collective-permute-start(bf16[2,384,640]{2,1,0:T(8,128)(2,1)S(1)} %get-tuple-element.59), channel_id=1, source_target_pairs={{0,16},{16,0},{1,17},{17,1},{2,18},{18,2},{3,19},{19,3},{4,20},{20... | collective-permute-start | bytes 2949128 | tf_op jit(solution)/shard_map/ppermute | solution.py:615
  63.7 23.9 %collective-permute-start.20 = (bf16[2,384,256]{2,1,0:T(8,128)(2,1)S(1)}, bf16[2,384,256]{2,1,0:T(8,128)(2,1)S(1)}, u32[]{:S(2)}, u32[]{:S(2)}) collective-permute-start(bf16[2,384,256]{2,1,0:T(8,128)(2,1)S(1)} %get-tuple-element.75), channel_id=1, source_target_pairs={{0,4},{1,5},{2,6},{3,7},{4,0},{5,1},{6,2},{7,3},{8,12},{9,13},{10,... | collective-permute-start | bytes 1179656 | tf_op jit(solution)/shard_map/ppermute | solution.py:596
  70.1 17.6 %collective-permute-start.21 = (bf16[2,384,256]{2,1,0:T(8,128)(2,1)S(1)}, bf16[2,384,256]{2,1,0:T(8,128)(2,1)S(1)}, u32[]{:S(2)}, u32[]{:S(2)}) collective-permute-start(bf16[2,384,256]{2,1,0:T(8,128)(2,1)S(1)} %get-tuple-element.76), channel_id=1, source_target_pairs={{0,1},{1,0},{2,3},{3,2},{4,8},{5,9},{6,10},{7,11},{8,4},{9,5},{10,... | collective-permute-start | bytes 1179656 | tf_op jit(solution)/shard_map/ppermute | solution.py:596
  81.4 4.9 %collective-permute-start.18 = (f32[2,128]{1,0:T(2,128)S(1)}, f32[2,128]{1,0:T(2,128)S(1)}, u32[]{:S(2)}, u32[]{:S(2)}) collective-permute-start(f32[2,128]{1,0:T(2,128)S(1)} %slice.12), channel_id=1, source_target_pairs={{0,16},{16,0},{1,17},{17,1},{2,18},{18,2},{3,19},{19,3},{4,20},{20... | collective-permute-start | bytes 3080 | tf_op jit(solution)/shard_map/ppermute | solution.py:615
  83.0 30.0 %collective-permute-start.13 = (bf16[2,384,640]{2,1,0:T(8,128)(2,1)S(1)}, bf16[2,384,640]{2,1,0:T(8,128)(2,1)S(1)}, u32[]{:S(2)}, u32[]{:S(2)}) collective-permute-start(bf16[2,384,640]{2,1,0:T(8,128)(2,1)S(1)} %get-tuple-element.65), channel_id=1, source_target_pairs={{0,4},{1,5},{2,6},{3,7},{4,0},{5,1},{6,2},{7,3},{8,12},{9,13},{10,... | collective-permute-start | bytes 2949128 | tf_op jit(solution)/shard_map/ppermute | solution.py:596
  84.9 28.0 %collective-permute-start.14 = (bf16[2,384,640]{2,1,0:T(8,128)(2,1)S(1)}, bf16[2,384,640]{2,1,0:T(8,128)(2,1)S(1)}, u32[]{:S(2)}, u32[]{:S(2)}) collective-permute-start(bf16[2,384,640]{2,1,0:T(8,128)(2,1)S(1)} %get-tuple-element.66), channel_id=1, source_target_pairs={{0,1},{1,0},{2,3},{3,2},{4,8},{5,9},{6,10},{7,11},{8,4},{9,5},{10,... | collective-permute-start | bytes 2949128 | tf_op jit(solution)/shard_map/ppermute | solution.py:596
  86.3 26.6 %collective-permute-start.19 = (bf16[384,896]{1,0:T(8,128)(2,1)S(1)}, bf16[384,896]{1,0:T(8,128)(2,1)S(1)}, u32[]{:S(2)}, u32[]{:S(2)}) collective-permute-start(bf16[384,896]{1,0:T(8,128)(2,1)S(1)} %shard_map.89), channel_id=1, source_target_pairs={{0,16},{16,0},{1,17},{17,1},{2,18},{18,2},{3,19},{19,3},{4,20},{20... | collective-permute-start | bytes 2064392 | tf_op jit(solution)/shard_map/ppermute | solution.py:615
  88.3 24.6 %collective-permute-start.22 = (bf16[2,384,256]{2,1,0:T(8,128)(2,1)S(1)}, bf16[2,384,256]{2,1,0:T(8,128)(2,1)S(1)}, u32[]{:S(2)}, u32[]{:S(2)}) collective-permute-start(bf16[2,384,256]{2,1,0:T(8,128)(2,1)S(1)} %shard_map.90), channel_id=1, source_target_pairs={{0,16},{16,0},{1,17},{17,1},{2,18},{18,2},{3,19},{19,3},{4,20},{20... | collective-permute-start | bytes 1179656 | tf_op jit(solution)/shard_map/ppermute | solution.py:615
  90.1 1.1 collective-permute-start.23
  91.2 3.6 %collective-permute-start.24 = (f32[2,128]{1,0:T(2,128)S(1)}, f32[2,128]{1,0:T(2,128)S(1)}, u32[]{:S(2)}, u32[]{:S(2)}) collective-permute-start(f32[2,128]{1,0:T(2,128)S(1)} %add.24), channel_id=1, source_target_pairs={{0,2},{1,3},{2,0},{3,1},{4,6},{5,7},{6,4},{7,5},{8,10},{9,11},{10,... | collective-permute-start | bytes 3080 | tf_op jit(solution)/shard_map/ppermute | solution.py:623
  94.8 13.1 %collective-permute-start.25 = (f32[2,128]{1,0:T(2,128)S(1)}, f32[2,128]{1,0:T(2,128)S(1)}, u32[]{:S(2)}, u32[]{:S(2)}) collective-permute-start(f32[2,128]{1,0:T(2,128)S(1)} %add.25), channel_id=1, source_target_pairs={{0,4},{4,0},{8,12},{12,8},{1,5},{5,1},{9,13},{13,9},{2,6},{6,2},{1... | collective-permute-start | bytes 3080 | tf_op jit(solution)/shard_map/ppermute | solution.py:623
  107.9 4.5 %collective-permute-start.26 = (f32[2,128]{1,0:T(2,128)S(1)}, f32[2,128]{1,0:T(2,128)S(1)}, u32[]{:S(2)}, u32[]{:S(2)}) collective-permute-start(f32[2,128]{1,0:T(2,128)S(1)} %add.26), channel_id=1, source_target_pairs={{0,8},{4,12},{8,0},{12,4},{1,9},{5,13},{9,1},{13,5},{2,10},{6,14},... | collective-permute-start | bytes 3080 | tf_op jit(solution)/shard_map/ppermute | solution.py:623
  (3 other events, 3.8 us)

commit v16 on v14

--- a/solution.py
+++ b/solution.py
@@ -281,8 +281,8 @@
     told = told_info(info) if len(info.shape) == 3 else info[...]
     key_gain = told[1:2]
     key_floats, key_scale, _, _ = normalize(key[...], key_gain)
-    key_grad = own[0] + from_even[0].astype(jnp.float32) + from_odd[0].astype(jnp.float32)
-    value_grad = own[1] + from_even[1].astype(jnp.float32) + from_odd[1].astype(jnp.float32)
+    key_grad = own[0].astype(jnp.float32) + from_even[0].astype(jnp.float32) + from_odd[0].astype(jnp.float32)
+    value_grad = own[1].astype(jnp.float32) + from_even[1].astype(jnp.float32) + from_odd[1].astype(jnp.float32)
     return norm_back(key_grad, key_floats, key_scale, key_gain), value_grad
 
 
@@ -441,7 +441,7 @@
         out_specs=[head_block(rows, place)] + [pair_block(rows)] * 3 + [whole_block((8, HEAD_DIM))],
         out_shape=[
             jax.ShapeDtypeStruct((rows, heads * HEAD_DIM), jnp.bfloat16),
-            jax.ShapeDtypeStruct((2, rows, lanes), jnp.float32),
+            jax.ShapeDtypeStruct((2, rows, lanes), jnp.bfloat16),
             jax.ShapeDtypeStruct((2, rows, lanes), jnp.bfloat16),
             jax.ShapeDtypeStruct((2, rows, lanes), jnp.bfloat16),
             jax.ShapeDtypeStruct((8, HEAD_DIM), jnp.float32),

time: 115 us -> 115 us (level)
  no operation moved by 1% of the time
where the time goes in v16:
time: 115 us
  waiting for transfers between devices  39 us (34%)
  Pallas kernels  38.7 us (34%)
  starting transfers between devices  32.4 us (28%)
  local copies, waits for them, and re-layouts  3.71 us (3%)
    ppermute x17, starting transfers between devices, paired(): return lax.ppermute(value, ('seq', 'dp'), pairs)  19.4 us
    ppermute x17, waiting for transfers between devices, paired(): return lax.ppermute(value, ('seq', 'dp'), pairs)  16.5 us
    pallas_call x2, Pallas kernels, main_call(): pl.pallas_call(main_kernel, grid=(count,), in_specs=[info_block(info)] +...  15.9 us
    ppermute x4, waiting for transfers between devices, total_over(): lax.ppermute(sent, axis, [(i, i ^ step) for i in range(count)])  13.7 us
    pallas_call x2, Pallas kernels, grads_call(): pl.pallas_call(functools.partial(grads_kernel, far_count=far_count), grid...  10.3 us
    ppermute x6, waiting for transfers between devices, turned(): lax.ppermute(value, 'pipe', [(i, (i + step) % count) for i in range(count)])  8.86 us
    ppermute x6, starting transfers between devices, turned(): lax.ppermute(value, 'pipe', [(i, (i + step) % count) for i in range(count)])  7.31 us
    ppermute x4, starting transfers between devices, total_over(): lax.ppermute(sent, axis, [(i, i ^ step) for i in range(count)])  5.6 us
  transfers between devices with their start and end apart: 27, of which 11 were waited for; matrix products, arithmetic and copies ran while one was open for 1% of the time, Pallas kernels for 31%

profile of v16, /device:TPU:0, one launch (start us, length us, event | category | flops | bytes accessed | tf_op | source)
XLA Modules:
  0.0 115.3 jit_solution(9975354446749294172)
XLA Ops:
  3.8 4.1 %collective-permute-start.3 = (bf16[2,384,384]{2,1,0:T(8,128)(2,1)S(1)}, bf16[2,384,384]{2,1,0:T(8,128)(2,1)S(1)}, u32[]{:S(2)}, u32[]{:S(2)}) collective-permute-start(bf16[2,384,384]{2,1,0:T(8,128)(2,1)S(1)} %shard_map.77), channel_id=1, source_target_pairs={{0,4},{1,5},{2,6},{3,7},{4,0},{5,1},{6,2},{7,3},{8,12},{9,13},{10,... | collective-permute-start | bytes 1769480 | tf_op jit(solution)/shard_map/ppermute | solution.py:595
  9.4 1.6 %collective-permute-start.1 = (bf16[2,384,256]{2,1,0:T(8,128)(2,1)S(1)}, bf16[2,384,256]{2,1,0:T(8,128)(2,1)S(1)}, u32[]{:S(2)}, u32[]{:S(2)}) collective-permute-start(bf16[2,384,256]{2,1,0:T(8,128)(2,1)S(1)} %shard_map.79), channel_id=1, source_target_pairs={{0,4},{1,5},{2,6},{3,7},{4,0},{5,1},{6,2},{7,3},{8,12},{9,13},{10,... | collective-permute-start | bytes 1179656 | tf_op jit(solution)/shard_map/ppermute | solution.py:595
  11.0 1.5 %collective-permute-start = (bf16[2,384,640]{2,1,0:T(8,128)(2,1)S(1)}, bf16[2,384,640]{2,1,0:T(8,128)(2,1)S(1)}, u32[]{:S(2)}, u32[]{:S(2)}) collective-permute-start(bf16[2,384,640]{2,1,0:T(8,128)(2,1)S(1)} %shard_map.78), channel_id=1, source_target_pairs={{0,16},{16,0},{1,17},{17,1},{2,18},{18,2},{3,19},{19,3},{4,20},{20... | collective-permute-start | bytes 2949128 | tf_op jit(solution)/shard_map/ppermute | solution.py:614
  13.1 9.0 %collective-permute-done.3.pair_even = bf16[2,384,384]{2,1,0:T(8,128)(2,1)S(1)} collective-permute-done((bf16[2,384,384]{2,1,0:T(8,128)(2,1)S(1)}, bf16[2,384,384]{2,1,0:T(8,128)(2,1)S(1)}, u32[]{:S(2)}, u32[]{:S(2)}) %collective-permute-start.3) | collective-permute-done | bytes 589856 | tf_op jit(solution)/shard_map/ppermute | solution.py:595
  22.1 2.5 %collective-permute-start.9 = (bf16[2,384,256]{2,1,0:T(8,128)(2,1)S(1)}, bf16[2,384,256]{2,1,0:T(8,128)(2,1)S(1)}, u32[]{:S(2)}, u32[]{:S(2)}) collective-permute-start(bf16[2,384,256]{2,1,0:T(8,128)(2,1)S(1)} %shard_map.86), channel_id=1, source_target_pairs={{0,4},{1,5},{2,6},{3,7},{4,0},{5,1},{6,2},{7,3},{8,12},{9,13},{10,... | collective-permute-start | bytes 1179656 | tf_op jit(solution)/shard_map/ppermute | solution.py:595
  24.6 2.8 %shard_map.81 = (f32[40,384]{1,0:T(8,128)S(1)}, f32[40,384]{1,0:T(8,128)S(1)}, f32[40,384]{1,0:T(8,128)S(1)}) custom-call(f32[8,128]{1,0:T(8,128)S(1)} %shard_map.80.info, bf16[384,1536]{1,0:T(8,128)(2,1)S(1)} %bitcast.29, bf16[384,1536]{1,0:T(8,128)(2,1)S(1)} %bitcast.21, bf16[384,1536]{1,0:T(8,128)(2,1)S(1)} %bitcast.13, bf16[384,1536]{1,0:T(8,128)(2,1)S(1)} %bitcast.38, ...), custom_call_target="tpu_custom_call" | custom-call | flops 6000000000 | bytes 1 | tf_op jit(solution)/shard_map/pallas_call | solution.py:476
  27.4 3.2 %collective-permute-done.1.pair_even = bf16[2,384,256]{2,1,0:T(8,128)(2,1)S(1)} collective-permute-done((bf16[2,384,256]{2,1,0:T(8,128)(2,1)S(1)}, bf16[2,384,256]{2,1,0:T(8,128)(2,1)S(1)}, u32[]{:S(2)}, u32[]{:S(2)}) %collective-permute-start.1) | collective-permute-done | bytes 393248 | tf_op jit(solution)/shard_map/ppermute | solution.py:595
  30.6 1.9 %shard_map.82 = (f32[40,384]{1,0:T(8,128)S(1)}, f32[40,384]{1,0:T(8,128)S(1)}, f32[40,384]{1,0:T(8,128)S(1)}) custom-call(f32[8,128]{1,0:T(8,128)S(1)} %shard_map.80.info, bf16[384,1536]{1,0:T(8,128)(2,1)S(1)} %bitcast.30, bf16[384,1536]{1,0:T(8,128)(2,1)S(1)} %bitcast.22, ...), custom_call_target="tpu_custom_call", output_to_operand_aliasing={{0}: (7, {}), {1}: (8, {}), {2}: (9, {})} | custom-call | flops 6000000000 | bytes 1 | tf_op jit(solution)/shard_map/pallas_call | solution.py:476
  32.4 2.0 %collective-permute-start.8 = (f32[40,384]{1,0:T(8,128)S(1)}, f32[40,384]{1,0:T(8,128)S(1)}, u32[]{:S(2)}, u32[]{:S(2)}) collective-permute-start(f32[40,384]{1,0:T(8,128)S(1)} %get-tuple-element.50), channel_id=1, source_target_pairs={{0,8},{1,9},{2,10},{3,11},{4,12},{5,13},{6,14},{7,15},{8,0},{9,1},... | collective-permute-start | bytes 184328 | tf_op jit(solution)/shard_map/ppermute | solution.py:595
  34.4 1.6 %collective-permute-start.6 = (f32[40,384]{1,0:T(8,128)S(1)}, f32[40,384]{1,0:T(8,128)S(1)}, u32[]{:S(2)}, u32[]{:S(2)}) collective-permute-start(f32[40,384]{1,0:T(8,128)S(1)} %get-tuple-element.47.sent_even), channel_id=1, source_target_pairs={{0,4},{1,5},{2,6},{3,7},{4,0},{5,1},{6,2},{7,3},{8,12},{9,13},{10,... | collective-permute-start | bytes 184328 | tf_op jit(solution)/shard_map/ppermute | solution.py:595
  36.1 4.3 %collective-permute-done.8.rest_0_ = f32[40,384]{1,0:T(8,128)S(1)} collective-permute-done((f32[40,384]{1,0:T(8,128)S(1)}, f32[40,384]{1,0:T(8,128)S(1)}, u32[]{:S(2)}, u32[]{:S(2)}) %collective-permute-start.8) | collective-permute-done | bytes 61472 | tf_op jit(solution)/shard_map/ppermute | solution.py:595
  40.5 1.5 %collective-permute-start.5 = (bf16[2,400,640]{2,1,0:T(8,128)(2,1)S(1)}, bf16[2,400,640]{2,1,0:T(8,128)(2,1)S(1)}, u32[]{:S(2)}, u32[]{:S(2)}) collective-permute-start(bf16[2,400,640]{2,1,0:T(8,128)(2,1)S(1)} %shard_map.83), channel_id=1, source_target_pairs={{0,16},{16,0},{1,17},{17,1},{2,18},{18,2},{3,19},{19,3},{4,20},{20... | collective-permute-start | bytes 3072008 | tf_op jit(solution)/shard_map/ppermute | solution.py:614
  42.0 2.6 %collective-permute-start.11 = (bf16[2,384,640]{2,1,0:T(8,128)(2,1)S(1)}, bf16[2,384,640]{2,1,0:T(8,128)(2,1)S(1)}, u32[]{:S(2)}, u32[]{:S(2)}) collective-permute-start(bf16[2,384,640]{2,1,0:T(8,128)(2,1)S(1)} %collective-permute-done.key.value), channel_id=1, source_target_pairs={{0,4},{1,5},{2,6},{3,7},{4,0},{5,1},{6,2},{7,3},{8,12},{9,13},{10,... | collective-permute-start | bytes 2949128 | tf_op jit(solution)/shard_map/ppermute | solution.py:595
  44.7 6.1 %shard_map.84 = (bf16[2,384,640]{2,1,0:T(8,128)(2,1)S(1)}, f32[384,640]{1,0:T(8,128)S(1)}, bf16[384,640]{1,0:T(8,128)(2,1)S(1)}, bf16[384,640]{1,0:T(8,128)(2,1)S(1)}, f32[8,128]{1,0:T(8,128)S(1)}) custom-call(f32[8,128]{1,0:T(8,128)S(1)} %shard_map.80.info, bf16[384,1536]{1,0:T(8,128)(2,1)S(1)} %bitcast.32, bf16[384,1536]{1,0:T(8,128)(2,1)S(1)} %bitcast.24, ...), custom_call_target="tpu_custom_call" | custom-call | flops 1 | bytes 1 | tf_op jit(solution)/shard_map/pallas_call | solution.py:496
  50.8 4.1 %shard_map.85 = (bf16[2,384,640]{2,1,0:T(8,128)(2,1)S(1)}, f32[384,640]{1,0:T(8,128)S(1)}, bf16[384,640]{1,0:T(8,128)(2,1)S(1)}, bf16[384,640]{1,0:T(8,128)(2,1)S(1)}, f32[8,128]{1,0:T(8,128)S(1)}) custom-call(f32[8,128]{1,0:T(8,128)S(1)} %shard_map.80.info, ...), custom_call_target="tpu_custom_call", output_to_operand_aliasing={{0}: (12, {}), {1}: (13, {}), {2}: (14, {}), {3}: (15, {})} | custom-call | flops 1 | bytes 1 | tf_op jit(solution)/shard_map/pallas_call | solution.py:496
  55.7 4.6 %shard_map.87 = (bf16[384,896]{1,0:T(8,128)(2,1)S(1)}, bf16[2,384,256]{2,1,0:T(8,128)(2,1)S(1)}, bf16[2,384,256]{2,1,0:T(8,128)(2,1)S(1)}, bf16[2,384,256]{2,1,0:T(8,128)(2,1)S(1)}, f32[8,128]{1,0:T(8,128)S(1)}) custom-call(f32[8,128]{1,0:T(8,128)S(1)} %shard_map.80.info, bf16[384,1536]{1,0:T(8,128)(2,1)S(1)} %bitcast.34, bf16[384,1536]{1,0:T(8,128)(2,1)S(1)} %bitcast.26, ...), custom_call_target="tpu_custom_call" | custom-call | flops 6000000000 | bytes 1 | tf_op jit(solution)/shard_map/pallas_call | solution.py:435
  60.3 5.7 %collective-permute-done.5.info.query.grad = bf16[2,400,640]{2,1,0:T(8,128)(2,1)S(1)} collective-permute-done((bf16[2,400,640]{2,1,0:T(8,128)(2,1)S(1)}, bf16[2,400,640]{2,1,0:T(8,128)(2,1)S(1)}, u32[]{:S(2)}, u32[]{:S(2)}) %collective-permute-start.5) | collective-permute-done | bytes 1024032 | tf_op jit(solution)/shard_map/ppermute | solution.py:614
  66.0 2.7 %collective-permute-start.20 = (bf16[2,384,256]{2,1,0:T(8,128)(2,1)S(1)}, bf16[2,384,256]{2,1,0:T(8,128)(2,1)S(1)}, u32[]{:S(2)}, u32[]{:S(2)}) collective-permute-start(bf16[2,384,256]{2,1,0:T(8,128)(2,1)S(1)} %get-tuple-element.73), channel_id=1, source_target_pairs={{0,4},{1,5},{2,6},{3,7},{4,0},{5,1},{6,2},{7,3},{8,12},{9,13},{10,... | collective-permute-start | bytes 1179656 | tf_op jit(solution)/shard_map/ppermute | solution.py:595
  68.7 11.4 %shard_map.88 = (bf16[384,640]{1,0:T(8,128)(2,1)S(1)}, bf16[2,384,640]{2,1,0:T(8,128)(2,1)S(1)}, bf16[2,384,640]{2,1,0:T(8,128)(2,1)S(1)}, bf16[2,384,640]{2,1,0:T(8,128)(2,1)S(1)}, f32[8,128]{1,0:T(8,128)S(1)}) custom-call(bf16[2,400,640]{2,1,0:T(8,128)(2,1)S(1)} %collective-permute-done.5.info.query.grad, ...), custom_call_target="tpu_custom_call" | custom-call | flops 6000000000 | bytes 1 | tf_op jit(solution)/shard_map/pallas_call | solution.py:435
  80.1 1.7 %collective-permute-start.13 = (bf16[2,384,640]{2,1,0:T(8,128)(2,1)S(1)}, bf16[2,384,640]{2,1,0:T(8,128)(2,1)S(1)}, u32[]{:S(2)}, u32[]{:S(2)}) collective-permute-start(bf16[2,384,640]{2,1,0:T(8,128)(2,1)S(1)} %get-tuple-element.63), channel_id=1, source_target_pairs={{0,4},{1,5},{2,6},{3,7},{4,0},{5,1},{6,2},{7,3},{8,12},{9,13},{10,... | collective-permute-start | bytes 2949128 | tf_op jit(solution)/shard_map/ppermute | solution.py:595
  81.7 1.4 %shard_map.89 = bf16[384,896]{1,0:T(8,128)(2,1)S(1)} custom-call(f32[8,128]{1,0:T(8,128)S(1)} %shard_map.80.info, bf16[384,1536]{1,0:T(8,128)(2,1)S(1)} %bitcast.35, f32[384,640]{1,0:T(8,128)S(1)} %get-tuple-element.65.own, bf16[384,640]{1,0:T(8,128)(2,1)S(1)} %collective-permute-done.15.from_even, ...), custom_call_target="tpu_custom_call", output_to_operand_aliasing={{}: (5, {})} | custom-call | flops 20000000000 | bytes 1 | tf_op jit(solution)/shard_map/pallas_call | solution.py:522
  83.3 1.5 %collective-permute-start.18 = (f32[2,128]{1,0:T(2,128)S(1)}, f32[2,128]{1,0:T(2,128)S(1)}, u32[]{:S(2)}, u32[]{:S(2)}) collective-permute-start(f32[2,128]{1,0:T(2,128)S(1)} %slice.12), channel_id=1, source_target_pairs={{0,16},{16,0},{1,17},{17,1},{2,18},{18,2},{3,19},{19,3},{4,20},{20... | collective-permute-start | bytes 3080 | tf_op jit(solution)/shard_map/ppermute | solution.py:614
  84.8 2.1 %collective-permute-done.18 = f32[2,128]{1,0:T(2,128)S(1)} collective-permute-done((f32[2,128]{1,0:T(2,128)S(1)}, f32[2,128]{1,0:T(2,128)S(1)}, u32[]{:S(2)}, u32[]{:S(2)}) %collective-permute-start.18) | collective-permute-done | bytes 1056 | tf_op jit(solution)/shard_map/ppermute | solution.py:614
  86.9 1.5 %collective-permute-start.19 = (bf16[384,896]{1,0:T(8,128)(2,1)S(1)}, bf16[384,896]{1,0:T(8,128)(2,1)S(1)}, u32[]{:S(2)}, u32[]{:S(2)}) collective-permute-start(bf16[384,896]{1,0:T(8,128)(2,1)S(1)} %shard_map.89), channel_id=1, source_target_pairs={{0,16},{16,0},{1,17},{17,1},{2,18},{18,2},{3,19},{19,3},{4,20},{20... | collective-permute-start | bytes 2064392 | tf_op jit(solution)/shard_map/ppermute | solution.py:614
  90.9 1.5 %collective-permute-start.24 = (f32[2,128]{1,0:T(2,128)S(1)}, f32[2,128]{1,0:T(2,128)S(1)}, u32[]{:S(2)}, u32[]{:S(2)}) collective-permute-start(f32[2,128]{1,0:T(2,128)S(1)} %add.24), channel_id=1, source_target_pairs={{0,2},{1,3},{2,0},{3,1},{4,6},{5,7},{6,4},{7,5},{8,10},{9,11},{10,... | collective-permute-start | bytes 3080 | tf_op jit(solution)/shard_map/ppermute | solution.py:622
  92.4 2.0 %collective-permute-done.24 = f32[2,128]{1,0:T(2,128)S(1)} collective-permute-done((f32[2,128]{1,0:T(2,128)S(1)}, f32[2,128]{1,0:T(2,128)S(1)}, u32[]{:S(2)}, u32[]{:S(2)}) %collective-permute-start.24) | collective-permute-done | bytes 1056 | tf_op jit(solution)/shard_map/ppermute | solution.py:622
  94.5 2.1 %collective-permute-start.25 = (f32[2,128]{1,0:T(2,128)S(1)}, f32[2,128]{1,0:T(2,128)S(1)}, u32[]{:S(2)}, u32[]{:S(2)}) collective-permute-start(f32[2,128]{1,0:T(2,128)S(1)} %add.25), channel_id=1, source_target_pairs={{0,4},{4,0},{8,12},{12,8},{1,5},{5,1},{9,13},{13,9},{2,6},{6,2},{1... | collective-permute-start | bytes 3080 | tf_op jit(solution)/shard_map/ppermute | solution.py:622
  96.6 1.8 %shard_map.91.rest_2_ = bf16[3,384,1536]{2,1,0:T(8,128)(2,1)} custom-call(bf16[2,384,640]{2,1,0:T(8,128)(2,1)S(1)} %collective-permute-done.17.refs_0_, bf16[384,640]{1,0:T(8,128)(2,1)S(1)} %get-tuple-element.75.refs_1_), custom_call_target="tpu_custom_call" | custom-call | flops 1 | bytes 1 | tf_op jit(solution)/shard_map/pallas_call | solution.py:539
  98.4 7.9 %collective-permute-done.25 = f32[2,128]{1,0:T(2,128)S(1)} collective-permute-done((f32[2,128]{1,0:T(2,128)S(1)}, f32[2,128]{1,0:T(2,128)S(1)}, u32[]{:S(2)}, u32[]{:S(2)}) %collective-permute-start.25) | collective-permute-done | bytes 1056 | tf_op jit(solution)/shard_map/ppermute | solution.py:622
  106.3 1.9 %collective-permute-start.26 = (f32[2,128]{1,0:T(2,128)S(1)}, f32[2,128]{1,0:T(2,128)S(1)}, u32[]{:S(2)}, u32[]{:S(2)}) collective-permute-start(f32[2,128]{1,0:T(2,128)S(1)} %add.26), channel_id=1, source_target_pairs={{0,8},{4,12},{8,0},{12,4},{1,9},{5,13},{9,1},{13,5},{2,10},{6,14},... | collective-permute-start | bytes 3080 | tf_op jit(solution)/shard_map/ppermute | solution.py:622
  108.2 2.5 %collective-permute-done.26 = f32[2,128]{1,0:T(2,128)S(1)} collective-permute-done((f32[2,128]{1,0:T(2,128)S(1)}, f32[2,128]{1,0:T(2,128)S(1)}, u32[]{:S(2)}, u32[]{:S(2)}) %collective-permute-start.26) | collective-permute-done | bytes 1056 | tf_op jit(solution)/shard_map/ppermute | solution.py:622
  112.2 3.0 %shard_map.92 = bf16[3,384,1536]{2,1,0:T(8,128)(2,1)} custom-call(bf16[2,400,640]{2,1,0:T(8,128)(2,1)S(1)} %collective-permute-done.5.info.query.grad, bf16[2,384,640]{2,1,0:T(8,128)(2,1)S(1)} %collective-permute-done.key.value, bf16[2,384,640]{2,1,0:T(8,128)(2,1)S(1)} %get-tuple-element.62.own, ...), custom_call_target="tpu_custom_call", output_to_operand_aliasing={{}: (7, {})} | custom-call | flops 1 | bytes 1 | tf_op jit(solution)/shard_map/pallas_call | solution.py:558
  (60 shorter events, 10.3 us)
Async XLA Ops:
  3.2 4.8 %copy-start = (bf16[1,1,1,384,1536]{4,3,2,1,0:T(8,128)(2,1)S(1)}, bf16[1,1,1,384,1536]{4,3,2,1,0:T(8,128)(2,1)}, u32[]{:S(2)}) copy-start(bf16[1,1,1,384,1536]{4,3,2,1,0:T(8,128)(2,1)} %param.7) | copy-start | bytes 3538948
  3.2 4.8 %copy-start.5 = (bf16[1,1,1,384,1536]{4,3,2,1,0:T(8,128)(2,1)S(1)}, bf16[1,1,1,384,1536]{4,3,2,1,0:T(8,128)(2,1)}, u32[]{:S(2)}) copy-start(bf16[1,1,1,384,1536]{4,3,2,1,0:T(8,128)(2,1)} %param.8) | copy-start | bytes 3538948
  3.3 9.9 %collective-permute-start.4 = (bf16[2,384,384]{2,1,0:T(8,128)(2,1)S(1)}, bf16[2,384,384]{2,1,0:T(8,128)(2,1)S(1)}, u32[]{:S(2)}, u32[]{:S(2)}) collective-permute-start(bf16[2,384,384]{2,1,0:T(8,128)(2,1)S(1)} %shard_map.77), channel_id=1, source_target_pairs={{0,1},{1,0},{2,3},{3,2},{4,8},{5,9},{6,10},{7,11},{8,4},{9,5},{10,... | collective-permute-start | bytes 1769480 | tf_op jit(solution)/shard_map/ppermute | solution.py:595
  3.8 18.3 %collective-permute-start.3 = (bf16[2,384,384]{2,1,0:T(8,128)(2,1)S(1)}, bf16[2,384,384]{2,1,0:T(8,128)(2,1)S(1)}, u32[]{:S(2)}, u32[]{:S(2)}) collective-permute-start(bf16[2,384,384]{2,1,0:T(8,128)(2,1)S(1)} %shard_map.77), channel_id=1, source_target_pairs={{0,4},{1,5},{2,6},{3,7},{4,0},{5,1},{6,2},{7,3},{8,12},{9,13},{10,... | collective-permute-start | bytes 1769480 | tf_op jit(solution)/shard_map/ppermute | solution.py:595
  9.2 3.3 %copy-start.6 = (f32[1,2,128]{2,1,0:T(2,128)S(1)}, f32[1,2,128]{2,1,0:T(2,128)}, u32[]{:S(2)}) copy-start(f32[1,2,128]{2,1,0:T(2,128)} %param.10) | copy-start | bytes 3076
  9.2 3.3 %copy-start.7 = (s32[1,1,1,3]{3,2,1,0:T(1,128)S(1)}, s32[1,1,1,3]{3,2,1,0:T(1,128)}, u32[]{:S(2)}) copy-start(s32[1,1,1,3]{3,2,1,0:T(1,128)} %param.11) | copy-start | bytes 40
  9.3 18.1 %collective-permute-start.2 = (bf16[2,384,256]{2,1,0:T(8,128)(2,1)S(1)}, bf16[2,384,256]{2,1,0:T(8,128)(2,1)S(1)}, u32[]{:S(2)}, u32[]{:S(2)}) collective-permute-start(bf16[2,384,256]{2,1,0:T(8,128)(2,1)S(1)} %shard_map.79), channel_id=1, source_target_pairs={{0,1},{1,0},{2,3},{3,2},{4,8},{5,9},{6,10},{7,11},{8,4},{9,5},{10,... | collective-permute-start | bytes 1179656 | tf_op jit(solution)/shard_map/ppermute | solution.py:595
  9.4 21.2 %collective-permute-start.1 = (bf16[2,384,256]{2,1,0:T(8,128)(2,1)S(1)}, bf16[2,384,256]{2,1,0:T(8,128)(2,1)S(1)}, u32[]{:S(2)}, u32[]{:S(2)}) collective-permute-start(bf16[2,384,256]{2,1,0:T(8,128)(2,1)S(1)} %shard_map.79), channel_id=1, source_target_pairs={{0,4},{1,5},{2,6},{3,7},{4,0},{5,1},{6,2},{7,3},{8,12},{9,13},{10,... | collective-permute-start | bytes 1179656 | tf_op jit(solution)/shard_map/ppermute | solution.py:595
  11.0 23.4 %collective-permute-start = (bf16[2,384,640]{2,1,0:T(8,128)(2,1)S(1)}, bf16[2,384,640]{2,1,0:T(8,128)(2,1)S(1)}, u32[]{:S(2)}, u32[]{:S(2)}) collective-permute-start(bf16[2,384,640]{2,1,0:T(8,128)(2,1)S(1)} %shard_map.78), channel_id=1, source_target_pairs={{0,16},{16,0},{1,17},{17,1},{2,18},{18,2},{3,19},{19,3},{4,20},{20... | collective-permute-start | bytes 2949128 | tf_op jit(solution)/shard_map/ppermute | solution.py:614
  13.1 11.5 %copy-start.4 = (bf16[1,1,1,384,1536]{4,3,2,1,0:T(8,128)(2,1)S(1)}, bf16[1,1,1,384,1536]{4,3,2,1,0:T(8,128)(2,1)}, u32[]{:S(2)}) copy-start(bf16[1,1,1,384,1536]{4,3,2,1,0:T(8,128)(2,1)} %param.6) | copy-start | bytes 3538948
  22.1 19.8 %collective-permute-start.10 = (bf16[2,384,256]{2,1,0:T(8,128)(2,1)S(1)}, bf16[2,384,256]{2,1,0:T(8,128)(2,1)S(1)}, u32[]{:S(2)}, u32[]{:S(2)}) collective-permute-start(bf16[2,384,256]{2,1,0:T(8,128)(2,1)S(1)} %shard_map.86), channel_id=1, source_target_pairs={{0,1},{1,0},{2,3},{3,2},{4,8},{5,9},{6,10},{7,11},{8,4},{9,5},{10,... | collective-permute-start | bytes 1179656 | tf_op jit(solution)/shard_map/ppermute | solution.py:595
  22.1 19.8 %collective-permute-start.9 = (bf16[2,384,256]{2,1,0:T(8,128)(2,1)S(1)}, bf16[2,384,256]{2,1,0:T(8,128)(2,1)S(1)}, u32[]{:S(2)}, u32[]{:S(2)}) collective-permute-start(bf16[2,384,256]{2,1,0:T(8,128)(2,1)S(1)} %shard_map.86), channel_id=1, source_target_pairs={{0,4},{1,5},{2,6},{3,7},{4,0},{5,1},{6,2},{7,3},{8,12},{9,13},{10,... | collective-permute-start | bytes 1179656 | tf_op jit(solution)/shard_map/ppermute | solution.py:595
  32.4 8.0 %collective-permute-start.8 = (f32[40,384]{1,0:T(8,128)S(1)}, f32[40,384]{1,0:T(8,128)S(1)}, u32[]{:S(2)}, u32[]{:S(2)}) collective-permute-start(f32[40,384]{1,0:T(8,128)S(1)} %get-tuple-element.50), channel_id=1, source_target_pairs={{0,8},{1,9},{2,10},{3,11},{4,12},{5,13},{6,14},{7,15},{8,0},{9,1},... | collective-permute-start | bytes 184328 | tf_op jit(solution)/shard_map/ppermute | solution.py:595
  34.4 7.5 %collective-permute-start.7 = (f32[40,384]{1,0:T(8,128)S(1)}, f32[40,384]{1,0:T(8,128)S(1)}, u32[]{:S(2)}, u32[]{:S(2)}) collective-permute-start(f32[40,384]{1,0:T(8,128)S(1)} %get-tuple-element.49.sent_odd), channel_id=1, source_target_pairs={{0,1},{1,0},{2,3},{3,2},{4,8},{5,9},{6,10},{7,11},{8,4},{9,5},{10,... | collective-permute-start | bytes 184328 | tf_op jit(solution)/shard_map/ppermute | solution.py:595
  34.4 7.5 %collective-permute-start.6 = (f32[40,384]{1,0:T(8,128)S(1)}, f32[40,384]{1,0:T(8,128)S(1)}, u32[]{:S(2)}, u32[]{:S(2)}) collective-permute-start(f32[40,384]{1,0:T(8,128)S(1)} %get-tuple-element.47.sent_even), channel_id=1, source_target_pairs={{0,4},{1,5},{2,6},{3,7},{4,0},{5,1},{6,2},{7,3},{8,12},{9,13},{10,... | collective-permute-start | bytes 184328 | tf_op jit(solution)/shard_map/ppermute | solution.py:595
  40.5 25.6 %collective-permute-start.5 = (bf16[2,400,640]{2,1,0:T(8,128)(2,1)S(1)}, bf16[2,400,640]{2,1,0:T(8,128)(2,1)S(1)}, u32[]{:S(2)}, u32[]{:S(2)}) collective-permute-start(bf16[2,400,640]{2,1,0:T(8,128)(2,1)S(1)} %shard_map.83), channel_id=1, source_target_pairs={{0,16},{16,0},{1,17},{17,1},{2,18},{18,2},{3,19},{19,3},{4,20},{20... | collective-permute-start | bytes 3072008 | tf_op jit(solution)/shard_map/ppermute | solution.py:614
  42.0 24.1 %collective-permute-start.12 = (bf16[2,384,640]{2,1,0:T(8,128)(2,1)S(1)}, bf16[2,384,640]{2,1,0:T(8,128)(2,1)S(1)}, u32[]{:S(2)}, u32[]{:S(2)}) collective-permute-start(bf16[2,384,640]{2,1,0:T(8,128)(2,1)S(1)} %collective-permute-done.key.value), channel_id=1, source_target_pairs={{0,1},{1,0},{2,3},{3,2},{4,8},{5,9},{6,10},{7,11},{8,4},{9,5},{10,... | collective-permute-start | bytes 2949128 | tf_op jit(solution)/shard_map/ppermute | solution.py:595
  42.0 26.6 %collective-permute-start.11 = (bf16[2,384,640]{2,1,0:T(8,128)(2,1)S(1)}, bf16[2,384,640]{2,1,0:T(8,128)(2,1)S(1)}, u32[]{:S(2)}, u32[]{:S(2)}) collective-permute-start(bf16[2,384,640]{2,1,0:T(8,128)(2,1)S(1)} %collective-permute-done.key.value), channel_id=1, source_target_pairs={{0,4},{1,5},{2,6},{3,7},{4,0},{5,1},{6,2},{7,3},{8,12},{9,13},{10,... | collective-permute-start | bytes 2949128 | tf_op jit(solution)/shard_map/ppermute | solution.py:595
  55.0 28.3 %collective-permute-start.17 = (bf16[2,384,640]{2,1,0:T(8,128)(2,1)S(1)}, bf16[2,384,640]{2,1,0:T(8,128)(2,1)S(1)}, u32[]{:S(2)}, u32[]{:S(2)}) collective-permute-start(bf16[2,384,640]{2,1,0:T(8,128)(2,1)S(1)} %get-tuple-element.55), channel_id=1, source_target_pairs={{0,16},{16,0},{1,17},{17,1},{2,18},{18,2},{3,19},{19,3},{4,20},{20... | collective-permute-start | bytes 2949128 | tf_op jit(solution)/shard_map/ppermute | solution.py:614
  55.7 24.3 %collective-permute-start.15 = (bf16[384,640]{1,0:T(8,128)(2,1)S(1)}, bf16[384,640]{1,0:T(8,128)(2,1)S(1)}, u32[]{:S(2)}, u32[]{:S(2)}) collective-permute-start(bf16[384,640]{1,0:T(8,128)(2,1)S(1)} %get-tuple-element.66), channel_id=1, source_target_pairs={{0,4},{1,5},{2,6},{3,7},{4,0},{5,1},{6,2},{7,3},{8,12},{9,13},{10,... | collective-permute-start | bytes 1474568 | tf_op jit(solution)/shard_map/ppermute | solution.py:595
  66.0 15.7 %collective-permute-start.16 = (bf16[384,640]{1,0:T(8,128)(2,1)S(1)}, bf16[384,640]{1,0:T(8,128)(2,1)S(1)}, u32[]{:S(2)}, u32[]{:S(2)}) collective-permute-start(bf16[384,640]{1,0:T(8,128)(2,1)S(1)} %get-tuple-element.67), channel_id=1, source_target_pairs={{0,1},{1,0},{2,3},{3,2},{4,8},{5,9},{6,10},{7,11},{8,4},{9,5},{10,... | collective-permute-start | bytes 1474568 | tf_op jit(solution)/shard_map/ppermute | solution.py:595
  66.0 22.3 %collective-permute-start.20 = (bf16[2,384,256]{2,1,0:T(8,128)(2,1)S(1)}, bf16[2,384,256]{2,1,0:T(8,128)(2,1)S(1)}, u32[]{:S(2)}, u32[]{:S(2)}) collective-permute-start(bf16[2,384,256]{2,1,0:T(8,128)(2,1)S(1)} %get-tuple-element.73), channel_id=1, source_target_pairs={{0,4},{1,5},{2,6},{3,7},{4,0},{5,1},{6,2},{7,3},{8,12},{9,13},{10,... | collective-permute-start | bytes 1179656 | tf_op jit(solution)/shard_map/ppermute | solution.py:595
  68.7 19.7 %collective-permute-start.21 = (bf16[2,384,256]{2,1,0:T(8,128)(2,1)S(1)}, bf16[2,384,256]{2,1,0:T(8,128)(2,1)S(1)}, u32[]{:S(2)}, u32[]{:S(2)}) collective-permute-start(bf16[2,384,256]{2,1,0:T(8,128)(2,1)S(1)} %get-tuple-element.74), channel_id=1, source_target_pairs={{0,1},{1,0},{2,3},{3,2},{4,8},{5,9},{6,10},{7,11},{8,4},{9,5},{10,... | collective-permute-start | bytes 1179656 | tf_op jit(solution)/shard_map/ppermute | solution.py:595
  80.1 32.2 %collective-permute-start.13 = (bf16[2,384,640]{2,1,0:T(8,128)(2,1)S(1)}, bf16[2,384,640]{2,1,0:T(8,128)(2,1)S(1)}, u32[]{:S(2)}, u32[]{:S(2)}) collective-permute-start(bf16[2,384,640]{2,1,0:T(8,128)(2,1)S(1)} %get-tuple-element.63), channel_id=1, source_target_pairs={{0,4},{1,5},{2,6},{3,7},{4,0},{5,1},{6,2},{7,3},{8,12},{9,13},{10,... | collective-permute-start | bytes 2949128 | tf_op jit(solution)/shard_map/ppermute | solution.py:595
  81.7 30.5 %collective-permute-start.14 = (bf16[2,384,640]{2,1,0:T(8,128)(2,1)S(1)}, bf16[2,384,640]{2,1,0:T(8,128)(2,1)S(1)}, u32[]{:S(2)}, u32[]{:S(2)}) collective-permute-start(bf16[2,384,640]{2,1,0:T(8,128)(2,1)S(1)} %get-tuple-element.64), channel_id=1, source_target_pairs={{0,1},{1,0},{2,3},{3,2},{4,8},{5,9},{6,10},{7,11},{8,4},{9,5},{10,... | collective-permute-start | bytes 2949128 | tf_op jit(solution)/shard_map/ppermute | solution.py:595
  83.3 3.6 %collective-permute-start.18 = (f32[2,128]{1,0:T(2,128)S(1)}, f32[2,128]{1,0:T(2,128)S(1)}, u32[]{:S(2)}, u32[]{:S(2)}) collective-permute-start(f32[2,128]{1,0:T(2,128)S(1)} %slice.12), channel_id=1, source_target_pairs={{0,16},{16,0},{1,17},{17,1},{2,18},{18,2},{3,19},{19,3},{4,20},{20... | collective-permute-start | bytes 3080 | tf_op jit(solution)/shard_map/ppermute | solution.py:614
  86.9 25.4 %collective-permute-start.19 = (bf16[384,896]{1,0:T(8,128)(2,1)S(1)}, bf16[384,896]{1,0:T(8,128)(2,1)S(1)}, u32[]{:S(2)}, u32[]{:S(2)}) collective-permute-start(bf16[384,896]{1,0:T(8,128)(2,1)S(1)} %shard_map.89), channel_id=1, source_target_pairs={{0,16},{16,0},{1,17},{17,1},{2,18},{18,2},{3,19},{19,3},{4,20},{20... | collective-permute-start | bytes 2064392 | tf_op jit(solution)/shard_map/ppermute | solution.py:614
  89.1 23.1 %collective-permute-start.22 = (bf16[2,384,256]{2,1,0:T(8,128)(2,1)S(1)}, bf16[2,384,256]{2,1,0:T(8,128)(2,1)S(1)}, u32[]{:S(2)}, u32[]{:S(2)}) collective-permute-start(bf16[2,384,256]{2,1,0:T(8,128)(2,1)S(1)} %shard_map.90), channel_id=1, source_target_pairs={{0,16},{16,0},{1,17},{17,1},{2,18},{18,2},{3,19},{19,3},{4,20},{20... | collective-permute-start | bytes 1179656 | tf_op jit(solution)/shard_map/ppermute | solution.py:614
  89.7 1.1 collective-permute-start.23
  90.9 3.6 %collective-permute-start.24 = (f32[2,128]{1,0:T(2,128)S(1)}, f32[2,128]{1,0:T(2,128)S(1)}, u32[]{:S(2)}, u32[]{:S(2)}) collective-permute-start(f32[2,128]{1,0:T(2,128)S(1)} %add.24), channel_id=1, source_target_pairs={{0,2},{1,3},{2,0},{3,1},{4,6},{5,7},{6,4},{7,5},{8,10},{9,11},{10,... | collective-permute-start | bytes 3080 | tf_op jit(solution)/shard_map/ppermute | solution.py:622
  94.5 11.8 %collective-permute-start.25 = (f32[2,128]{1,0:T(2,128)S(1)}, f32[2,128]{1,0:T(2,128)S(1)}, u32[]{:S(2)}, u32[]{:S(2)}) collective-permute-start(f32[2,128]{1,0:T(2,128)S(1)} %add.25), channel_id=1, source_target_pairs={{0,4},{4,0},{8,12},{12,8},{1,5},{5,1},{9,13},{13,9},{2,6},{6,2},{1... | collective-permute-start | bytes 3080 | tf_op jit(solution)/shard_map/ppermute | solution.py:622
  106.3 4.5 %collective-permute-start.26 = (f32[2,128]{1,0:T(2,128)S(1)}, f32[2,128]{1,0:T(2,128)S(1)}, u32[]{:S(2)}, u32[]{:S(2)}) collective-permute-start(f32[2,128]{1,0:T(2,128)S(1)} %add.26), channel_id=1, source_target_pairs={{0,8},{4,12},{8,0},{12,4},{1,9},{5,13},{9,1},{13,5},{2,10},{6,14},... | collective-permute-start | bytes 3080 | tf_op jit(solution)/shard_map/ppermute | solution.py:622
  (3 other events, 3.8 us)
